TPU v7x, 32 devices: a whole 2x2x4 slice. The times are simulated.
32 devices in a mesh: loop: 16 (over z, x, core), own: 2 (over y).
Axes of the slice: x: 2, y: 2, z: 4, core: 2. Of those that a mesh axis runs over, the one named last changes fastest.
Arguments:
- factor_start: float32 [4096, 128], P(('loop', 'own')), may hold values from -6 to 6
- activity: float32 [4096], P(('loop', 'own')), may hold values from 0.05 to 2
- word_factors: bfloat16 [16, 8, 128, 128], P('loop'), may hold values from -0.09375 to 0.09375
- sub_factors: bfloat16 [2048, 128], replicated, may hold values from -6 to 6
- ratings: bfloat16 [16, 2, 16, 8, 128, 128], P('loop', 'own'), may hold values from -6 to 6
- user_tile: int32 [16, 2, 16, 8], P('loop', 'own'), may hold values from 0 to 1
- word_tile: int32 [16, 2, 16, 8], P('loop', 'own'), may hold values from 0 to 7
- subreddit: int32 [16, 2, 16, 8], P('loop', 'own'), may hold values from 0 to 2047
- counts: int32 [16, 2, 16], P('loop', 'own'), may hold values from 1 to 8
- runs: int32 [16, 2, 16, 8, 2, 128], P('loop', 'own'), may hold values from 0 to 128, as said below
Outputs:
- solution: float32 [4096, 128], P(('loop', 'own'))
- residual: float32 [4096, 128], P(('loop', 'own'))
Inputs may be any that keep to these rules, and one draw needn't show every extreme that they name: runs[..., 0, a] is the first observed column of row a of a block and runs[..., 1, a] the number of observed columns, counted cyclically from it; each block has a row observed in full.
All inputs are finite; a program needn't handle non-finite values.
Results may differ from a plain program's by a relative error of at most 0.03.
Values may be sent and summed in bfloat16 or wider, within the bound.
No kernel may reach another device: no remote copies, remote signals or barrier semaphores. Data moves between devices by JAX's collectives and lax.ppermute only.
A program may use at most 128 MiB of HBM per device.

v0:
```python
import jax
import jax.numpy as jnp
from jax import lax
from jax.sharding import PartitionSpec as P

TILE = 128
UT = 2
SLOTS = 8
ITERS = 2


ridge = 0.05


def on_device(
    factor_start,
    activity,
    word_factors,
    sub_factors,
    ratings,
    user_tile,
    word_tile,
    subreddit,
    counts,
    runs,
):
    group_rows = UT * TILE
    groups = lax.axis_size("loop")
    word_rows = word_factors[0][word_tile[0, 0]]
    sub_rows = sub_factors[subreddit[0, 0]]
    products = (word_rows.astype(jnp.float32) * sub_rows[:, :, None, :].astype(jnp.float32)).astype(
        jnp.bfloat16
    )
    slot_live = jnp.arange(SLOTS)[None, :] < counts[0, 0][:, None]
    first_col = runs[0, 0][:, :, 0, :]
    run_len = runs[0, 0][:, :, 1, :]
    columns = jnp.arange(TILE)
    observed = (
        (columns[None, None, None, :] - first_col[:, :, :, None]) % TILE < run_len[:, :, :, None]
    ) & slot_live[:, :, None, None]
    selector = (user_tile[0, 0][:, :, None] == jnp.arange(UT)[None, None, :]).astype(jnp.bfloat16)
    values = ratings[0, 0]

    def group_terms(span, gathered, with_values):
        rows_part = gathered
        rows_part = rows_part.reshape(span, UT, TILE, rows_part.shape[-1])
        picked = jnp.einsum(
            "gsu,guar->gsar", selector, rows_part, preferred_element_type=jnp.float32
        ).astype(jnp.bfloat16)
        scores = jnp.einsum("gsar,gscr->gsac", picked, products, preferred_element_type=jnp.float32)
        if with_values:
            scores = values.astype(jnp.float32) - scores
        weights = jnp.where(observed, scores, 0.0).astype(jnp.bfloat16)
        rows_out = jnp.einsum(
            "gsac,gscr->gsar", weights, products, preferred_element_type=jnp.float32
        )
        summed = jnp.einsum("gsu,gsar->guar", selector.astype(jnp.float32), rows_out)
        return summed.reshape(span * group_rows, summed.shape[-1])

    def make_summand(gathered, with_values):
        whole = lax.axis_size("loop") * group_rows // group_rows
        extra = 0
        span = min(groups, whole + extra)
        result = group_terms(span, gathered, with_values)
        return result

    def data_part(vector, with_values):
        halves = vector.astype(jnp.bfloat16)
        grouped = lax.all_gather(halves, "own", axis=0, tiled=True)
        gathered = lax.all_gather(grouped, "loop", axis=0, tiled=True)
        loop_sums = lax.psum_scatter(
            make_summand(gathered, with_values), "loop", scatter_dimension=0, tiled=True
        )
        return lax.psum_scatter(loop_sums, "own", scatter_dimension=0, tiled=True)

    def global_sum(value):
        return lax.psum(value, ("loop", "own"))

    weight_rows = activity[:, None]
    solution = factor_start
    residual = weight_rows * data_part(solution, True) - ridge * solution
    direction = residual
    norm_now = global_sum(jnp.sum(residual * residual))
    for iteration in range(ITERS):
        image = weight_rows * data_part(direction, False) + ridge * direction
        step_size = norm_now / global_sum(jnp.sum(direction * image))
        solution = solution + step_size * direction
        residual = residual - step_size * image
        if iteration + 1 < ITERS:
            norm_next = global_sum(jnp.sum(residual * residual))
            direction = residual + norm_next / norm_now * direction
            norm_now = norm_next
    return (solution, residual)


def solution(mesh):
    placed = (
        P(("loop", "own"), None),
        P(("loop", "own")),
        P("loop", None, None, None),
        P(),
        P("loop", "own", None, None, None, None),
        P("loop", "own", None, None),
        P("loop", "own", None, None),
        P("loop", "own", None, None),
        P("loop", "own", None),
        P("loop", "own", None, None, None, None),
    )
    return jax.shard_map(
        on_device,
        mesh=mesh,
        in_specs=placed,
        out_specs=(P(("loop", "own"), None), P(("loop", "own"), None)),
        check_vma=False,
    )
```

profile of v0, /device:TPU:0, one launch (start us, length us, event | category | flops | bytes accessed | tf_op | source)
XLA Modules:
  0.0 563.4 jit_solution(13797846498303750438)
XLA Ops:
  7.2 0.9 convert_element_type.53
  8.1 5.6 all_gather.18
  13.8 0.0 reduce-scatter.7.cloned.1.call-start
  13.8 0.7 compare_select_fusion.1
  14.5 0.1 copy.16
  14.6 0.1 reshape.121
  14.7 0.7 compare_select_fusion
  15.4 0.1 copy.17
  15.4 0.1 reshape.129
  15.5 0.8 copy.15
  16.3 0.7 gather_fusion.1
  17.0 4.0 gather_fusion
  21.0 0.1 iota_compare_fusion.7
  21.1 0.1 fusion.67
  21.2 32.4 %all-gather.4.cloned.1.call-done = bf16[4096,128]{1,0:T(8,128)(2,1)} async-done(((bf16[256,128]{1,0:T(8,128)(2,1)}), bf16[4096,128]{1,0:T(8,128)(2,1)}) %all-gather.4.cloned.1.call-update) | async-done | bytes 1048592 | tf_op jit(solution)/shard_map/all_gather | solution.py:70
  53.6 4.4 fusion.36
  58.0 12.9 %fusion.20 = bf16[16,8,128,128]{3,2,1,0:T(8,128)(2,1)} fusion(bf16[1,1,16,8,128,128]{5,4,3,2,1,0:T(8,128)(2,1)} %param.14, bf16[16,8,128,128]{3,1,2,0:T(8,128)(2,1)} %fusion.36, bf16[16,8,128,128]{3,2,1,0:T(8,128)(2,1)} %bitcast.50, f32[16,8,128]{2,1,0:T(8,128)S(1)} %bitcast_convert_fusion, s32[16,8,128]{2,1,0:T(8,128)S(1)} %bitcast.60, ...), kind=kOutput, calls=%fused_computation.32 | convolution fusion | flops 1124073472 | bytes 16973952 | tf_op jit(solution)/shard_map/gsac,gscr->gsar/dot_general | solution.py:54
  71.0 5.0 fusion.9
  75.9 1.6 copy.18
  77.6 60.5 %reduce-scatter.7.cloned.1.call-done = f32[256,128]{1,0:T(8,128)} async-done(((f32[4096,128]{1,0:T(8,128)}), f32[256,128]{1,0:T(8,128)}) %reduce-scatter.7.cloned.1.call-update) | async-done | bytes 131088 | tf_op jit(solution)/shard_map/reduce_scatter | solution.py:71
  138.2 11.6 %reduce-scatter.9.cloned.1.call-done = f32[128,128]{1,0:T(8,128)} async-done(((f32[256,128]{1,0:T(8,128)}), f32[128,128]{1,0:T(8,128)}) %reduce-scatter.9.cloned.1.call-update) | async-done | bytes 65552 | tf_op jit(solution)/shard_map/reduce_scatter | solution.py:74
  149.8 0.9 fusion.66
  150.7 4.7 all_gather.20
  155.5 0.2 reduce-scatter.11.cloned.1.call-start
  155.7 37.9 %all-gather.6.cloned.1.call-done = bf16[4096,128]{1,0:T(8,128)(2,1)} async-done(((bf16[256,128]{1,0:T(8,128)(2,1)}), bf16[4096,128]{1,0:T(8,128)(2,1)}) %all-gather.6.cloned.1.call-update) | async-done | bytes 1048592 | tf_op jit(solution)/shard_map/all_gather | solution.py:70
  193.6 4.4 fusion.34
  198.0 11.3 %fusion.15 = bf16[16,8,128,128]{3,2,1,0:T(8,128)(2,1)} fusion(bf16[16,8,128,128]{3,1,2,0:T(8,128)(2,1)} %fusion.34, bf16[16,8,128,128]{3,2,1,0:T(8,128)(2,1)} %bitcast.51, f32[16,8,128]{2,1,0:T(8,128)S(1)} %bitcast_convert_fusion, s32[16,8,128]{2,1,0:T(8,128)S(1)} %bitcast.61, s32[16,8,128]{2,1,0:T(8,128)S(1)} %bitcast.58, ...), kind=kOutput, calls=%fused_computation.27 | convolution fusion | flops 1119879168 | bytes 12779648 | tf_op jit(solution)/shard_map/gsac,gscr->gsar/dot_general | solution.py:54
  209.3 5.0 fusion.7
  214.3 1.6 copy.19
  216.0 60.6 %reduce-scatter.11.cloned.1.call-done = f32[256,128]{1,0:T(8,128)} async-done(((f32[4096,128]{1,0:T(8,128)}), f32[256,128]{1,0:T(8,128)}) %reduce-scatter.11.cloned.1.call-update) | async-done | bytes 131088 | tf_op jit(solution)/shard_map/reduce_scatter | solution.py:71
  276.6 11.2 %reduce-scatter.13.cloned.1.call-done = f32[128,128]{1,0:T(8,128)} async-done(((f32[256,128]{1,0:T(8,128)}), f32[128,128]{1,0:T(8,128)}) %reduce-scatter.13.cloned.1.call-update) | async-done | bytes 65552 | tf_op jit(solution)/shard_map/reduce_scatter | solution.py:74
  287.9 1.5 multiply_reduce_fusion.2
  289.4 39.6 %all-reduce = (f32[]{:T(128)}, f32[]{:T(128)}) all-reduce(f32[]{:T(128)} %get-tuple-element.3, f32[]{:T(128)} %get-tuple-element.2), channel_id=1, replica_groups=mesh['loop'=16,'own'=2] {'loop','own'}, use_global_device_ids=true, to_apply=%region_3.4 | all-reduce | flops 2 | bytes 16 | tf_op jit(solution)/shard_map/psum | solution.py:77
  330.3 1.5 multiply_reduce_fusion.1
  331.9 41.4 %psum.30 = f32[]{:T(128)} all-reduce(f32[]{:T(128)} %multiply_reduce_fusion.1), channel_id=1, replica_groups=mesh['loop'=16,'own'=2] {'loop','own'}, use_global_device_ids=true, to_apply=%region_9.10 | all-reduce | flops 1 | bytes 8 | tf_op jit(solution)/shard_map/psum | solution.py:77
  374.6 0.9 fusion.47
  375.5 5.1 all_gather.22
  380.6 0.3 reduce-scatter.15.cloned.1.call-start
  380.9 37.4 %all-gather.8.cloned.1.call-done = bf16[4096,128]{1,0:T(8,128)(2,1)} async-done(((bf16[256,128]{1,0:T(8,128)(2,1)}), bf16[4096,128]{1,0:T(8,128)(2,1)}) %all-gather.8.cloned.1.call-update) | async-done | bytes 1048592 | tf_op jit(solution)/shard_map/all_gather | solution.py:70
  418.3 4.4 fusion.32
  422.7 11.3 %fusion.16 = bf16[16,8,128,128]{3,2,1,0:T(8,128)(2,1)} fusion(bf16[16,8,128,128]{3,1,2,0:T(8,128)(2,1)} %fusion.32, bf16[16,8,128,128]{3,2,1,0:T(8,128)(2,1)} %bitcast.52, f32[16,8,128]{2,1,0:T(8,128)S(1)} %bitcast_convert_fusion, s32[16,8,128]{2,1,0:T(8,128)S(1)} %bitcast.62, s32[16,8,128]{2,1,0:T(8,128)S(1)} %bitcast.59, ...), kind=kOutput, calls=%fused_computation.28 | convolution fusion | flops 1119879168 | bytes 12779648 | tf_op jit(solution)/shard_map/gsac,gscr->gsar/dot_general | solution.py:54
  434.1 5.0 fusion.5
  439.0 1.6 copy.20
  440.7 60.5 %reduce-scatter.15.cloned.1.call-done = f32[256,128]{1,0:T(8,128)} async-done(((f32[4096,128]{1,0:T(8,128)}), f32[256,128]{1,0:T(8,128)}) %reduce-scatter.15.cloned.1.call-update) | async-done | bytes 131088 | tf_op jit(solution)/shard_map/reduce_scatter | solution.py:71
  501.3 11.6 %reduce-scatter.17.cloned.1.call-done = f32[128,128]{1,0:T(8,128)} async-done(((f32[256,128]{1,0:T(8,128)}), f32[128,128]{1,0:T(8,128)}) %reduce-scatter.17.cloned.1.call-update) | async-done | bytes 65552 | tf_op jit(solution)/shard_map/reduce_scatter | solution.py:74
  512.9 1.5 multiply_reduce_fusion
  514.5 39.5 %psum.31 = f32[]{:T(128)} all-reduce(f32[]{:T(128)} %multiply_reduce_fusion), channel_id=1, replica_groups=mesh['loop'=16,'own'=2] {'loop','own'}, use_global_device_ids=true, to_apply=%region_13.14 | all-reduce | flops 1 | bytes 8 | tf_op jit(solution)/shard_map/psum | solution.py:77
  555.3 1.6 multiply_subtract_fusion
  (30 shorter events, 0.4 us)
Async XLA Ops:
  7.2 9.1 %copy-start = (bf16[2048,128]{1,0:T(8,128)(2,1)S(1)}, bf16[2048,128]{1,0:T(8,128)(2,1)}, u32[]{:S(2)}) copy-start(bf16[2048,128]{1,0:T(8,128)(2,1)} %param.13) | copy-start | bytes 1572868
  7.2 46.4 %all-gather.4.cloned.1.call-start = ((), (), s32[]{:S(2)}) async-start(), calls=%async_computation.6 | async-start | bytes 1114112 | tf_op jit(solution)/shard_map/all_gather | solution.py:70
  13.8 124.4 %reduce-scatter.7.cloned.1.call-start = ((), (), s32[]{:S(2)}) async-start(), calls=%async_computation.7 | async-start | bytes 2228224 | tf_op jit(solution)/shard_map/reduce_scatter | solution.py:71
  17.0 4.0 copy-start.5
  17.0 4.1 copy-start.3
  75.9 73.9 %copy-start.2 = (f32[128,128]{1,0:T(8,128)S(1)}, f32[128,128]{1,0:T(8,128)}, u32[]{:S(2)}) copy-start(f32[128,128]{1,0:T(8,128)} %param.10) | copy-start | bytes 196612
  75.9 73.9 %copy-start.4 = (f32[128]{0:T(128)S(1)}, f32[128]{0:T(128)}, u32[]{:S(2)}) copy-start(f32[128]{0:T(128)} %param.11) | copy-start | bytes 1540
  77.6 72.2 %reduce-scatter.9.cloned.1.call-start = ((), (), s32[]{:S(2)}) async-start(), calls=%async_computation.8 | async-start | bytes 196608 | tf_op jit(solution)/shard_map/reduce_scatter | solution.py:74
  138.2 55.4 %all-gather.6.cloned.1.call-start = ((), (), s32[]{:S(2)}) async-start(), calls=%async_computation.9 | async-start | bytes 1114112 | tf_op jit(solution)/shard_map/all_gather | solution.py:70
  155.5 121.1 %reduce-scatter.11.cloned.1.call-start = ((), (), s32[]{:S(2)}) async-start(), calls=%async_computation.10 | async-start | bytes 2228224 | tf_op jit(solution)/shard_map/reduce_scatter | solution.py:71
  215.9 72.0 %reduce-scatter.13.cloned.1.call-start = ((), (), s32[]{:S(2)}) async-start(), calls=%async_computation.11 | async-start | bytes 196608 | tf_op jit(solution)/shard_map/reduce_scatter | solution.py:74
  276.6 141.7 %all-gather.8.cloned.1.call-start = ((), (), s32[]{:S(2)}) async-start(), calls=%async_computation.12 | async-start | bytes 1114112 | tf_op jit(solution)/shard_map/all_gather | solution.py:70
  380.6 120.6 %reduce-scatter.15.cloned.1.call-start = ((), (), s32[]{:S(2)}) async-start(), calls=%async_computation.13 | async-start | bytes 2228224 | tf_op jit(solution)/shard_map/reduce_scatter | solution.py:71
  439.0 73.9 %copy-start.1 = (f32[128,128]{1,0:T(8,128)S(1)}, f32[128,128]{1,0:T(8,128)}, u32[]{:S(2)}) copy-start(f32[128,128]{1,0:T(8,128)} %reduce-scatter.13.cloned.1.call-done) | copy-start | bytes 196612
  440.7 72.2 %reduce-scatter.17.cloned.1.call-start = ((), (), s32[]{:S(2)}) async-start(), calls=%async_computation.14 | async-start | bytes 196608 | tf_op jit(solution)/shard_map/reduce_scatter | solution.py:74
Sparse Core Ops, SparseCore 0:
  13.9 39.7 all-gather.3
  77.7 60.4 reduce-scatter.6
  140.5 9.2 reduce-scatter.8
  155.6 37.9 all-gather.5
  216.0 60.4 reduce-scatter.10
  278.6 9.1 reduce-scatter.12
  380.8 37.4 all-gather.7
  440.8 60.4 reduce-scatter.14
  503.6 9.2 reduce-scatter.16
where the time goes:
time: 564 us; the launch traced here: 563 us
  waiting for transfers between devices  324 us (57%)
  blocking collectives  136 us (24%)
  matrix products  63.7 us (11%)
  between operations  18 us (3%)
  local copies, waits for them, and re-layouts  10.7 us (2%)
  other arithmetic  10.4 us (2%)
    reduce_scatter x3, waiting for transfers between devices, data_part(): lax.psum_scatter(make_summand(gathered, with_values), 'loop', scatter_dim...  182 us
    psum x3, blocking collectives, global_sum(): return lax.psum(value, ('loop', 'own'))  120 us
    all_gather x3, waiting for transfers between devices, data_part(): gathered = lax.all_gather(grouped, 'loop', axis=0, tiled=True)  108 us
    dot_general x3, matrix products, group_terms(): jnp.einsum('gsac,gscr->gsar', weights, products, preferred_element_type=j...  35.6 us
    reduce_scatter x3, waiting for transfers between devices, data_part(): return lax.psum_scatter(loop_sums, 'own', scatter_dimension=0, tiled=True)  34.4 us
    all_gather x3, blocking collectives, data_part(): grouped = lax.all_gather(halves, 'own', axis=0, tiled=True)  15.4 us
    dot_general x3, matrix products, group_terms(): jnp.einsum('gsu,gsar->guar', selector.astype(jnp.float32), rows_out)  14.9 us
    dot_general x3, matrix products, group_terms(): jnp.einsum('gsu,guar->gsar', selector, rows_part, preferred_element_type=...  13.3 us
  transfers between devices with their start and end apart: 9, of which 9 were waited for; matrix products, arithmetic and copies ran while one was open for 1% of the time, Pallas kernels for 0%

commit v1 on v0

v1 whole, which is shorter than its diff:
```python
import jax
import jax.numpy as jnp
from jax import lax
from jax.experimental import pallas as pl
from jax.experimental.pallas import tpu as pltpu
from jax.sharding import PartitionSpec as P

AXES = ("loop", "own")
CHUNK = 4
ridge = 0.05
f32 = jnp.float32
bf16 = jnp.bfloat16


def dot_nt(left, right):
    return lax.dot_general(left, right, (((1,), (1,)), ((), ())), preferred_element_type=f32)


def dot_nn(left, right):
    return jnp.dot(left, right, preferred_element_type=f32)


def mask_columns(first, length, tile):
    column = lax.broadcasted_iota(jnp.int32, (tile, first.shape[-1]), 0)
    inside = ((column - first) & (tile - 1)) < length
    return jnp.where(inside, 1.0, 0.0).astype(bf16)


def rhs_kernel(counts, user_tile, word_tile, ratings, runs, sub_rows, words, out):
    slots, tile = ratings.shape[1], ratings.shape[2]
    tiles = out.shape[1] // tile
    group = pl.program_id(0)
    eye = (
        lax.broadcasted_iota(jnp.int32, (tile, tile), 0)
        == lax.broadcasted_iota(jnp.int32, (tile, tile), 1)
    ).astype(f32).astype(bf16)
    products, weights = [], []
    for s in range(slots):
        block = group * slots + s
        rows = words[word_tile[block]].astype(f32)
        products.append((rows * sub_rows[0, s : s + 1, :]).astype(bf16))
        first = runs[0, 2 * s : 2 * s + 1, :]
        length = runs[0, 2 * s + 1 : 2 * s + 2, :]
        seen = dot_nt(eye, mask_columns(first, length, tile))
        value = seen * ratings[0, s].astype(f32)
        live = s < counts[group]
        parts = []
        for u in range(tiles):
            mine = jnp.where(live & (user_tile[block] == u), 1.0, 0.0)
            parts.append((value * mine).astype(bf16))
        weights.append(jnp.concatenate(parts, axis=0))
    total = dot_nn(jnp.concatenate(weights, axis=1), jnp.concatenate(products, axis=0))
    out[0] = total.astype(out.dtype)


def rhs_partial(ratings, runs, sub_rows, words, counts, user_tile, word_tile, tiles):
    groups, slots, tile, _ = ratings.shape
    rank = words.shape[-1]
    return pl.pallas_call(
        rhs_kernel,
        grid_spec=pltpu.PrefetchScalarGridSpec(
            num_scalar_prefetch=3,
            grid=(groups,),
            in_specs=[
                pl.BlockSpec((1, slots, tile, tile), lambda g, *_: (g, 0, 0, 0)),
                pl.BlockSpec((1, 2 * slots, tile), lambda g, *_: (g, 0, 0)),
                pl.BlockSpec((1, slots, rank), lambda g, *_: (g, 0, 0)),
                pl.BlockSpec(words.shape, lambda g, *_: (0, 0, 0)),
            ],
            out_specs=pl.BlockSpec((1, tiles * tile, rank), lambda g, *_: (g, 0, 0)),
        ),
        out_shape=jax.ShapeDtypeStruct((groups, tiles * tile, rank), bf16),
        compiler_params=pltpu.CompilerParams(vmem_limit_bytes=32 * 2**20),
        cost_estimate=pl.CostEstimate(
            flops=2 * ratings.size * rank * 2, bytes_accessed=2 * ratings.size, transcendentals=0
        ),
        name="rhs",
    )(
        counts,
        user_tile.reshape(-1),
        word_tile.reshape(-1),
        ratings,
        runs.reshape(groups, 2 * slots, tile),
        sub_rows.astype(f32),
        words,
    )


def steps_kernel(
    flags, word_index, start, activity, received, words,
    first_out, second_out, third_out, dots_out,
    chosen, runs, subs, masks, products,
):
    own_rows, rank = start.shape
    sources = received.shape[0]
    tile = words.shape[1]
    slots = flags.shape[0] // sources
    blocks = flags.shape[0]
    cached = products is not None

    def gather_one(src, total):
        runs[pl.ds(pl.multiple_of(src * 2 * slots, 2 * slots), 2 * slots), :] = received[
            src, own_rows : own_rows + 2 * slots, :
        ].astype(f32)
        subs[pl.ds(pl.multiple_of(src * slots, slots), slots), :] = received[
            src, own_rows + 2 * slots : own_rows + 4 * slots, :
        ].astype(f32)[:slots]
        return total + received[src, :own_rows, :].astype(f32)

    rhs = lax.fori_loop(0, sources, gather_one, jnp.zeros((own_rows, rank), f32))

    def choose(j, n):
        chosen[n] = j
        return n + flags[j]

    used = lax.fori_loop(0, blocks, choose, 0)
    chunks = lax.div(used + CHUNK - 1, CHUNK)

    offset = lax.rem(lax.axis_index("own") * own_rows, tile)
    pick = (
        lax.broadcasted_iota(jnp.int32, (own_rows, tile), 0) + offset
        == lax.broadcasted_iota(jnp.int32, (own_rows, tile), 1)
    ).astype(f32).astype(bf16)

    def product(i):
        j = jnp.where(i < used, chosen[jnp.minimum(i, blocks - 1)], 0)
        return j, (words[word_index[j]].astype(f32) * subs[pl.ds(j, 1), :]).astype(bf16)

    def build(chunk, carry):
        parts = []
        for b in range(CHUNK):
            i = chunk * CHUNK + b
            j, block = product(i)
            if cached:
                products[chunk, b * tile : (b + 1) * tile, :] = block
            first = runs[pl.ds(2 * j, 1), :].astype(jnp.int32)
            length = runs[pl.ds(2 * j + 1, 1), :].astype(jnp.int32)
            length = jnp.where(i < used, length, 0)
            parts.append(dot_nt(pick, mask_columns(first, length, tile)).astype(bf16))
        masks[chunk] = jnp.concatenate(parts, axis=1)
        return carry

    lax.fori_loop(0, chunks, build, 0)

    def split(value):
        high = value.astype(bf16)
        low = (value - high.astype(f32)).astype(bf16)
        return jnp.concatenate([high, low], axis=0)

    def gram(vector):
        stacked = split(vector)

        def body(chunk, total):
            if cached:
                block = products[chunk]
            else:
                block = jnp.concatenate(
                    [product(chunk * CHUNK + b)[1] for b in range(CHUNK)], axis=0
                )
            scores = dot_nt(stacked, block)
            scores = scores[:own_rows] + scores[own_rows:]
            weights = scores * masks[chunk].astype(f32)
            return total + dot_nn(split(weights), block)

        total = lax.fori_loop(0, chunks, body, jnp.zeros((2 * own_rows, rank), f32))
        return total[:own_rows] + total[own_rows:]

    scale = activity[...]
    first = scale * (rhs - gram(start[...])) - ridge * start[...]
    second = scale * gram(first) + ridge * first
    third = scale * gram(second) + ridge * second
    first_out[...] = first
    second_out[...] = second
    third_out[...] = third
    pairs = [(first, first), (first, second), (second, second), (first, third), (second, third)]
    for k, (a, b) in enumerate(pairs):
        dots_out[k : k + 1, :] = jnp.sum(a * b, axis=0, keepdims=True)
    dots_out[len(pairs) :, :] = jnp.zeros((8 - len(pairs), rank), f32)


def krylov(flags, word_index, start, activity, received, words):
    own_rows, rank = start.shape
    blocks = flags.shape[0]
    tile = words.shape[1]
    chunks = -(-blocks // CHUNK)
    cached = blocks * tile * rank * 2 <= 16 * 2**20
    whole = pl.BlockSpec(memory_space=pltpu.VMEM)
    scalars = pl.BlockSpec(memory_space=pltpu.SMEM)
    vector = jax.ShapeDtypeStruct((own_rows, rank), f32)
    scratch = [
        pltpu.SMEM((blocks + 1,), jnp.int32),
        pltpu.VMEM((2 * blocks, tile), f32),
        pltpu.VMEM((blocks, rank), f32),
        pltpu.VMEM((chunks, own_rows, CHUNK * tile), bf16),
    ]
    kernel = steps_kernel
    if cached:
        scratch.append(pltpu.VMEM((chunks, CHUNK * tile, rank), bf16))
    else:

        def kernel(*refs):
            steps_kernel(*refs, None)

    return pl.pallas_call(
        kernel,
        in_specs=[scalars, scalars, whole, whole, whole, whole],
        out_specs=[whole] * 4,
        out_shape=[vector, vector, vector, jax.ShapeDtypeStruct((8, rank), f32)],
        scratch_shapes=scratch,
        compiler_params=pltpu.CompilerParams(vmem_limit_bytes=48 * 2**20),
        name="krylov",
    )(flags, word_index, start, activity, received, words)


def on_device(
    factor_start,
    activity,
    word_factors,
    sub_factors,
    ratings,
    user_tile,
    word_tile,
    subreddit,
    counts,
    runs,
):
    own_rows, rank = factor_start.shape
    owners = lax.axis_size("own")
    _, _, groups, slots, tile, _ = ratings.shape
    word_tiles = word_factors.shape[1]
    tiles = own_rows * owners // tile
    devices = groups * owners

    words = lax.all_gather(word_factors[0], "loop", axis=0, tiled=True)

    sub_rows = sub_factors[subreddit[0, 0]]
    partial = rhs_partial(
        ratings[0, 0], runs[0, 0], sub_rows, word_factors[0], counts[0, 0],
        user_tile[0, 0], word_tile[0, 0], tiles,
    )
    live = jnp.arange(slots)[None, :] < counts[0, 0][:, None]
    owner_tile = (jnp.arange(owners) * own_rows) // tile
    wanted = live[:, None, :] & (user_tile[0, 0][:, None, :] == owner_tile[None, :, None])
    facts = jnp.concatenate(
        [wanted.astype(bf16), jnp.broadcast_to(word_tile[0, 0][:, None, :], wanted.shape).astype(bf16)],
        axis=-1,
    )
    facts = jnp.pad(facts[:, :, None, :], ((0, 0), (0, 0), (0, slots - 1), (0, rank - 2 * slots)))

    def to_owners(value):
        return jnp.broadcast_to(value[:, None], (groups, owners) + value.shape[1:])

    message = jnp.concatenate(
        [
            partial.reshape(groups, owners, own_rows, rank),
            to_owners(runs[0, 0].reshape(groups, 2 * slots, tile).astype(bf16)),
            to_owners(sub_rows),
            facts,
        ],
        axis=2,
    ).reshape(devices, own_rows + 4 * slots, rank)
    received = lax.all_to_all(message, AXES, 0, 0, tiled=True)

    got = received[:, own_rows + 3 * slots, : 2 * slots].astype(jnp.int32)
    flags = got[:, :slots].reshape(-1)
    shard = jnp.arange(devices, dtype=jnp.int32)[:, None] // owners
    word_index = (got[:, slots:] + word_tiles * shard).reshape(-1)

    first, second, third, dots = krylov(
        flags, word_index, factor_start, activity[:, None], received, words
    )
    everyone = lax.all_to_all(
        jnp.broadcast_to(dots[None], (devices,) + dots.shape), AXES, 0, 0, tiled=True
    )
    sums = jnp.sum(everyone, axis=(0, 2))
    rr, rq, qq, rz, qz = (sums[k] for k in range(5))
    step0 = rr / rq
    next_rr = rr - 2.0 * step0 * rq + step0 * step0 * qq
    grow = 1.0 + next_rr / rr
    slope = grow * (grow * rq - step0 * (rz + qq)) + step0 * step0 * qz
    step1 = next_rr / slope
    solution = factor_start + (step0 + step1 * grow) * first - (step1 * step0) * second
    residual = first - (step0 + step1 * grow) * second + (step1 * step0) * third
    return (solution, residual)


def solution(mesh):
    placed = (
        P(("loop", "own"), None),
        P(("loop", "own")),
        P("loop", None, None, None),
        P(),
        P("loop", "own", None, None, None, None),
        P("loop", "own", None, None),
        P("loop", "own", None, None),
        P("loop", "own", None, None),
        P("loop", "own", None),
        P("loop", "own", None, None, None, None),
    )
    return jax.shard_map(
        on_device,
        mesh=mesh,
        in_specs=placed,
        out_specs=(P(("loop", "own"), None), P(("loop", "own"), None)),
        check_vma=False,
    )
```

time: 564 us -> 150 us (0.27)
  waiting for transfers between devices: 324 us -> 49.3 us
  blocking collectives: 136 us -> 18.5 us
  matrix products: 63.7 us -> 0 us
  Pallas kernels: 0 us -> 36.4 us
  starting transfers between devices: 0.77 us -> 7.34 us
    reduce_scatter x6 -> x0, waiting for transfers between devices: 216 us -> none  [the longest x3 182 us: data_part(): lax.psum_scatter(make_summand(gathered, with_values), 'loop', scatter_dim...]
    psum x3 -> x0, blocking collectives: 120 us -> none  [global_sum(): return lax.psum(value, ('loop', 'own'))]
    all_gather x3 -> x1, waiting for transfers between devices: 108 us -> 0.02 us  [on_device(): words = lax.all_gather(word_factors[0], 'loop', axis=0, tiled=True)]
    dot_general x9 -> x0, matrix products: 63.7 us -> none  [the longest x3 35.6 us: group_terms(): jnp.einsum('gsac,gscr->gsar', weights, products, preferred_element_type=j...]
    all_to_all x0 -> x1, waiting for transfers between devices: none -> 48.6 us  [on_device(): received = lax.all_to_all(message, AXES, 0, 0, tiled=True)]
    pallas_call x0 -> x2, Pallas kernels: none -> 36.4 us  [the longest x1 27.8 us: krylov(): pl.pallas_call(kernel, in_specs=[scalars, scalars, whole, whole, whole, w...]
    all_to_all x0 -> x1, blocking collectives: none -> 18.5 us  [on_device(): lax.all_to_all(jnp.broadcast_to(dots[None], (devices,) + dots.shape), AXE...]
    all_gather x3 -> x0, blocking collectives: 15.4 us -> none  [data_part(): grouped = lax.all_gather(halves, 'own', axis=0, tiled=True)]
  transfers between devices with their start and end apart: 9 -> 2, of which waited for: 9 -> 1; matrix products, arithmetic and copies ran while one was open for 1% -> 6% of each run, Pallas kernels for 0% -> 6%
where the time goes in v1:
time: 150 us; the launch traced here: 149 us
  waiting for transfers between devices  49.3 us (33%)
  Pallas kernels  36.4 us (24%)
  between operations  20.7 us (14%)
  blocking collectives  18.5 us (12%)
  local copies, waits for them, and re-layouts  11.3 us (8%)
  starting transfers between devices  7.34 us (5%)
  other arithmetic  5.32 us (4%)
    all_to_all x1, waiting for transfers between devices, on_device(): received = lax.all_to_all(message, AXES, 0, 0, tiled=True)  48.6 us
    pallas_call x1, Pallas kernels, krylov(): pl.pallas_call(kernel, in_specs=[scalars, scalars, whole, whole, whole, w...  27.8 us
    all_to_all x1, blocking collectives, on_device(): lax.all_to_all(jnp.broadcast_to(dots[None], (devices,) + dots.shape), AXE...  18.5 us
    pallas_call x1, Pallas kernels, rhs_partial(): pl.pallas_call(rhs_kernel, grid_spec=pltpu.PrefetchScalarGridSpec(num_sca...  8.6 us
    unnamed x19, local copies, waits for them, and re-layouts  8.43 us
    all_to_all x1, starting transfers between devices, on_device(): received = lax.all_to_all(message, AXES, 0, 0, tiled=True)  7.31 us
  transfers between devices with their start and end apart: 2, of which 1 were waited for; matrix products, arithmetic and copies ran while one was open for 6% of the time, Pallas kernels for 6%

profile of v1, /device:TPU:0, one launch (start us, length us, event | category | flops | bytes accessed | tf_op | source)
XLA Modules:
  0.0 148.9 jit_solution(744383768155201499)
XLA Ops:
  7.2 0.0 copy-start
  7.2 0.0 all-gather.3.cloned.1.call-start
  7.2 0.7 all-gather.3.cloned.1.call-update
  7.9 0.7 compare_select_fusion
  8.6 0.1 copy.35
  8.7 0.1 reshape.140
  8.8 0.8 copy.33
  9.5 0.1 reshape_squeeze.10.user_tile
  9.6 0.8 copy.34
  10.4 0.1 reshape_squeeze.11.word_tile
  10.5 0.9 convert_element_type.29
  11.4 0.8 copy.36
  12.2 0.7 convert_bitcast_fusion
  12.8 0.1 copy.37
  12.9 0.7 iota_compare_fusion
  13.7 0.1 and_convert_fusion
  13.7 0.1 maximum_bitcast_fusion
  13.9 0.0 copy-done
  13.9 0.7 gather_fusion
  14.6 0.0 copy-start.2
  14.6 2.2 %copy-done.2 = bf16[1,1,16,8,128,128]{5,4,3,2,1,0:T(8,128)(2,1)S(1)} copy-done((bf16[1,1,16,8,128,128]{5,4,3,2,1,0:T(8,128)(2,1)S(1)}, bf16[1,1,16,8,128,128]{5,4,3,2,1,0:T(8,128)(2,1)}, u32[]{:S(2)}) %copy-start.2) | copy-done | bytes 4194328
  16.8 0.0 copy-start.3
  16.8 0.9 copy-done.3
  17.8 0.0 copy-start.4
  17.8 0.9 copy-done.4
  18.7 0.0 copy-start.6
  18.7 0.7 copy-done.6
  19.3 8.6 %rhs.1 = bf16[16,256,128]{2,1,0:T(8,128)(2,1)S(1)} custom-call(s32[16]{0:T(128)S(1)} %bitcast.40, s32[128]{0:T(128)S(1)} %reshape_squeeze.10.user_tile, s32[128]{0:T(128)S(1)} %reshape_squeeze.11.word_tile, bf16[16,8,128,128]{3,2,1,0:T(8,128)(2,1)S(1)} %bitcast.34, s32[16,16,128]{2,1,0:T(8,128)S(1)} %bitcast.38, ...), custom_call_target="tpu_custom_call" | custom-call | flops 1073741824 | bytes 4194304 | tf_op jit(solution)/shard_map/rhs/pallas_call | solution.py:59
  28.0 0.0 copy-start.7
  28.0 0.0 copy-start.5
  28.0 1.2 pad_maximum_fusion
  29.2 7.3 %all-to-all-start = ((bf16[32,160,128]{2,1,0:T(8,128)(2,1)}), bf16[32,160,128]{2,1,0:T(8,128)(2,1)S(1)}, u32[]{:S(2)}, u32[]{:S(2)}) async-start(bf16[32,160,128]{2,1,0:T(8,128)(2,1)} %pad_maximum_fusion), calls=%async_computation | async-start | bytes 2621440 | tf_op jit(solution)/shard_map/all_to_all | solution.py:262
  36.5 0.0 copy-done.7
  36.5 0.1 copy.40.activity
  36.7 48.6 %all-to-all-done.received = bf16[32,160,128]{2,1,0:T(8,128)(2,1)S(1)} async-done(((bf16[32,160,128]{2,1,0:T(8,128)(2,1)}), bf16[32,160,128]{2,1,0:T(8,128)(2,1)S(1)}, u32[]{:S(2)}, u32[]{:S(2)}) %all-to-all-start) | async-done | bytes 1310752 | tf_op jit(solution)/shard_map/all_to_all | solution.py:262
  85.3 0.1 slice_add_fusion
  85.3 0.1 reshape.135.flags
  85.4 0.1 reshape.136.word_index
  85.5 0.0 all-gather.3.cloned.1.call-done
  85.5 0.0 copy-done.5
  85.5 0.0 copy-start.1
  85.6 2.2 %copy-done.1 = bf16[1,128,128,128]{3,2,0,1:T(8,128)(2,1)S(1)} copy-done((bf16[1,128,128,128]{3,2,0,1:T(8,128)(2,1)S(1)}, bf16[1,128,128,128]{3,2,0,1:T(8,128)(2,1)}, u32[]{:S(2)}) %copy-start.1) | copy-done | bytes 4194328
  87.7 27.8 %krylov.1 = (f32[128,128]{1,0:T(8,128)S(1)}, f32[128,128]{1,0:T(8,128)S(1)}, f32[128,128]{1,0:T(8,128)S(1)}, f32[8,128]{1,0:T(8,128)S(1)}) custom-call(s32[256]{0:T(256)S(1)} %reshape.135.flags, s32[256]{0:T(256)S(1)} %reshape.136.word_index, f32[128,128]{1,0:T(8,128)S(1)} %copy-done.5, f32[128,1]{1,0:T(8,128)S(1)} %copy.40.activity, ...), custom_call_target="tpu_custom_call" | custom-call | tf_op jit(solution)/shard_map/krylov/pallas_call | solution.py:204
  115.6 18.5 %all_to_all.10 = f32[32,8,128]{2,1,0:T(8,128)S(1)} all-to-all(f32[32,8,128]{2,1,0:T(8,128)S(1)} %broadcast_in_dim.17), channel_id=1, replica_groups=mesh['loop'=16,'own'=2] {'loop','own'}, dimensions={0} | all-to-all | bytes 262144 | tf_op jit(solution)/shard_map/all_to_all | solution.py:272
  134.1 0.1 reduce_sum.9
  134.3 0.7 fusion.1
  141.4 0.7 multiply_add_fusion
  (11 shorter events, 0.1 us)
Async XLA Ops:
  7.2 6.7 %copy-start = (bf16[2048,128]{1,0:T(8,128)(2,1)S(1)}, bf16[2048,128]{1,0:T(8,128)(2,1)}, u32[]{:S(2)}) copy-start(bf16[2048,128]{1,0:T(8,128)(2,1)} %param.13) | copy-start | bytes 1572868
  7.2 78.3 %all-gather.3.cloned.1.call-start = ((), (), s32[]{:S(2)}) async-start(), calls=%async_computation.2 | async-start | bytes 4456448 | tf_op jit(solution)/shard_map/all_gather | solution.py:234
  14.6 2.2 %copy-start.2 = (bf16[1,1,16,8,128,128]{5,4,3,2,1,0:T(8,128)(2,1)S(1)}, bf16[1,1,16,8,128,128]{5,4,3,2,1,0:T(8,128)(2,1)}, u32[]{:S(2)}) copy-start(bf16[1,1,16,8,128,128]{5,4,3,2,1,0:T(8,128)(2,1)} %param.14) | copy-start | bytes 12582916
  16.8 0.9 copy-start.3
  17.8 0.9 copy-start.4
  18.7 0.7 copy-start.6
  28.0 8.5 %copy-start.7 = (f32[128]{0:T(128)S(1)}, f32[128]{0:T(128)}, u32[]{:S(2)}) copy-start(f32[128]{0:T(128)} %param.11) | copy-start | bytes 1540
  28.0 57.5 %copy-start.5 = (f32[128,128]{1,0:T(8,128)S(1)}, f32[128,128]{1,0:T(8,128)}, u32[]{:S(2)}) copy-start(f32[128,128]{1,0:T(8,128)} %start.1) | copy-start | bytes 196612
  29.2 56.0 %all-to-all-start = ((bf16[32,160,128]{2,1,0:T(8,128)(2,1)}), bf16[32,160,128]{2,1,0:T(8,128)(2,1)S(1)}, u32[]{:S(2)}, u32[]{:S(2)}) async-start(bf16[32,160,128]{2,1,0:T(8,128)(2,1)} %pad_maximum_fusion), calls=%async_computation | async-start | bytes 2621440 | tf_op jit(solution)/shard_map/all_to_all | solution.py:262
  85.5 2.2 %copy-start.1 = (bf16[1,128,128,128]{3,2,0,1:T(8,128)(2,1)S(1)}, bf16[1,128,128,128]{3,2,0,1:T(8,128)(2,1)}, u32[]{:S(2)}) copy-start(bf16[1,128,128,128]{3,2,0,1:T(8,128)(2,1)} %all-gather.3.cloned.1.call-done) | copy-start | bytes 12582916
Sparse Core Ops, SparseCore 0:
  10.2 73.1 all-gather.2

commit v2 on v1

v2 whole, which is shorter than its diff:
```python
import functools

import jax
import jax.numpy as jnp
from jax import lax
from jax.experimental import pallas as pl
from jax.experimental.pallas import tpu as pltpu
from jax.sharding import PartitionSpec as P

AXES = ("loop", "own")
CHUNK = 8
ridge = 0.05
f32 = jnp.float32
bf16 = jnp.bfloat16


def dot_nt(left, right):
    return lax.dot_general(left, right, (((1,), (1,)), ((), ())), preferred_element_type=f32)


def dot_nn(left, right):
    return jnp.dot(left, right, preferred_element_type=f32)


def mask_columns(first, length, tile):
    column = lax.broadcasted_iota(jnp.int32, (tile, first.shape[-1]), 0)
    inside = ((column - first) & (tile - 1)) < length
    return jnp.where(inside, 1.0, 0.0).astype(bf16)


def message_kernel(counts, user_tile, word_tile, subreddit, ratings, runs, words, subs, out, table):
    slots, tile = ratings.shape[1], ratings.shape[2]
    owners, rank = out.shape[1], out.shape[3]
    own_rows = out.shape[2] - 4 * slots
    tiles = owners * own_rows // tile
    group = pl.program_id(0)

    @pl.when(group == 0)
    def _():
        table[...] = subs[...].astype(f32)

    eye = (
        lax.broadcasted_iota(jnp.int32, (tile, tile), 0)
        == lax.broadcasted_iota(jnp.int32, (tile, tile), 1)
    ).astype(f32).astype(bf16)
    lane = lax.broadcasted_iota(jnp.int32, (1, rank), 1)
    products, weights, sub_rows, run_rows = [], [], [], []
    facts = [jnp.zeros((1, rank), f32) for _ in range(owners)]
    for s in range(slots):
        sub_row = table[pl.ds(subreddit[group, s], 1), :]
        sub_rows.append(sub_row)
        products.append((words[word_tile[group, s]].astype(f32) * sub_row).astype(bf16))
        pair = runs[0, s]
        run_rows.append(pair)
        seen = dot_nt(eye, mask_columns(pair[0:1], pair[1:2], tile))
        value = seen * ratings[0, s].astype(f32)
        live = s < counts[0, group]
        parts = []
        for u in range(tiles):
            mine = jnp.where(live & (user_tile[group, s] == u), 1.0, 0.0)
            parts.append((value * mine).astype(bf16))
        weights.append(jnp.concatenate(parts, axis=0))
        for o in range(owners):
            wanted = live & (user_tile[group, s] == (o * own_rows) // tile)
            facts[o] = facts[o] + jnp.where(lane == s, jnp.where(wanted, 1.0, 0.0), 0.0)
            facts[o] = facts[o] + jnp.where(
                lane == slots + s, word_tile[group, s].astype(f32), 0.0
            )
    total = dot_nn(jnp.concatenate(weights, axis=1), jnp.concatenate(products, axis=0))
    run_rows = jnp.concatenate(run_rows, axis=0).astype(f32).astype(out.dtype)
    for o in range(owners):
        out[0, o, :own_rows, :] = total[o * own_rows : (o + 1) * own_rows].astype(out.dtype)
        out[0, o, own_rows : own_rows + 2 * slots, :] = run_rows
        out[0, o, own_rows + 2 * slots :, :] = jnp.concatenate(
            sub_rows + [facts[o]] + [jnp.zeros((slots - 1, rank), f32)], axis=0
        ).astype(out.dtype)


def messages(counts, user_tile, word_tile, subreddit, ratings, runs, words, subs, owners, own_rows):
    groups, slots, tile, _ = ratings.shape
    rank = words.shape[-1]
    shape = (owners, own_rows + 4 * slots, rank)
    return pl.pallas_call(
        message_kernel,
        grid_spec=pltpu.PrefetchScalarGridSpec(
            num_scalar_prefetch=4,
            grid=(groups,),
            in_specs=[
                pl.BlockSpec((1, slots, tile, tile), lambda g, *_: (g, 0, 0, 0)),
                pl.BlockSpec((1, slots, 2, tile), lambda g, *_: (g, 0, 0, 0)),
                pl.BlockSpec(words.shape, lambda g, *_: (0, 0, 0)),
                pl.BlockSpec(subs.shape, lambda g, *_: (0, 0)),
            ],
            out_specs=pl.BlockSpec((1,) + shape, lambda g, *_: (g, 0, 0, 0)),
            scratch_shapes=[pltpu.VMEM(subs.shape, f32)],
        ),
        out_shape=jax.ShapeDtypeStruct((groups,) + shape, bf16),
        compiler_params=pltpu.CompilerParams(vmem_limit_bytes=32 * 2**20),
        cost_estimate=pl.CostEstimate(
            flops=2 * ratings.size * rank * 2, bytes_accessed=2 * ratings.size, transcendentals=0
        ),
        name="messages",
    )(counts, user_tile, word_tile, subreddit, ratings, runs, words, subs)


def steps_kernel(flags, word_index, start, activity, received, *refs, cached):
    own_rows, rank = start.shape
    sources, _, _ = received.shape
    blocks = flags.shape[0]
    slots = blocks // sources
    shards = len(refs) - 10 - int(cached)
    pieces = refs[:shards]
    first_out, second_out, third_out, dots_out = refs[shards : shards + 4]
    chosen, runs, subs, masks, words, arrived = refs[shards + 4 : shards + 10]
    products = refs[-1]
    word_tiles, tile, _ = pieces[0].shape

    copies = [
        pltpu.make_async_copy(
            piece, words.at[k * word_tiles : (k + 1) * word_tiles], arrived.at[k]
        )
        for k, piece in enumerate(pieces)
    ]
    for copy in copies:
        copy.start()

    def gather_one(src, total):
        runs[pl.ds(pl.multiple_of(src * 2 * slots, 2 * slots), 2 * slots), :] = received[
            src, own_rows : own_rows + 2 * slots, :
        ].astype(f32)
        subs[pl.ds(pl.multiple_of(src * slots, slots), slots), :] = received[
            src, own_rows + 2 * slots : own_rows + 4 * slots, :
        ].astype(f32)[:slots]
        return total + received[src, :own_rows, :].astype(f32)

    rhs = lax.fori_loop(0, sources, gather_one, jnp.zeros((own_rows, rank), f32))

    def choose(j, n):
        chosen[n] = j
        return n + flags[j]

    used = lax.fori_loop(0, blocks, choose, 0, unroll=8)
    chunks = lax.div(used + CHUNK - 1, CHUNK)

    offset = lax.rem(lax.axis_index("own") * own_rows, tile)
    pick = (
        lax.broadcasted_iota(jnp.int32, (own_rows, tile), 0) + offset
        == lax.broadcasted_iota(jnp.int32, (own_rows, tile), 1)
    ).astype(f32).astype(bf16)

    def block_at(i):
        return jnp.where(i < used, chosen[jnp.minimum(i, blocks - 1)], 0)

    def product(i):
        j = block_at(i)
        return (words[word_index[j]].astype(f32) * subs[pl.ds(j, 1), :]).astype(bf16)

    def build_masks(chunk, carry):
        parts = []
        for b in range(CHUNK):
            i = chunk * CHUNK + b
            j = block_at(i)
            first = runs[pl.ds(2 * j, 1), :].astype(jnp.int32)
            length = runs[pl.ds(2 * j + 1, 1), :].astype(jnp.int32)
            length = jnp.where(i < used, length, 0)
            parts.append(dot_nt(pick, mask_columns(first, length, tile)).astype(bf16))
        masks[chunk] = jnp.concatenate(parts, axis=1)
        return carry

    def build_products(chunk, carry):
        for b in range(CHUNK):
            products[chunk, b * tile : (b + 1) * tile, :] = product(chunk * CHUNK + b)
        return carry

    lax.fori_loop(0, chunks, build_masks, 0)
    for copy in copies:
        copy.wait()
    if cached:
        lax.fori_loop(0, chunks, build_products, 0)

    def gram(vector):
        rounded = vector.astype(bf16)

        def body(chunk, total):
            if cached:
                block = products[chunk]
            else:
                block = jnp.concatenate(
                    [product(chunk * CHUNK + b) for b in range(CHUNK)], axis=0
                )
            weights = dot_nt(rounded, block).astype(bf16) * masks[chunk]
            return total + dot_nn(weights, block)

        return lax.fori_loop(0, chunks, body, jnp.zeros((own_rows, rank), f32))

    def over_row(a, b):
        return jnp.sum(a * b, axis=1, keepdims=True)

    scale = activity[...]
    first = scale * (rhs - gram(start[...])) - ridge * start[...]
    second = scale * gram(first) + ridge * first
    norms, overlaps = over_row(first, first), over_row(first, second)
    share = jnp.where(norms > 0.0, overlaps / jnp.where(norms > 0.0, norms, 1.0), 0.0)
    rest = second - share * first
    third = scale * gram(rest) + ridge * rest + share * second
    first_out[...] = first
    second_out[...] = second
    third_out[...] = third
    rows = [norms, overlaps, over_row(second, second), over_row(first, third), over_row(second, third)]
    lane = lax.broadcasted_iota(jnp.int32, (1, rank), 1)
    line = jnp.zeros((1, rank), f32)
    for k, value in enumerate(rows):
        line = line + jnp.where(lane == k, jnp.sum(value, axis=0, keepdims=True), 0.0)
    dots_out[...] = jnp.broadcast_to(line[None], dots_out.shape)


def krylov(flags, word_index, start, activity, received, pieces):
    own_rows, rank = start.shape
    sources = received.shape[0]
    blocks = flags.shape[0]
    word_tiles, tile, _ = pieces[0].shape
    chunks = -(-blocks // CHUNK)
    cached = blocks * tile * rank * 2 <= 16 * 2**20
    whole = pl.BlockSpec(memory_space=pltpu.VMEM)
    scalars = pl.BlockSpec(memory_space=pltpu.SMEM)
    vector = jax.ShapeDtypeStruct((own_rows, rank), f32)
    scratch = [
        pltpu.SMEM((blocks + 1,), jnp.int32),
        pltpu.VMEM((2 * blocks, tile), f32),
        pltpu.VMEM((blocks, rank), f32),
        pltpu.VMEM((chunks, own_rows, CHUNK * tile), bf16),
        pltpu.VMEM((len(pieces) * word_tiles, tile, rank), bf16),
        pltpu.SemaphoreType.DMA((len(pieces),)),
    ]
    if cached:
        scratch.append(pltpu.VMEM((chunks, CHUNK * tile, rank), bf16))
    return pl.pallas_call(
        functools.partial(steps_kernel, cached=cached),
        in_specs=[scalars, scalars, whole, whole, whole]
        + [pl.BlockSpec(memory_space=pl.ANY)] * len(pieces),
        out_specs=[whole] * 4,
        out_shape=[vector, vector, vector, jax.ShapeDtypeStruct((sources, 1, rank), f32)],
        scratch_shapes=scratch,
        compiler_params=pltpu.CompilerParams(vmem_limit_bytes=48 * 2**20),
        name="krylov",
    )(flags, word_index, start, activity, received, *pieces)


def last_kernel(dots, start, first, second, third, solution_out, residual_out):
    line = dots[0]
    for k in range(1, dots.shape[0]):
        line = line + dots[k]
    rr, rq, qq, rz, qz = (line[:, k : k + 1] for k in range(5))
    step0 = rr / rq
    next_rr = rr - 2.0 * step0 * rq + step0 * step0 * qq
    grow = 1.0 + next_rr / rr
    slope = grow * (grow * rq - step0 * (rz + qq)) + step0 * step0 * qz
    step1 = next_rr / slope
    near, far = step0 + step1 * grow, step1 * step0
    solution_out[...] = start[...] + near * first[...] - far * second[...]
    residual_out[...] = first[...] - near * second[...] + far * third[...]


def last_step(dots, start, first, second, third):
    whole = pl.BlockSpec(memory_space=pltpu.VMEM)
    vector = jax.ShapeDtypeStruct(start.shape, f32)
    return pl.pallas_call(
        last_kernel,
        in_specs=[whole] * 5,
        out_specs=[whole] * 2,
        out_shape=[vector, vector],
        name="last_step",
    )(dots, start, first, second, third)


def ring_place(shard, chips):
    chip = shard // 2
    level, column = chip // 2, chip % 2
    return jnp.where(column == 0, level, chips - 1 - level)


def ring_gather(mine, shards):
    chips = shards // 2
    levels = chips // 2
    order = [2 * level for level in range(levels)] + [
        2 * level + 1 for level in reversed(range(levels))
    ]

    def shift(by):
        return [
            (2 * order[p] + core, 2 * order[(p + by) % chips] + core)
            for p in range(chips)
            for core in range(2)
        ]

    other = [(shard, shard ^ 1) for shard in range(shards)]
    up = down = mine
    held = {0: mine}
    for step in range(1, chips // 2 + 1):
        up = lax.ppermute(up, "loop", shift(1))
        held[chips - step] = up
        if step < chips - step:
            down = lax.ppermute(down, "loop", shift(-1))
            held[step] = down
    pieces = []
    for distance in range(chips):
        pieces += [held[distance], lax.ppermute(held[distance], "loop", other)]
    return pieces


def on_device(
    factor_start,
    activity,
    word_factors,
    sub_factors,
    ratings,
    user_tile,
    word_tile,
    subreddit,
    counts,
    runs,
):
    own_rows, rank = factor_start.shape
    owners, shards = lax.axis_size("own"), lax.axis_size("loop")
    _, _, groups, slots, tile, _ = ratings.shape
    word_tiles = word_factors.shape[1]
    devices = shards * owners

    pieces = ring_gather(word_factors[0], shards)
    message = messages(
        counts[0], user_tile[0, 0], word_tile[0, 0], subreddit[0, 0],
        ratings[0, 0], runs[0, 0], word_factors[0], sub_factors, owners, own_rows,
    ).reshape(devices, own_rows + 4 * slots, rank)
    received = lax.all_to_all(message, AXES, 0, 0, tiled=True)

    got = received[:, own_rows + 3 * slots, : 2 * slots].astype(jnp.int32)
    flags = got[:, :slots].reshape(-1)
    me = lax.axis_index("loop")
    chips = shards // 2
    shard = jnp.arange(devices, dtype=jnp.int32)[:, None] // owners
    distance = (ring_place(shard, chips) - ring_place(me, chips)) % chips
    piece = 2 * distance + (shard + me) % 2
    word_index = (got[:, slots:] + word_tiles * piece).reshape(-1)

    first, second, third, dots = krylov(
        flags, word_index, factor_start, activity[:, None], received, pieces
    )
    everyone = lax.all_to_all(dots, AXES, 0, 0, tiled=True)
    return tuple(last_step(everyone, factor_start, first, second, third))


def solution(mesh):
    placed = (
        P(("loop", "own"), None),
        P(("loop", "own")),
        P("loop", None, None, None),
        P(),
        P("loop", "own", None, None, None, None),
        P("loop", "own", None, None),
        P("loop", "own", None, None),
        P("loop", "own", None, None),
        P("loop", "own", None),
        P("loop", "own", None, None, None, None),
    )
    return jax.shard_map(
        on_device,
        mesh=mesh,
        in_specs=placed,
        out_specs=(P(("loop", "own"), None), P(("loop", "own"), None)),
        check_vma=False,
    )
```

time: 150 us -> 121 us (0.81)
  between operations: 20.7 us -> 0.77 us
  starting transfers between devices: 7.34 us -> 23.3 us
  waiting for transfers between devices: 49.3 us -> 41.8 us
  Pallas kernels: 36.4 us -> 29.5 us
  blocking collectives: 18.5 us -> 12.8 us
  other arithmetic: 5.32 us -> 0.73 us
    all_to_all x1, waiting for transfers between devices: 48.6 us -> 0.01 us  [on_device(): received = lax.all_to_all(message, AXES, 0, 0, tiled=True)]
    ppermute x0 -> x15, waiting for transfers between devices: none -> 41.8 us  [the longest x4 39.9 us: ring_gather(): up = lax.ppermute(up, 'loop', shift(1))]
    ppermute x0 -> x15, starting transfers between devices: none -> 16 us  [the longest x4 13.1 us: ring_gather(): up = lax.ppermute(up, 'loop', shift(1))]
    pallas_call x2 -> x3, Pallas kernels: 36.4 us -> 29.5 us  [the longest x1 17.1 us: krylov(): pl.pallas_call(functools.partial(steps_kernel, cached=cached), in_specs=[...]
    all_to_all x1, blocking collectives: 18.5 us -> 12.8 us  [on_device(): everyone = lax.all_to_all(dots, AXES, 0, 0, tiled=True)]
    squeeze x0 -> x3, local copies, waits for them, and re-layouts: none -> 2.27 us  [the longest x1 0.76 us: on_device(): user_tile[0, 0]]
    convert_element_type x4 -> x0, other arithmetic: 1.69 us -> none  [the longest x1 0.92 us: on_device(): runs[0, 0].reshape(groups, 2 * slots, tile).astype(bf16)]
    unnamed x19 -> x22, local copies, waits for them, and re-layouts: 8.43 us -> 7.59 us
  transfers between devices with their start and end apart: 2 -> 16, of which waited for: 1 -> 5; matrix products, arithmetic and copies ran while one was open for 6% -> 2% of each run, Pallas kernels for 6% -> 0%
where the time goes in v2:
time: 121 us
  waiting for transfers between devices  41.8 us (35%)
  Pallas kernels  29.5 us (24%)
  starting transfers between devices  23.3 us (19%)
  blocking collectives  12.8 us (11%)
  local copies, waits for them, and re-layouts  11.6 us (10%)
    ppermute x4, waiting for transfers between devices, ring_gather(): up = lax.ppermute(up, 'loop', shift(1))  39.9 us
    pallas_call x1, Pallas kernels, krylov(): pl.pallas_call(functools.partial(steps_kernel, cached=cached), in_specs=[...  17.1 us
    ppermute x4, starting transfers between devices, ring_gather(): up = lax.ppermute(up, 'loop', shift(1))  13.1 us
    all_to_all x1, blocking collectives, on_device(): everyone = lax.all_to_all(dots, AXES, 0, 0, tiled=True)  12.8 us
    pallas_call x1, Pallas kernels, messages(): pl.pallas_call(message_kernel, grid_spec=pltpu.PrefetchScalarGridSpec(num...  10.6 us
    unnamed x22, local copies, waits for them, and re-layouts  7.59 us
    all_to_all x1, starting transfers between devices, on_device(): received = lax.all_to_all(message, AXES, 0, 0, tiled=True)  7.3 us
  transfers between devices with their start and end apart: 16, of which 5 were waited for; matrix products, arithmetic and copies ran while one was open for 2% of the time, Pallas kernels for 0%

profile of v2, /device:TPU:0, one launch (start us, length us, event | category | flops | bytes accessed | tf_op | source)
XLA Modules:
  0.0 120.6 jit_solution(17553774687560887351)
XLA Ops:
  0.6 0.8 copy.16.user_tile
  1.4 0.8 copy.17.word_tile
  2.1 0.8 copy.18.subreddit
  2.9 2.2 %copy-done = bf16[1,1,16,8,128,128]{5,4,3,2,1,0:T(8,128)(2,1)S(1)} copy-done((bf16[1,1,16,8,128,128]{5,4,3,2,1,0:T(8,128)(2,1)S(1)}, bf16[1,1,16,8,128,128]{5,4,3,2,1,0:T(8,128)(2,1)}, u32[]{:S(2)}) %copy-start) | copy-done | bytes 4194328
  5.1 0.9 copy-done.1
  6.0 1.0 copy-done.3
  7.1 0.9 copy-done.5
  8.0 0.7 copy-done.9
  8.6 10.6 %messages.1 = bf16[16,2,160,128]{3,2,1,0:T(8,128)(2,1)} custom-call(s32[1,16]{1,0:T(1,128)S(1)} %bitcast.17, s32[16,8]{1,0:T(8,128)S(1)} %copy.16.user_tile, s32[16,8]{1,0:T(8,128)S(1)} %copy.17.word_tile, s32[16,8]{1,0:T(8,128)S(1)} %copy.18.subreddit, bf16[16,8,128,128]{3,2,1,0:T(8,128)(2,1)S(1)} %bitcast.10, s32[16,8,2,128]{3,2,1,0:T(2,128)S(1)} %bitcast.16, ...), custom_call_target="tpu_custom_call" | custom-call | flops 1073741824 | bytes 4194304 | tf_op jit(solution)/shard_map/messages/pallas_call | solution.py:83
  19.3 7.3 %all-to-all-start = ((bf16[32,160,128]{2,1,0:T(8,128)(2,1)}), bf16[32,160,128]{2,1,0:T(8,128)(2,1)S(1)}, u32[]{:S(2)}, u32[]{:S(2)}) async-start(bf16[32,160,128]{2,1,0:T(8,128)(2,1)} %bitcast.7), calls=%async_computation | async-start | bytes 2621440 | tf_op jit(solution)/shard_map/all_to_all | solution.py:334
  26.6 1.8 %collective-permute-start.7 = (bf16[8,128,128]{2,1,0:T(8,128)(2,1)S(1)}, bf16[8,128,128]{2,1,0:T(8,128)(2,1)S(1)}, u32[]{:S(2)}, u32[]{:S(2)}) collective-permute-start(bf16[8,128,128]{2,1,0:T(8,128)(2,1)S(1)} %bitcast.12), channel_id=1, source_target_pairs={{0,8},{2,10},{8,16},{10,18},{16,24},{18,26},{24,28},{26,30},{28,20... | collective-permute-start | bytes 786440 | tf_op jit(solution)/shard_map/ppermute | solution.py:300
  28.4 0.3 collective-permute-start.1
  28.7 25.4 %collective-permute-done.7.refs_14_ = bf16[8,128,128]{2,1,0:T(8,128)(2,1)S(1)} collective-permute-done((bf16[8,128,128]{2,1,0:T(8,128)(2,1)S(1)}, bf16[8,128,128]{2,1,0:T(8,128)(2,1)S(1)}, u32[]{:S(2)}, u32[]{:S(2)}) %collective-permute-start.7) | collective-permute-done | bytes 262176 | tf_op jit(solution)/shard_map/ppermute | solution.py:300
  54.1 8.4 %collective-permute-start.8 = (bf16[8,128,128]{2,1,0:T(8,128)(2,1)S(1)}, bf16[8,128,128]{2,1,0:T(8,128)(2,1)S(1)}, u32[]{:S(2)}, u32[]{:S(2)}) collective-permute-start(bf16[8,128,128]{2,1,0:T(8,128)(2,1)S(1)} %collective-permute-done.7.refs_14_), channel_id=1, source_target_pairs={{0,8},{2,10},{8,16},{10,18},{16,24},{18,26},{24,28},{26,30},{28,20... | collective-permute-start | bytes 786440 | tf_op jit(solution)/shard_map/ppermute | solution.py:300
  62.5 0.0 collective-permute-done.1.refs_2_
  62.5 0.0 collective-permute-start.3
  62.5 5.7 %collective-permute-done.8.refs_12_ = bf16[8,128,128]{2,1,0:T(8,128)(2,1)S(1)} collective-permute-done((bf16[8,128,128]{2,1,0:T(8,128)(2,1)S(1)}, bf16[8,128,128]{2,1,0:T(8,128)(2,1)S(1)}, u32[]{:S(2)}, u32[]{:S(2)}) %collective-permute-start.8) | collective-permute-done | bytes 262176 | tf_op jit(solution)/shard_map/ppermute | solution.py:300
  68.3 2.5 %collective-permute-start.9 = (bf16[8,128,128]{2,1,0:T(8,128)(2,1)S(1)}, bf16[8,128,128]{2,1,0:T(8,128)(2,1)S(1)}, u32[]{:S(2)}, u32[]{:S(2)}) collective-permute-start(bf16[8,128,128]{2,1,0:T(8,128)(2,1)S(1)} %collective-permute-done.8.refs_12_), channel_id=1, source_target_pairs={{0,8},{2,10},{8,16},{10,18},{16,24},{18,26},{24,28},{26,30},{28,20... | collective-permute-start | bytes 786440 | tf_op jit(solution)/shard_map/ppermute | solution.py:300
  70.8 0.0 collective-permute-start
  70.8 0.5 collective-permute-start.14
  71.3 0.0 collective-permute-start.2
  71.3 0.0 collective-permute-done.3.refs_4_
  71.3 1.5 %collective-permute-start.5 = (bf16[8,128,128]{2,1,0:T(8,128)(2,1)S(1)}, bf16[8,128,128]{2,1,0:T(8,128)(2,1)}, u32[]{:S(2)}, u32[]{:S(2)}) collective-permute-start(bf16[8,128,128]{2,1,0:T(8,128)(2,1)S(1)} %collective-permute-done.3.refs_4_), channel_id=1, source_target_pairs={{0,4},{2,6},{8,0},{10,2},{16,8},{18,10},{24,16},{26,18},{28,24},{3... | collective-permute-start | bytes 786440 | tf_op jit(solution)/shard_map/ppermute | solution.py:303
  72.7 5.0 %collective-permute-done.9.refs_10_ = bf16[8,128,128]{2,1,0:T(8,128)(2,1)S(1)} collective-permute-done((bf16[8,128,128]{2,1,0:T(8,128)(2,1)S(1)}, bf16[8,128,128]{2,1,0:T(8,128)(2,1)S(1)}, u32[]{:S(2)}, u32[]{:S(2)}) %collective-permute-start.9) | collective-permute-done | bytes 262176 | tf_op jit(solution)/shard_map/ppermute | solution.py:300
  77.7 0.4 collective-permute-start.10
  78.1 0.1 copy.19.activity
  78.3 0.0 collective-permute-done.refs_1_
  78.3 0.1 collective-permute-start.13
  78.4 0.0 collective-permute-done.14.refs_15_
  78.4 0.5 collective-permute-start.4
  78.9 0.0 collective-permute-done.2.refs_3_
  78.9 0.1 collective-permute-start.12
  79.0 1.9 %collective-permute-done.5.refs_6_ = bf16[8,128,128]{2,1,0:T(8,128)(2,1)} collective-permute-done((bf16[8,128,128]{2,1,0:T(8,128)(2,1)S(1)}, bf16[8,128,128]{2,1,0:T(8,128)(2,1)}, u32[]{:S(2)}, u32[]{:S(2)}) %collective-permute-start.5) | collective-permute-done | bytes 262176 | tf_op jit(solution)/shard_map/ppermute | solution.py:303
  80.8 0.0 collective-permute-start.6
  80.8 3.7 %collective-permute-done.10.refs_8_ = bf16[8,128,128]{2,1,0:T(8,128)(2,1)} collective-permute-done((bf16[8,128,128]{2,1,0:T(8,128)(2,1)S(1)}, bf16[8,128,128]{2,1,0:T(8,128)(2,1)}, u32[]{:S(2)}, u32[]{:S(2)}) %collective-permute-start.10) | collective-permute-done | bytes 262176 | tf_op jit(solution)/shard_map/ppermute | solution.py:300
  84.6 0.0 collective-permute-start.11
  84.6 0.7 slice_add_fusion
  85.3 0.8 reshape.186.flags
  86.1 0.8 reshape.187.word_index
  86.9 0.0 collective-permute-done.13.refs_13_
  86.9 0.0 collective-permute-done.12.refs_11_
  86.9 0.0 collective-permute-done.6.refs_7_
  87.0 17.1 %krylov.1 = (f32[128,128]{1,0:T(8,128)S(1)}, f32[128,128]{1,0:T(8,128)S(1)}, f32[128,128]{1,0:T(8,128)S(1)}, f32[32,1,128]{2,1,0:T(1,128)S(1)}) custom-call(s32[256]{0:T(256)S(1)} %reshape.186.flags, s32[256]{0:T(256)S(1)} %reshape.187.word_index, f32[128,128]{1,0:T(8,128)S(1)} %copy-done.4, f32[128,1]{1,0:T(8,128)S(1)} %copy.19.activity, ...), custom_call_target="tpu_custom_call" | custom-call | tf_op jit(solution)/shard_map/krylov/pallas_call | solution.py:237
  104.0 0.6 copy-done.6
  104.6 0.6 copy-done.7
  105.3 0.6 copy-done.8
  105.9 12.8 %all_to_all.10.dots = f32[32,1,128]{2,1,0:T(1,128)} all-to-all(f32[32,1,128]{2,1,0:T(1,128)S(1)} %get-tuple-element.6), channel_id=1, replica_groups=mesh['loop'=16,'own'=2] {'loop','own'}, dimensions={0} | all-to-all | bytes 32768 | tf_op jit(solution)/shard_map/all_to_all | solution.py:348
  118.7 1.9 %last_step.1 = (f32[128,128]{1,0:T(8,128)}, f32[128,128]{1,0:T(8,128)}) custom-call(f32[32,1,128]{2,1,0:T(1,128)} %all_to_all.10.dots, f32[128,128]{1,0:T(8,128)} %start.3, f32[128,128]{1,0:T(8,128)} %copy-done.6, f32[128,128]{1,0:T(8,128)} %copy-done.7, f32[128,128]{1,0:T(8,128)} %copy-done.8), custom_call_target="tpu_custom_call" | custom-call | tf_op jit(solution)/shard_map/last_step/pallas_call | solution.py:267
  (19 shorter events, 0.1 us)
Async XLA Ops:
  2.9 2.2 %copy-start = (bf16[1,1,16,8,128,128]{5,4,3,2,1,0:T(8,128)(2,1)S(1)}, bf16[1,1,16,8,128,128]{5,4,3,2,1,0:T(8,128)(2,1)}, u32[]{:S(2)}) copy-start(bf16[1,1,16,8,128,128]{5,4,3,2,1,0:T(8,128)(2,1)} %param.14) | copy-start | bytes 12582916
  5.1 0.9 copy-start.1
  6.0 1.0 copy-start.3
  7.1 0.9 copy-start.5
  8.0 0.7 copy-start.9
  19.3 7.3 %copy-start.2 = (bf16[1,8,128,128]{3,2,1,0:T(8,128)(2,1)S(1)}, bf16[1,8,128,128]{3,2,1,0:T(8,128)(2,1)}, u32[]{:S(2)}) copy-start(bf16[1,8,128,128]{3,2,1,0:T(8,128)(2,1)} %param.12) | copy-start | bytes 786436
  19.3 58.9 %copy-start.10 = (f32[128]{0:T(128)S(1)}, f32[128]{0:T(128)}, u32[]{:S(2)}) copy-start(f32[128]{0:T(128)} %param.11) | copy-start | bytes 1540
  19.3 67.7 %copy-start.4 = (f32[128,128]{1,0:T(8,128)S(1)}, f32[128,128]{1,0:T(8,128)}, u32[]{:S(2)}) copy-start(f32[128,128]{1,0:T(8,128)} %start.3) | copy-start | bytes 196612
  19.3 65.3 %all-to-all-start = ((bf16[32,160,128]{2,1,0:T(8,128)(2,1)}), bf16[32,160,128]{2,1,0:T(8,128)(2,1)S(1)}, u32[]{:S(2)}, u32[]{:S(2)}) async-start(bf16[32,160,128]{2,1,0:T(8,128)(2,1)} %bitcast.7), calls=%async_computation | async-start | bytes 2621440 | tf_op jit(solution)/shard_map/all_to_all | solution.py:334
  26.6 27.5 %collective-permute-start.7 = (bf16[8,128,128]{2,1,0:T(8,128)(2,1)S(1)}, bf16[8,128,128]{2,1,0:T(8,128)(2,1)S(1)}, u32[]{:S(2)}, u32[]{:S(2)}) collective-permute-start(bf16[8,128,128]{2,1,0:T(8,128)(2,1)S(1)} %bitcast.12), channel_id=1, source_target_pairs={{0,8},{2,10},{8,16},{10,18},{16,24},{18,26},{24,28},{26,30},{28,20... | collective-permute-start | bytes 786440 | tf_op jit(solution)/shard_map/ppermute | solution.py:300
  28.4 34.1 %collective-permute-start.1 = (bf16[8,128,128]{2,1,0:T(8,128)(2,1)S(1)}, bf16[8,128,128]{2,1,0:T(8,128)(2,1)S(1)}, u32[]{:S(2)}, u32[]{:S(2)}) collective-permute-start(bf16[8,128,128]{2,1,0:T(8,128)(2,1)S(1)} %bitcast.13), channel_id=1, source_target_pairs={{0,4},{2,6},{8,0},{10,2},{16,8},{18,10},{24,16},{26,18},{28,24},{3... | collective-permute-start | bytes 786440 | tf_op jit(solution)/shard_map/ppermute | solution.py:303
  54.1 14.2 %collective-permute-start.8 = (bf16[8,128,128]{2,1,0:T(8,128)(2,1)S(1)}, bf16[8,128,128]{2,1,0:T(8,128)(2,1)S(1)}, u32[]{:S(2)}, u32[]{:S(2)}) collective-permute-start(bf16[8,128,128]{2,1,0:T(8,128)(2,1)S(1)} %collective-permute-done.7.refs_14_), channel_id=1, source_target_pairs={{0,8},{2,10},{8,16},{10,18},{16,24},{18,26},{24,28},{26,30},{28,20... | collective-permute-start | bytes 786440 | tf_op jit(solution)/shard_map/ppermute | solution.py:300
  62.5 8.7 %collective-permute-start.3 = (bf16[8,128,128]{2,1,0:T(8,128)(2,1)S(1)}, bf16[8,128,128]{2,1,0:T(8,128)(2,1)S(1)}, u32[]{:S(2)}, u32[]{:S(2)}) collective-permute-start(bf16[8,128,128]{2,1,0:T(8,128)(2,1)S(1)} %collective-permute-done.1.refs_2_), channel_id=1, source_target_pairs={{0,4},{2,6},{8,0},{10,2},{16,8},{18,10},{24,16},{26,18},{28,24},{3... | collective-permute-start | bytes 786440 | tf_op jit(solution)/shard_map/ppermute | solution.py:303
  68.3 9.5 %collective-permute-start.9 = (bf16[8,128,128]{2,1,0:T(8,128)(2,1)S(1)}, bf16[8,128,128]{2,1,0:T(8,128)(2,1)S(1)}, u32[]{:S(2)}, u32[]{:S(2)}) collective-permute-start(bf16[8,128,128]{2,1,0:T(8,128)(2,1)S(1)} %collective-permute-done.8.refs_12_), channel_id=1, source_target_pairs={{0,8},{2,10},{8,16},{10,18},{16,24},{18,26},{24,28},{26,30},{28,20... | collective-permute-start | bytes 786440 | tf_op jit(solution)/shard_map/ppermute | solution.py:300
  70.8 7.5 %collective-permute-start = (bf16[8,128,128]{2,1,0:T(8,128)(2,1)S(1)}, bf16[8,128,128]{2,1,0:T(8,128)(2,1)S(1)}, u32[]{:S(2)}, u32[]{:S(2)}) collective-permute-start(bf16[8,128,128]{2,1,0:T(8,128)(2,1)S(1)} %bitcast.14), channel_id=1, source_target_pairs={{0,2},{2,0},{4,6},{6,4},{8,10},{10,8},{12,14},{14,12},{16,18},{18,... | collective-permute-start | bytes 786440 | tf_op jit(solution)/shard_map/ppermute | solution.py:307
  70.8 7.6 %collective-permute-start.14 = (bf16[8,128,128]{2,1,0:T(8,128)(2,1)S(1)}, bf16[8,128,128]{2,1,0:T(8,128)(2,1)S(1)}, u32[]{:S(2)}, u32[]{:S(2)}) collective-permute-start(bf16[8,128,128]{2,1,0:T(8,128)(2,1)S(1)} %collective-permute-done.7.refs_14_), channel_id=1, source_target_pairs={{0,2},{2,0},{4,6},{6,4},{8,10},{10,8},{12,14},{14,12},{16,18},{18,... | collective-permute-start | bytes 786440 | tf_op jit(solution)/shard_map/ppermute | solution.py:307
  71.3 7.6 %collective-permute-start.2 = (bf16[8,128,128]{2,1,0:T(8,128)(2,1)S(1)}, bf16[8,128,128]{2,1,0:T(8,128)(2,1)}, u32[]{:S(2)}, u32[]{:S(2)}) collective-permute-start(bf16[8,128,128]{2,1,0:T(8,128)(2,1)S(1)} %collective-permute-done.1.refs_2_), channel_id=1, source_target_pairs={{0,2},{2,0},{4,6},{6,4},{8,10},{10,8},{12,14},{14,12},{16,18},{18,... | collective-permute-start | bytes 786440 | tf_op jit(solution)/shard_map/ppermute | solution.py:307
  71.3 9.6 %collective-permute-start.5 = (bf16[8,128,128]{2,1,0:T(8,128)(2,1)S(1)}, bf16[8,128,128]{2,1,0:T(8,128)(2,1)}, u32[]{:S(2)}, u32[]{:S(2)}) collective-permute-start(bf16[8,128,128]{2,1,0:T(8,128)(2,1)S(1)} %collective-permute-done.3.refs_4_), channel_id=1, source_target_pairs={{0,4},{2,6},{8,0},{10,2},{16,8},{18,10},{24,16},{26,18},{28,24},{3... | collective-permute-start | bytes 786440 | tf_op jit(solution)/shard_map/ppermute | solution.py:303
  77.7 6.8 %collective-permute-start.10 = (bf16[8,128,128]{2,1,0:T(8,128)(2,1)S(1)}, bf16[8,128,128]{2,1,0:T(8,128)(2,1)}, u32[]{:S(2)}, u32[]{:S(2)}) collective-permute-start(bf16[8,128,128]{2,1,0:T(8,128)(2,1)S(1)} %collective-permute-done.9.refs_10_), channel_id=1, source_target_pairs={{0,8},{2,10},{8,16},{10,18},{16,24},{18,26},{24,28},{26,30},{28,20... | collective-permute-start | bytes 786440 | tf_op jit(solution)/shard_map/ppermute | solution.py:300
  78.3 8.6 %collective-permute-start.13 = (bf16[8,128,128]{2,1,0:T(8,128)(2,1)S(1)}, bf16[8,128,128]{2,1,0:T(8,128)(2,1)}, u32[]{:S(2)}, u32[]{:S(2)}) collective-permute-start(bf16[8,128,128]{2,1,0:T(8,128)(2,1)S(1)} %collective-permute-done.8.refs_12_), channel_id=1, source_target_pairs={{0,2},{2,0},{4,6},{6,4},{8,10},{10,8},{12,14},{14,12},{16,18},{18,... | collective-permute-start | bytes 786440 | tf_op jit(solution)/shard_map/ppermute | solution.py:307
  78.4 8.5 %collective-permute-start.4 = (bf16[8,128,128]{2,1,0:T(8,128)(2,1)S(1)}, bf16[8,128,128]{2,1,0:T(8,128)(2,1)}, u32[]{:S(2)}, u32[]{:S(2)}) collective-permute-start(bf16[8,128,128]{2,1,0:T(8,128)(2,1)S(1)} %collective-permute-done.3.refs_4_), channel_id=1, source_target_pairs={{0,2},{2,0},{4,6},{6,4},{8,10},{10,8},{12,14},{14,12},{16,18},{18,... | collective-permute-start | bytes 786440 | tf_op jit(solution)/shard_map/ppermute | solution.py:307
  78.9 8.0 %collective-permute-start.12 = (bf16[8,128,128]{2,1,0:T(8,128)(2,1)S(1)}, bf16[8,128,128]{2,1,0:T(8,128)(2,1)}, u32[]{:S(2)}, u32[]{:S(2)}) collective-permute-start(bf16[8,128,128]{2,1,0:T(8,128)(2,1)S(1)} %collective-permute-done.9.refs_10_), channel_id=1, source_target_pairs={{0,2},{2,0},{4,6},{6,4},{8,10},{10,8},{12,14},{14,12},{16,18},{18,... | collective-permute-start | bytes 786440 | tf_op jit(solution)/shard_map/ppermute | solution.py:307
  80.8 6.1 %collective-permute-start.6 = (bf16[8,128,128]{2,1,0:T(8,128)(2,1)}, bf16[8,128,128]{2,1,0:T(8,128)(2,1)}, u32[]{:S(2)}, u32[]{:S(2)}) collective-permute-start(bf16[8,128,128]{2,1,0:T(8,128)(2,1)} %collective-permute-done.5.refs_6_), channel_id=1, source_target_pairs={{0,2},{2,0},{4,6},{6,4},{8,10},{10,8},{12,14},{14,12},{16,18},{18,... | collective-permute-start | bytes 786440 | tf_op jit(solution)/shard_map/ppermute | solution.py:307
  84.6 2.4 %collective-permute-start.11 = (bf16[8,128,128]{2,1,0:T(8,128)(2,1)}, bf16[8,128,128]{2,1,0:T(8,128)(2,1)}, u32[]{:S(2)}, u32[]{:S(2)}) collective-permute-start(bf16[8,128,128]{2,1,0:T(8,128)(2,1)} %collective-permute-done.10.refs_8_), channel_id=1, source_target_pairs={{0,2},{2,0},{4,6},{6,4},{8,10},{10,8},{12,14},{14,12},{16,18},{18,... | collective-permute-start | bytes 786440 | tf_op jit(solution)/shard_map/ppermute | solution.py:307
  104.0 0.6 copy-start.6
  104.6 0.6 copy-start.7
  105.3 0.6 copy-start.8

commit v3 on v2

v3 whole, which is shorter than its diff:
```python
import functools

import jax
import jax.numpy as jnp
from jax import lax
from jax.experimental import pallas as pl
from jax.experimental.pallas import tpu as pltpu
from jax.sharding import PartitionSpec as P

AXES = ("loop", "own")
CHUNK = 8
ridge = 0.05
VMEM_LIMIT = 60 * 2**20
f32 = jnp.float32
bf16 = jnp.bfloat16


def dot_nt(left, right):
    return lax.dot_general(left, right, (((1,), (1,)), ((), ())), preferred_element_type=f32)


def dot_nn(left, right):
    return jnp.dot(left, right, preferred_element_type=f32)


def mask_columns(first, length, tile):
    column = lax.broadcasted_iota(jnp.int32, (tile, first.shape[-1]), 0)
    inside = ((column - first) & (tile - 1)) < length
    return jnp.where(inside, 1.0, 0.0).astype(bf16)


def facts_kernel(scalars, runs, subs, out, table):
    groups, slots = runs.shape[0], runs.shape[1]
    owners, rank = out.shape[1], out.shape[3]
    table[...] = subs[...].astype(f32)
    lane = lax.broadcasted_iota(jnp.int32, (1, rank), 1)

    def body(group, carry):
        sub_rows, run_rows = [], []
        marks = jnp.zeros((1, rank), jnp.int32)
        live = scalars[group, 3 * slots]
        for s in range(slots):
            sub_rows.append(table[pl.ds(scalars[group, 2 * slots + s], 1), :])
            run_rows.append(runs[group, s])
            marks = jnp.where(lane == s, jnp.where(s < live, scalars[group, s] + 1, 0), marks)
            marks = jnp.where(lane == slots + s, scalars[group, slots + s], marks)
        run_rows = jnp.concatenate(run_rows, axis=0).astype(f32).astype(out.dtype)
        rest = jnp.concatenate(
            sub_rows + [marks.astype(f32), jnp.zeros((slots - 1, rank), f32)], axis=0
        ).astype(out.dtype)
        for o in range(owners):
            out[group, o, : 2 * slots, :] = run_rows
            out[group, o, 2 * slots :, :] = rest
        return carry

    lax.fori_loop(0, groups, body, 0)


def facts(scalars, runs, subs, owners):
    groups, slots, _, _ = runs.shape
    rank = subs.shape[1]
    whole = pl.BlockSpec(memory_space=pltpu.VMEM)
    return pl.pallas_call(
        facts_kernel,
        in_specs=[pl.BlockSpec(memory_space=pltpu.SMEM), whole, whole],
        out_specs=whole,
        out_shape=jax.ShapeDtypeStruct((groups, owners, 4 * slots, rank), bf16),
        scratch_shapes=[pltpu.VMEM(subs.shape, f32)],
        compiler_params=pltpu.CompilerParams(vmem_limit_bytes=VMEM_LIMIT),
        name="facts",
    )(scalars, runs, subs)


def rhs_kernel(scalars, ratings, runs, words, subs, out, table, sums):
    slots, tile = ratings.shape[1], ratings.shape[2]
    owners, own_rows = out.shape[1], out.shape[4]
    tiles = owners * own_rows // tile
    step = pl.program_id(0)
    group = scalars[step, 3 * slots + 1]

    @pl.when(step == 0)
    def _():
        table[...] = subs[...].astype(f32)

    eye = (
        lax.broadcasted_iota(jnp.int32, (tile, tile), 0)
        == lax.broadcasted_iota(jnp.int32, (tile, tile), 1)
    ).astype(f32).astype(bf16)
    products, weights = [], []
    live = scalars[group, 3 * slots]
    for s in range(slots):
        sub_row = table[pl.ds(scalars[group, 2 * slots + s], 1), :]
        products.append(
            (words[scalars[group, slots + s]].astype(f32) * sub_row).astype(bf16)
        )
        pair = runs[0, s]
        seen = dot_nt(eye, mask_columns(pair[0:1], pair[1:2], tile)).astype(bf16)
        value = seen * ratings[0, s]
        user = jnp.where(s < live, scalars[group, s], -1)
        weights.append(
            jnp.concatenate(
                [value * jnp.where(user == u, 1.0, 0.0).astype(bf16) for u in range(tiles)], axis=0
            )
        )
    sums[...] = dot_nn(jnp.concatenate(weights, axis=1), jnp.concatenate(products, axis=0))
    me = lax.axis_index("own")
    for o in range(owners):
        owner = lax.rem(me + o, owners)
        rows = pl.ds(pl.multiple_of(owner * own_rows, own_rows), own_rows)
        out[0, o, 0, 0] = sums[rows, :].astype(out.dtype)


def rhs_sums(scalars, ratings, runs, words, subs, owners, own_rows):
    groups, slots, tile, _ = ratings.shape
    rank = words.shape[-1]
    levels = groups // 4

    def there(i, scalars):
        return scalars[i, 3 * slots + 1]

    return pl.pallas_call(
        rhs_kernel,
        grid_spec=pltpu.PrefetchScalarGridSpec(
            num_scalar_prefetch=1,
            grid=(groups,),
            in_specs=[
                pl.BlockSpec((1, slots, tile, tile), lambda i, s: (there(i, s), 0, 0, 0)),
                pl.BlockSpec((1, slots, 2, tile), lambda i, s: (there(i, s), 0, 0, 0)),
                pl.BlockSpec(words.shape, lambda i, s: (0, 0, 0)),
                pl.BlockSpec(subs.shape, lambda i, s: (0, 0)),
            ],
            out_specs=pl.BlockSpec(
                (1, owners, 1, 1, own_rows, rank),
                lambda i, s: (i // (2 * levels), 0, (i // levels) % 2, i % levels, 0, 0),
            ),
            scratch_shapes=[pltpu.VMEM(subs.shape, f32), pltpu.VMEM((owners * own_rows, rank), f32)],
        ),
        out_shape=jax.ShapeDtypeStruct((2, owners, 2, levels, own_rows, rank), bf16),
        compiler_params=pltpu.CompilerParams(vmem_limit_bytes=VMEM_LIMIT),
        cost_estimate=pl.CostEstimate(
            flops=16 * ratings.size * rank, bytes_accessed=2 * ratings.size, transcendentals=0
        ),
        name="rhs",
    )(scalars, ratings, runs, words, subs)


def add(left, right):
    return (left.astype(f32) + right.astype(f32)).astype(bf16)


def reduce_rhs(sums, shards, owners):
    levels = shards // 4
    core = [(shard, shard ^ 1) for shard in range(shards)]
    column = [(shard, shard ^ 2) for shard in range(shards)]
    sums = add(sums[0], lax.ppermute(sums[1], "loop", core))
    total = sums[0]
    for o in range(1, owners):
        total = add(total, lax.ppermute(sums[o], "own", [(k, (k + o) % owners) for k in range(owners)]))
    total = add(total[0], lax.ppermute(total[1], "loop", column))
    terms = [total[0]]
    for up in range(1, levels):
        shift = [(shard, (shard + 4 * up) % shards) for shard in range(shards)]
        terms.append(lax.ppermute(total[up], "loop", shift))
    return terms


def masks_kernel(marks, received, chosen, subs, masks_out, runs, masks, sent):
    sources = received.shape[0]
    own_rows = masks.shape[1]
    tile = received.shape[2]
    blocks = subs.shape[0]
    slots = blocks // sources

    def choose(j, n):
        chosen[n] = j
        return n + marks[j]

    used = lax.fori_loop(0, blocks, choose, 0, unroll=8)
    chosen[blocks] = used
    chunks = lax.div(used + CHUNK - 1, CHUNK)

    def unpack(src, carry):
        runs[pl.ds(pl.multiple_of(src * 2 * slots, 2 * slots), 2 * slots), :] = received[
            src, : 2 * slots, :
        ].astype(f32)
        subs[pl.ds(pl.multiple_of(src * slots, slots), slots), :] = received[
            src, 2 * slots :, :
        ].astype(f32)[:slots]
        return carry

    lax.fori_loop(0, sources, unpack, 0)

    offset = lax.rem(lax.axis_index("own") * own_rows, tile)
    pick = (
        lax.broadcasted_iota(jnp.int32, (own_rows, tile), 0) + offset
        == lax.broadcasted_iota(jnp.int32, (own_rows, tile), 1)
    ).astype(f32).astype(bf16)

    def send(chunk):
        return pltpu.make_async_copy(masks.at[chunk], masks_out.at[chunk], sent.at[chunk])

    def build(chunk, carry):
        parts = []
        for b in range(CHUNK):
            i = chunk * CHUNK + b
            j = jnp.where(i < used, chosen[jnp.minimum(i, blocks - 1)], 0)
            first = runs[pl.ds(2 * j, 1), :].astype(jnp.int32)
            length = runs[pl.ds(2 * j + 1, 1), :].astype(jnp.int32)
            length = jnp.where(i < used, length, 0)
            parts.append(dot_nt(pick, mask_columns(first, length, tile)).astype(bf16))
        masks[chunk] = jnp.concatenate(parts, axis=1)
        send(chunk).start()
        return carry

    def finish(chunk, carry):
        send(chunk).wait()
        return carry

    lax.fori_loop(0, chunks, build, 0)
    lax.fori_loop(0, chunks, finish, 0)


def build_masks(marks, received, own_rows):
    sources, rows, tile = received.shape
    blocks = marks.shape[0]
    rank = received.shape[2]
    chunks = -(-blocks // CHUNK)
    whole = pl.BlockSpec(memory_space=pltpu.VMEM)
    scalars = pl.BlockSpec(memory_space=pltpu.SMEM)
    return pl.pallas_call(
        masks_kernel,
        in_specs=[scalars, whole],
        out_specs=[scalars, whole, pl.BlockSpec(memory_space=pl.ANY)],
        out_shape=[
            jax.ShapeDtypeStruct((blocks + 1,), jnp.int32),
            jax.ShapeDtypeStruct((blocks, rank), f32),
            jax.ShapeDtypeStruct((chunks, own_rows, CHUNK * tile), bf16),
        ],
        scratch_shapes=[
            pltpu.VMEM((2 * blocks, tile), f32),
            pltpu.VMEM((chunks, own_rows, CHUNK * tile), bf16),
            pltpu.SemaphoreType.DMA((chunks,)),
        ],
        compiler_params=pltpu.CompilerParams(vmem_limit_bytes=VMEM_LIMIT),
        name="masks",
    )(marks, received)


def steps_kernel(chosen, word_index, start, activity, subs, masks_in, *refs, shards, levels, cached):
    own_rows, rank = start.shape
    blocks = subs.shape[0]
    pieces, refs = refs[:shards], refs[shards:]
    terms, refs = refs[:levels], refs[levels:]
    first_out, second_out, third_out, dots_out = refs[:4]
    masks, words, arrived, loaded = refs[4:8]
    products = refs[-1]
    word_tiles, tile, _ = pieces[0].shape
    used = chosen[blocks]
    chunks = lax.div(used + CHUNK - 1, CHUNK)

    copies = [
        pltpu.make_async_copy(
            piece, words.at[k * word_tiles : (k + 1) * word_tiles], arrived.at[k]
        )
        for k, piece in enumerate(pieces)
    ]
    for copy in copies:
        copy.start()

    def load(chunk):
        return pltpu.make_async_copy(masks_in.at[chunk], masks.at[chunk], loaded.at[chunk])

    def begin(chunk, carry):
        load(chunk).start()
        return carry

    lax.fori_loop(0, chunks, begin, 0)

    def product(i):
        j = jnp.where(i < used, chosen[jnp.minimum(i, blocks - 1)], 0)
        return (words[word_index[j]].astype(f32) * subs[pl.ds(j, 1), :]).astype(bf16)

    def build(chunk, carry):
        load(chunk).wait()
        if cached:
            for b in range(CHUNK):
                products[chunk, b * tile : (b + 1) * tile, :] = product(chunk * CHUNK + b)
        return carry

    for copy in copies:
        copy.wait()
    lax.fori_loop(0, chunks, build, 0)

    def gram(vector):
        rounded = vector.astype(bf16)

        def body(chunk, total):
            if cached:
                block = products[chunk]
            else:
                block = jnp.concatenate(
                    [product(chunk * CHUNK + b) for b in range(CHUNK)], axis=0
                )
            weights = dot_nt(rounded, block).astype(bf16) * masks[chunk]
            return total + dot_nn(weights, block)

        return lax.fori_loop(0, chunks, body, jnp.zeros((own_rows, rank), f32))

    def over_row(a, b):
        return jnp.sum(a * b, axis=1, keepdims=True)

    scale = activity[...]
    rhs = terms[0][...].astype(f32)
    for term in terms[1:]:
        rhs = rhs + term[...].astype(f32)
    first = scale * (rhs - gram(start[...])) - ridge * start[...]
    second = scale * gram(first) + ridge * first
    norms, overlaps = over_row(first, first), over_row(first, second)
    share = jnp.where(norms > 0.0, overlaps / jnp.where(norms > 0.0, norms, 1.0), 0.0)
    rest = second - share * first
    third = scale * gram(rest) + ridge * rest + share * second
    first_out[...] = first
    second_out[...] = second
    third_out[...] = third
    rows = [norms, overlaps, over_row(second, second), over_row(first, third), over_row(second, third)]
    lane = lax.broadcasted_iota(jnp.int32, (1, rank), 1)
    line = jnp.zeros((1, rank), f32)
    for k, value in enumerate(rows):
        line = line + jnp.where(lane == k, jnp.sum(value, axis=0, keepdims=True), 0.0)
    dots_out[...] = jnp.broadcast_to(line[None], dots_out.shape)


def krylov(chosen, word_index, start, activity, subs, masks, pieces, terms, devices):
    own_rows, rank = start.shape
    blocks = subs.shape[0]
    word_tiles, tile, _ = pieces[0].shape
    chunks = masks.shape[0]
    cached = blocks * tile * rank * 2 <= 16 * 2**20
    whole = pl.BlockSpec(memory_space=pltpu.VMEM)
    scalars = pl.BlockSpec(memory_space=pltpu.SMEM)
    anywhere = pl.BlockSpec(memory_space=pl.ANY)
    vector = jax.ShapeDtypeStruct((own_rows, rank), f32)
    scratch = [
        pltpu.VMEM(masks.shape, bf16),
        pltpu.VMEM((len(pieces) * word_tiles, tile, rank), bf16),
        pltpu.SemaphoreType.DMA((len(pieces),)),
        pltpu.SemaphoreType.DMA((chunks,)),
    ]
    if cached:
        scratch.append(pltpu.VMEM((chunks, CHUNK * tile, rank), bf16))
    return pl.pallas_call(
        functools.partial(
            steps_kernel, shards=len(pieces), levels=len(terms), cached=cached
        ),
        in_specs=[scalars, scalars, whole, whole, whole, anywhere]
        + [anywhere] * len(pieces)
        + [whole] * len(terms),
        out_specs=[whole] * 4,
        out_shape=[vector, vector, vector, jax.ShapeDtypeStruct((devices, 1, rank), f32)],
        scratch_shapes=scratch,
        compiler_params=pltpu.CompilerParams(vmem_limit_bytes=VMEM_LIMIT),
        name="krylov",
    )(chosen, word_index, start, activity, subs, masks, *pieces, *terms)


def last_kernel(dots, start, first, second, third, solution_out, residual_out):
    line = dots[0]
    for k in range(1, dots.shape[0]):
        line = line + dots[k]
    rr, rq, qq, rz, qz = (line[:, k : k + 1] for k in range(5))
    step0 = rr / rq
    next_rr = rr - 2.0 * step0 * rq + step0 * step0 * qq
    grow = 1.0 + next_rr / rr
    slope = grow * (grow * rq - step0 * (rz + qq)) + step0 * step0 * qz
    step1 = next_rr / slope
    near, far = step0 + step1 * grow, step1 * step0
    solution_out[...] = start[...] + near * first[...] - far * second[...]
    residual_out[...] = first[...] - near * second[...] + far * third[...]


def last_step(dots, start, first, second, third):
    whole = pl.BlockSpec(memory_space=pltpu.VMEM)
    vector = jax.ShapeDtypeStruct(start.shape, f32)
    return pl.pallas_call(
        last_kernel,
        in_specs=[whole] * 5,
        out_specs=[whole] * 2,
        out_shape=[vector, vector],
        compiler_params=pltpu.CompilerParams(vmem_limit_bytes=VMEM_LIMIT),
        name="last_step",
    )(dots, start, first, second, third)


def ring_place(shard, chips):
    chip = shard // 2
    level, column = chip // 2, chip % 2
    return jnp.where(column == 0, level, chips - 1 - level)


def ring_gather(mine, shards):
    chips = shards // 2
    levels = chips // 2
    order = [2 * level for level in range(levels)] + [
        2 * level + 1 for level in reversed(range(levels))
    ]

    def shift(by):
        return [
            (2 * order[p] + core, 2 * order[(p + by) % chips] + core)
            for p in range(chips)
            for core in range(2)
        ]

    other = [(shard, shard ^ 1) for shard in range(shards)]
    up = down = mine
    held = {0: mine}
    for step in range(1, chips // 2 + 1):
        up = lax.ppermute(up, "loop", shift(1))
        held[chips - step] = up
        if step < chips - step:
            down = lax.ppermute(down, "loop", shift(-1))
            held[step] = down
    pieces = []
    for distance in range(chips):
        pieces += [held[distance], lax.ppermute(held[distance], "loop", other)]
    return pieces


def on_device(
    factor_start,
    activity,
    word_factors,
    sub_factors,
    ratings,
    user_tile,
    word_tile,
    subreddit,
    counts,
    runs,
):
    own_rows, rank = factor_start.shape
    owners, shards = lax.axis_size("own"), lax.axis_size("loop")
    _, _, groups, slots, tile, _ = ratings.shape
    word_tiles = word_factors.shape[1]
    devices = shards * owners
    chips, levels = shards // 2, shards // 4
    me, owner = lax.axis_index("loop"), lax.axis_index("own")

    step = jnp.arange(groups, dtype=jnp.int32)
    level = (me // 4 + step % levels) % levels
    order = 4 * level + (me % 4) ^ (2 * ((step // levels) % 2) + step // (2 * levels))
    scalars = jnp.concatenate(
        [user_tile[0, 0], word_tile[0, 0], subreddit[0, 0], counts[0, 0][:, None], order[:, None]],
        axis=1,
    )

    pieces = ring_gather(word_factors[0], shards)
    message = facts(scalars, runs[0, 0], sub_factors, owners).reshape(devices, 4 * slots, rank)
    received = lax.all_to_all(message, AXES, 0, 0, tiled=True)
    sums = rhs_sums(
        scalars, ratings[0, 0], runs[0, 0], word_factors[0], sub_factors, owners, own_rows
    )
    terms = reduce_rhs(sums, shards, owners)

    got = received[:, 3 * slots, : 2 * slots].astype(jnp.int32)
    marks = (got[:, :slots] == owner * own_rows // tile + 1).astype(jnp.int32).reshape(-1)
    shard = jnp.arange(devices, dtype=jnp.int32)[:, None] // owners
    distance = (ring_place(shard, chips) - ring_place(me, chips)) % chips
    piece = 2 * distance + (shard + me) % 2
    word_index = (got[:, slots:] + word_tiles * piece).reshape(-1)

    chosen, subs, masks = build_masks(marks, received, own_rows)
    first, second, third, dots = krylov(
        chosen, word_index, factor_start, activity[:, None], subs, masks, pieces, terms, devices
    )
    everyone = lax.all_to_all(dots, AXES, 0, 0, tiled=True)
    return tuple(last_step(everyone, factor_start, first, second, third))


def solution(mesh):
    placed = (
        P(("loop", "own"), None),
        P(("loop", "own")),
        P("loop", None, None, None),
        P(),
        P("loop", "own", None, None, None, None),
        P("loop", "own", None, None),
        P("loop", "own", None, None),
        P("loop", "own", None, None),
        P("loop", "own", None),
        P("loop", "own", None, None, None, None),
    )
    return jax.shard_map(
        on_device,
        mesh=mesh,
        in_specs=placed,
        out_specs=(P(("loop", "own"), None), P(("loop", "own"), None)),
        check_vma=False,
    )
```

time: 121 us -> 110 us (0.909)
  waiting for transfers between devices: 41.8 us -> 23.8 us
  Pallas kernels: 29.5 us -> 42 us
  local copies, waits for them, and re-layouts: 11.6 us -> 7.94 us
  starting transfers between devices: 23.3 us -> 20.2 us
    ppermute x4, waiting for transfers between devices: 39.9 us -> 7.19 us  [ring_gather(): up = lax.ppermute(up, 'loop', shift(1))]
    pallas_call x2 -> x4, Pallas kernels: 27.7 us -> 40.1 us  [the longest x1 16.5 us: krylov(): pl.pallas_call(functools.partial(steps_kernel, shards=len(pieces), levels...]
    ppermute x4, starting transfers between devices: 13.1 us -> 5.36 us  [ring_gather(): up = lax.ppermute(up, 'loop', shift(1))]
    unnamed x22 -> x36, local copies, waits for them, and re-layouts: 7.59 us -> 0.51 us
    ppermute x0 -> x6, starting transfers between devices: none -> 6.68 us  [the longest x3 2.81 us: reduce_rhs(): terms.append(lax.ppermute(total[up], 'loop', shift))]
    all_to_all x1, waiting for transfers between devices: 0.01 us -> 6.17 us  [on_device(): received = lax.all_to_all(message, AXES, 0, 0, tiled=True)]
    ppermute x3, waiting for transfers between devices: 1.86 us -> 6.97 us  [ring_gather(): down = lax.ppermute(down, 'loop', shift(-1))]
    ppermute x0 -> x6, waiting for transfers between devices: none -> 3.47 us  [the longest x3 2.76 us: reduce_rhs(): terms.append(lax.ppermute(total[up], 'loop', shift))]
  transfers between devices with their start and end apart: 16 -> 22, of which waited for: 5 -> 7; matrix products, arithmetic and copies ran while one was open for 2% -> 4% of each run, Pallas kernels for 0% -> 8%
where the time goes in v3:
time: 110 us; the launch traced here: 109 us
  Pallas kernels  42 us (38%)
  waiting for transfers between devices  23.8 us (22%)
  starting transfers between devices  20.2 us (18%)
  blocking collectives  13.1 us (12%)
  local copies, waits for them, and re-layouts  7.94 us (7%)
  other arithmetic  1.43 us (1%)
    pallas_call x1, Pallas kernels, krylov(): pl.pallas_call(functools.partial(steps_kernel, shards=len(pieces), levels...  16.5 us
    pallas_call x1, Pallas kernels, rhs_sums(): pl.pallas_call(rhs_kernel, grid_spec=pltpu.PrefetchScalarGridSpec(num_sca...  14.8 us
    all_to_all x1, blocking collectives, on_device(): everyone = lax.all_to_all(dots, AXES, 0, 0, tiled=True)  13.1 us
    ppermute x4, waiting for transfers between devices, ring_gather(): up = lax.ppermute(up, 'loop', shift(1))  7.19 us
    ppermute x3, waiting for transfers between devices, ring_gather(): down = lax.ppermute(down, 'loop', shift(-1))  6.97 us
    pallas_call x1, Pallas kernels, build_masks(): pl.pallas_call(masks_kernel, in_specs=[scalars, whole], out_specs=[scalar...  6.44 us
    all_to_all x1, waiting for transfers between devices, on_device(): received = lax.all_to_all(message, AXES, 0, 0, tiled=True)  6.17 us
    ppermute x4, starting transfers between devices, ring_gather(): up = lax.ppermute(up, 'loop', shift(1))  5.36 us
  transfers between devices with their start and end apart: 22, of which 7 were waited for; matrix products, arithmetic and copies ran while one was open for 4% of the time, Pallas kernels for 8%

profile of v3, /device:TPU:0, one launch (start us, length us, event | category | flops | bytes accessed | tf_op | source)
XLA Modules:
  0.0 109.5 jit_solution(389596252100218098)
XLA Ops:
  0.6 0.8 copy.17
  1.4 0.8 copy.18
  2.2 0.8 copy.19
  2.9 0.7 copy.20
  3.7 0.7 concatenate.3.scalars
  4.4 14.8 %rhs.1 = bf16[2,2,2,4,128,128]{5,4,3,2,1,0:T(8,128)(2,1)} custom-call(s32[16,26]{1,0:T(8,128)} %concatenate.3.scalars, bf16[16,8,128,128]{3,2,1,0:T(8,128)(2,1)} %bitcast.54, s32[16,8,2,128]{3,2,1,0:T(2,128)} %bitcast.47, bf16[8,128,128]{2,1,0:T(8,128)(2,1)} %bitcast.40, bf16[2048,128]{1,0:T(8,128)(2,1)} %subs.3), custom_call_target="tpu_custom_call" | custom-call | flops 4294967296 | bytes 4194304 | tf_op jit(solution)/shard_map/rhs/pallas_call | solution.py:121
  19.2 1.1 slice_bitcast_fusion
  20.3 0.5 collective-permute-start.15
  20.8 2.6 %collective-permute-start.7 = (bf16[8,128,128]{2,1,0:T(8,128)(2,1)S(1)}, bf16[8,128,128]{2,1,0:T(8,128)(2,1)S(1)}, u32[]{:S(2)}, u32[]{:S(2)}) collective-permute-start(bf16[8,128,128]{2,1,0:T(8,128)(2,1)S(1)} %bitcast.42), channel_id=1, source_target_pairs={{0,8},{2,10},{8,16},{10,18},{16,24},{18,26},{24,28},{26,30},{28,20... | collective-permute-start | bytes 786440 | tf_op jit(solution)/shard_map/ppermute | solution.py:418
  23.4 6.8 %collective-permute-done.7.refs_14_ = bf16[8,128,128]{2,1,0:T(8,128)(2,1)S(1)} collective-permute-done((bf16[8,128,128]{2,1,0:T(8,128)(2,1)S(1)}, bf16[8,128,128]{2,1,0:T(8,128)(2,1)S(1)}, u32[]{:S(2)}, u32[]{:S(2)}) %collective-permute-start.7) | collective-permute-done | bytes 262176 | tf_op jit(solution)/shard_map/ppermute | solution.py:418
  30.2 1.8 %collective-permute-start.8 = (bf16[8,128,128]{2,1,0:T(8,128)(2,1)S(1)}, bf16[8,128,128]{2,1,0:T(8,128)(2,1)S(1)}, u32[]{:S(2)}, u32[]{:S(2)}) collective-permute-start(bf16[8,128,128]{2,1,0:T(8,128)(2,1)S(1)} %collective-permute-done.7.refs_14_), channel_id=1, source_target_pairs={{0,8},{2,10},{8,16},{10,18},{16,24},{18,26},{24,28},{26,30},{28,20... | collective-permute-start | bytes 786440 | tf_op jit(solution)/shard_map/ppermute | solution.py:418
  32.1 0.0 collective-permute-done.15
  32.1 1.2 %fusion = bf16[2,2,4,128,128]{4,3,2,1,0:T(8,128)(2,1)S(1)} fusion(bf16[2,2,4,128,128]{4,3,2,1,0:T(8,128)(2,1)S(1)} %collective-permute-done.15, bf16[2,2,2,4,128,128]{5,4,3,2,1,0:T(8,128)(2,1)} %rhs.1), kind=kLoop, calls=%fused_computation.1 | loop fusion | flops 1048576 | bytes 1572864 | tf_op jit(solution)/shard_map/convert_element_type | solution.py:148
  33.3 1.6 %collective-permute-start.16 = (bf16[2,4,128,128]{3,2,1,0:T(8,128)(2,1)S(1)}, bf16[2,4,128,128]{3,2,1,0:T(8,128)(2,1)S(1)}, u32[]{:S(2)}, u32[]{:S(2)}) collective-permute-start(bf16[2,4,128,128]{3,2,1,0:T(8,128)(2,1)S(1)} %slice_bitcast_fusion.2), channel_id=1, source_target_pairs={{0,1},{1,0},{2,3},{3,2},{4,5},{5,4},{6,7},{7,6},{8,9},{9,8},{10,11... | collective-permute-start | bytes 786440 | tf_op jit(solution)/shard_map/ppermute | solution.py:158
  34.9 0.0 collective-permute-start
  34.9 2.4 %facts.1 = bf16[16,2,32,128]{3,2,1,0:T(8,128)(2,1)} custom-call(s32[16,26]{1,0:T(8,128)} %concatenate.3.scalars, s32[16,8,2,128]{3,2,1,0:T(2,128)} %bitcast.48, bf16[2048,128]{1,0:T(8,128)(2,1)} %subs.3), custom_call_target="tpu_custom_call" | custom-call | tf_op jit(solution)/shard_map/facts/pallas_call | solution.py:63
  37.3 4.0 %all-to-all-start = ((bf16[32,32,128]{2,1,0:T(8,128)(2,1)}), bf16[32,32,128]{2,1,0:T(8,128)(2,1)S(1)}, u32[]{:S(2)}, u32[]{:S(2)}) async-start(bf16[32,32,128]{2,1,0:T(8,128)(2,1)} %bitcast.39), calls=%async_computation | async-start | bytes 524288 | tf_op jit(solution)/shard_map/all_to_all | solution.py:459
  41.4 0.7 copy.21.activity
  42.1 0.3 collective-permute-start.14
  42.4 1.7 %collective-permute-start.3 = (bf16[8,128,128]{2,1,0:T(8,128)(2,1)S(1)}, bf16[8,128,128]{2,1,0:T(8,128)(2,1)S(1)}, u32[]{:S(2)}, u32[]{:S(2)}) collective-permute-start(bf16[8,128,128]{2,1,0:T(8,128)(2,1)S(1)} %collective-permute-done.1.refs_2_), channel_id=1, source_target_pairs={{0,4},{2,6},{8,0},{10,2},{16,8},{18,10},{24,16},{26,18},{28,24},{3... | collective-permute-start | bytes 786440 | tf_op jit(solution)/shard_map/ppermute | solution.py:421
  44.1 0.3 collective-permute-start.9
  44.4 0.1 fusion.1
  44.5 1.7 %collective-permute-start.17 = (bf16[4,128,128]{2,1,0:T(8,128)(2,1)S(1)}, bf16[4,128,128]{2,1,0:T(8,128)(2,1)S(1)}, u32[]{:S(2)}, u32[]{:S(2)}) collective-permute-start(bf16[4,128,128]{2,1,0:T(8,128)(2,1)S(1)} %slice_bitcast_fusion.4), channel_id=1, source_target_pairs={{0,4},{2,6},{4,0},{6,2},{8,12},{10,14},{12,8},{14,10},{16,20},{18,... | collective-permute-start | bytes 393224 | tf_op jit(solution)/shard_map/ppermute | solution.py:159
  46.3 6.2 %all-to-all-done.received = bf16[32,32,128]{2,1,0:T(8,128)(2,1)S(1)} async-done(((bf16[32,32,128]{2,1,0:T(8,128)(2,1)}), bf16[32,32,128]{2,1,0:T(8,128)(2,1)S(1)}, u32[]{:S(2)}, u32[]{:S(2)}) %all-to-all-start) | async-done | bytes 262176 | tf_op jit(solution)/shard_map/all_to_all | solution.py:459
  52.5 0.1 collective-permute-start.2
  52.6 1.4 %collective-permute-done.3.refs_4_ = bf16[8,128,128]{2,1,0:T(8,128)(2,1)S(1)} collective-permute-done((bf16[8,128,128]{2,1,0:T(8,128)(2,1)S(1)}, bf16[8,128,128]{2,1,0:T(8,128)(2,1)S(1)}, u32[]{:S(2)}, u32[]{:S(2)}) %collective-permute-start.3) | collective-permute-done | bytes 262176 | tf_op jit(solution)/shard_map/ppermute | solution.py:421
  54.0 0.4 collective-permute-done.9.refs_10_
  54.4 1.4 %collective-permute-start.5 = (bf16[8,128,128]{2,1,0:T(8,128)(2,1)S(1)}, bf16[8,128,128]{2,1,0:T(8,128)(2,1)S(1)}, u32[]{:S(2)}, u32[]{:S(2)}) collective-permute-start(bf16[8,128,128]{2,1,0:T(8,128)(2,1)S(1)} %collective-permute-done.3.refs_4_), channel_id=1, source_target_pairs={{0,4},{2,6},{8,0},{10,2},{16,8},{18,10},{24,16},{26,18},{28,24},{3... | collective-permute-start | bytes 786440 | tf_op jit(solution)/shard_map/ppermute | solution.py:421
  55.8 0.7 collective-permute-done.17
  56.5 0.5 collective-permute-start.10
  57.1 0.2 collective-permute-start.4
  57.3 0.6 slice_bitcast_fusion.6
  57.9 0.4 collective-permute-start.12
  58.3 5.6 %collective-permute-done.5.refs_6_ = bf16[8,128,128]{2,1,0:T(8,128)(2,1)S(1)} collective-permute-done((bf16[8,128,128]{2,1,0:T(8,128)(2,1)S(1)}, bf16[8,128,128]{2,1,0:T(8,128)(2,1)S(1)}, u32[]{:S(2)}, u32[]{:S(2)}) %collective-permute-start.5) | collective-permute-done | bytes 262176 | tf_op jit(solution)/shard_map/ppermute | solution.py:421
  63.9 1.8 %collective-permute-start.18 = (bf16[128,128]{1,0:T(8,128)(2,1)S(1)}, bf16[128,128]{1,0:T(8,128)(2,1)S(1)}, u32[]{:S(2)}, u32[]{:S(2)}) collective-permute-start(bf16[128,128]{1,0:T(8,128)(2,1)S(1)} %get-tuple-element.18), channel_id=1, source_target_pairs={{0,8},{2,10},{4,12},{6,14},{8,16},{10,18},{12,20},{14,22},{16,24},... | collective-permute-start | bytes 98312 | tf_op jit(solution)/shard_map/ppermute | solution.py:163
  65.7 0.2 collective-permute-start.11
  65.8 0.1 slice_add_fusion
  65.9 1.0 collective-permute-start.19
  66.9 2.8 %collective-permute-done.18.refs_17_ = bf16[128,128]{1,0:T(8,128)(2,1)S(1)} collective-permute-done((bf16[128,128]{1,0:T(8,128)(2,1)S(1)}, bf16[128,128]{1,0:T(8,128)(2,1)S(1)}, u32[]{:S(2)}, u32[]{:S(2)}) %collective-permute-start.18) | collective-permute-done | bytes 32800 | tf_op jit(solution)/shard_map/ppermute | solution.py:163
  69.7 0.6 reshape.356.marks
  70.3 0.7 reshape.353.word_index
  71.0 6.4 %masks.1 = (s32[257]{0:T(512)}, f32[256,128]{1,0:T(8,128)}, bf16[32,128,1024]{2,1,0:T(8,128)(2,1)}) custom-call(s32[256]{0:T(256)} %reshape.356.marks, bf16[32,32,128]{2,1,0:T(8,128)(2,1)} %copy-done), custom_call_target="tpu_custom_call" | custom-call | tf_op jit(solution)/shard_map/masks/pallas_call | solution.py:230
  77.5 0.0 copy-start.16
  77.6 0.4 copy-done.15
  78.0 0.0 copy-done.16
  78.1 16.5 %krylov.1 = (f32[128,128]{1,0:T(8,128)}, f32[128,128]{1,0:T(8,128)}, f32[128,128]{1,0:T(8,128)}, f32[32,1,128]{2,1,0:T(1,128)}) custom-call(s32[257]{0:T(512)} %get-tuple-element.9.chosen, s32[256]{0:T(256)} %reshape.353.word_index, f32[128,128]{1,0:T(8,128)} %start.3, f32[128,1]{1,0:T(8,128)} %copy.21.activity, f32[256,128]{1,0:T(8,128)} %get-tuple-element.10.subs, ...), custom_call_target="tpu_custom_call" | custom-call | tf_op jit(solution)/shard_map/krylov/pallas_call | solution.py:351
  94.5 13.1 %all_to_all.10.dots = f32[32,1,128]{2,1,0:T(1,128)} all-to-all(f32[32,1,128]{2,1,0:T(1,128)} %get-tuple-element.12), channel_id=1, replica_groups=mesh['loop'=16,'own'=2] {'loop','own'}, dimensions={0} | all-to-all | bytes 32768 | tf_op jit(solution)/shard_map/all_to_all | solution.py:476
  107.6 1.9 %last_step.1 = (f32[128,128]{1,0:T(8,128)}, f32[128,128]{1,0:T(8,128)}) custom-call(f32[32,1,128]{2,1,0:T(1,128)} %all_to_all.10.dots, f32[128,128]{1,0:T(8,128)} %start.3, f32[128,128]{1,0:T(8,128)} %get-tuple-element.13.first, f32[128,128]{1,0:T(8,128)} %get-tuple-element.14.second, f32[128,128]{1,0:T(8,128)} %get-tuple-element.15.third), custom_call_target="tpu_custom_call" | custom-call | tf_op jit(solution)/shard_map/last_step/pallas_call | solution.py:384
  (58 shorter events, 0.2 us)
Async XLA Ops:
  4.4 16.4 %copy-start.1 = (bf16[1,8,128,128]{3,2,1,0:T(8,128)(2,1)S(1)}, bf16[1,8,128,128]{3,2,1,0:T(8,128)(2,1)}, u32[]{:S(2)}) copy-start(bf16[1,8,128,128]{3,2,1,0:T(8,128)(2,1)} %param.12) | copy-start | bytes 786436
  4.4 37.0 %copy-start.17 = (f32[128]{0:T(128)S(1)}, f32[128]{0:T(128)}, u32[]{:S(2)}) copy-start(f32[128]{0:T(128)} %param.11) | copy-start | bytes 1540
  20.3 11.8 %collective-permute-start.15 = (bf16[2,2,4,128,128]{4,3,2,1,0:T(8,128)(2,1)S(1)}, bf16[2,2,4,128,128]{4,3,2,1,0:T(8,128)(2,1)S(1)}, u32[]{:S(2)}, u32[]{:S(2)}) collective-permute-start(bf16[2,2,4,128,128]{4,3,2,1,0:T(8,128)(2,1)S(1)} %slice_bitcast_fusion), channel_id=1, source_target_pairs={{0,2},{2,0},{4,6},{6,4},{8,10},{10,8},{12,14},{14,12},{16,18},{18,... | collective-permute-start | bytes 1572872 | tf_op jit(solution)/shard_map/ppermute | solution.py:155
  20.8 9.5 %collective-permute-start.7 = (bf16[8,128,128]{2,1,0:T(8,128)(2,1)S(1)}, bf16[8,128,128]{2,1,0:T(8,128)(2,1)S(1)}, u32[]{:S(2)}, u32[]{:S(2)}) collective-permute-start(bf16[8,128,128]{2,1,0:T(8,128)(2,1)S(1)} %bitcast.42), channel_id=1, source_target_pairs={{0,8},{2,10},{8,16},{10,18},{16,24},{18,26},{24,28},{26,30},{28,20... | collective-permute-start | bytes 786440 | tf_op jit(solution)/shard_map/ppermute | solution.py:418
  23.4 19.0 %collective-permute-start.1 = (bf16[8,128,128]{2,1,0:T(8,128)(2,1)S(1)}, bf16[8,128,128]{2,1,0:T(8,128)(2,1)S(1)}, u32[]{:S(2)}, u32[]{:S(2)}) collective-permute-start(bf16[8,128,128]{2,1,0:T(8,128)(2,1)S(1)} %bitcast.43), channel_id=1, source_target_pairs={{0,4},{2,6},{8,0},{10,2},{16,8},{18,10},{24,16},{26,18},{28,24},{3... | collective-permute-start | bytes 786440 | tf_op jit(solution)/shard_map/ppermute | solution.py:421
  30.2 47.3 %copy-start.2 = (bf16[8,128,128]{2,1,0:T(8,128)(2,1)}, bf16[8,128,128]{2,1,0:T(8,128)(2,1)S(1)}, u32[]{:S(2)}) copy-start(bf16[8,128,128]{2,1,0:T(8,128)(2,1)S(1)} %collective-permute-done.7.refs_14_) | copy-start | bytes 786436
  30.2 13.8 %collective-permute-start.8 = (bf16[8,128,128]{2,1,0:T(8,128)(2,1)S(1)}, bf16[8,128,128]{2,1,0:T(8,128)(2,1)S(1)}, u32[]{:S(2)}, u32[]{:S(2)}) collective-permute-start(bf16[8,128,128]{2,1,0:T(8,128)(2,1)S(1)} %collective-permute-done.7.refs_14_), channel_id=1, source_target_pairs={{0,8},{2,10},{8,16},{10,18},{16,24},{18,26},{24,28},{26,30},{28,20... | collective-permute-start | bytes 786440 | tf_op jit(solution)/shard_map/ppermute | solution.py:418
  33.3 11.1 %collective-permute-start.16 = (bf16[2,4,128,128]{3,2,1,0:T(8,128)(2,1)S(1)}, bf16[2,4,128,128]{3,2,1,0:T(8,128)(2,1)S(1)}, u32[]{:S(2)}, u32[]{:S(2)}) collective-permute-start(bf16[2,4,128,128]{3,2,1,0:T(8,128)(2,1)S(1)} %slice_bitcast_fusion.2), channel_id=1, source_target_pairs={{0,1},{1,0},{2,3},{3,2},{4,5},{5,4},{6,7},{7,6},{8,9},{9,8},{10,11... | collective-permute-start | bytes 786440 | tf_op jit(solution)/shard_map/ppermute | solution.py:158
  34.9 17.6 %collective-permute-start = (bf16[8,128,128]{2,1,0:T(8,128)(2,1)S(1)}, bf16[8,128,128]{2,1,0:T(8,128)(2,1)S(1)}, u32[]{:S(2)}, u32[]{:S(2)}) collective-permute-start(bf16[8,128,128]{2,1,0:T(8,128)(2,1)S(1)} %bitcast.44), channel_id=1, source_target_pairs={{0,2},{2,0},{4,6},{6,4},{8,10},{10,8},{12,14},{14,12},{16,18},{18,... | collective-permute-start | bytes 786440 | tf_op jit(solution)/shard_map/ppermute | solution.py:425
  37.3 15.1 %all-to-all-start = ((bf16[32,32,128]{2,1,0:T(8,128)(2,1)}), bf16[32,32,128]{2,1,0:T(8,128)(2,1)S(1)}, u32[]{:S(2)}, u32[]{:S(2)}) async-start(bf16[32,32,128]{2,1,0:T(8,128)(2,1)} %bitcast.39), calls=%async_computation | async-start | bytes 524288 | tf_op jit(solution)/shard_map/all_to_all | solution.py:459
  42.1 14.9 %collective-permute-start.14 = (bf16[8,128,128]{2,1,0:T(8,128)(2,1)S(1)}, bf16[8,128,128]{2,1,0:T(8,128)(2,1)S(1)}, u32[]{:S(2)}, u32[]{:S(2)}) collective-permute-start(bf16[8,128,128]{2,1,0:T(8,128)(2,1)S(1)} %collective-permute-done.7.refs_14_), channel_id=1, source_target_pairs={{0,2},{2,0},{4,6},{6,4},{8,10},{10,8},{12,14},{14,12},{16,18},{18,... | collective-permute-start | bytes 786440 | tf_op jit(solution)/shard_map/ppermute | solution.py:425
  42.4 35.1 %copy-start.3 = (bf16[8,128,128]{2,1,0:T(8,128)(2,1)}, bf16[8,128,128]{2,1,0:T(8,128)(2,1)S(1)}, u32[]{:S(2)}) copy-start(bf16[8,128,128]{2,1,0:T(8,128)(2,1)S(1)} %collective-permute-done.1.refs_2_) | copy-start | bytes 786436
  42.4 11.6 %collective-permute-start.3 = (bf16[8,128,128]{2,1,0:T(8,128)(2,1)S(1)}, bf16[8,128,128]{2,1,0:T(8,128)(2,1)S(1)}, u32[]{:S(2)}, u32[]{:S(2)}) collective-permute-start(bf16[8,128,128]{2,1,0:T(8,128)(2,1)S(1)} %collective-permute-done.1.refs_2_), channel_id=1, source_target_pairs={{0,4},{2,6},{8,0},{10,2},{16,8},{18,10},{24,16},{26,18},{28,24},{3... | collective-permute-start | bytes 786440 | tf_op jit(solution)/shard_map/ppermute | solution.py:421
  44.1 33.4 %copy-start.4 = (bf16[8,128,128]{2,1,0:T(8,128)(2,1)}, bf16[8,128,128]{2,1,0:T(8,128)(2,1)S(1)}, u32[]{:S(2)}) copy-start(bf16[8,128,128]{2,1,0:T(8,128)(2,1)S(1)} %collective-permute-done.8.refs_12_) | copy-start | bytes 786436
  44.1 10.3 %collective-permute-start.9 = (bf16[8,128,128]{2,1,0:T(8,128)(2,1)S(1)}, bf16[8,128,128]{2,1,0:T(8,128)(2,1)S(1)}, u32[]{:S(2)}, u32[]{:S(2)}) collective-permute-start(bf16[8,128,128]{2,1,0:T(8,128)(2,1)S(1)} %collective-permute-done.8.refs_12_), channel_id=1, source_target_pairs={{0,8},{2,10},{8,16},{10,18},{16,24},{18,26},{24,28},{26,30},{28,20... | collective-permute-start | bytes 786440 | tf_op jit(solution)/shard_map/ppermute | solution.py:418
  44.5 12.0 %collective-permute-start.17 = (bf16[4,128,128]{2,1,0:T(8,128)(2,1)S(1)}, bf16[4,128,128]{2,1,0:T(8,128)(2,1)S(1)}, u32[]{:S(2)}, u32[]{:S(2)}) collective-permute-start(bf16[4,128,128]{2,1,0:T(8,128)(2,1)S(1)} %slice_bitcast_fusion.4), channel_id=1, source_target_pairs={{0,4},{2,6},{4,0},{6,2},{8,12},{10,14},{12,8},{14,10},{16,20},{18,... | collective-permute-start | bytes 393224 | tf_op jit(solution)/shard_map/ppermute | solution.py:159
  52.4 18.5 %copy-start = (bf16[32,32,128]{2,1,0:T(8,128)(2,1)}, bf16[32,32,128]{2,1,0:T(8,128)(2,1)S(1)}, u32[]{:S(2)}) copy-start(bf16[32,32,128]{2,1,0:T(8,128)(2,1)S(1)} %all-to-all-done.received) | copy-start | bytes 786436
  52.5 25.1 %copy-start.5 = (bf16[8,128,128]{2,1,0:T(8,128)(2,1)}, bf16[8,128,128]{2,1,0:T(8,128)(2,1)S(1)}, u32[]{:S(2)}) copy-start(bf16[8,128,128]{2,1,0:T(8,128)(2,1)S(1)} %collective-permute-done.refs_1_) | copy-start | bytes 786436
  52.5 5.5 %collective-permute-start.2 = (bf16[8,128,128]{2,1,0:T(8,128)(2,1)S(1)}, bf16[8,128,128]{2,1,0:T(8,128)(2,1)S(1)}, u32[]{:S(2)}, u32[]{:S(2)}) collective-permute-start(bf16[8,128,128]{2,1,0:T(8,128)(2,1)S(1)} %collective-permute-done.1.refs_2_), channel_id=1, source_target_pairs={{0,2},{2,0},{4,6},{6,4},{8,10},{10,8},{12,14},{14,12},{16,18},{18,... | collective-permute-start | bytes 786440 | tf_op jit(solution)/shard_map/ppermute | solution.py:425
  54.0 23.6 %copy-start.7 = (bf16[8,128,128]{2,1,0:T(8,128)(2,1)}, bf16[8,128,128]{2,1,0:T(8,128)(2,1)S(1)}, u32[]{:S(2)}) copy-start(bf16[8,128,128]{2,1,0:T(8,128)(2,1)S(1)} %collective-permute-done.3.refs_4_) | copy-start | bytes 786436
  54.0 9.9 %collective-permute-start.13 = (bf16[8,128,128]{2,1,0:T(8,128)(2,1)S(1)}, bf16[8,128,128]{2,1,0:T(8,128)(2,1)S(1)}, u32[]{:S(2)}, u32[]{:S(2)}) collective-permute-start(bf16[8,128,128]{2,1,0:T(8,128)(2,1)S(1)} %collective-permute-done.8.refs_12_), channel_id=1, source_target_pairs={{0,2},{2,0},{4,6},{6,4},{8,10},{10,8},{12,14},{14,12},{16,18},{18,... | collective-permute-start | bytes 786440 | tf_op jit(solution)/shard_map/ppermute | solution.py:425
  54.4 23.2 %copy-start.8 = (bf16[8,128,128]{2,1,0:T(8,128)(2,1)}, bf16[8,128,128]{2,1,0:T(8,128)(2,1)S(1)}, u32[]{:S(2)}) copy-start(bf16[8,128,128]{2,1,0:T(8,128)(2,1)S(1)} %collective-permute-done.9.refs_10_) | copy-start | bytes 786436
  54.4 9.5 %collective-permute-start.5 = (bf16[8,128,128]{2,1,0:T(8,128)(2,1)S(1)}, bf16[8,128,128]{2,1,0:T(8,128)(2,1)S(1)}, u32[]{:S(2)}, u32[]{:S(2)}) collective-permute-start(bf16[8,128,128]{2,1,0:T(8,128)(2,1)S(1)} %collective-permute-done.3.refs_4_), channel_id=1, source_target_pairs={{0,4},{2,6},{8,0},{10,2},{16,8},{18,10},{24,16},{26,18},{28,24},{3... | collective-permute-start | bytes 786440 | tf_op jit(solution)/shard_map/ppermute | solution.py:421
  56.5 9.2 %collective-permute-start.10 = (bf16[8,128,128]{2,1,0:T(8,128)(2,1)S(1)}, bf16[8,128,128]{2,1,0:T(8,128)(2,1)S(1)}, u32[]{:S(2)}, u32[]{:S(2)}) collective-permute-start(bf16[8,128,128]{2,1,0:T(8,128)(2,1)S(1)} %collective-permute-done.9.refs_10_), channel_id=1, source_target_pairs={{0,8},{2,10},{8,16},{10,18},{16,24},{18,26},{24,28},{26,30},{28,20... | collective-permute-start | bytes 786440 | tf_op jit(solution)/shard_map/ppermute | solution.py:418
  57.1 20.5 %copy-start.6 = (bf16[8,128,128]{2,1,0:T(8,128)(2,1)}, bf16[8,128,128]{2,1,0:T(8,128)(2,1)S(1)}, u32[]{:S(2)}) copy-start(bf16[8,128,128]{2,1,0:T(8,128)(2,1)S(1)} %collective-permute-done.14.refs_15_) | copy-start | bytes 786436
  57.1 8.8 %collective-permute-start.4 = (bf16[8,128,128]{2,1,0:T(8,128)(2,1)S(1)}, bf16[8,128,128]{2,1,0:T(8,128)(2,1)S(1)}, u32[]{:S(2)}, u32[]{:S(2)}) collective-permute-start(bf16[8,128,128]{2,1,0:T(8,128)(2,1)S(1)} %collective-permute-done.3.refs_4_), channel_id=1, source_target_pairs={{0,2},{2,0},{4,6},{6,4},{8,10},{10,8},{12,14},{14,12},{16,18},{18,... | collective-permute-start | bytes 786440 | tf_op jit(solution)/shard_map/ppermute | solution.py:425
  57.9 19.6 %copy-start.9 = (bf16[8,128,128]{2,1,0:T(8,128)(2,1)}, bf16[8,128,128]{2,1,0:T(8,128)(2,1)S(1)}, u32[]{:S(2)}) copy-start(bf16[8,128,128]{2,1,0:T(8,128)(2,1)S(1)} %collective-permute-done.2.refs_3_) | copy-start | bytes 786436
  57.9 19.5 %collective-permute-start.12 = (bf16[8,128,128]{2,1,0:T(8,128)(2,1)S(1)}, bf16[8,128,128]{2,1,0:T(8,128)(2,1)}, u32[]{:S(2)}, u32[]{:S(2)}) collective-permute-start(bf16[8,128,128]{2,1,0:T(8,128)(2,1)S(1)} %collective-permute-done.9.refs_10_), channel_id=1, source_target_pairs={{0,2},{2,0},{4,6},{6,4},{8,10},{10,8},{12,14},{14,12},{16,18},{18,... | collective-permute-start | bytes 786440 | tf_op jit(solution)/shard_map/ppermute | solution.py:425
  63.8 13.7 %copy-start.11 = (bf16[8,128,128]{2,1,0:T(8,128)(2,1)}, bf16[8,128,128]{2,1,0:T(8,128)(2,1)S(1)}, u32[]{:S(2)}) copy-start(bf16[8,128,128]{2,1,0:T(8,128)(2,1)S(1)} %collective-permute-done.5.refs_6_) | copy-start | bytes 786436
  63.8 13.6 %collective-permute-start.6 = (bf16[8,128,128]{2,1,0:T(8,128)(2,1)S(1)}, bf16[8,128,128]{2,1,0:T(8,128)(2,1)}, u32[]{:S(2)}, u32[]{:S(2)}) collective-permute-start(bf16[8,128,128]{2,1,0:T(8,128)(2,1)S(1)} %collective-permute-done.5.refs_6_), channel_id=1, source_target_pairs={{0,2},{2,0},{4,6},{6,4},{8,10},{10,8},{12,14},{14,12},{16,18},{18,... | collective-permute-start | bytes 786440 | tf_op jit(solution)/shard_map/ppermute | solution.py:425
  63.9 13.7 %copy-start.10 = (bf16[8,128,128]{2,1,0:T(8,128)(2,1)}, bf16[8,128,128]{2,1,0:T(8,128)(2,1)S(1)}, u32[]{:S(2)}) copy-start(bf16[8,128,128]{2,1,0:T(8,128)(2,1)S(1)} %collective-permute-done.13.refs_13_) | copy-start | bytes 786436
  63.9 5.8 %collective-permute-start.18 = (bf16[128,128]{1,0:T(8,128)(2,1)S(1)}, bf16[128,128]{1,0:T(8,128)(2,1)S(1)}, u32[]{:S(2)}, u32[]{:S(2)}) collective-permute-start(bf16[128,128]{1,0:T(8,128)(2,1)S(1)} %get-tuple-element.18), channel_id=1, source_target_pairs={{0,8},{2,10},{4,12},{6,14},{8,16},{10,18},{12,20},{14,22},{16,24},... | collective-permute-start | bytes 98312 | tf_op jit(solution)/shard_map/ppermute | solution.py:163
  65.7 11.9 %copy-start.12 = (bf16[8,128,128]{2,1,0:T(8,128)(2,1)}, bf16[8,128,128]{2,1,0:T(8,128)(2,1)S(1)}, u32[]{:S(2)}) copy-start(bf16[8,128,128]{2,1,0:T(8,128)(2,1)S(1)} %collective-permute-done.10.refs_8_) | copy-start | bytes 786436
  65.7 11.8 %collective-permute-start.11 = (bf16[8,128,128]{2,1,0:T(8,128)(2,1)S(1)}, bf16[8,128,128]{2,1,0:T(8,128)(2,1)}, u32[]{:S(2)}, u32[]{:S(2)}) collective-permute-start(bf16[8,128,128]{2,1,0:T(8,128)(2,1)S(1)} %collective-permute-done.10.refs_8_), channel_id=1, source_target_pairs={{0,2},{2,0},{4,6},{6,4},{8,10},{10,8},{12,14},{14,12},{16,18},{18,... | collective-permute-start | bytes 786440 | tf_op jit(solution)/shard_map/ppermute | solution.py:425
  65.9 11.7 %copy-start.13 = (bf16[8,128,128]{2,1,0:T(8,128)(2,1)}, bf16[8,128,128]{2,1,0:T(8,128)(2,1)S(1)}, u32[]{:S(2)}) copy-start(bf16[8,128,128]{2,1,0:T(8,128)(2,1)S(1)} %collective-permute-done.4.refs_5_) | copy-start | bytes 786436
  65.9 11.5 %collective-permute-start.19 = (bf16[128,128]{1,0:T(8,128)(2,1)}, bf16[128,128]{1,0:T(8,128)(2,1)S(1)}, u32[]{:S(2)}, u32[]{:S(2)}) collective-permute-start(bf16[128,128]{1,0:T(8,128)(2,1)} %get-tuple-element.17), channel_id=1, source_target_pairs={{0,16},{2,18},{4,20},{6,22},{8,24},{10,26},{12,28},{14,30},{16,0},... | collective-permute-start | bytes 98312 | tf_op jit(solution)/shard_map/ppermute | solution.py:163
  69.7 7.9 %copy-start.14 = (bf16[128,128]{1,0:T(8,128)(2,1)}, bf16[128,128]{1,0:T(8,128)(2,1)S(1)}, u32[]{:S(2)}) copy-start(bf16[128,128]{1,0:T(8,128)(2,1)S(1)} %collective-permute-done.18.refs_17_) | copy-start | bytes 98308
  69.7 7.8 %collective-permute-start.20 = (bf16[128,128]{1,0:T(8,128)(2,1)}, bf16[128,128]{1,0:T(8,128)(2,1)S(1)}, u32[]{:S(2)}, u32[]{:S(2)}) collective-permute-start(bf16[128,128]{1,0:T(8,128)(2,1)} %get-tuple-element.16), channel_id=1, source_target_pairs={{0,24},{2,26},{4,28},{6,30},{8,0},{10,2},{12,4},{14,6},{16,8},{18,... | collective-permute-start | bytes 98312 | tf_op jit(solution)/shard_map/ppermute | solution.py:163
  77.4 0.6 copy-start.15
  77.5 0.6 copy-start.16

commit v4 on v3

--- a/solution.py
+++ b/solution.py
@@ -71,92 +71,112 @@
     )(scalars, runs, subs)
 
 
-def rhs_kernel(scalars, ratings, runs, words, subs, out, table, sums):
-    slots, tile = ratings.shape[1], ratings.shape[2]
-    owners, own_rows = out.shape[1], out.shape[4]
-    tiles = owners * own_rows // tile
-    step = pl.program_id(0)
-    group = scalars[step, 3 * slots + 1]
-
-    @pl.when(step == 0)
-    def _():
-        table[...] = subs[...].astype(f32)
+def rhs_kernel(scalars, ratings_in, runs_in, words_in, subs_in, *refs, half, owners, own_rows):
+    given, refs = (refs[0], refs[1:]) if half == 0 else (None, refs)
+    outs, (ratings, runs, words, subs, table, sums, arrived, loaded) = refs[:-8], refs[-8:]
+    steps, slots, tile = ratings.shape[0], ratings.shape[1], ratings.shape[2]
+    levels = steps // 2
+
+    def load(step):
+        group = scalars[half * steps + step, 3 * slots + 1]
+        return pltpu.make_async_copy(ratings_in.at[group], ratings.at[step], arrived.at[step])
+
+    tables = [
+        pltpu.make_async_copy(source, target, loaded.at[k])
+        for k, (source, target) in enumerate(
+            [(subs_in, subs), (runs_in, runs), (words_in, words)]
+        )
+    ]
+    for copy in tables:
+        copy.start()
+    for step in range(steps):
+        load(step).start()
+    tables[0].wait()
+    table[...] = subs[...].astype(f32)
+    tables[1].wait()
+    tables[2].wait()
 
     eye = (
         lax.broadcasted_iota(jnp.int32, (tile, tile), 0)
         == lax.broadcasted_iota(jnp.int32, (tile, tile), 1)
     ).astype(f32).astype(bf16)
-    products, weights = [], []
-    live = scalars[group, 3 * slots]
-    for s in range(slots):
-        sub_row = table[pl.ds(scalars[group, 2 * slots + s], 1), :]
-        products.append(
-            (words[scalars[group, slots + s]].astype(f32) * sub_row).astype(bf16)
-        )
-        pair = runs[0, s]
-        seen = dot_nt(eye, mask_columns(pair[0:1], pair[1:2], tile)).astype(bf16)
-        value = seen * ratings[0, s]
-        user = jnp.where(s < live, scalars[group, s], -1)
-        weights.append(
-            jnp.concatenate(
-                [value * jnp.where(user == u, 1.0, 0.0).astype(bf16) for u in range(tiles)], axis=0
+    me = lax.axis_index("own")
+    for step in range(steps):
+        group = scalars[half * steps + step, 3 * slots + 1]
+        live = scalars[group, 3 * slots]
+        columns = []
+        for s in range(slots):
+            pair = runs[group, s]
+            columns.append(
+                mask_columns(pair[0:1], jnp.where(s < live, pair[1:2], 0), tile)
             )
-        )
-    sums[...] = dot_nn(jnp.concatenate(weights, axis=1), jnp.concatenate(products, axis=0))
-    me = lax.axis_index("own")
-    for o in range(owners):
-        owner = lax.rem(me + o, owners)
-        rows = pl.ds(pl.multiple_of(owner * own_rows, own_rows), own_rows)
-        out[0, o, 0, 0] = sums[rows, :].astype(out.dtype)
-
-
-def rhs_sums(scalars, ratings, runs, words, subs, owners, own_rows):
+        seen = dot_nt(eye, jnp.concatenate(columns, axis=0)).astype(bf16)
+        load(step).wait()
+        sums[step % 2] = jnp.zeros(sums.shape[1:], f32)
+        for s in range(slots):
+            sub_row = table[pl.ds(scalars[group, 2 * slots + s], 1), :]
+            product = (words[scalars[group, slots + s]].astype(f32) * sub_row).astype(bf16)
+            weights = seen[:, s * tile : (s + 1) * tile] * ratings[step, s]
+            rows = pl.ds(pl.multiple_of(scalars[group, s] * tile, tile), tile)
+            sums[step % 2, rows, :] += dot_nn(weights, product)
+        for o in range(owners):
+            owner = lax.rem(me + o, owners)
+            rows = pl.ds(pl.multiple_of(owner * own_rows, own_rows), own_rows)
+            value = sums[step % 2, rows, :]
+            if half == 0:
+                value = value + given[o, step // levels, step % levels].astype(f32)
+                outs[2 * o + step // levels][step % levels] = value.astype(bf16)
+            else:
+                outs[0][o, step // levels, step % levels] = value.astype(bf16)
+
+
+def rhs_sums(scalars, ratings, runs, words, subs, half, given, owners, own_rows):
     groups, slots, tile, _ = ratings.shape
     rank = words.shape[-1]
-    levels = groups // 4
-
-    def there(i, scalars):
-        return scalars[i, 3 * slots + 1]
-
+    steps, levels = groups // 2, groups // 4
+    anywhere = pl.BlockSpec(memory_space=pl.ANY)
+    whole = pl.BlockSpec(memory_space=pltpu.VMEM)
+    part = (levels, own_rows, rank)
+    shapes = [part] * (2 * owners) if half == 0 else [(owners, 2) + part]
     return pl.pallas_call(
-        rhs_kernel,
-        grid_spec=pltpu.PrefetchScalarGridSpec(
-            num_scalar_prefetch=1,
-            grid=(groups,),
-            in_specs=[
-                pl.BlockSpec((1, slots, tile, tile), lambda i, s: (there(i, s), 0, 0, 0)),
-                pl.BlockSpec((1, slots, 2, tile), lambda i, s: (there(i, s), 0, 0, 0)),
-                pl.BlockSpec(words.shape, lambda i, s: (0, 0, 0)),
-                pl.BlockSpec(subs.shape, lambda i, s: (0, 0)),
-            ],
-            out_specs=pl.BlockSpec(
-                (1, owners, 1, 1, own_rows, rank),
-                lambda i, s: (i // (2 * levels), 0, (i // levels) % 2, i % levels, 0, 0),
-            ),
-            scratch_shapes=[pltpu.VMEM(subs.shape, f32), pltpu.VMEM((owners * own_rows, rank), f32)],
-        ),
-        out_shape=jax.ShapeDtypeStruct((2, owners, 2, levels, own_rows, rank), bf16),
+        functools.partial(rhs_kernel, half=half, owners=owners, own_rows=own_rows),
+        in_specs=[pl.BlockSpec(memory_space=pltpu.SMEM)] + [anywhere] * 4 + [whole] * (1 - half),
+        out_specs=[whole] * len(shapes),
+        out_shape=[jax.ShapeDtypeStruct(shape, bf16) for shape in shapes],
+        scratch_shapes=[
+            pltpu.VMEM((steps,) + ratings.shape[1:], bf16),
+            pltpu.VMEM(runs.shape, jnp.int32),
+            pltpu.VMEM(words.shape, bf16),
+            pltpu.VMEM(subs.shape, bf16),
+            pltpu.VMEM(subs.shape, f32),
+            pltpu.VMEM((2, owners * own_rows, rank), f32),
+            pltpu.SemaphoreType.DMA((steps,)),
+            pltpu.SemaphoreType.DMA((3,)),
+        ],
         compiler_params=pltpu.CompilerParams(vmem_limit_bytes=VMEM_LIMIT),
         cost_estimate=pl.CostEstimate(
-            flops=16 * ratings.size * rank, bytes_accessed=2 * ratings.size, transcendentals=0
+            flops=8 * ratings.size * rank, bytes_accessed=8 * ratings.size, transcendentals=0
         ),
         name="rhs",
-    )(scalars, ratings, runs, words, subs)
-
-
-def add(left, right):
-    return (left.astype(f32) + right.astype(f32)).astype(bf16)
-
-
-def reduce_rhs(sums, shards, owners):
+    )(scalars, ratings, runs, words, subs, *([given] if half == 0 else []))
+
+
+def reduce_chip(parts, shards, owners):
+    total = [part.astype(f32) for part in parts[:1]]
+    for o in range(owners):
+        for column in range(2):
+            if o or column:
+                pairs = [
+                    (shard * owners + k, (shard ^ 2 * column) * owners + (k + o) % owners)
+                    for shard in range(shards)
+                    for k in range(owners)
+                ]
+                total.append(lax.ppermute(parts[2 * o + column], AXES, pairs).astype(f32))
+    return sum(total[1:], total[0]).astype(bf16)
+
+
+def reduce_levels(total, shards):
     levels = shards // 4
-    core = [(shard, shard ^ 1) for shard in range(shards)]
-    column = [(shard, shard ^ 2) for shard in range(shards)]
-    sums = add(sums[0], lax.ppermute(sums[1], "loop", core))
-    total = sums[0]
-    for o in range(1, owners):
-        total = add(total, lax.ppermute(sums[o], "own", [(k, (k + o) % owners) for k in range(owners)]))
-    total = add(total[0], lax.ppermute(total[1], "loop", column))
     terms = [total[0]]
     for up in range(1, levels):
         shift = [(shard, (shard + 4 * up) % shards) for shard in range(shards)]
@@ -397,7 +417,7 @@
     return jnp.where(column == 0, level, chips - 1 - level)
 
 
-def ring_gather(mine, shards):
+def ring_round(up, down, held, step, shards):
     chips = shards // 2
     levels = chips // 2
     order = [2 * level for level in range(levels)] + [
@@ -411,19 +431,16 @@
             for core in range(2)
         ]
 
-    other = [(shard, shard ^ 1) for shard in range(shards)]
-    up = down = mine
-    held = {0: mine}
-    for step in range(1, chips // 2 + 1):
-        up = lax.ppermute(up, "loop", shift(1))
-        held[chips - step] = up
-        if step < chips - step:
-            down = lax.ppermute(down, "loop", shift(-1))
-            held[step] = down
-    pieces = []
-    for distance in range(chips):
-        pieces += [held[distance], lax.ppermute(held[distance], "loop", other)]
-    return pieces
+    up = lax.ppermute(up, "loop", shift(1))
+    held[chips - step] = up
+    if step < chips - step:
+        down = lax.ppermute(down, "loop", shift(-1))
+        held[step] = down
+    return up, down
+
+
+def other_core(value, shards):
+    return lax.ppermute(value, "loop", [(shard, shard ^ 1) for shard in range(shards)])
 
 
 def on_device(
@@ -445,6 +462,7 @@
     devices = shards * owners
     chips, levels = shards // 2, shards // 4
     me, owner = lax.axis_index("loop"), lax.axis_index("own")
+    together = lax.optimization_barrier
 
     step = jnp.arange(groups, dtype=jnp.int32)
     level = (me // 4 + step % levels) % levels
@@ -454,13 +472,29 @@
         axis=1,
     )
 
-    pieces = ring_gather(word_factors[0], shards)
+    mine = word_factors[0]
+    inputs = (scalars, ratings[0, 0], runs[0, 0], mine, sub_factors)
+    held = {0: mine}
+    up, down = ring_round(mine, mine, held, 1, shards)
+    (away,) = rhs_sums(*inputs, 1, None, owners, own_rows)
+    up, down, away, scalars = together((up, down, away, scalars))
+
+    up, down = ring_round(up, down, held, 2, shards)
     message = facts(scalars, runs[0, 0], sub_factors, owners).reshape(devices, 4 * slots, rank)
     received = lax.all_to_all(message, AXES, 0, 0, tiled=True)
-    sums = rhs_sums(
-        scalars, ratings[0, 0], runs[0, 0], word_factors[0], sub_factors, owners, own_rows
-    )
-    terms = reduce_rhs(sums, shards, owners)
+    parts = rhs_sums(*inputs, 0, other_core(away, shards), owners, own_rows)
+    up, down, parts = together((up, down, parts))
+
+    up, down = ring_round(up, down, held, 3, shards)
+    total = reduce_chip(parts, shards, owners)
+    up, down, total = together((up, down, total))
+
+    for step in range(4, chips // 2 + 1):
+        up, down = ring_round(up, down, held, step, shards)
+    terms = reduce_levels(total, shards)
+    pieces = []
+    for distance in range(chips):
+        pieces += [held[distance], other_core(held[distance], shards)]
 
     got = received[:, 3 * slots, : 2 * slots].astype(jnp.int32)
     marks = (got[:, :slots] == owner * own_rows // tile + 1).astype(jnp.int32).reshape(-1)

time: 110 us -> 99.5 us (0.905)
  waiting for transfers between devices: 23.8 us -> 13.3 us
  starting transfers between devices: 20.2 us -> 22 us
  Pallas kernels: 42 us -> 40.9 us
    all_to_all x1, waiting for transfers between devices: 6.17 us -> 0.01 us  [on_device(): received = lax.all_to_all(message, AXES, 0, 0, tiled=True)]
    ppermute x21 -> x22, waiting for transfers between devices: 17.7 us -> 13.3 us  [the longest x4 8.76 us: ring_round(): up = lax.ppermute(up, 'loop', shift(1))]
    all_to_all x1, starting transfers between devices: 3.99 us -> 6.22 us  [on_device(): received = lax.all_to_all(message, AXES, 0, 0, tiled=True)]
    pallas_call x1 -> x2, Pallas kernels: 14.8 us -> 13.7 us  [rhs_sums(): pl.pallas_call(functools.partial(rhs_kernel, half=half, owners=owners, ow...]
    ppermute x21 -> x22, starting transfers between devices: 16.2 us -> 15.8 us  [the longest x4 5.03 us: ring_round(): up = lax.ppermute(up, 'loop', shift(1))]
  transfers between devices with their start and end apart: 22 -> 23, of which waited for: 7 -> 4; matrix products, arithmetic and copies ran while one was open for 4% -> 7% of each run, Pallas kernels for 8% -> 23%
where the time goes in v4:
time: 99.5 us; the launch traced here: 100 us
  Pallas kernels  40.9 us (41%)
  starting transfers between devices  22 us (22%)
  blocking collectives  14.1 us (14%)
  waiting for transfers between devices  13.3 us (13%)
  local copies, waits for them, and re-layouts  7.62 us (8%)
  other arithmetic  1.12 us (1%)
  between operations  1.04 us (1%)
    pallas_call x1, Pallas kernels, krylov(): pl.pallas_call(functools.partial(steps_kernel, shards=len(pieces), levels...  16.5 us
    all_to_all x1, blocking collectives, on_device(): everyone = lax.all_to_all(dots, AXES, 0, 0, tiled=True)  14.1 us
    pallas_call x2, Pallas kernels, rhs_sums(): pl.pallas_call(functools.partial(rhs_kernel, half=half, owners=owners, ow...  13.7 us
    ppermute x4, waiting for transfers between devices, ring_round(): up = lax.ppermute(up, 'loop', shift(1))  8.76 us
    pallas_call x1, Pallas kernels, build_masks(): pl.pallas_call(masks_kernel, in_specs=[scalars, whole], out_specs=[scalar...  6.46 us
    all_to_all x1, starting transfers between devices, on_device(): received = lax.all_to_all(message, AXES, 0, 0, tiled=True)  6.22 us
    ppermute x4, starting transfers between devices, ring_round(): up = lax.ppermute(up, 'loop', shift(1))  5.03 us
    ppermute x3, waiting for transfers between devices, reduce_chip(): total.append(lax.ppermute(parts[2 * o + column], AXES, pairs).astype(f32))  4.47 us
  transfers between devices with their start and end apart: 23, of which 4 were waited for; matrix products, arithmetic and copies ran while one was open for 7% of the time, Pallas kernels for 23%

profile of v4, /device:TPU:0, one launch (start us, length us, event | category | flops | bytes accessed | tf_op | source)
XLA Modules:
  0.0 100.0 jit_solution(15884239514247338948)
XLA Ops:
  0.6 3.1 %collective-permute-start = (bf16[8,128,128]{2,1,0:T(8,128)(2,1)}, bf16[8,128,128]{2,1,0:T(8,128)(2,1)S(1)}, u32[]{:S(2)}, u32[]{:S(2)}) collective-permute-start(bf16[8,128,128]{2,1,0:T(8,128)(2,1)} %bitcast.19), channel_id=1, source_target_pairs={{0,8},{2,10},{8,16},{10,18},{16,24},{18,26},{24,28},{26,30},{28,20... | collective-permute-start | bytes 786440 | tf_op jit(solution)/shard_map/ppermute | solution.py:434
  3.7 0.0 collective-permute-start.1
  3.7 0.8 copy.17
  4.5 0.8 copy.18
  5.2 0.8 copy.19
  6.0 0.7 copy.20
  6.7 0.7 concatenate.3.scalars
  7.4 6.8 %rhs.2 = bf16[2,2,4,128,128]{4,3,2,1,0:T(8,128)(2,1)} custom-call(s32[16,26]{1,0:T(8,128)} %concatenate.3.scalars, bf16[16,8,128,128]{3,2,1,0:T(8,128)(2,1)} %bitcast.35, s32[16,8,2,128]{3,2,1,0:T(2,128)} %bitcast.27, bf16[8,128,128]{2,1,0:T(8,128)(2,1)} %bitcast.21, bf16[2048,128]{1,0:T(8,128)(2,1)} %subs_in.3), custom_call_target="tpu_custom_call" | custom-call | flops 2147483648 | bytes 16777216 | tf_op jit(solution)/shard_map/rhs/pallas_call | solution.py:141
  14.2 0.0 collective-permute-done.1.refs_2_
  14.3 0.1 collective-permute-start.7
  14.3 2.0 %collective-permute-start.4 = (bf16[8,128,128]{2,1,0:T(8,128)(2,1)S(1)}, bf16[8,128,128]{2,1,0:T(8,128)(2,1)S(1)}, u32[]{:S(2)}, u32[]{:S(2)}) collective-permute-start(bf16[8,128,128]{2,1,0:T(8,128)(2,1)S(1)} %collective-permute-done.1.refs_2_), channel_id=1, source_target_pairs={{0,4},{2,6},{8,0},{10,2},{16,8},{18,10},{24,16},{26,18},{28,24},{3... | collective-permute-start | bytes 786440 | tf_op jit(solution)/shard_map/ppermute | solution.py:437
  16.3 0.1 collective-permute-start.6
  16.5 2.4 %facts.1 = bf16[16,2,32,128]{3,2,1,0:T(8,128)(2,1)} custom-call(s32[16,26]{1,0:T(8,128)} %concatenate.3.scalars, s32[16,8,2,128]{3,2,1,0:T(2,128)} %bitcast.28, bf16[2048,128]{1,0:T(8,128)(2,1)} %subs_in.3), custom_call_target="tpu_custom_call" | custom-call | tf_op jit(solution)/shard_map/facts/pallas_call | solution.py:63
  18.9 6.2 %all-to-all-start = ((bf16[32,32,128]{2,1,0:T(8,128)(2,1)}), bf16[32,32,128]{2,1,0:T(8,128)(2,1)S(1)}, u32[]{:S(2)}, u32[]{:S(2)}) async-start(bf16[32,32,128]{2,1,0:T(8,128)(2,1)} %bitcast.18), calls=%async_computation | async-start | bytes 524288 | tf_op jit(solution)/shard_map/all_to_all | solution.py:484
  25.1 0.8 copy-done.18
  25.9 6.9 %rhs.3 = (bf16[4,128,128]{2,1,0:T(8,128)(2,1)}, bf16[4,128,128]{2,1,0:T(8,128)(2,1)}, bf16[4,128,128]{2,1,0:T(8,128)(2,1)}, bf16[4,128,128]{2,1,0:T(8,128)(2,1)}) custom-call(s32[16,26]{1,0:T(8,128)} %concatenate.3.scalars, bf16[16,8,128,128]{3,2,1,0:T(8,128)(2,1)} %bitcast.36, s32[16,8,2,128]{3,2,1,0:T(2,128)} %bitcast.29, bf16[8,128,128]{2,1,0:T(8,128)(2,1)} %bitcast.22, ...), custom_call_target="tpu_custom_call" | custom-call | flops 2147483648 | bytes 16777216 | tf_op jit(solution)/shard_map/rhs/pallas_call | solution.py:141
  32.8 0.0 collective-permute-done.4.refs_4_
  32.9 0.0 collective-permute-done.6.refs_12_
  32.9 1.8 %collective-permute-start.11 = (bf16[4,128,128]{2,1,0:T(8,128)(2,1)}, bf16[4,128,128]{2,1,0:T(8,128)(2,1)S(1)}, u32[]{:S(2)}, u32[]{:S(2)}) collective-permute-start(bf16[4,128,128]{2,1,0:T(8,128)(2,1)} %get-tuple-element.39), channel_id=1, source_target_pairs={{0,4},{1,5},{2,6},{3,7},{4,0},{5,1},{6,2},{7,3},{8,12},{9,13},{10,... | collective-permute-start | bytes 393224 | tf_op jit(solution)/shard_map/ppermute | solution.py:174
  34.7 1.5 %collective-permute-start.12 = (bf16[4,128,128]{2,1,0:T(8,128)(2,1)}, bf16[4,128,128]{2,1,0:T(8,128)(2,1)S(1)}, u32[]{:S(2)}, u32[]{:S(2)}) collective-permute-start(bf16[4,128,128]{2,1,0:T(8,128)(2,1)} %get-tuple-element.40), channel_id=1, source_target_pairs={{0,1},{1,0},{2,3},{3,2},{4,5},{5,4},{6,7},{7,6},{8,9},{9,8},{10,11... | collective-permute-start | bytes 393224 | tf_op jit(solution)/shard_map/ppermute | solution.py:174
  36.2 0.3 collective-permute-start.13
  36.4 1.7 %collective-permute-start.10 = (bf16[8,128,128]{2,1,0:T(8,128)(2,1)S(1)}, bf16[8,128,128]{2,1,0:T(8,128)(2,1)S(1)}, u32[]{:S(2)}, u32[]{:S(2)}) collective-permute-start(bf16[8,128,128]{2,1,0:T(8,128)(2,1)S(1)} %collective-permute-done.6.refs_12_), channel_id=1, source_target_pairs={{0,8},{2,10},{8,16},{10,18},{16,24},{18,26},{24,28},{26,30},{28,20... | collective-permute-start | bytes 786440 | tf_op jit(solution)/shard_map/ppermute | solution.py:434
  38.2 0.3 collective-permute-start.8
  38.5 0.7 copy.21.activity
  39.3 0.0 collective-permute-start.2
  39.3 3.0 %collective-permute-done.12 = bf16[4,128,128]{2,1,0:T(8,128)(2,1)S(1)} collective-permute-done((bf16[4,128,128]{2,1,0:T(8,128)(2,1)}, bf16[4,128,128]{2,1,0:T(8,128)(2,1)S(1)}, u32[]{:S(2)}, u32[]{:S(2)}) %collective-permute-start.12) | collective-permute-done | bytes 131104 | tf_op jit(solution)/shard_map/ppermute | solution.py:174
  42.3 1.5 %collective-permute-done.13 = bf16[4,128,128]{2,1,0:T(8,128)(2,1)S(1)} collective-permute-done((bf16[4,128,128]{2,1,0:T(8,128)(2,1)}, bf16[4,128,128]{2,1,0:T(8,128)(2,1)S(1)}, u32[]{:S(2)}, u32[]{:S(2)}) %collective-permute-start.13) | collective-permute-done | bytes 131104 | tf_op jit(solution)/shard_map/ppermute | solution.py:174
  43.7 1.0 add_convert_fusion
  44.7 2.6 %collective-permute-done.10.refs_10_ = bf16[8,128,128]{2,1,0:T(8,128)(2,1)S(1)} collective-permute-done((bf16[8,128,128]{2,1,0:T(8,128)(2,1)S(1)}, bf16[8,128,128]{2,1,0:T(8,128)(2,1)S(1)}, u32[]{:S(2)}, u32[]{:S(2)}) %collective-permute-start.10) | collective-permute-done | bytes 262176 | tf_op jit(solution)/shard_map/ppermute | solution.py:434
  47.3 0.1 collective-permute-start.14
  47.4 0.5 collective-permute-start.5
  47.9 0.7 slice_bitcast_fusion
  48.6 0.7 collective-permute-start.19
  49.3 0.1 collective-permute-start.16
  49.4 0.4 collective-permute-start.9
  49.8 6.2 %collective-permute-done.14.refs_8_ = bf16[8,128,128]{2,1,0:T(8,128)(2,1)S(1)} collective-permute-done((bf16[8,128,128]{2,1,0:T(8,128)(2,1)S(1)}, bf16[8,128,128]{2,1,0:T(8,128)(2,1)S(1)}, u32[]{:S(2)}, u32[]{:S(2)}) %collective-permute-start.14) | collective-permute-done | bytes 262176 | tf_op jit(solution)/shard_map/ppermute | solution.py:434
  56.0 0.1 slice_add_fusion
  56.1 1.0 %collective-permute-start.20 = (bf16[128,128]{1,0:T(8,128)(2,1)}, bf16[128,128]{1,0:T(8,128)(2,1)S(1)}, u32[]{:S(2)}, u32[]{:S(2)}) collective-permute-start(bf16[128,128]{1,0:T(8,128)(2,1)} %get-tuple-element.49), channel_id=1, source_target_pairs={{0,16},{2,18},{4,20},{6,22},{8,24},{10,26},{12,28},{14,30},{16,0},... | collective-permute-start | bytes 98312 | tf_op jit(solution)/shard_map/ppermute | solution.py:183
  57.1 2.1 %collective-permute-start.21 = (bf16[128,128]{1,0:T(8,128)(2,1)}, bf16[128,128]{1,0:T(8,128)(2,1)S(1)}, u32[]{:S(2)}, u32[]{:S(2)}) collective-permute-start(bf16[128,128]{1,0:T(8,128)(2,1)} %get-tuple-element.48), channel_id=1, source_target_pairs={{0,24},{2,26},{4,28},{6,30},{8,0},{10,2},{12,4},{14,6},{16,8},{18,... | collective-permute-start | bytes 98312 | tf_op jit(solution)/shard_map/ppermute | solution.py:183
  59.3 0.6 reshape.350.marks
  59.9 0.6 reshape.347.word_index
  60.5 6.5 %masks.1 = (s32[257]{0:T(512)}, f32[256,128]{1,0:T(8,128)}, bf16[32,128,1024]{2,1,0:T(8,128)(2,1)}) custom-call(s32[256]{0:T(256)} %reshape.350.marks, bf16[32,32,128]{2,1,0:T(8,128)(2,1)} %copy-done), custom_call_target="tpu_custom_call" | custom-call | tf_op jit(solution)/shard_map/masks/pallas_call | solution.py:250
  67.0 0.0 copy-start.16
  67.2 0.4 copy-done.15
  67.6 0.0 copy-done.16
  67.6 16.5 %krylov.1 = (f32[128,128]{1,0:T(8,128)}, f32[128,128]{1,0:T(8,128)}, f32[128,128]{1,0:T(8,128)}, f32[32,1,128]{2,1,0:T(1,128)}) custom-call(s32[257]{0:T(512)} %get-tuple-element.26.chosen, s32[256]{0:T(256)} %reshape.347.word_index, f32[128,128]{1,0:T(8,128)} %start.3, f32[128,1]{1,0:T(8,128)} %copy.21.activity, f32[256,128]{1,0:T(8,128)} %get-tuple-element.27.subs, ...), custom_call_target="tpu_custom_call" | custom-call | tf_op jit(solution)/shard_map/krylov/pallas_call | solution.py:371
  84.1 14.1 %all_to_all.10.dots = f32[32,1,128]{2,1,0:T(1,128)} all-to-all(f32[32,1,128]{2,1,0:T(1,128)} %get-tuple-element.44), channel_id=1, replica_groups=mesh['loop'=16,'own'=2] {'loop','own'}, dimensions={0} | all-to-all | bytes 32768 | tf_op jit(solution)/shard_map/all_to_all | solution.py:510
  98.1 1.9 %last_step.1 = (f32[128,128]{1,0:T(8,128)}, f32[128,128]{1,0:T(8,128)}) custom-call(f32[32,1,128]{2,1,0:T(1,128)} %all_to_all.10.dots, f32[128,128]{1,0:T(8,128)} %start.3, f32[128,128]{1,0:T(8,128)} %get-tuple-element.45.first, f32[128,128]{1,0:T(8,128)} %get-tuple-element.46.second, f32[128,128]{1,0:T(8,128)} %get-tuple-element.47.third), custom_call_target="tpu_custom_call" | custom-call | tf_op jit(solution)/shard_map/last_step/pallas_call | solution.py:404
  (58 shorter events, 0.2 us)
Async XLA Ops:
  0.6 13.6 %collective-permute-start = (bf16[8,128,128]{2,1,0:T(8,128)(2,1)}, bf16[8,128,128]{2,1,0:T(8,128)(2,1)S(1)}, u32[]{:S(2)}, u32[]{:S(2)}) collective-permute-start(bf16[8,128,128]{2,1,0:T(8,128)(2,1)} %bitcast.19), channel_id=1, source_target_pairs={{0,8},{2,10},{8,16},{10,18},{16,24},{18,26},{24,28},{26,30},{28,20... | collective-permute-start | bytes 786440 | tf_op jit(solution)/shard_map/ppermute | solution.py:434
  3.7 10.5 %collective-permute-start.1 = (bf16[8,128,128]{2,1,0:T(8,128)(2,1)}, bf16[8,128,128]{2,1,0:T(8,128)(2,1)S(1)}, u32[]{:S(2)}, u32[]{:S(2)}) collective-permute-start(bf16[8,128,128]{2,1,0:T(8,128)(2,1)} %bitcast.20), channel_id=1, source_target_pairs={{0,4},{2,6},{8,0},{10,2},{16,8},{18,10},{24,16},{26,18},{28,24},{3... | collective-permute-start | bytes 786440 | tf_op jit(solution)/shard_map/ppermute | solution.py:437
  7.4 31.1 %copy-start.17 = (f32[128]{0:T(128)S(1)}, f32[128]{0:T(128)}, u32[]{:S(2)}) copy-start(f32[128]{0:T(128)} %param.11) | copy-start | bytes 1540
  7.4 31.9 %copy-start.1 = (bf16[1,8,128,128]{3,2,1,0:T(8,128)(2,1)S(1)}, bf16[1,8,128,128]{3,2,1,0:T(8,128)(2,1)}, u32[]{:S(2)}) copy-start(bf16[1,8,128,128]{3,2,1,0:T(8,128)(2,1)} %param.12) | copy-start | bytes 786436
  14.2 52.8 %copy-start.2 = (bf16[8,128,128]{2,1,0:T(8,128)(2,1)}, bf16[8,128,128]{2,1,0:T(8,128)(2,1)S(1)}, u32[]{:S(2)}) copy-start(bf16[8,128,128]{2,1,0:T(8,128)(2,1)S(1)} %collective-permute-done.refs_14_) | copy-start | bytes 786436
  14.2 52.8 %copy-start.3 = (bf16[8,128,128]{2,1,0:T(8,128)(2,1)}, bf16[8,128,128]{2,1,0:T(8,128)(2,1)S(1)}, u32[]{:S(2)}) copy-start(bf16[8,128,128]{2,1,0:T(8,128)(2,1)S(1)} %collective-permute-done.1.refs_2_) | copy-start | bytes 786436
  14.3 10.9 %collective-permute-start.7 = (bf16[2,2,4,128,128]{4,3,2,1,0:T(8,128)(2,1)}, bf16[2,2,4,128,128]{4,3,2,1,0:T(8,128)(2,1)S(1)}, u32[]{:S(2)}, u32[]{:S(2)}) collective-permute-start(bf16[2,2,4,128,128]{4,3,2,1,0:T(8,128)(2,1)} %rhs.2), channel_id=1, source_target_pairs={{0,2},{2,0},{4,6},{6,4},{8,10},{10,8},{12,14},{14,12},{16,18},{18,... | collective-permute-start | bytes 1572872 | tf_op jit(solution)/shard_map/ppermute | solution.py:443
  14.3 18.5 %collective-permute-start.4 = (bf16[8,128,128]{2,1,0:T(8,128)(2,1)S(1)}, bf16[8,128,128]{2,1,0:T(8,128)(2,1)S(1)}, u32[]{:S(2)}, u32[]{:S(2)}) collective-permute-start(bf16[8,128,128]{2,1,0:T(8,128)(2,1)S(1)} %collective-permute-done.1.refs_2_), channel_id=1, source_target_pairs={{0,4},{2,6},{8,0},{10,2},{16,8},{18,10},{24,16},{26,18},{28,24},{3... | collective-permute-start | bytes 786440 | tf_op jit(solution)/shard_map/ppermute | solution.py:437
  16.3 16.5 %collective-permute-start.6 = (bf16[8,128,128]{2,1,0:T(8,128)(2,1)S(1)}, bf16[8,128,128]{2,1,0:T(8,128)(2,1)S(1)}, u32[]{:S(2)}, u32[]{:S(2)}) collective-permute-start(bf16[8,128,128]{2,1,0:T(8,128)(2,1)S(1)} %collective-permute-done.refs_14_), channel_id=1, source_target_pairs={{0,8},{2,10},{8,16},{10,18},{16,24},{18,26},{24,28},{26,30},{28,20... | collective-permute-start | bytes 786440 | tf_op jit(solution)/shard_map/ppermute | solution.py:434
  18.9 28.5 %all-to-all-start = ((bf16[32,32,128]{2,1,0:T(8,128)(2,1)}), bf16[32,32,128]{2,1,0:T(8,128)(2,1)S(1)}, u32[]{:S(2)}, u32[]{:S(2)}) async-start(bf16[32,32,128]{2,1,0:T(8,128)(2,1)} %bitcast.18), calls=%async_computation | async-start | bytes 524288 | tf_op jit(solution)/shard_map/all_to_all | solution.py:484
  25.1 0.8 copy-start.18
  32.9 34.2 %copy-start.4 = (bf16[8,128,128]{2,1,0:T(8,128)(2,1)}, bf16[8,128,128]{2,1,0:T(8,128)(2,1)S(1)}, u32[]{:S(2)}) copy-start(bf16[8,128,128]{2,1,0:T(8,128)(2,1)S(1)} %collective-permute-done.4.refs_4_) | copy-start | bytes 786436
  32.9 34.2 %copy-start.5 = (bf16[8,128,128]{2,1,0:T(8,128)(2,1)}, bf16[8,128,128]{2,1,0:T(8,128)(2,1)S(1)}, u32[]{:S(2)}) copy-start(bf16[8,128,128]{2,1,0:T(8,128)(2,1)S(1)} %collective-permute-done.6.refs_12_) | copy-start | bytes 786436
  32.9 6.4 %collective-permute-start.11 = (bf16[4,128,128]{2,1,0:T(8,128)(2,1)}, bf16[4,128,128]{2,1,0:T(8,128)(2,1)S(1)}, u32[]{:S(2)}, u32[]{:S(2)}) collective-permute-start(bf16[4,128,128]{2,1,0:T(8,128)(2,1)} %get-tuple-element.39), channel_id=1, source_target_pairs={{0,4},{1,5},{2,6},{3,7},{4,0},{5,1},{6,2},{7,3},{8,12},{9,13},{10,... | collective-permute-start | bytes 393224 | tf_op jit(solution)/shard_map/ppermute | solution.py:174
  34.7 7.6 %collective-permute-start.12 = (bf16[4,128,128]{2,1,0:T(8,128)(2,1)}, bf16[4,128,128]{2,1,0:T(8,128)(2,1)S(1)}, u32[]{:S(2)}, u32[]{:S(2)}) collective-permute-start(bf16[4,128,128]{2,1,0:T(8,128)(2,1)} %get-tuple-element.40), channel_id=1, source_target_pairs={{0,1},{1,0},{2,3},{3,2},{4,5},{5,4},{6,7},{7,6},{8,9},{9,8},{10,11... | collective-permute-start | bytes 393224 | tf_op jit(solution)/shard_map/ppermute | solution.py:174
  36.2 7.6 %collective-permute-start.13 = (bf16[4,128,128]{2,1,0:T(8,128)(2,1)}, bf16[4,128,128]{2,1,0:T(8,128)(2,1)S(1)}, u32[]{:S(2)}, u32[]{:S(2)}) collective-permute-start(bf16[4,128,128]{2,1,0:T(8,128)(2,1)} %get-tuple-element.41), channel_id=1, source_target_pairs={{0,5},{1,4},{2,7},{3,6},{4,1},{5,0},{6,3},{7,2},{8,13},{9,12},{10,... | collective-permute-start | bytes 393224 | tf_op jit(solution)/shard_map/ppermute | solution.py:174
  36.4 10.8 %collective-permute-start.10 = (bf16[8,128,128]{2,1,0:T(8,128)(2,1)S(1)}, bf16[8,128,128]{2,1,0:T(8,128)(2,1)S(1)}, u32[]{:S(2)}, u32[]{:S(2)}) collective-permute-start(bf16[8,128,128]{2,1,0:T(8,128)(2,1)S(1)} %collective-permute-done.6.refs_12_), channel_id=1, source_target_pairs={{0,8},{2,10},{8,16},{10,18},{16,24},{18,26},{24,28},{26,30},{28,20... | collective-permute-start | bytes 786440 | tf_op jit(solution)/shard_map/ppermute | solution.py:434
  38.2 9.1 %collective-permute-start.8 = (bf16[8,128,128]{2,1,0:T(8,128)(2,1)S(1)}, bf16[8,128,128]{2,1,0:T(8,128)(2,1)S(1)}, u32[]{:S(2)}, u32[]{:S(2)}) collective-permute-start(bf16[8,128,128]{2,1,0:T(8,128)(2,1)S(1)} %collective-permute-done.4.refs_4_), channel_id=1, source_target_pairs={{0,4},{2,6},{8,0},{10,2},{16,8},{18,10},{24,16},{26,18},{28,24},{3... | collective-permute-start | bytes 786440 | tf_op jit(solution)/shard_map/ppermute | solution.py:437
  39.3 8.1 %collective-permute-start.2 = (bf16[8,128,128]{2,1,0:T(8,128)(2,1)S(1)}, bf16[8,128,128]{2,1,0:T(8,128)(2,1)S(1)}, u32[]{:S(2)}, u32[]{:S(2)}) collective-permute-start(bf16[8,128,128]{2,1,0:T(8,128)(2,1)S(1)} %bitcast.24), channel_id=1, source_target_pairs={{0,2},{2,0},{4,6},{6,4},{8,10},{10,8},{12,14},{14,12},{16,18},{18,... | collective-permute-start | bytes 786440 | tf_op jit(solution)/shard_map/ppermute | solution.py:443
  42.3 6.3 %collective-permute-start.18 = (bf16[8,128,128]{2,1,0:T(8,128)(2,1)S(1)}, bf16[8,128,128]{2,1,0:T(8,128)(2,1)S(1)}, u32[]{:S(2)}, u32[]{:S(2)}) collective-permute-start(bf16[8,128,128]{2,1,0:T(8,128)(2,1)S(1)} %collective-permute-done.refs_14_), channel_id=1, source_target_pairs={{0,2},{2,0},{4,6},{6,4},{8,10},{10,8},{12,14},{14,12},{16,18},{18,... | collective-permute-start | bytes 786440 | tf_op jit(solution)/shard_map/ppermute | solution.py:443
  43.7 5.5 %collective-permute-start.3 = (bf16[8,128,128]{2,1,0:T(8,128)(2,1)S(1)}, bf16[8,128,128]{2,1,0:T(8,128)(2,1)S(1)}, u32[]{:S(2)}, u32[]{:S(2)}) collective-permute-start(bf16[8,128,128]{2,1,0:T(8,128)(2,1)S(1)} %collective-permute-done.1.refs_2_), channel_id=1, source_target_pairs={{0,2},{2,0},{4,6},{6,4},{8,10},{10,8},{12,14},{14,12},{16,18},{18,... | collective-permute-start | bytes 786440 | tf_op jit(solution)/shard_map/ppermute | solution.py:443
  47.3 19.8 %copy-start.6 = (bf16[8,128,128]{2,1,0:T(8,128)(2,1)}, bf16[8,128,128]{2,1,0:T(8,128)(2,1)S(1)}, u32[]{:S(2)}) copy-start(bf16[8,128,128]{2,1,0:T(8,128)(2,1)S(1)} %collective-permute-done.10.refs_10_) | copy-start | bytes 786436
  47.3 2.2 %collective-permute-start.17 = (bf16[8,128,128]{2,1,0:T(8,128)(2,1)S(1)}, bf16[8,128,128]{2,1,0:T(8,128)(2,1)S(1)}, u32[]{:S(2)}, u32[]{:S(2)}) collective-permute-start(bf16[8,128,128]{2,1,0:T(8,128)(2,1)S(1)} %collective-permute-done.6.refs_12_), channel_id=1, source_target_pairs={{0,2},{2,0},{4,6},{6,4},{8,10},{10,8},{12,14},{14,12},{16,18},{18,... | collective-permute-start | bytes 786440 | tf_op jit(solution)/shard_map/ppermute | solution.py:443
  47.3 19.8 %copy-start.7 = (bf16[8,128,128]{2,1,0:T(8,128)(2,1)}, bf16[8,128,128]{2,1,0:T(8,128)(2,1)S(1)}, u32[]{:S(2)}) copy-start(bf16[8,128,128]{2,1,0:T(8,128)(2,1)S(1)} %collective-permute-done.8.refs_6_) | copy-start | bytes 786436
  47.3 8.7 %collective-permute-start.14 = (bf16[8,128,128]{2,1,0:T(8,128)(2,1)S(1)}, bf16[8,128,128]{2,1,0:T(8,128)(2,1)S(1)}, u32[]{:S(2)}, u32[]{:S(2)}) collective-permute-start(bf16[8,128,128]{2,1,0:T(8,128)(2,1)S(1)} %collective-permute-done.10.refs_10_), channel_id=1, source_target_pairs={{0,8},{2,10},{8,16},{10,18},{16,24},{18,26},{24,28},{26,30},{28,20... | collective-permute-start | bytes 786440 | tf_op jit(solution)/shard_map/ppermute | solution.py:434
  47.4 13.1 %copy-start = (bf16[32,32,128]{2,1,0:T(8,128)(2,1)}, bf16[32,32,128]{2,1,0:T(8,128)(2,1)S(1)}, u32[]{:S(2)}) copy-start(bf16[32,32,128]{2,1,0:T(8,128)(2,1)S(1)} %all-to-all-done.received) | copy-start | bytes 786436
  47.4 19.7 %copy-start.8 = (bf16[8,128,128]{2,1,0:T(8,128)(2,1)}, bf16[8,128,128]{2,1,0:T(8,128)(2,1)S(1)}, u32[]{:S(2)}) copy-start(bf16[8,128,128]{2,1,0:T(8,128)(2,1)S(1)} %collective-permute-done.2.refs_1_) | copy-start | bytes 786436
  47.4 8.7 %collective-permute-start.5 = (bf16[8,128,128]{2,1,0:T(8,128)(2,1)S(1)}, bf16[8,128,128]{2,1,0:T(8,128)(2,1)S(1)}, u32[]{:S(2)}, u32[]{:S(2)}) collective-permute-start(bf16[8,128,128]{2,1,0:T(8,128)(2,1)S(1)} %collective-permute-done.4.refs_4_), channel_id=1, source_target_pairs={{0,2},{2,0},{4,6},{6,4},{8,10},{10,8},{12,14},{14,12},{16,18},{18,... | collective-permute-start | bytes 786440 | tf_op jit(solution)/shard_map/ppermute | solution.py:443
  48.6 18.5 %copy-start.9 = (bf16[8,128,128]{2,1,0:T(8,128)(2,1)}, bf16[8,128,128]{2,1,0:T(8,128)(2,1)S(1)}, u32[]{:S(2)}) copy-start(bf16[8,128,128]{2,1,0:T(8,128)(2,1)S(1)} %collective-permute-done.18.refs_15_) | copy-start | bytes 786436
  48.6 8.5 %collective-permute-start.19 = (bf16[128,128]{1,0:T(8,128)(2,1)S(1)}, bf16[128,128]{1,0:T(8,128)(2,1)S(1)}, u32[]{:S(2)}, u32[]{:S(2)}) collective-permute-start(bf16[128,128]{1,0:T(8,128)(2,1)S(1)} %get-tuple-element.50), channel_id=1, source_target_pairs={{0,8},{2,10},{4,12},{6,14},{8,16},{10,18},{12,20},{14,22},{16,24},... | collective-permute-start | bytes 98312 | tf_op jit(solution)/shard_map/ppermute | solution.py:183
  49.3 17.8 %copy-start.10 = (bf16[8,128,128]{2,1,0:T(8,128)(2,1)}, bf16[8,128,128]{2,1,0:T(8,128)(2,1)S(1)}, u32[]{:S(2)}) copy-start(bf16[8,128,128]{2,1,0:T(8,128)(2,1)S(1)} %collective-permute-done.3.refs_3_) | copy-start | bytes 786436
  49.3 17.7 %collective-permute-start.16 = (bf16[8,128,128]{2,1,0:T(8,128)(2,1)S(1)}, bf16[8,128,128]{2,1,0:T(8,128)(2,1)}, u32[]{:S(2)}, u32[]{:S(2)}) collective-permute-start(bf16[8,128,128]{2,1,0:T(8,128)(2,1)S(1)} %collective-permute-done.10.refs_10_), channel_id=1, source_target_pairs={{0,2},{2,0},{4,6},{6,4},{8,10},{10,8},{12,14},{14,12},{16,18},{18,... | collective-permute-start | bytes 786440 | tf_op jit(solution)/shard_map/ppermute | solution.py:443
  49.4 17.7 %copy-start.11 = (bf16[8,128,128]{2,1,0:T(8,128)(2,1)}, bf16[8,128,128]{2,1,0:T(8,128)(2,1)S(1)}, u32[]{:S(2)}) copy-start(bf16[8,128,128]{2,1,0:T(8,128)(2,1)S(1)} %collective-permute-done.17.refs_13_) | copy-start | bytes 786436
  49.4 17.6 %collective-permute-start.9 = (bf16[8,128,128]{2,1,0:T(8,128)(2,1)S(1)}, bf16[8,128,128]{2,1,0:T(8,128)(2,1)}, u32[]{:S(2)}, u32[]{:S(2)}) collective-permute-start(bf16[8,128,128]{2,1,0:T(8,128)(2,1)S(1)} %collective-permute-done.8.refs_6_), channel_id=1, source_target_pairs={{0,2},{2,0},{4,6},{6,4},{8,10},{10,8},{12,14},{14,12},{16,18},{18,... | collective-permute-start | bytes 786440 | tf_op jit(solution)/shard_map/ppermute | solution.py:443
  56.0 11.1 %copy-start.12 = (bf16[8,128,128]{2,1,0:T(8,128)(2,1)}, bf16[8,128,128]{2,1,0:T(8,128)(2,1)S(1)}, u32[]{:S(2)}) copy-start(bf16[8,128,128]{2,1,0:T(8,128)(2,1)S(1)} %collective-permute-done.14.refs_8_) | copy-start | bytes 786436
  56.0 11.0 %collective-permute-start.15 = (bf16[8,128,128]{2,1,0:T(8,128)(2,1)S(1)}, bf16[8,128,128]{2,1,0:T(8,128)(2,1)}, u32[]{:S(2)}, u32[]{:S(2)}) collective-permute-start(bf16[8,128,128]{2,1,0:T(8,128)(2,1)S(1)} %collective-permute-done.14.refs_8_), channel_id=1, source_target_pairs={{0,2},{2,0},{4,6},{6,4},{8,10},{10,8},{12,14},{14,12},{16,18},{18,... | collective-permute-start | bytes 786440 | tf_op jit(solution)/shard_map/ppermute | solution.py:443
  56.1 11.1 %copy-start.13 = (bf16[8,128,128]{2,1,0:T(8,128)(2,1)}, bf16[8,128,128]{2,1,0:T(8,128)(2,1)S(1)}, u32[]{:S(2)}) copy-start(bf16[8,128,128]{2,1,0:T(8,128)(2,1)S(1)} %collective-permute-done.5.refs_5_) | copy-start | bytes 786436
  56.1 10.9 %collective-permute-start.20 = (bf16[128,128]{1,0:T(8,128)(2,1)}, bf16[128,128]{1,0:T(8,128)(2,1)S(1)}, u32[]{:S(2)}, u32[]{:S(2)}) collective-permute-start(bf16[128,128]{1,0:T(8,128)(2,1)} %get-tuple-element.49), channel_id=1, source_target_pairs={{0,16},{2,18},{4,20},{6,22},{8,24},{10,26},{12,28},{14,30},{16,0},... | collective-permute-start | bytes 98312 | tf_op jit(solution)/shard_map/ppermute | solution.py:183
  57.1 10.1 %copy-start.14 = (bf16[128,128]{1,0:T(8,128)(2,1)}, bf16[128,128]{1,0:T(8,128)(2,1)S(1)}, u32[]{:S(2)}) copy-start(bf16[128,128]{1,0:T(8,128)(2,1)S(1)} %collective-permute-done.19.refs_17_) | copy-start | bytes 98308
  57.1 9.9 %collective-permute-start.21 = (bf16[128,128]{1,0:T(8,128)(2,1)}, bf16[128,128]{1,0:T(8,128)(2,1)S(1)}, u32[]{:S(2)}, u32[]{:S(2)}) collective-permute-start(bf16[128,128]{1,0:T(8,128)(2,1)} %get-tuple-element.48), channel_id=1, source_target_pairs={{0,24},{2,26},{4,28},{6,30},{8,0},{10,2},{12,4},{14,6},{16,8},{18,... | collective-permute-start | bytes 98312 | tf_op jit(solution)/shard_map/ppermute | solution.py:183
  67.0 0.6 copy-start.15
  67.0 0.6 copy-start.16

commit v5 on v4

--- a/solution.py
+++ b/solution.py
@@ -29,7 +29,7 @@
     return jnp.where(inside, 1.0, 0.0).astype(bf16)
 
 
-def facts_kernel(scalars, runs, subs, out, table):
+def facts_kernel(user_tile, word_tile, subreddit, counts, runs, subs, out, table):
     groups, slots = runs.shape[0], runs.shape[1]
     owners, rank = out.shape[1], out.shape[3]
     table[...] = subs[...].astype(f32)
@@ -38,12 +38,12 @@
     def body(group, carry):
         sub_rows, run_rows = [], []
         marks = jnp.zeros((1, rank), jnp.int32)
-        live = scalars[group, 3 * slots]
+        live = counts[0, group]
         for s in range(slots):
-            sub_rows.append(table[pl.ds(scalars[group, 2 * slots + s], 1), :])
+            sub_rows.append(table[pl.ds(subreddit[s, group], 1), :])
             run_rows.append(runs[group, s])
-            marks = jnp.where(lane == s, jnp.where(s < live, scalars[group, s] + 1, 0), marks)
-            marks = jnp.where(lane == slots + s, scalars[group, slots + s], marks)
+            marks = jnp.where(lane == s, jnp.where(s < live, user_tile[s, group] + 1, 0), marks)
+            marks = jnp.where(lane == slots + s, word_tile[s, group], marks)
         run_rows = jnp.concatenate(run_rows, axis=0).astype(f32).astype(out.dtype)
         rest = jnp.concatenate(
             sub_rows + [marks.astype(f32), jnp.zeros((slots - 1, rank), f32)], axis=0
@@ -62,23 +62,35 @@
     whole = pl.BlockSpec(memory_space=pltpu.VMEM)
     return pl.pallas_call(
         facts_kernel,
-        in_specs=[pl.BlockSpec(memory_space=pltpu.SMEM), whole, whole],
+        in_specs=[pl.BlockSpec(memory_space=pltpu.SMEM)] * 4 + [whole, whole],
         out_specs=whole,
         out_shape=jax.ShapeDtypeStruct((groups, owners, 4 * slots, rank), bf16),
         scratch_shapes=[pltpu.VMEM(subs.shape, f32)],
         compiler_params=pltpu.CompilerParams(vmem_limit_bytes=VMEM_LIMIT),
         name="facts",
-    )(scalars, runs, subs)
-
-
-def rhs_kernel(scalars, ratings_in, runs_in, words_in, subs_in, *refs, half, owners, own_rows):
+    )(*scalars, runs, subs)
+
+
+def rhs_kernel(
+    user_tile, word_tile, subreddit, counts, ratings_in, runs_in, words_in, subs_in, *refs,
+    half, owners, own_rows,
+):
     given, refs = (refs[0], refs[1:]) if half == 0 else (None, refs)
     outs, (ratings, runs, words, subs, table, sums, arrived, loaded) = refs[:-8], refs[-8:]
     steps, slots, tile = ratings.shape[0], ratings.shape[1], ratings.shape[2]
     levels = steps // 2
 
+    place = lax.axis_index("loop")
+    level, seat = lax.div(place, 4), lax.rem(place, 4)
+
+    def group_at(step):
+        there = lax.rem(seat + 2 * (step // levels), 4)
+        if half:
+            there = there + 1 - 2 * lax.rem(there, 2)
+        return 4 * lax.rem(level + step % levels, levels) + there
+
     def load(step):
-        group = scalars[half * steps + step, 3 * slots + 1]
+        group = group_at(step)
         return pltpu.make_async_copy(ratings_in.at[group], ratings.at[step], arrived.at[step])
 
     tables = [
@@ -102,8 +114,8 @@
     ).astype(f32).astype(bf16)
     me = lax.axis_index("own")
     for step in range(steps):
-        group = scalars[half * steps + step, 3 * slots + 1]
-        live = scalars[group, 3 * slots]
+        group = group_at(step)
+        live = counts[0, group]
         columns = []
         for s in range(slots):
             pair = runs[group, s]
@@ -114,10 +126,10 @@
         load(step).wait()
         sums[step % 2] = jnp.zeros(sums.shape[1:], f32)
         for s in range(slots):
-            sub_row = table[pl.ds(scalars[group, 2 * slots + s], 1), :]
-            product = (words[scalars[group, slots + s]].astype(f32) * sub_row).astype(bf16)
+            sub_row = table[pl.ds(subreddit[s, group], 1), :]
+            product = (words[word_tile[s, group]].astype(f32) * sub_row).astype(bf16)
             weights = seen[:, s * tile : (s + 1) * tile] * ratings[step, s]
-            rows = pl.ds(pl.multiple_of(scalars[group, s] * tile, tile), tile)
+            rows = pl.ds(pl.multiple_of(user_tile[s, group] * tile, tile), tile)
             sums[step % 2, rows, :] += dot_nn(weights, product)
         for o in range(owners):
             owner = lax.rem(me + o, owners)
@@ -140,7 +152,9 @@
     shapes = [part] * (2 * owners) if half == 0 else [(owners, 2) + part]
     return pl.pallas_call(
         functools.partial(rhs_kernel, half=half, owners=owners, own_rows=own_rows),
-        in_specs=[pl.BlockSpec(memory_space=pltpu.SMEM)] + [anywhere] * 4 + [whole] * (1 - half),
+        in_specs=[pl.BlockSpec(memory_space=pltpu.SMEM)] * 4
+        + [anywhere] * 4
+        + [whole] * (1 - half),
         out_specs=[whole] * len(shapes),
         out_shape=[jax.ShapeDtypeStruct(shape, bf16) for shape in shapes],
         scratch_shapes=[
@@ -158,7 +172,7 @@
             flops=8 * ratings.size * rank, bytes_accessed=8 * ratings.size, transcendentals=0
         ),
         name="rhs",
-    )(scalars, ratings, runs, words, subs, *([given] if half == 0 else []))
+    )(*scalars, ratings, runs, words, subs, *([given] if half == 0 else []))
 
 
 def reduce_chip(parts, shards, owners):
@@ -184,31 +198,51 @@
     return terms
 
 
-def masks_kernel(marks, received, chosen, subs, masks_out, runs, masks, sent):
+def masks_kernel(
+    received, chosen, places, subs, masks_out, runs, masks, lines, facts, sent, moved, *, word_tiles
+):
     sources = received.shape[0]
     own_rows = masks.shape[1]
     tile = received.shape[2]
     blocks = subs.shape[0]
     slots = blocks // sources
-
-    def choose(j, n):
-        chosen[n] = j
-        return n + marks[j]
-
-    used = lax.fori_loop(0, blocks, choose, 0, unroll=8)
-    chosen[blocks] = used
-    chunks = lax.div(used + CHUNK - 1, CHUNK)
+    owners = lax.axis_size("own")
+    chips = lax.axis_size("loop") // 2
 
     def unpack(src, carry):
         runs[pl.ds(pl.multiple_of(src * 2 * slots, 2 * slots), 2 * slots), :] = received[
             src, : 2 * slots, :
         ].astype(f32)
-        subs[pl.ds(pl.multiple_of(src * slots, slots), slots), :] = received[
-            src, 2 * slots :, :
-        ].astype(f32)[:slots]
+        rest = received[src, 2 * slots :, :].astype(f32)
+        subs[pl.ds(pl.multiple_of(src * slots, slots), slots), :] = rest[:slots]
+        lines[pl.ds(src, 1), :] = rest[slots : slots + 1].astype(jnp.int32)
         return carry
 
-    lax.fori_loop(0, sources, unpack, 0)
+    lax.fori_loop(0, sources, unpack, 0, unroll=4)
+    move = pltpu.make_async_copy(lines, facts, moved.at[0])
+    move.start()
+    move.wait()
+
+    me = lax.axis_index("loop")
+    wanted = lax.div(lax.axis_index("own") * own_rows, tile) + 1
+
+    def ring_at(shard):
+        level, column = lax.div(shard, 4), lax.rem(lax.div(shard, 2), 2)
+        return jnp.where(column == 0, level, chips - 1 - level)
+
+    def choose(src, n):
+        shard = lax.div(src, owners)
+        distance = lax.rem(ring_at(shard) - ring_at(me) + chips, chips)
+        first = word_tiles * (2 * distance + lax.rem(shard + me, 2))
+        for s in range(slots):
+            chosen[n] = src * slots + s
+            places[n] = first + facts[src, slots + s]
+            n = n + jnp.where(facts[src, s] == wanted, 1, 0)
+        return n
+
+    used = lax.fori_loop(0, sources, choose, 0)
+    chosen[blocks] = used
+    chunks = lax.div(used + CHUNK - 1, CHUNK)
 
     offset = lax.rem(lax.axis_index("own") * own_rows, tile)
     pick = (
@@ -227,8 +261,8 @@
             first = runs[pl.ds(2 * j, 1), :].astype(jnp.int32)
             length = runs[pl.ds(2 * j + 1, 1), :].astype(jnp.int32)
             length = jnp.where(i < used, length, 0)
-            parts.append(dot_nt(pick, mask_columns(first, length, tile)).astype(bf16))
-        masks[chunk] = jnp.concatenate(parts, axis=1)
+            parts.append(mask_columns(first, length, tile))
+        masks[chunk] = dot_nt(pick, jnp.concatenate(parts, axis=0)).astype(bf16)
         send(chunk).start()
         return carry
 
@@ -240,33 +274,40 @@
     lax.fori_loop(0, chunks, finish, 0)
 
 
-def build_masks(marks, received, own_rows):
-    sources, rows, tile = received.shape
-    blocks = marks.shape[0]
-    rank = received.shape[2]
+def build_masks(received, slots, word_tiles, own_rows):
+    sources, _, tile = received.shape
+    blocks = sources * slots
+    rank = tile
     chunks = -(-blocks // CHUNK)
     whole = pl.BlockSpec(memory_space=pltpu.VMEM)
     scalars = pl.BlockSpec(memory_space=pltpu.SMEM)
     return pl.pallas_call(
-        masks_kernel,
-        in_specs=[scalars, whole],
-        out_specs=[scalars, whole, pl.BlockSpec(memory_space=pl.ANY)],
+        functools.partial(masks_kernel, word_tiles=word_tiles),
+        in_specs=[whole],
+        out_specs=[scalars, scalars, whole, pl.BlockSpec(memory_space=pl.ANY)],
         out_shape=[
             jax.ShapeDtypeStruct((blocks + 1,), jnp.int32),
+            jax.ShapeDtypeStruct((blocks,), jnp.int32),
             jax.ShapeDtypeStruct((blocks, rank), f32),
             jax.ShapeDtypeStruct((chunks, own_rows, CHUNK * tile), bf16),
         ],
         scratch_shapes=[
             pltpu.VMEM((2 * blocks, tile), f32),
             pltpu.VMEM((chunks, own_rows, CHUNK * tile), bf16),
+            pltpu.VMEM((sources, tile), jnp.int32),
+            pltpu.SMEM((sources, tile), jnp.int32),
             pltpu.SemaphoreType.DMA((chunks,)),
+            pltpu.SemaphoreType.DMA((1,)),
         ],
         compiler_params=pltpu.CompilerParams(vmem_limit_bytes=VMEM_LIMIT),
+        cost_estimate=pl.CostEstimate(
+            flops=40 * received.size * tile, bytes_accessed=40 * received.size, transcendentals=0
+        ),
         name="masks",
-    )(marks, received)
-
-
-def steps_kernel(chosen, word_index, start, activity, subs, masks_in, *refs, shards, levels, cached):
+    )(received)
+
+
+def steps_kernel(chosen, places, start, activity, subs, masks_in, *refs, shards, levels, cached):
     own_rows, rank = start.shape
     blocks = subs.shape[0]
     pieces, refs = refs[:shards], refs[shards:]
@@ -297,8 +338,8 @@
     lax.fori_loop(0, chunks, begin, 0)
 
     def product(i):
-        j = jnp.where(i < used, chosen[jnp.minimum(i, blocks - 1)], 0)
-        return (words[word_index[j]].astype(f32) * subs[pl.ds(j, 1), :]).astype(bf16)
+        i = jnp.minimum(i, used - 1)
+        return (words[places[i]].astype(f32) * subs[pl.ds(chosen[i], 1), :]).astype(bf16)
 
     def build(chunk, carry):
         load(chunk).wait()
@@ -329,7 +370,7 @@
     def over_row(a, b):
         return jnp.sum(a * b, axis=1, keepdims=True)
 
-    scale = activity[...]
+    scale = jnp.broadcast_to(activity[...], (rank, own_rows)).T
     rhs = terms[0][...].astype(f32)
     for term in terms[1:]:
         rhs = rhs + term[...].astype(f32)
@@ -350,7 +391,7 @@
     dots_out[...] = jnp.broadcast_to(line[None], dots_out.shape)
 
 
-def krylov(chosen, word_index, start, activity, subs, masks, pieces, terms, devices):
+def krylov(chosen, places, start, activity, subs, masks, pieces, terms, devices):
     own_rows, rank = start.shape
     blocks = subs.shape[0]
     word_tiles, tile, _ = pieces[0].shape
@@ -380,7 +421,7 @@
         scratch_shapes=scratch,
         compiler_params=pltpu.CompilerParams(vmem_limit_bytes=VMEM_LIMIT),
         name="krylov",
-    )(chosen, word_index, start, activity, subs, masks, *pieces, *terms)
+    )(chosen, places, start, activity, subs, masks, *pieces, *terms)
 
 
 def last_kernel(dots, start, first, second, third, solution_out, residual_out):
@@ -409,12 +450,6 @@
         compiler_params=pltpu.CompilerParams(vmem_limit_bytes=VMEM_LIMIT),
         name="last_step",
     )(dots, start, first, second, third)
-
-
-def ring_place(shard, chips):
-    chip = shard // 2
-    level, column = chip // 2, chip % 2
-    return jnp.where(column == 0, level, chips - 1 - level)
 
 
 def ring_round(up, down, held, step, shards):
@@ -457,55 +492,43 @@
 ):
     own_rows, rank = factor_start.shape
     owners, shards = lax.axis_size("own"), lax.axis_size("loop")
-    _, _, groups, slots, tile, _ = ratings.shape
+    slots = ratings.shape[3]
     word_tiles = word_factors.shape[1]
     devices = shards * owners
-    chips, levels = shards // 2, shards // 4
-    me, owner = lax.axis_index("loop"), lax.axis_index("own")
+    chips = shards // 2
     together = lax.optimization_barrier
 
-    step = jnp.arange(groups, dtype=jnp.int32)
-    level = (me // 4 + step % levels) % levels
-    order = 4 * level + (me % 4) ^ (2 * ((step // levels) % 2) + step // (2 * levels))
-    scalars = jnp.concatenate(
-        [user_tile[0, 0], word_tile[0, 0], subreddit[0, 0], counts[0, 0][:, None], order[:, None]],
-        axis=1,
-    )
-
+    scalars = (user_tile[0, 0].T, word_tile[0, 0].T, subreddit[0, 0].T, counts[0])
     mine = word_factors[0]
-    inputs = (scalars, ratings[0, 0], runs[0, 0], mine, sub_factors)
     held = {0: mine}
-    up, down = ring_round(mine, mine, held, 1, shards)
-    (away,) = rhs_sums(*inputs, 1, None, owners, own_rows)
-    up, down, away, scalars = together((up, down, away, scalars))
-
-    up, down = ring_round(up, down, held, 2, shards)
+
     message = facts(scalars, runs[0, 0], sub_factors, owners).reshape(devices, 4 * slots, rank)
     received = lax.all_to_all(message, AXES, 0, 0, tiled=True)
-    parts = rhs_sums(*inputs, 0, other_core(away, shards), owners, own_rows)
+    up, down = ring_round(mine, mine, held, 1, shards)
+    up, down, _, *inputs = together(
+        (up, down, message, ratings[0, 0], runs[0, 0], mine, sub_factors)
+    )
+
+    up, down = ring_round(up, down, held, 2, shards)
+    (away,) = rhs_sums(scalars, *inputs, 1, None, owners, own_rows)
+    up, down, away, received = together((up, down, away, received))
+
+    up, down = ring_round(up, down, held, 3, shards)
+    parts = rhs_sums(scalars, *inputs, 0, other_core(away, shards), owners, own_rows)
     up, down, parts = together((up, down, parts))
-
-    up, down = ring_round(up, down, held, 3, shards)
-    total = reduce_chip(parts, shards, owners)
-    up, down, total = together((up, down, total))
 
     for step in range(4, chips // 2 + 1):
         up, down = ring_round(up, down, held, step, shards)
+    total = reduce_chip(parts, shards, owners)
+    held[chips // 2], total, received = together((held[chips // 2], total, received))
+
     terms = reduce_levels(total, shards)
     pieces = []
     for distance in range(chips):
         pieces += [held[distance], other_core(held[distance], shards)]
-
-    got = received[:, 3 * slots, : 2 * slots].astype(jnp.int32)
-    marks = (got[:, :slots] == owner * own_rows // tile + 1).astype(jnp.int32).reshape(-1)
-    shard = jnp.arange(devices, dtype=jnp.int32)[:, None] // owners
-    distance = (ring_place(shard, chips) - ring_place(me, chips)) % chips
-    piece = 2 * distance + (shard + me) % 2
-    word_index = (got[:, slots:] + word_tiles * piece).reshape(-1)
-
-    chosen, subs, masks = build_masks(marks, received, own_rows)
+    chosen, places, subs, masks = build_masks(received, slots, word_tiles, own_rows)
     first, second, third, dots = krylov(
-        chosen, word_index, factor_start, activity[:, None], subs, masks, pieces, terms, devices
+        chosen, places, factor_start, activity[None], subs, masks, pieces, terms, devices
     )
     everyone = lax.all_to_all(dots, AXES, 0, 0, tiled=True)
     return tuple(last_step(everyone, factor_start, first, second, third))

time: 99.5 us -> 95.4 us (0.959); the launches traced: 100 us -> 94.3 us
  local copies, waits for them, and re-layouts: 7.62 us -> 2.12 us
  blocking collectives: 14.1 us -> 10.4 us
  starting transfers between devices: 22 us -> 24.7 us
  Pallas kernels: 40.9 us -> 42 us
    ppermute x4, waiting for transfers between devices: 8.76 us -> 0.15 us  [ring_round(): up = lax.ppermute(up, 'loop', shift(1))]
    ppermute x3, waiting for transfers between devices: 4.47 us -> 8.8 us  [reduce_chip(): total.append(lax.ppermute(parts[2 * o + column], AXES, pairs).astype(f32))]
    ppermute x4, starting transfers between devices: 5.03 us -> 9.29 us  [ring_round(): up = lax.ppermute(up, 'loop', shift(1))]
    all_to_all x1, blocking collectives: 14.1 us -> 10.4 us  [on_device(): everyone = lax.all_to_all(dots, AXES, 0, 0, tiled=True)]
    squeeze x3 -> x0, local copies, waits for them, and re-layouts: 2.27 us -> none  [the longest x1 0.76 us: on_device(): user_tile[0, 0]]
    all_to_all x1, waiting for transfers between devices: 0.01 us -> 2.2 us  [on_device(): received = lax.all_to_all(message, AXES, 0, 0, tiled=True)]
    ppermute x3, starting transfers between devices: 2.29 us -> 0.26 us  [ring_round(): down = lax.ppermute(down, 'loop', shift(-1))]
    ppermute x3, waiting for transfers between devices: 0.01 us -> 1.77 us  [ring_round(): down = lax.ppermute(down, 'loop', shift(-1))]
  transfers between devices with their start and end apart: 23 -> 23, of which waited for: 4 -> 6; matrix products, arithmetic and copies ran while one was open for 7% -> 2% of each run, Pallas kernels for 23% -> 25%
where the time goes in v5:
time: 95.4 us; the launch traced here: 94.3 us
  Pallas kernels  42 us (44%)
  starting transfers between devices  24.7 us (26%)
  waiting for transfers between devices  13 us (14%)
  blocking collectives  10.4 us (11%)
  local copies, waits for them, and re-layouts  2.12 us (2%)
  other arithmetic  1.01 us (1%)
  between operations  0.98 us (1%)
    pallas_call x1, Pallas kernels, krylov(): pl.pallas_call(functools.partial(steps_kernel, shards=len(pieces), levels...  16.4 us
    pallas_call x2, Pallas kernels, rhs_sums(): pl.pallas_call(functools.partial(rhs_kernel, half=half, owners=owners, ow...  13.8 us
    all_to_all x1, blocking collectives, on_device(): everyone = lax.all_to_all(dots, AXES, 0, 0, tiled=True)  10.4 us
    ppermute x4, starting transfers between devices, ring_round(): up = lax.ppermute(up, 'loop', shift(1))  9.29 us
    ppermute x3, waiting for transfers between devices, reduce_chip(): total.append(lax.ppermute(parts[2 * o + column], AXES, pairs).astype(f32))  8.8 us
    pallas_call x1, Pallas kernels, build_masks(): pl.pallas_call(functools.partial(masks_kernel, word_tiles=word_tiles), in...  7.6 us
    all_to_all x1, starting transfers between devices, on_device(): received = lax.all_to_all(message, AXES, 0, 0, tiled=True)  6.3 us
    ppermute x3, starting transfers between devices, reduce_levels(): terms.append(lax.ppermute(total[up], 'loop', shift))  3.93 us
  transfers between devices with their start and end apart: 23, of which 6 were waited for; matrix products, arithmetic and copies ran while one was open for 2% of the time, Pallas kernels for 25%

profile of v5, /device:TPU:0, one launch (start us, length us, event | category | flops | bytes accessed | tf_op | source)
XLA Modules:
  0.0 94.3 jit_solution(16039467468974118231)
XLA Ops:
  0.6 0.0 copy-start
  0.6 3.1 %collective-permute-start = (bf16[8,128,128]{2,1,0:T(8,128)(2,1)}, bf16[8,128,128]{2,1,0:T(8,128)(2,1)S(1)}, u32[]{:S(2)}, u32[]{:S(2)}) collective-permute-start(bf16[8,128,128]{2,1,0:T(8,128)(2,1)} %bitcast.24), channel_id=1, source_target_pairs={{0,8},{2,10},{8,16},{10,18},{16,24},{18,26},{24,28},{26,30},{28,20... | collective-permute-start | bytes 786440 | tf_op jit(solution)/shard_map/ppermute | solution.py:469
  3.7 0.0 collective-permute-start.1
  3.7 2.4 %facts.1 = bf16[16,2,32,128]{3,2,1,0:T(8,128)(2,1)} custom-call(s32[8,16]{1,0:T(8,128)} %bitcast.33, s32[8,16]{1,0:T(8,128)} %bitcast.36, s32[8,16]{1,0:T(8,128)} %bitcast.39, s32[1,16]{1,0:T(1,128)} %bitcast.42, s32[16,8,2,128]{3,2,1,0:T(2,128)} %bitcast.30, bf16[2048,128]{1,0:T(8,128)(2,1)} %subs_in.1), custom_call_target="tpu_custom_call" | custom-call | tf_op jit(solution)/shard_map/facts/pallas_call | solution.py:63
  6.1 6.3 %all-to-all-start = ((bf16[32,32,128]{2,1,0:T(8,128)(2,1)}), bf16[32,32,128]{2,1,0:T(8,128)(2,1)S(1)}, u32[]{:S(2)}, u32[]{:S(2)}) async-start(bf16[32,32,128]{2,1,0:T(8,128)(2,1)} %bitcast.23), calls=%async_computation | async-start | bytes 524288 | tf_op jit(solution)/shard_map/all_to_all | solution.py:506
  12.4 0.0 collective-permute-done.refs_14_
  12.5 1.8 %collective-permute-start.2 = (bf16[8,128,128]{2,1,0:T(8,128)(2,1)S(1)}, bf16[8,128,128]{2,1,0:T(8,128)(2,1)S(1)}, u32[]{:S(2)}, u32[]{:S(2)}) collective-permute-start(bf16[8,128,128]{2,1,0:T(8,128)(2,1)S(1)} %collective-permute-done.refs_14_), channel_id=1, source_target_pairs={{0,8},{2,10},{8,16},{10,18},{16,24},{18,26},{24,28},{26,30},{28,20... | collective-permute-start | bytes 786440 | tf_op jit(solution)/shard_map/ppermute | solution.py:469
  14.3 0.3 collective-permute-start.3
  14.5 6.8 %rhs.2 = bf16[2,2,4,128,128]{4,3,2,1,0:T(8,128)(2,1)} custom-call(s32[8,16]{1,0:T(8,128)} %bitcast.34, s32[8,16]{1,0:T(8,128)} %bitcast.37, s32[8,16]{1,0:T(8,128)} %bitcast.40, s32[1,16]{1,0:T(1,128)} %bitcast.43, bf16[16,8,128,128]{3,2,1,0:T(8,128)(2,1)} %bitcast.46, s32[16,8,2,128]{3,2,1,0:T(2,128)} %bitcast.31, bf16[8,128,128]{2,1,0:T(8,128)(2,1)} %bitcast.26, ...), custom_call_target="tpu_custom_call" | custom-call | flops 2147483648 | bytes 16777216 | tf_op jit(solution)/shard_map/rhs/pallas_call | solution.py:153
  21.4 2.2 %all-to-all-done.received = bf16[32,32,128]{2,1,0:T(8,128)(2,1)S(1)} async-done(((bf16[32,32,128]{2,1,0:T(8,128)(2,1)}), bf16[32,32,128]{2,1,0:T(8,128)(2,1)S(1)}, u32[]{:S(2)}, u32[]{:S(2)}) %all-to-all-start) | async-done | bytes 262176 | tf_op jit(solution)/shard_map/all_to_all | solution.py:506
  23.6 0.1 collective-permute-done.2.refs_12_
  23.7 1.4 %collective-permute-done.3.refs_4_ = bf16[8,128,128]{2,1,0:T(8,128)(2,1)S(1)} collective-permute-done((bf16[8,128,128]{2,1,0:T(8,128)(2,1)S(1)}, bf16[8,128,128]{2,1,0:T(8,128)(2,1)S(1)}, u32[]{:S(2)}, u32[]{:S(2)}) %collective-permute-start.3) | collective-permute-done | bytes 262176 | tf_op jit(solution)/shard_map/ppermute | solution.py:472
  25.1 0.0 collective-permute-start.6
  25.1 2.9 %collective-permute-start.4 = (bf16[8,128,128]{2,1,0:T(8,128)(2,1)S(1)}, bf16[8,128,128]{2,1,0:T(8,128)(2,1)S(1)}, u32[]{:S(2)}, u32[]{:S(2)}) collective-permute-start(bf16[8,128,128]{2,1,0:T(8,128)(2,1)S(1)} %collective-permute-done.2.refs_12_), channel_id=1, source_target_pairs={{0,8},{2,10},{8,16},{10,18},{16,24},{18,26},{24,28},{26,30},{28,20... | collective-permute-start | bytes 786440 | tf_op jit(solution)/shard_map/ppermute | solution.py:469
  28.0 0.0 collective-permute-start.5
  28.0 0.3 collective-permute-start.11
  28.3 0.8 copy-done.20
  29.1 6.9 %rhs.3 = (bf16[4,128,128]{2,1,0:T(8,128)(2,1)}, bf16[4,128,128]{2,1,0:T(8,128)(2,1)}, bf16[4,128,128]{2,1,0:T(8,128)(2,1)}, bf16[4,128,128]{2,1,0:T(8,128)(2,1)}) custom-call(s32[8,16]{1,0:T(8,128)} %bitcast.35, s32[8,16]{1,0:T(8,128)} %bitcast.38, s32[8,16]{1,0:T(8,128)} %bitcast.41, s32[1,16]{1,0:T(1,128)} %bitcast.44, bf16[16,8,128,128]{3,2,1,0:T(8,128)(2,1)} %bitcast.47, ...), custom_call_target="tpu_custom_call" | custom-call | flops 2147483648 | bytes 16777216 | tf_op jit(solution)/shard_map/rhs/pallas_call | solution.py:153
  36.0 0.0 collective-permute-done.4.refs_10_
  36.1 0.4 collective-permute-done.5.refs_6_
  36.4 1.5 %collective-permute-start.7 = (bf16[8,128,128]{2,1,0:T(8,128)(2,1)S(1)}, bf16[8,128,128]{2,1,0:T(8,128)(2,1)S(1)}, u32[]{:S(2)}, u32[]{:S(2)}) collective-permute-start(bf16[8,128,128]{2,1,0:T(8,128)(2,1)S(1)} %collective-permute-done.4.refs_10_), channel_id=1, source_target_pairs={{0,8},{2,10},{8,16},{10,18},{16,24},{18,26},{24,28},{26,30},{28,20... | collective-permute-start | bytes 786440 | tf_op jit(solution)/shard_map/ppermute | solution.py:469
  38.0 1.4 %collective-permute-start.10 = (bf16[4,128,128]{2,1,0:T(8,128)(2,1)}, bf16[4,128,128]{2,1,0:T(8,128)(2,1)S(1)}, u32[]{:S(2)}, u32[]{:S(2)}) collective-permute-start(bf16[4,128,128]{2,1,0:T(8,128)(2,1)} %get-tuple-element.49), channel_id=1, source_target_pairs={{0,5},{1,4},{2,7},{3,6},{4,1},{5,0},{6,3},{7,2},{8,13},{9,12},{10,... | collective-permute-start | bytes 393224 | tf_op jit(solution)/shard_map/ppermute | solution.py:188
  39.4 1.5 %collective-permute-start.8 = (bf16[4,128,128]{2,1,0:T(8,128)(2,1)}, bf16[4,128,128]{2,1,0:T(8,128)(2,1)S(1)}, u32[]{:S(2)}, u32[]{:S(2)}) collective-permute-start(bf16[4,128,128]{2,1,0:T(8,128)(2,1)} %get-tuple-element.47), channel_id=1, source_target_pairs={{0,4},{1,5},{2,6},{3,7},{4,0},{5,1},{6,2},{7,3},{8,12},{9,13},{10,... | collective-permute-start | bytes 393224 | tf_op jit(solution)/shard_map/ppermute | solution.py:188
  40.9 0.6 collective-permute-start.9
  41.5 7.9 %collective-permute-done.10 = bf16[4,128,128]{2,1,0:T(8,128)(2,1)S(1)} collective-permute-done((bf16[4,128,128]{2,1,0:T(8,128)(2,1)}, bf16[4,128,128]{2,1,0:T(8,128)(2,1)S(1)}, u32[]{:S(2)}, u32[]{:S(2)}) %collective-permute-start.10) | collective-permute-done | bytes 131104 | tf_op jit(solution)/shard_map/ppermute | solution.py:188
  49.3 0.0 collective-permute-start.18
  49.3 0.9 collective-permute-done.8
  50.3 0.0 collective-permute-start.13
  50.3 0.0 collective-permute-done.9
  50.3 0.5 collective-permute-start.17
  50.8 0.1 collective-permute-start.14
  50.9 1.0 %add_convert_fusion = bf16[4,128,128]{2,1,0:T(8,128)(2,1)S(1)} fusion(bf16[4,128,128]{2,1,0:T(8,128)(2,1)S(1)} %collective-permute-done.10, bf16[4,128,128]{2,1,0:T(8,128)(2,1)S(1)} %collective-permute-done.9, bf16[4,128,128]{2,1,0:T(8,128)(2,1)S(1)} %collective-permute-done.8, bf16[4,128,128]{2,1,0:T(8,128)(2,1)} %get-tuple-element.46), kind=kLoop, calls=%fused_computation | loop fusion | flops 524288 | bytes 655360 | tf_op jit(solution)/shard_map/convert_element_type | solution.py:189
  51.9 0.5 collective-permute-start.16
  52.4 0.0 collective-permute-done.18.refs_15_
  52.4 0.1 collective-permute-start.15
  52.5 0.6 slice_bitcast_fusion
  53.1 0.1 collective-permute-start.19
  53.2 1.1 %collective-permute-start.20 = (bf16[128,128]{1,0:T(8,128)(2,1)S(1)}, bf16[128,128]{1,0:T(8,128)(2,1)S(1)}, u32[]{:S(2)}, u32[]{:S(2)}) collective-permute-start(bf16[128,128]{1,0:T(8,128)(2,1)S(1)} %get-tuple-element.63), channel_id=1, source_target_pairs={{0,16},{2,18},{4,20},{6,22},{8,24},{10,26},{12,28},{14,30},{16,0},... | collective-permute-start | bytes 98312 | tf_op jit(solution)/shard_map/ppermute | solution.py:197
  54.3 0.0 collective-permute-done.14.refs_7_
  54.3 2.8 %collective-permute-start.21 = (bf16[128,128]{1,0:T(8,128)(2,1)S(1)}, bf16[128,128]{1,0:T(8,128)(2,1)S(1)}, u32[]{:S(2)}, u32[]{:S(2)}) collective-permute-start(bf16[128,128]{1,0:T(8,128)(2,1)S(1)} %get-tuple-element.62), channel_id=1, source_target_pairs={{0,24},{2,26},{4,28},{6,30},{8,0},{10,2},{12,4},{14,6},{16,8},{18,... | collective-permute-start | bytes 98312 | tf_op jit(solution)/shard_map/ppermute | solution.py:197
  57.1 7.6 %masks.1 = (s32[257]{0:T(512)}, s32[256]{0:T(256)}, f32[256,128]{1,0:T(8,128)}, bf16[32,128,1024]{2,1,0:T(8,128)(2,1)}) custom-call(bf16[32,32,128]{2,1,0:T(8,128)(2,1)} %copy-done.16), custom_call_target="tpu_custom_call" | custom-call | flops 671088640 | bytes 5242880 | tf_op jit(solution)/shard_map/masks/pallas_call | solution.py:284
  64.7 0.0 collective-permute-done.19.refs_17_
  64.7 0.0 copy-start.17
  64.9 0.5 copy-done.14
  65.4 0.1 copy-done.15
  65.5 16.4 %krylov.1 = (f32[128,128]{1,0:T(8,128)}, f32[128,128]{1,0:T(8,128)}, f32[128,128]{1,0:T(8,128)}, f32[32,1,128]{2,1,0:T(1,128)}) custom-call(s32[257]{0:T(512)} %get-tuple-element.52.chosen, s32[256]{0:T(256)} %get-tuple-element.53.places, f32[128,128]{1,0:T(8,128)} %start.3, f32[1,128]{1,0:T(1,128)} %bitcast.45, f32[256,128]{1,0:T(8,128)} %get-tuple-element.54.subs, ...), custom_call_target="tpu_custom_call" | custom-call | tf_op jit(solution)/shard_map/krylov/pallas_call | solution.py:412
  82.0 10.4 %all_to_all.10.dots = f32[32,1,128]{2,1,0:T(1,128)} all-to-all(f32[32,1,128]{2,1,0:T(1,128)} %get-tuple-element.58), channel_id=1, replica_groups=mesh['loop'=16,'own'=2] {'loop','own'}, dimensions={0} | all-to-all | bytes 32768 | tf_op jit(solution)/shard_map/all_to_all | solution.py:533
  92.4 1.9 %last_step.1 = (f32[128,128]{1,0:T(8,128)}, f32[128,128]{1,0:T(8,128)}) custom-call(f32[32,1,128]{2,1,0:T(1,128)} %all_to_all.10.dots, f32[128,128]{1,0:T(8,128)} %start.3, f32[128,128]{1,0:T(8,128)} %get-tuple-element.59.first, f32[128,128]{1,0:T(8,128)} %get-tuple-element.60.second, f32[128,128]{1,0:T(8,128)} %get-tuple-element.61.third), custom_call_target="tpu_custom_call" | custom-call | tf_op jit(solution)/shard_map/last_step/pallas_call | solution.py:445
  (49 shorter events, 0.1 us)
Async XLA Ops:
  0.6 27.4 %copy-start = (bf16[1,8,128,128]{3,2,1,0:T(8,128)(2,1)S(1)}, bf16[1,8,128,128]{3,2,1,0:T(8,128)(2,1)}, u32[]{:S(2)}) copy-start(bf16[1,8,128,128]{3,2,1,0:T(8,128)(2,1)} %param.12) | copy-start | bytes 786436
  0.6 11.8 %collective-permute-start = (bf16[8,128,128]{2,1,0:T(8,128)(2,1)}, bf16[8,128,128]{2,1,0:T(8,128)(2,1)S(1)}, u32[]{:S(2)}, u32[]{:S(2)}) collective-permute-start(bf16[8,128,128]{2,1,0:T(8,128)(2,1)} %bitcast.24), channel_id=1, source_target_pairs={{0,8},{2,10},{8,16},{10,18},{16,24},{18,26},{24,28},{26,30},{28,20... | collective-permute-start | bytes 786440 | tf_op jit(solution)/shard_map/ppermute | solution.py:469
  3.7 8.7 %collective-permute-start.1 = (bf16[8,128,128]{2,1,0:T(8,128)(2,1)}, bf16[8,128,128]{2,1,0:T(8,128)(2,1)S(1)}, u32[]{:S(2)}, u32[]{:S(2)}) collective-permute-start(bf16[8,128,128]{2,1,0:T(8,128)(2,1)} %bitcast.25), channel_id=1, source_target_pairs={{0,4},{2,6},{8,0},{10,2},{16,8},{18,10},{24,16},{26,18},{28,24},{3... | collective-permute-start | bytes 786440 | tf_op jit(solution)/shard_map/ppermute | solution.py:472
  6.1 17.4 %all-to-all-start = ((bf16[32,32,128]{2,1,0:T(8,128)(2,1)}), bf16[32,32,128]{2,1,0:T(8,128)(2,1)S(1)}, u32[]{:S(2)}, u32[]{:S(2)}) async-start(bf16[32,32,128]{2,1,0:T(8,128)(2,1)} %bitcast.23), calls=%async_computation | async-start | bytes 524288 | tf_op jit(solution)/shard_map/all_to_all | solution.py:506
  12.4 40.7 %copy-start.1 = (bf16[8,128,128]{2,1,0:T(8,128)(2,1)}, bf16[8,128,128]{2,1,0:T(8,128)(2,1)S(1)}, u32[]{:S(2)}) copy-start(bf16[8,128,128]{2,1,0:T(8,128)(2,1)S(1)} %collective-permute-done.refs_14_) | copy-start | bytes 786436
  12.4 40.6 %copy-start.2 = (bf16[8,128,128]{2,1,0:T(8,128)(2,1)}, bf16[8,128,128]{2,1,0:T(8,128)(2,1)S(1)}, u32[]{:S(2)}) copy-start(bf16[8,128,128]{2,1,0:T(8,128)(2,1)S(1)} %collective-permute-done.1.refs_2_) | copy-start | bytes 786436
  12.5 11.2 %collective-permute-start.2 = (bf16[8,128,128]{2,1,0:T(8,128)(2,1)S(1)}, bf16[8,128,128]{2,1,0:T(8,128)(2,1)S(1)}, u32[]{:S(2)}, u32[]{:S(2)}) collective-permute-start(bf16[8,128,128]{2,1,0:T(8,128)(2,1)S(1)} %collective-permute-done.refs_14_), channel_id=1, source_target_pairs={{0,8},{2,10},{8,16},{10,18},{16,24},{18,26},{24,28},{26,30},{28,20... | collective-permute-start | bytes 786440 | tf_op jit(solution)/shard_map/ppermute | solution.py:469
  14.3 10.8 %collective-permute-start.3 = (bf16[8,128,128]{2,1,0:T(8,128)(2,1)S(1)}, bf16[8,128,128]{2,1,0:T(8,128)(2,1)S(1)}, u32[]{:S(2)}, u32[]{:S(2)}) collective-permute-start(bf16[8,128,128]{2,1,0:T(8,128)(2,1)S(1)} %collective-permute-done.1.refs_2_), channel_id=1, source_target_pairs={{0,4},{2,6},{8,0},{10,2},{16,8},{18,10},{24,16},{26,18},{28,24},{3... | collective-permute-start | bytes 786440 | tf_op jit(solution)/shard_map/ppermute | solution.py:472
  23.6 4.4 %copy-start.16 = (bf16[32,32,128]{2,1,0:T(8,128)(2,1)}, bf16[32,32,128]{2,1,0:T(8,128)(2,1)S(1)}, u32[]{:S(2)}) copy-start(bf16[32,32,128]{2,1,0:T(8,128)(2,1)S(1)} %all-to-all-done.received) | copy-start | bytes 786436
  23.7 41.1 %copy-start.3 = (bf16[8,128,128]{2,1,0:T(8,128)(2,1)}, bf16[8,128,128]{2,1,0:T(8,128)(2,1)S(1)}, u32[]{:S(2)}) copy-start(bf16[8,128,128]{2,1,0:T(8,128)(2,1)S(1)} %collective-permute-done.2.refs_12_) | copy-start | bytes 786436
  25.1 39.7 %copy-start.4 = (bf16[8,128,128]{2,1,0:T(8,128)(2,1)}, bf16[8,128,128]{2,1,0:T(8,128)(2,1)S(1)}, u32[]{:S(2)}) copy-start(bf16[8,128,128]{2,1,0:T(8,128)(2,1)S(1)} %collective-permute-done.3.refs_4_) | copy-start | bytes 786436
  25.1 3.2 %collective-permute-start.6 = (bf16[2,2,4,128,128]{4,3,2,1,0:T(8,128)(2,1)}, bf16[2,2,4,128,128]{4,3,2,1,0:T(8,128)(2,1)S(1)}, u32[]{:S(2)}, u32[]{:S(2)}) collective-permute-start(bf16[2,2,4,128,128]{4,3,2,1,0:T(8,128)(2,1)} %rhs.2), channel_id=1, source_target_pairs={{0,2},{2,0},{4,6},{6,4},{8,10},{10,8},{12,14},{14,12},{16,18},{18,... | collective-permute-start | bytes 1572872 | tf_op jit(solution)/shard_map/ppermute | solution.py:478
  25.1 10.9 %collective-permute-start.4 = (bf16[8,128,128]{2,1,0:T(8,128)(2,1)S(1)}, bf16[8,128,128]{2,1,0:T(8,128)(2,1)S(1)}, u32[]{:S(2)}, u32[]{:S(2)}) collective-permute-start(bf16[8,128,128]{2,1,0:T(8,128)(2,1)S(1)} %collective-permute-done.2.refs_12_), channel_id=1, source_target_pairs={{0,8},{2,10},{8,16},{10,18},{16,24},{18,26},{24,28},{26,30},{28,20... | collective-permute-start | bytes 786440 | tf_op jit(solution)/shard_map/ppermute | solution.py:469
  28.0 8.4 %collective-permute-start.5 = (bf16[8,128,128]{2,1,0:T(8,128)(2,1)S(1)}, bf16[8,128,128]{2,1,0:T(8,128)(2,1)S(1)}, u32[]{:S(2)}, u32[]{:S(2)}) collective-permute-start(bf16[8,128,128]{2,1,0:T(8,128)(2,1)S(1)} %collective-permute-done.3.refs_4_), channel_id=1, source_target_pairs={{0,4},{2,6},{8,0},{10,2},{16,8},{18,10},{24,16},{26,18},{28,24},{3... | collective-permute-start | bytes 786440 | tf_op jit(solution)/shard_map/ppermute | solution.py:472
  28.0 13.4 %collective-permute-start.11 = (bf16[8,128,128]{2,1,0:T(8,128)(2,1)S(1)}, bf16[8,128,128]{2,1,0:T(8,128)(2,1)S(1)}, u32[]{:S(2)}, u32[]{:S(2)}) collective-permute-start(bf16[8,128,128]{2,1,0:T(8,128)(2,1)S(1)} %bitcast.29), channel_id=1, source_target_pairs={{0,2},{2,0},{4,6},{6,4},{8,10},{10,8},{12,14},{14,12},{16,18},{18,... | collective-permute-start | bytes 786440 | tf_op jit(solution)/shard_map/ppermute | solution.py:478
  28.3 0.8 copy-start.20
  36.1 28.8 %copy-start.5 = (bf16[8,128,128]{2,1,0:T(8,128)(2,1)}, bf16[8,128,128]{2,1,0:T(8,128)(2,1)S(1)}, u32[]{:S(2)}) copy-start(bf16[8,128,128]{2,1,0:T(8,128)(2,1)S(1)} %collective-permute-done.4.refs_10_) | copy-start | bytes 786436
  36.4 28.4 %copy-start.6 = (bf16[8,128,128]{2,1,0:T(8,128)(2,1)}, bf16[8,128,128]{2,1,0:T(8,128)(2,1)S(1)}, u32[]{:S(2)}) copy-start(bf16[8,128,128]{2,1,0:T(8,128)(2,1)S(1)} %collective-permute-done.5.refs_6_) | copy-start | bytes 786436
  36.4 14.3 %collective-permute-start.7 = (bf16[8,128,128]{2,1,0:T(8,128)(2,1)S(1)}, bf16[8,128,128]{2,1,0:T(8,128)(2,1)S(1)}, u32[]{:S(2)}, u32[]{:S(2)}) collective-permute-start(bf16[8,128,128]{2,1,0:T(8,128)(2,1)S(1)} %collective-permute-done.4.refs_10_), channel_id=1, source_target_pairs={{0,8},{2,10},{8,16},{10,18},{16,24},{18,26},{24,28},{26,30},{28,20... | collective-permute-start | bytes 786440 | tf_op jit(solution)/shard_map/ppermute | solution.py:469
  38.0 11.4 %collective-permute-start.10 = (bf16[4,128,128]{2,1,0:T(8,128)(2,1)}, bf16[4,128,128]{2,1,0:T(8,128)(2,1)S(1)}, u32[]{:S(2)}, u32[]{:S(2)}) collective-permute-start(bf16[4,128,128]{2,1,0:T(8,128)(2,1)} %get-tuple-element.49), channel_id=1, source_target_pairs={{0,5},{1,4},{2,7},{3,6},{4,1},{5,0},{6,3},{7,2},{8,13},{9,12},{10,... | collective-permute-start | bytes 393224 | tf_op jit(solution)/shard_map/ppermute | solution.py:188
  39.4 10.9 %collective-permute-start.8 = (bf16[4,128,128]{2,1,0:T(8,128)(2,1)}, bf16[4,128,128]{2,1,0:T(8,128)(2,1)S(1)}, u32[]{:S(2)}, u32[]{:S(2)}) collective-permute-start(bf16[4,128,128]{2,1,0:T(8,128)(2,1)} %get-tuple-element.47), channel_id=1, source_target_pairs={{0,4},{1,5},{2,6},{3,7},{4,0},{5,1},{6,2},{7,3},{8,12},{9,13},{10,... | collective-permute-start | bytes 393224 | tf_op jit(solution)/shard_map/ppermute | solution.py:188
  40.9 9.4 %collective-permute-start.9 = (bf16[4,128,128]{2,1,0:T(8,128)(2,1)}, bf16[4,128,128]{2,1,0:T(8,128)(2,1)S(1)}, u32[]{:S(2)}, u32[]{:S(2)}) collective-permute-start(bf16[4,128,128]{2,1,0:T(8,128)(2,1)} %get-tuple-element.48), channel_id=1, source_target_pairs={{0,1},{1,0},{2,3},{3,2},{4,5},{5,4},{6,7},{7,6},{8,9},{9,8},{10,11... | collective-permute-start | bytes 393224 | tf_op jit(solution)/shard_map/ppermute | solution.py:188
  41.4 23.4 %copy-start.7 = (bf16[8,128,128]{2,1,0:T(8,128)(2,1)}, bf16[8,128,128]{2,1,0:T(8,128)(2,1)S(1)}, u32[]{:S(2)}) copy-start(bf16[8,128,128]{2,1,0:T(8,128)(2,1)S(1)} %collective-permute-done.11.refs_1_) | copy-start | bytes 786436
  41.5 10.4 %collective-permute-start.12 = (bf16[8,128,128]{2,1,0:T(8,128)(2,1)S(1)}, bf16[8,128,128]{2,1,0:T(8,128)(2,1)S(1)}, u32[]{:S(2)}, u32[]{:S(2)}) collective-permute-start(bf16[8,128,128]{2,1,0:T(8,128)(2,1)S(1)} %collective-permute-done.1.refs_2_), channel_id=1, source_target_pairs={{0,2},{2,0},{4,6},{6,4},{8,10},{10,8},{12,14},{14,12},{16,18},{18,... | collective-permute-start | bytes 786440 | tf_op jit(solution)/shard_map/ppermute | solution.py:478
  49.3 3.0 %collective-permute-start.18 = (bf16[8,128,128]{2,1,0:T(8,128)(2,1)S(1)}, bf16[8,128,128]{2,1,0:T(8,128)(2,1)S(1)}, u32[]{:S(2)}, u32[]{:S(2)}) collective-permute-start(bf16[8,128,128]{2,1,0:T(8,128)(2,1)S(1)} %collective-permute-done.refs_14_), channel_id=1, source_target_pairs={{0,2},{2,0},{4,6},{6,4},{8,10},{10,8},{12,14},{14,12},{16,18},{18,... | collective-permute-start | bytes 786440 | tf_op jit(solution)/shard_map/ppermute | solution.py:478
  50.3 2.8 %collective-permute-start.13 = (bf16[8,128,128]{2,1,0:T(8,128)(2,1)S(1)}, bf16[8,128,128]{2,1,0:T(8,128)(2,1)S(1)}, u32[]{:S(2)}, u32[]{:S(2)}) collective-permute-start(bf16[8,128,128]{2,1,0:T(8,128)(2,1)S(1)} %collective-permute-done.3.refs_4_), channel_id=1, source_target_pairs={{0,2},{2,0},{4,6},{6,4},{8,10},{10,8},{12,14},{14,12},{16,18},{18,... | collective-permute-start | bytes 786440 | tf_op jit(solution)/shard_map/ppermute | solution.py:478
  50.3 2.9 %collective-permute-start.17 = (bf16[8,128,128]{2,1,0:T(8,128)(2,1)S(1)}, bf16[8,128,128]{2,1,0:T(8,128)(2,1)S(1)}, u32[]{:S(2)}, u32[]{:S(2)}) collective-permute-start(bf16[8,128,128]{2,1,0:T(8,128)(2,1)S(1)} %collective-permute-done.2.refs_12_), channel_id=1, source_target_pairs={{0,2},{2,0},{4,6},{6,4},{8,10},{10,8},{12,14},{14,12},{16,18},{18,... | collective-permute-start | bytes 786440 | tf_op jit(solution)/shard_map/ppermute | solution.py:478
  50.8 14.1 %copy-start.8 = (bf16[8,128,128]{2,1,0:T(8,128)(2,1)}, bf16[8,128,128]{2,1,0:T(8,128)(2,1)S(1)}, u32[]{:S(2)}) copy-start(bf16[8,128,128]{2,1,0:T(8,128)(2,1)S(1)} %collective-permute-done.7.refs_8_) | copy-start | bytes 786436
  50.8 3.5 %collective-permute-start.14 = (bf16[8,128,128]{2,1,0:T(8,128)(2,1)S(1)}, bf16[8,128,128]{2,1,0:T(8,128)(2,1)S(1)}, u32[]{:S(2)}, u32[]{:S(2)}) collective-permute-start(bf16[8,128,128]{2,1,0:T(8,128)(2,1)S(1)} %collective-permute-done.5.refs_6_), channel_id=1, source_target_pairs={{0,2},{2,0},{4,6},{6,4},{8,10},{10,8},{12,14},{14,12},{16,18},{18,... | collective-permute-start | bytes 786440 | tf_op jit(solution)/shard_map/ppermute | solution.py:478
  51.9 13.0 %copy-start.9 = (bf16[8,128,128]{2,1,0:T(8,128)(2,1)}, bf16[8,128,128]{2,1,0:T(8,128)(2,1)S(1)}, u32[]{:S(2)}) copy-start(bf16[8,128,128]{2,1,0:T(8,128)(2,1)S(1)} %collective-permute-done.12.refs_3_) | copy-start | bytes 786436
  51.9 12.8 %collective-permute-start.16 = (bf16[8,128,128]{2,1,0:T(8,128)(2,1)S(1)}, bf16[8,128,128]{2,1,0:T(8,128)(2,1)S(1)}, u32[]{:S(2)}, u32[]{:S(2)}) collective-permute-start(bf16[8,128,128]{2,1,0:T(8,128)(2,1)S(1)} %collective-permute-done.4.refs_10_), channel_id=1, source_target_pairs={{0,2},{2,0},{4,6},{6,4},{8,10},{10,8},{12,14},{14,12},{16,18},{18,... | collective-permute-start | bytes 786440 | tf_op jit(solution)/shard_map/ppermute | solution.py:478
  52.4 12.5 %copy-start.10 = (bf16[8,128,128]{2,1,0:T(8,128)(2,1)}, bf16[8,128,128]{2,1,0:T(8,128)(2,1)S(1)}, u32[]{:S(2)}) copy-start(bf16[8,128,128]{2,1,0:T(8,128)(2,1)S(1)} %collective-permute-done.18.refs_15_) | copy-start | bytes 786436
  52.4 12.4 %collective-permute-start.15 = (bf16[8,128,128]{2,1,0:T(8,128)(2,1)S(1)}, bf16[8,128,128]{2,1,0:T(8,128)(2,1)S(1)}, u32[]{:S(2)}, u32[]{:S(2)}) collective-permute-start(bf16[8,128,128]{2,1,0:T(8,128)(2,1)S(1)} %collective-permute-done.7.refs_8_), channel_id=1, source_target_pairs={{0,2},{2,0},{4,6},{6,4},{8,10},{10,8},{12,14},{14,12},{16,18},{18,... | collective-permute-start | bytes 786440 | tf_op jit(solution)/shard_map/ppermute | solution.py:478
  53.1 11.8 %copy-start.11 = (bf16[8,128,128]{2,1,0:T(8,128)(2,1)}, bf16[8,128,128]{2,1,0:T(8,128)(2,1)S(1)}, u32[]{:S(2)}) copy-start(bf16[8,128,128]{2,1,0:T(8,128)(2,1)S(1)} %collective-permute-done.13.refs_5_) | copy-start | bytes 786436
  53.1 11.6 %collective-permute-start.19 = (bf16[128,128]{1,0:T(8,128)(2,1)S(1)}, bf16[128,128]{1,0:T(8,128)(2,1)S(1)}, u32[]{:S(2)}, u32[]{:S(2)}) collective-permute-start(bf16[128,128]{1,0:T(8,128)(2,1)S(1)} %get-tuple-element.64), channel_id=1, source_target_pairs={{0,8},{2,10},{4,12},{6,14},{8,16},{10,18},{12,20},{14,22},{16,24},... | collective-permute-start | bytes 98312 | tf_op jit(solution)/shard_map/ppermute | solution.py:197
  53.2 11.7 %copy-start.12 = (bf16[8,128,128]{2,1,0:T(8,128)(2,1)}, bf16[8,128,128]{2,1,0:T(8,128)(2,1)S(1)}, u32[]{:S(2)}) copy-start(bf16[8,128,128]{2,1,0:T(8,128)(2,1)S(1)} %collective-permute-done.17.refs_13_) | copy-start | bytes 786436
  53.2 11.5 %collective-permute-start.20 = (bf16[128,128]{1,0:T(8,128)(2,1)S(1)}, bf16[128,128]{1,0:T(8,128)(2,1)S(1)}, u32[]{:S(2)}, u32[]{:S(2)}) collective-permute-start(bf16[128,128]{1,0:T(8,128)(2,1)S(1)} %get-tuple-element.63), channel_id=1, source_target_pairs={{0,16},{2,18},{4,20},{6,22},{8,24},{10,26},{12,28},{14,30},{16,0},... | collective-permute-start | bytes 98312 | tf_op jit(solution)/shard_map/ppermute | solution.py:197
  54.3 10.6 %copy-start.13 = (bf16[8,128,128]{2,1,0:T(8,128)(2,1)}, bf16[8,128,128]{2,1,0:T(8,128)(2,1)S(1)}, u32[]{:S(2)}) copy-start(bf16[8,128,128]{2,1,0:T(8,128)(2,1)S(1)} %collective-permute-done.14.refs_7_) | copy-start | bytes 786436
  54.3 10.5 %collective-permute-start.21 = (bf16[128,128]{1,0:T(8,128)(2,1)S(1)}, bf16[128,128]{1,0:T(8,128)(2,1)S(1)}, u32[]{:S(2)}, u32[]{:S(2)}) collective-permute-start(bf16[128,128]{1,0:T(8,128)(2,1)S(1)} %get-tuple-element.62), channel_id=1, source_target_pairs={{0,24},{2,26},{4,28},{6,30},{8,0},{10,2},{12,4},{14,6},{16,8},{18,... | collective-permute-start | bytes 98312 | tf_op jit(solution)/shard_map/ppermute | solution.py:197
  64.7 0.7 copy-start.14
  64.7 0.7 copy-start.17
  64.7 0.7 copy-start.18
  64.8 0.7 copy-start.19
  64.8 0.7 copy-start.15

commit v6 on v5

--- a/solution.py
+++ b/solution.py
@@ -8,7 +8,7 @@
 from jax.sharding import PartitionSpec as P
 
 AXES = ("loop", "own")
-CHUNK = 8
+CHUNK = 16
 ridge = 0.05
 VMEM_LIMIT = 60 * 2**20
 f32 = jnp.float32
@@ -341,27 +341,23 @@
         i = jnp.minimum(i, used - 1)
         return (words[places[i]].astype(f32) * subs[pl.ds(chosen[i], 1), :]).astype(bf16)
 
-    def build(chunk, carry):
-        load(chunk).wait()
-        if cached:
-            for b in range(CHUNK):
-                products[chunk, b * tile : (b + 1) * tile, :] = product(chunk * CHUNK + b)
-        return carry
-
     for copy in copies:
         copy.wait()
-    lax.fori_loop(0, chunks, build, 0)
-
-    def gram(vector):
+
+    def gram(vector, build=False):
         rounded = vector.astype(bf16)
 
         def body(chunk, total):
-            if cached:
+            if build:
+                load(chunk).wait()
+            if cached and not build:
                 block = products[chunk]
             else:
                 block = jnp.concatenate(
                     [product(chunk * CHUNK + b) for b in range(CHUNK)], axis=0
                 )
+                if cached:
+                    products[chunk] = block
             weights = dot_nt(rounded, block).astype(bf16) * masks[chunk]
             return total + dot_nn(weights, block)
 
@@ -374,7 +370,7 @@
     rhs = terms[0][...].astype(f32)
     for term in terms[1:]:
         rhs = rhs + term[...].astype(f32)
-    first = scale * (rhs - gram(start[...])) - ridge * start[...]
+    first = scale * (rhs - gram(start[...], build=True)) - ridge * start[...]
     second = scale * gram(first) + ridge * first
     norms, overlaps = over_row(first, first), over_row(first, second)
     share = jnp.where(norms > 0.0, overlaps / jnp.where(norms > 0.0, norms, 1.0), 0.0)
@@ -520,13 +516,14 @@
     for step in range(4, chips // 2 + 1):
         up, down = ring_round(up, down, held, step, shards)
     total = reduce_chip(parts, shards, owners)
-    held[chips // 2], total, received = together((held[chips // 2], total, received))
+    lists = build_masks(received, slots, word_tiles, own_rows)
+    held[chips // 2], total, *lists = together((held[chips // 2], total, *lists))
+    chosen, places, subs, masks = lists
 
     terms = reduce_levels(total, shards)
     pieces = []
     for distance in range(chips):
         pieces += [held[distance], other_core(held[distance], shards)]
-    chosen, places, subs, masks = build_masks(received, slots, word_tiles, own_rows)
     first, second, third, dots = krylov(
         chosen, places, factor_start, activity[None], subs, masks, pieces, terms, devices
     )

time: 95.4 us -> 91.3 us (0.957)
  Pallas kernels: 42 us -> 36 us
  waiting for transfers between devices: 13 us -> 15.7 us
  blocking collectives: 10.4 us -> 11.9 us
  starting transfers between devices: 24.7 us -> 23.3 us
    pallas_call x1, Pallas kernels: 16.4 us -> 11.2 us  [krylov(): pl.pallas_call(functools.partial(steps_kernel, shards=len(pieces), levels...]
    ppermute x3, waiting for transfers between devices: 0.01 us -> 4.51 us  [reduce_levels(): terms.append(lax.ppermute(total[up], 'loop', shift))]
    ppermute x3, starting transfers between devices: 0.26 us -> 3.25 us  [ring_round(): down = lax.ppermute(down, 'loop', shift(-1))]
    ppermute x4, starting transfers between devices: 9.29 us -> 6.39 us  [ring_round(): up = lax.ppermute(up, 'loop', shift(1))]
    ppermute x3, starting transfers between devices: 3.93 us -> 2.08 us  [reduce_levels(): terms.append(lax.ppermute(total[up], 'loop', shift))]
    ppermute x3, waiting for transfers between devices: 8.8 us -> 6.95 us  [reduce_chip(): total.append(lax.ppermute(parts[2 * o + column], AXES, pairs).astype(f32))]
    all_to_all x1, blocking collectives: 10.4 us -> 11.9 us  [on_device(): everyone = lax.all_to_all(dots, AXES, 0, 0, tiled=True)]
  transfers between devices with their start and end apart: 23 -> 23, of which waited for: 6 -> 8; matrix products, arithmetic and copies ran while one was open for 2% -> 2% of each run, Pallas kernels for 25% -> 25%
where the time goes in v6:
time: 91.3 us; the launch traced here: 90.8 us
  Pallas kernels  36 us (39%)
  starting transfers between devices  23.3 us (26%)
  waiting for transfers between devices  15.7 us (17%)
  blocking collectives  11.9 us (13%)
  local copies, waits for them, and re-layouts  2.06 us (2%)
  other arithmetic  0.98 us (1%)
  between operations  0.93 us (1%)
    pallas_call x2, Pallas kernels, rhs_sums(): pl.pallas_call(functools.partial(rhs_kernel, half=half, owners=owners, ow...  13.8 us
    all_to_all x1, blocking collectives, on_device(): everyone = lax.all_to_all(dots, AXES, 0, 0, tiled=True)  11.9 us
    pallas_call x1, Pallas kernels, krylov(): pl.pallas_call(functools.partial(steps_kernel, shards=len(pieces), levels...  11.2 us
    ppermute x3, waiting for transfers between devices, reduce_chip(): total.append(lax.ppermute(parts[2 * o + column], AXES, pairs).astype(f32))  6.95 us
    pallas_call x1, Pallas kernels, build_masks(): pl.pallas_call(functools.partial(masks_kernel, word_tiles=word_tiles), in...  6.73 us
    ppermute x4, starting transfers between devices, ring_round(): up = lax.ppermute(up, 'loop', shift(1))  6.39 us
    all_to_all x1, starting transfers between devices, on_device(): received = lax.all_to_all(message, AXES, 0, 0, tiled=True)  6.23 us
    ppermute x3, waiting for transfers between devices, reduce_levels(): terms.append(lax.ppermute(total[up], 'loop', shift))  4.51 us
  transfers between devices with their start and end apart: 23, of which 8 were waited for; matrix products, arithmetic and copies ran while one was open for 2% of the time, Pallas kernels for 25%

profile of v6, /device:TPU:0, one launch (start us, length us, event | category | flops | bytes accessed | tf_op | source)
XLA Modules:
  0.0 90.8 jit_solution(9252258512045550429)
XLA Ops:
  0.6 0.0 copy-start
  0.6 3.0 %collective-permute-start.1 = (bf16[8,128,128]{2,1,0:T(8,128)(2,1)}, bf16[8,128,128]{2,1,0:T(8,128)(2,1)S(1)}, u32[]{:S(2)}, u32[]{:S(2)}) collective-permute-start(bf16[8,128,128]{2,1,0:T(8,128)(2,1)} %bitcast.24), channel_id=1, source_target_pairs={{0,4},{2,6},{8,0},{10,2},{16,8},{18,10},{24,16},{26,18},{28,24},{3... | collective-permute-start | bytes 786440 | tf_op jit(solution)/shard_map/ppermute | solution.py:468
  3.6 0.2 collective-permute-start
  3.8 2.4 %facts.1 = bf16[16,2,32,128]{3,2,1,0:T(8,128)(2,1)} custom-call(s32[8,16]{1,0:T(8,128)} %bitcast.33, s32[8,16]{1,0:T(8,128)} %bitcast.36, s32[8,16]{1,0:T(8,128)} %bitcast.39, s32[1,16]{1,0:T(1,128)} %bitcast.42, s32[16,8,2,128]{3,2,1,0:T(2,128)} %bitcast.30, bf16[2048,128]{1,0:T(8,128)(2,1)} %subs_in.1), custom_call_target="tpu_custom_call" | custom-call | tf_op jit(solution)/shard_map/facts/pallas_call | solution.py:63
  6.2 6.2 %all-to-all-start = ((bf16[32,32,128]{2,1,0:T(8,128)(2,1)}), bf16[32,32,128]{2,1,0:T(8,128)(2,1)S(1)}, u32[]{:S(2)}, u32[]{:S(2)}) async-start(bf16[32,32,128]{2,1,0:T(8,128)(2,1)} %bitcast.23), calls=%async_computation | async-start | bytes 524288 | tf_op jit(solution)/shard_map/all_to_all | solution.py:502
  12.4 0.0 collective-permute-done.1.refs_2_
  12.5 1.8 %collective-permute-start.2 = (bf16[8,128,128]{2,1,0:T(8,128)(2,1)S(1)}, bf16[8,128,128]{2,1,0:T(8,128)(2,1)S(1)}, u32[]{:S(2)}, u32[]{:S(2)}) collective-permute-start(bf16[8,128,128]{2,1,0:T(8,128)(2,1)S(1)} %collective-permute-done.refs_14_), channel_id=1, source_target_pairs={{0,8},{2,10},{8,16},{10,18},{16,24},{18,26},{24,28},{26,30},{28,20... | collective-permute-start | bytes 786440 | tf_op jit(solution)/shard_map/ppermute | solution.py:465
  14.3 0.3 collective-permute-start.3
  14.5 6.8 %rhs.2 = bf16[2,2,4,128,128]{4,3,2,1,0:T(8,128)(2,1)} custom-call(s32[8,16]{1,0:T(8,128)} %bitcast.34, s32[8,16]{1,0:T(8,128)} %bitcast.37, s32[8,16]{1,0:T(8,128)} %bitcast.40, s32[1,16]{1,0:T(1,128)} %bitcast.43, bf16[16,8,128,128]{3,2,1,0:T(8,128)(2,1)} %bitcast.46, s32[16,8,2,128]{3,2,1,0:T(2,128)} %bitcast.31, bf16[8,128,128]{2,1,0:T(8,128)(2,1)} %bitcast.26, ...), custom_call_target="tpu_custom_call" | custom-call | flops 2147483648 | bytes 16777216 | tf_op jit(solution)/shard_map/rhs/pallas_call | solution.py:153
  21.3 2.2 %all-to-all-done.received = bf16[32,32,128]{2,1,0:T(8,128)(2,1)S(1)} async-done(((bf16[32,32,128]{2,1,0:T(8,128)(2,1)}), bf16[32,32,128]{2,1,0:T(8,128)(2,1)S(1)}, u32[]{:S(2)}, u32[]{:S(2)}) %all-to-all-start) | async-done | bytes 262176 | tf_op jit(solution)/shard_map/all_to_all | solution.py:502
  23.6 0.1 collective-permute-done.2.refs_12_
  23.7 1.4 %collective-permute-done.3.refs_4_ = bf16[8,128,128]{2,1,0:T(8,128)(2,1)S(1)} collective-permute-done((bf16[8,128,128]{2,1,0:T(8,128)(2,1)S(1)}, bf16[8,128,128]{2,1,0:T(8,128)(2,1)S(1)}, u32[]{:S(2)}, u32[]{:S(2)}) %collective-permute-start.3) | collective-permute-done | bytes 262176 | tf_op jit(solution)/shard_map/ppermute | solution.py:468
  25.1 0.0 collective-permute-start.6
  25.1 2.9 %collective-permute-start.4 = (bf16[8,128,128]{2,1,0:T(8,128)(2,1)S(1)}, bf16[8,128,128]{2,1,0:T(8,128)(2,1)S(1)}, u32[]{:S(2)}, u32[]{:S(2)}) collective-permute-start(bf16[8,128,128]{2,1,0:T(8,128)(2,1)S(1)} %collective-permute-done.2.refs_12_), channel_id=1, source_target_pairs={{0,8},{2,10},{8,16},{10,18},{16,24},{18,26},{24,28},{26,30},{28,20... | collective-permute-start | bytes 786440 | tf_op jit(solution)/shard_map/ppermute | solution.py:465
  28.0 0.2 collective-permute-start.11
  28.2 0.8 copy-done.20
  29.0 7.0 %rhs.3 = (bf16[4,128,128]{2,1,0:T(8,128)(2,1)}, bf16[4,128,128]{2,1,0:T(8,128)(2,1)}, bf16[4,128,128]{2,1,0:T(8,128)(2,1)}, bf16[4,128,128]{2,1,0:T(8,128)(2,1)}) custom-call(s32[8,16]{1,0:T(8,128)} %bitcast.35, s32[8,16]{1,0:T(8,128)} %bitcast.38, s32[8,16]{1,0:T(8,128)} %bitcast.41, s32[1,16]{1,0:T(1,128)} %bitcast.44, bf16[16,8,128,128]{3,2,1,0:T(8,128)(2,1)} %bitcast.47, ...), custom_call_target="tpu_custom_call" | custom-call | flops 2147483648 | bytes 16777216 | tf_op jit(solution)/shard_map/rhs/pallas_call | solution.py:153
  36.0 0.0 collective-permute-done.4.refs_10_
  36.0 0.4 collective-permute-done.5.refs_6_
  36.4 1.5 %collective-permute-start.7 = (bf16[8,128,128]{2,1,0:T(8,128)(2,1)S(1)}, bf16[8,128,128]{2,1,0:T(8,128)(2,1)S(1)}, u32[]{:S(2)}, u32[]{:S(2)}) collective-permute-start(bf16[8,128,128]{2,1,0:T(8,128)(2,1)S(1)} %collective-permute-done.4.refs_10_), channel_id=1, source_target_pairs={{0,8},{2,10},{8,16},{10,18},{16,24},{18,26},{24,28},{26,30},{28,20... | collective-permute-start | bytes 786440 | tf_op jit(solution)/shard_map/ppermute | solution.py:465
  38.0 0.5 collective-permute-start.8
  38.5 1.5 %collective-permute-start.9 = (bf16[4,128,128]{2,1,0:T(8,128)(2,1)}, bf16[4,128,128]{2,1,0:T(8,128)(2,1)S(1)}, u32[]{:S(2)}, u32[]{:S(2)}) collective-permute-start(bf16[4,128,128]{2,1,0:T(8,128)(2,1)} %get-tuple-element.51), channel_id=1, source_target_pairs={{0,1},{1,0},{2,3},{3,2},{4,5},{5,4},{6,7},{7,6},{8,9},{9,8},{10,11... | collective-permute-start | bytes 393224 | tf_op jit(solution)/shard_map/ppermute | solution.py:188
  39.9 1.5 %collective-permute-start.10 = (bf16[4,128,128]{2,1,0:T(8,128)(2,1)}, bf16[4,128,128]{2,1,0:T(8,128)(2,1)S(1)}, u32[]{:S(2)}, u32[]{:S(2)}) collective-permute-start(bf16[4,128,128]{2,1,0:T(8,128)(2,1)} %get-tuple-element.52), channel_id=1, source_target_pairs={{0,5},{1,4},{2,7},{3,6},{4,1},{5,0},{6,3},{7,2},{8,13},{9,12},{10,... | collective-permute-start | bytes 393224 | tf_op jit(solution)/shard_map/ppermute | solution.py:188
  41.5 0.0 collective-permute-start.12
  41.5 6.9 %collective-permute-done.8 = bf16[4,128,128]{2,1,0:T(8,128)(2,1)S(1)} collective-permute-done((bf16[4,128,128]{2,1,0:T(8,128)(2,1)}, bf16[4,128,128]{2,1,0:T(8,128)(2,1)S(1)}, u32[]{:S(2)}, u32[]{:S(2)}) %collective-permute-start.8) | collective-permute-done | bytes 131104 | tf_op jit(solution)/shard_map/ppermute | solution.py:188
  48.4 6.7 %masks.1 = (s32[257]{0:T(512)}, s32[256]{0:T(256)}, f32[256,128]{1,0:T(8,128)}, bf16[16,128,2048]{2,1,0:T(8,128)(2,1)}) custom-call(bf16[32,32,128]{2,1,0:T(8,128)(2,1)} %copy-done.16), custom_call_target="tpu_custom_call" | custom-call | flops 671088640 | bytes 5242880 | tf_op jit(solution)/shard_map/masks/pallas_call | solution.py:284
  55.2 0.0 collective-permute-done.9
  55.2 0.6 collective-permute-start.17
  55.8 0.0 collective-permute-done.10
  55.8 0.1 collective-permute-start.13
  55.9 0.0 collective-permute-done.7.refs_8_
  55.9 0.4 collective-permute-start.16
  56.3 1.0 %add_convert_fusion = bf16[4,128,128]{2,1,0:T(8,128)(2,1)S(1)} fusion(bf16[4,128,128]{2,1,0:T(8,128)(2,1)S(1)} %collective-permute-done.10, bf16[4,128,128]{2,1,0:T(8,128)(2,1)S(1)} %collective-permute-done.9, bf16[4,128,128]{2,1,0:T(8,128)(2,1)S(1)} %collective-permute-done.8, bf16[4,128,128]{2,1,0:T(8,128)(2,1)} %get-tuple-element.49), kind=kLoop, calls=%fused_computation | loop fusion | flops 524288 | bytes 655360 | tf_op jit(solution)/shard_map/convert_element_type | solution.py:189
  57.3 0.0 collective-permute-done.12.refs_3_
  57.3 0.2 collective-permute-start.14
  57.5 0.0 collective-permute-done.18.refs_15_
  57.5 0.4 collective-permute-start.15
  57.9 0.6 slice_bitcast_fusion
  58.5 0.5 collective-permute-start.21
  59.1 1.5 %collective-permute-start.19 = (bf16[128,128]{1,0:T(8,128)(2,1)S(1)}, bf16[128,128]{1,0:T(8,128)(2,1)S(1)}, u32[]{:S(2)}, u32[]{:S(2)}) collective-permute-start(bf16[128,128]{1,0:T(8,128)(2,1)S(1)} %get-tuple-element.70), channel_id=1, source_target_pairs={{0,8},{2,10},{4,12},{6,14},{8,16},{10,18},{12,20},{14,22},{16,24},... | collective-permute-start | bytes 98312 | tf_op jit(solution)/shard_map/ppermute | solution.py:197
  60.6 1.8 %collective-permute-done.21.refs_19_ = bf16[128,128]{1,0:T(8,128)(2,1)S(1)} collective-permute-done((bf16[128,128]{1,0:T(8,128)(2,1)S(1)}, bf16[128,128]{1,0:T(8,128)(2,1)S(1)}, u32[]{:S(2)}, u32[]{:S(2)}) %collective-permute-start.21) | collective-permute-done | bytes 32800 | tf_op jit(solution)/shard_map/ppermute | solution.py:197
  62.4 1.9 %collective-permute-done.20.refs_18_ = bf16[128,128]{1,0:T(8,128)(2,1)S(1)} collective-permute-done((bf16[128,128]{1,0:T(8,128)(2,1)S(1)}, bf16[128,128]{1,0:T(8,128)(2,1)S(1)}, u32[]{:S(2)}, u32[]{:S(2)}) %collective-permute-start.20) | collective-permute-done | bytes 32800 | tf_op jit(solution)/shard_map/ppermute | solution.py:197
  64.4 0.8 collective-permute-done.19.refs_17_
  65.3 0.5 copy-done.19
  65.7 0.1 copy-done.15
  65.8 11.2 %krylov.1 = (f32[128,128]{1,0:T(8,128)}, f32[128,128]{1,0:T(8,128)}, f32[128,128]{1,0:T(8,128)}, f32[32,1,128]{2,1,0:T(1,128)}) custom-call(s32[257]{0:T(512)} %get-tuple-element.58.chosen, s32[256]{0:T(256)} %get-tuple-element.59.places, f32[128,128]{1,0:T(8,128)} %start.3, f32[1,128]{1,0:T(1,128)} %bitcast.45, f32[256,128]{1,0:T(8,128)} %get-tuple-element.60.subs, ...), custom_call_target="tpu_custom_call" | custom-call | tf_op jit(solution)/shard_map/krylov/pallas_call | solution.py:408
  77.1 11.9 %all_to_all.10.dots = f32[32,1,128]{2,1,0:T(1,128)} all-to-all(f32[32,1,128]{2,1,0:T(1,128)} %get-tuple-element.64), channel_id=1, replica_groups=mesh['loop'=16,'own'=2] {'loop','own'}, dimensions={0} | all-to-all | bytes 32768 | tf_op jit(solution)/shard_map/all_to_all | solution.py:530
  89.0 1.9 %last_step.1 = (f32[128,128]{1,0:T(8,128)}, f32[128,128]{1,0:T(8,128)}) custom-call(f32[32,1,128]{2,1,0:T(1,128)} %all_to_all.10.dots, f32[128,128]{1,0:T(8,128)} %start.3, f32[128,128]{1,0:T(8,128)} %get-tuple-element.65.first, f32[128,128]{1,0:T(8,128)} %get-tuple-element.66.second, f32[128,128]{1,0:T(8,128)} %get-tuple-element.67.third), custom_call_target="tpu_custom_call" | custom-call | tf_op jit(solution)/shard_map/last_step/pallas_call | solution.py:441
  (49 shorter events, 0.1 us)
Async XLA Ops:
  0.6 27.4 %copy-start = (bf16[1,8,128,128]{3,2,1,0:T(8,128)(2,1)S(1)}, bf16[1,8,128,128]{3,2,1,0:T(8,128)(2,1)}, u32[]{:S(2)}) copy-start(bf16[1,8,128,128]{3,2,1,0:T(8,128)(2,1)} %param.12) | copy-start | bytes 786436
  0.6 11.8 %collective-permute-start.1 = (bf16[8,128,128]{2,1,0:T(8,128)(2,1)}, bf16[8,128,128]{2,1,0:T(8,128)(2,1)S(1)}, u32[]{:S(2)}, u32[]{:S(2)}) collective-permute-start(bf16[8,128,128]{2,1,0:T(8,128)(2,1)} %bitcast.24), channel_id=1, source_target_pairs={{0,4},{2,6},{8,0},{10,2},{16,8},{18,10},{24,16},{26,18},{28,24},{3... | collective-permute-start | bytes 786440 | tf_op jit(solution)/shard_map/ppermute | solution.py:468
  3.6 8.8 %collective-permute-start = (bf16[8,128,128]{2,1,0:T(8,128)(2,1)}, bf16[8,128,128]{2,1,0:T(8,128)(2,1)S(1)}, u32[]{:S(2)}, u32[]{:S(2)}) collective-permute-start(bf16[8,128,128]{2,1,0:T(8,128)(2,1)} %bitcast.25), channel_id=1, source_target_pairs={{0,8},{2,10},{8,16},{10,18},{16,24},{18,26},{24,28},{26,30},{28,20... | collective-permute-start | bytes 786440 | tf_op jit(solution)/shard_map/ppermute | solution.py:465
  6.2 17.4 %all-to-all-start = ((bf16[32,32,128]{2,1,0:T(8,128)(2,1)}), bf16[32,32,128]{2,1,0:T(8,128)(2,1)S(1)}, u32[]{:S(2)}, u32[]{:S(2)}) async-start(bf16[32,32,128]{2,1,0:T(8,128)(2,1)} %bitcast.23), calls=%async_computation | async-start | bytes 524288 | tf_op jit(solution)/shard_map/all_to_all | solution.py:502
  12.4 42.7 %copy-start.1 = (bf16[8,128,128]{2,1,0:T(8,128)(2,1)}, bf16[8,128,128]{2,1,0:T(8,128)(2,1)S(1)}, u32[]{:S(2)}) copy-start(bf16[8,128,128]{2,1,0:T(8,128)(2,1)S(1)} %collective-permute-done.1.refs_2_) | copy-start | bytes 786436
  12.4 42.7 %copy-start.2 = (bf16[8,128,128]{2,1,0:T(8,128)(2,1)}, bf16[8,128,128]{2,1,0:T(8,128)(2,1)S(1)}, u32[]{:S(2)}) copy-start(bf16[8,128,128]{2,1,0:T(8,128)(2,1)S(1)} %collective-permute-done.refs_14_) | copy-start | bytes 786436
  12.5 11.2 %collective-permute-start.2 = (bf16[8,128,128]{2,1,0:T(8,128)(2,1)S(1)}, bf16[8,128,128]{2,1,0:T(8,128)(2,1)S(1)}, u32[]{:S(2)}, u32[]{:S(2)}) collective-permute-start(bf16[8,128,128]{2,1,0:T(8,128)(2,1)S(1)} %collective-permute-done.refs_14_), channel_id=1, source_target_pairs={{0,8},{2,10},{8,16},{10,18},{16,24},{18,26},{24,28},{26,30},{28,20... | collective-permute-start | bytes 786440 | tf_op jit(solution)/shard_map/ppermute | solution.py:465
  14.3 10.8 %collective-permute-start.3 = (bf16[8,128,128]{2,1,0:T(8,128)(2,1)S(1)}, bf16[8,128,128]{2,1,0:T(8,128)(2,1)S(1)}, u32[]{:S(2)}, u32[]{:S(2)}) collective-permute-start(bf16[8,128,128]{2,1,0:T(8,128)(2,1)S(1)} %collective-permute-done.1.refs_2_), channel_id=1, source_target_pairs={{0,4},{2,6},{8,0},{10,2},{16,8},{18,10},{24,16},{26,18},{28,24},{3... | collective-permute-start | bytes 786440 | tf_op jit(solution)/shard_map/ppermute | solution.py:468
  23.6 24.9 %copy-start.16 = (bf16[32,32,128]{2,1,0:T(8,128)(2,1)}, bf16[32,32,128]{2,1,0:T(8,128)(2,1)S(1)}, u32[]{:S(2)}) copy-start(bf16[32,32,128]{2,1,0:T(8,128)(2,1)S(1)} %all-to-all-done.received) | copy-start | bytes 786436
  23.7 41.4 %copy-start.3 = (bf16[8,128,128]{2,1,0:T(8,128)(2,1)}, bf16[8,128,128]{2,1,0:T(8,128)(2,1)S(1)}, u32[]{:S(2)}) copy-start(bf16[8,128,128]{2,1,0:T(8,128)(2,1)S(1)} %collective-permute-done.2.refs_12_) | copy-start | bytes 786436
  25.1 40.0 %copy-start.4 = (bf16[8,128,128]{2,1,0:T(8,128)(2,1)}, bf16[8,128,128]{2,1,0:T(8,128)(2,1)S(1)}, u32[]{:S(2)}) copy-start(bf16[8,128,128]{2,1,0:T(8,128)(2,1)S(1)} %collective-permute-done.3.refs_4_) | copy-start | bytes 786436
  25.1 3.1 %collective-permute-start.6 = (bf16[2,2,4,128,128]{4,3,2,1,0:T(8,128)(2,1)}, bf16[2,2,4,128,128]{4,3,2,1,0:T(8,128)(2,1)S(1)}, u32[]{:S(2)}, u32[]{:S(2)}) collective-permute-start(bf16[2,2,4,128,128]{4,3,2,1,0:T(8,128)(2,1)} %rhs.2), channel_id=1, source_target_pairs={{0,2},{2,0},{4,6},{6,4},{8,10},{10,8},{12,14},{14,12},{16,18},{18,... | collective-permute-start | bytes 1572872 | tf_op jit(solution)/shard_map/ppermute | solution.py:474
  25.1 10.9 %collective-permute-start.4 = (bf16[8,128,128]{2,1,0:T(8,128)(2,1)S(1)}, bf16[8,128,128]{2,1,0:T(8,128)(2,1)S(1)}, u32[]{:S(2)}, u32[]{:S(2)}) collective-permute-start(bf16[8,128,128]{2,1,0:T(8,128)(2,1)S(1)} %collective-permute-done.2.refs_12_), channel_id=1, source_target_pairs={{0,8},{2,10},{8,16},{10,18},{16,24},{18,26},{24,28},{26,30},{28,20... | collective-permute-start | bytes 786440 | tf_op jit(solution)/shard_map/ppermute | solution.py:465
  28.0 8.4 %collective-permute-start.5 = (bf16[8,128,128]{2,1,0:T(8,128)(2,1)S(1)}, bf16[8,128,128]{2,1,0:T(8,128)(2,1)S(1)}, u32[]{:S(2)}, u32[]{:S(2)}) collective-permute-start(bf16[8,128,128]{2,1,0:T(8,128)(2,1)S(1)} %collective-permute-done.3.refs_4_), channel_id=1, source_target_pairs={{0,4},{2,6},{8,0},{10,2},{16,8},{18,10},{24,16},{26,18},{28,24},{3... | collective-permute-start | bytes 786440 | tf_op jit(solution)/shard_map/ppermute | solution.py:468
  28.0 13.5 %collective-permute-start.11 = (bf16[8,128,128]{2,1,0:T(8,128)(2,1)S(1)}, bf16[8,128,128]{2,1,0:T(8,128)(2,1)S(1)}, u32[]{:S(2)}, u32[]{:S(2)}) collective-permute-start(bf16[8,128,128]{2,1,0:T(8,128)(2,1)S(1)} %bitcast.29), channel_id=1, source_target_pairs={{0,2},{2,0},{4,6},{6,4},{8,10},{10,8},{12,14},{14,12},{16,18},{18,... | collective-permute-start | bytes 786440 | tf_op jit(solution)/shard_map/ppermute | solution.py:474
  28.2 0.8 copy-start.20
  36.0 29.2 %copy-start.5 = (bf16[8,128,128]{2,1,0:T(8,128)(2,1)}, bf16[8,128,128]{2,1,0:T(8,128)(2,1)S(1)}, u32[]{:S(2)}) copy-start(bf16[8,128,128]{2,1,0:T(8,128)(2,1)S(1)} %collective-permute-done.4.refs_10_) | copy-start | bytes 786436
  36.4 28.7 %copy-start.6 = (bf16[8,128,128]{2,1,0:T(8,128)(2,1)}, bf16[8,128,128]{2,1,0:T(8,128)(2,1)S(1)}, u32[]{:S(2)}) copy-start(bf16[8,128,128]{2,1,0:T(8,128)(2,1)S(1)} %collective-permute-done.5.refs_6_) | copy-start | bytes 786436
  36.4 19.4 %collective-permute-start.7 = (bf16[8,128,128]{2,1,0:T(8,128)(2,1)S(1)}, bf16[8,128,128]{2,1,0:T(8,128)(2,1)S(1)}, u32[]{:S(2)}, u32[]{:S(2)}) collective-permute-start(bf16[8,128,128]{2,1,0:T(8,128)(2,1)S(1)} %collective-permute-done.4.refs_10_), channel_id=1, source_target_pairs={{0,8},{2,10},{8,16},{10,18},{16,24},{18,26},{24,28},{26,30},{28,20... | collective-permute-start | bytes 786440 | tf_op jit(solution)/shard_map/ppermute | solution.py:465
  38.0 10.4 %collective-permute-start.8 = (bf16[4,128,128]{2,1,0:T(8,128)(2,1)}, bf16[4,128,128]{2,1,0:T(8,128)(2,1)S(1)}, u32[]{:S(2)}, u32[]{:S(2)}) collective-permute-start(bf16[4,128,128]{2,1,0:T(8,128)(2,1)} %get-tuple-element.50), channel_id=1, source_target_pairs={{0,4},{1,5},{2,6},{3,7},{4,0},{5,1},{6,2},{7,3},{8,12},{9,13},{10,... | collective-permute-start | bytes 393224 | tf_op jit(solution)/shard_map/ppermute | solution.py:188
  38.5 16.7 %collective-permute-start.9 = (bf16[4,128,128]{2,1,0:T(8,128)(2,1)}, bf16[4,128,128]{2,1,0:T(8,128)(2,1)S(1)}, u32[]{:S(2)}, u32[]{:S(2)}) collective-permute-start(bf16[4,128,128]{2,1,0:T(8,128)(2,1)} %get-tuple-element.51), channel_id=1, source_target_pairs={{0,1},{1,0},{2,3},{3,2},{4,5},{5,4},{6,7},{7,6},{8,9},{9,8},{10,11... | collective-permute-start | bytes 393224 | tf_op jit(solution)/shard_map/ppermute | solution.py:188
  39.9 15.8 %collective-permute-start.10 = (bf16[4,128,128]{2,1,0:T(8,128)(2,1)}, bf16[4,128,128]{2,1,0:T(8,128)(2,1)S(1)}, u32[]{:S(2)}, u32[]{:S(2)}) collective-permute-start(bf16[4,128,128]{2,1,0:T(8,128)(2,1)} %get-tuple-element.52), channel_id=1, source_target_pairs={{0,5},{1,4},{2,7},{3,6},{4,1},{5,0},{6,3},{7,2},{8,13},{9,12},{10,... | collective-permute-start | bytes 393224 | tf_op jit(solution)/shard_map/ppermute | solution.py:188
  41.5 23.7 %copy-start.7 = (bf16[8,128,128]{2,1,0:T(8,128)(2,1)}, bf16[8,128,128]{2,1,0:T(8,128)(2,1)S(1)}, u32[]{:S(2)}) copy-start(bf16[8,128,128]{2,1,0:T(8,128)(2,1)S(1)} %collective-permute-done.11.refs_1_) | copy-start | bytes 786436
  41.5 15.8 %collective-permute-start.12 = (bf16[8,128,128]{2,1,0:T(8,128)(2,1)S(1)}, bf16[8,128,128]{2,1,0:T(8,128)(2,1)S(1)}, u32[]{:S(2)}, u32[]{:S(2)}) collective-permute-start(bf16[8,128,128]{2,1,0:T(8,128)(2,1)S(1)} %collective-permute-done.1.refs_2_), channel_id=1, source_target_pairs={{0,2},{2,0},{4,6},{6,4},{8,10},{10,8},{12,14},{14,12},{16,18},{18,... | collective-permute-start | bytes 786440 | tf_op jit(solution)/shard_map/ppermute | solution.py:474
  48.4 9.0 %collective-permute-start.18 = (bf16[8,128,128]{2,1,0:T(8,128)(2,1)S(1)}, bf16[8,128,128]{2,1,0:T(8,128)(2,1)S(1)}, u32[]{:S(2)}, u32[]{:S(2)}) collective-permute-start(bf16[8,128,128]{2,1,0:T(8,128)(2,1)S(1)} %collective-permute-done.refs_14_), channel_id=1, source_target_pairs={{0,2},{2,0},{4,6},{6,4},{8,10},{10,8},{12,14},{14,12},{16,18},{18,... | collective-permute-start | bytes 786440 | tf_op jit(solution)/shard_map/ppermute | solution.py:474
  55.2 3.3 %collective-permute-start.17 = (bf16[8,128,128]{2,1,0:T(8,128)(2,1)S(1)}, bf16[8,128,128]{2,1,0:T(8,128)(2,1)S(1)}, u32[]{:S(2)}, u32[]{:S(2)}) collective-permute-start(bf16[8,128,128]{2,1,0:T(8,128)(2,1)S(1)} %collective-permute-done.2.refs_12_), channel_id=1, source_target_pairs={{0,2},{2,0},{4,6},{6,4},{8,10},{10,8},{12,14},{14,12},{16,18},{18,... | collective-permute-start | bytes 786440 | tf_op jit(solution)/shard_map/ppermute | solution.py:474
  55.8 3.3 %collective-permute-start.13 = (bf16[8,128,128]{2,1,0:T(8,128)(2,1)S(1)}, bf16[8,128,128]{2,1,0:T(8,128)(2,1)S(1)}, u32[]{:S(2)}, u32[]{:S(2)}) collective-permute-start(bf16[8,128,128]{2,1,0:T(8,128)(2,1)S(1)} %collective-permute-done.3.refs_4_), channel_id=1, source_target_pairs={{0,2},{2,0},{4,6},{6,4},{8,10},{10,8},{12,14},{14,12},{16,18},{18,... | collective-permute-start | bytes 786440 | tf_op jit(solution)/shard_map/ppermute | solution.py:474
  55.9 9.3 %copy-start.8 = (bf16[8,128,128]{2,1,0:T(8,128)(2,1)}, bf16[8,128,128]{2,1,0:T(8,128)(2,1)S(1)}, u32[]{:S(2)}) copy-start(bf16[8,128,128]{2,1,0:T(8,128)(2,1)S(1)} %collective-permute-done.7.refs_8_) | copy-start | bytes 786436
  55.9 3.2 %collective-permute-start.16 = (bf16[8,128,128]{2,1,0:T(8,128)(2,1)S(1)}, bf16[8,128,128]{2,1,0:T(8,128)(2,1)S(1)}, u32[]{:S(2)}, u32[]{:S(2)}) collective-permute-start(bf16[8,128,128]{2,1,0:T(8,128)(2,1)S(1)} %collective-permute-done.4.refs_10_), channel_id=1, source_target_pairs={{0,2},{2,0},{4,6},{6,4},{8,10},{10,8},{12,14},{14,12},{16,18},{18,... | collective-permute-start | bytes 786440 | tf_op jit(solution)/shard_map/ppermute | solution.py:474
  57.3 7.9 %copy-start.9 = (bf16[8,128,128]{2,1,0:T(8,128)(2,1)}, bf16[8,128,128]{2,1,0:T(8,128)(2,1)S(1)}, u32[]{:S(2)}) copy-start(bf16[8,128,128]{2,1,0:T(8,128)(2,1)S(1)} %collective-permute-done.12.refs_3_) | copy-start | bytes 786436
  57.3 3.3 %collective-permute-start.14 = (bf16[8,128,128]{2,1,0:T(8,128)(2,1)S(1)}, bf16[8,128,128]{2,1,0:T(8,128)(2,1)S(1)}, u32[]{:S(2)}, u32[]{:S(2)}) collective-permute-start(bf16[8,128,128]{2,1,0:T(8,128)(2,1)S(1)} %collective-permute-done.5.refs_6_), channel_id=1, source_target_pairs={{0,2},{2,0},{4,6},{6,4},{8,10},{10,8},{12,14},{14,12},{16,18},{18,... | collective-permute-start | bytes 786440 | tf_op jit(solution)/shard_map/ppermute | solution.py:474
  57.5 7.7 %copy-start.10 = (bf16[8,128,128]{2,1,0:T(8,128)(2,1)}, bf16[8,128,128]{2,1,0:T(8,128)(2,1)S(1)}, u32[]{:S(2)}) copy-start(bf16[8,128,128]{2,1,0:T(8,128)(2,1)S(1)} %collective-permute-done.18.refs_15_) | copy-start | bytes 786436
  57.5 7.7 %collective-permute-start.15 = (bf16[8,128,128]{2,1,0:T(8,128)(2,1)S(1)}, bf16[8,128,128]{2,1,0:T(8,128)(2,1)S(1)}, u32[]{:S(2)}, u32[]{:S(2)}) collective-permute-start(bf16[8,128,128]{2,1,0:T(8,128)(2,1)S(1)} %collective-permute-done.7.refs_8_), channel_id=1, source_target_pairs={{0,2},{2,0},{4,6},{6,4},{8,10},{10,8},{12,14},{14,12},{16,18},{18,... | collective-permute-start | bytes 786440 | tf_op jit(solution)/shard_map/ppermute | solution.py:474
  58.5 6.7 %copy-start.11 = (bf16[8,128,128]{2,1,0:T(8,128)(2,1)}, bf16[8,128,128]{2,1,0:T(8,128)(2,1)S(1)}, u32[]{:S(2)}) copy-start(bf16[8,128,128]{2,1,0:T(8,128)(2,1)S(1)} %collective-permute-done.17.refs_13_) | copy-start | bytes 786436
  58.5 3.9 %collective-permute-start.21 = (bf16[128,128]{1,0:T(8,128)(2,1)S(1)}, bf16[128,128]{1,0:T(8,128)(2,1)S(1)}, u32[]{:S(2)}, u32[]{:S(2)}) collective-permute-start(bf16[128,128]{1,0:T(8,128)(2,1)S(1)} %get-tuple-element.68), channel_id=1, source_target_pairs={{0,24},{2,26},{4,28},{6,30},{8,0},{10,2},{12,4},{14,6},{16,8},{18,... | collective-permute-start | bytes 98312 | tf_op jit(solution)/shard_map/ppermute | solution.py:197
  59.0 6.2 %copy-start.12 = (bf16[8,128,128]{2,1,0:T(8,128)(2,1)}, bf16[8,128,128]{2,1,0:T(8,128)(2,1)S(1)}, u32[]{:S(2)}) copy-start(bf16[8,128,128]{2,1,0:T(8,128)(2,1)S(1)} %collective-permute-done.13.refs_5_) | copy-start | bytes 786436
  59.0 5.3 %collective-permute-start.20 = (bf16[128,128]{1,0:T(8,128)(2,1)S(1)}, bf16[128,128]{1,0:T(8,128)(2,1)S(1)}, u32[]{:S(2)}, u32[]{:S(2)}) collective-permute-start(bf16[128,128]{1,0:T(8,128)(2,1)S(1)} %get-tuple-element.69), channel_id=1, source_target_pairs={{0,16},{2,18},{4,20},{6,22},{8,24},{10,26},{12,28},{14,30},{16,0},... | collective-permute-start | bytes 98312 | tf_op jit(solution)/shard_map/ppermute | solution.py:197
  59.0 6.2 %copy-start.13 = (bf16[8,128,128]{2,1,0:T(8,128)(2,1)}, bf16[8,128,128]{2,1,0:T(8,128)(2,1)S(1)}, u32[]{:S(2)}) copy-start(bf16[8,128,128]{2,1,0:T(8,128)(2,1)S(1)} %collective-permute-done.16.refs_11_) | copy-start | bytes 786436
  59.1 6.1 %collective-permute-start.19 = (bf16[128,128]{1,0:T(8,128)(2,1)S(1)}, bf16[128,128]{1,0:T(8,128)(2,1)S(1)}, u32[]{:S(2)}, u32[]{:S(2)}) collective-permute-start(bf16[128,128]{1,0:T(8,128)(2,1)S(1)} %get-tuple-element.70), channel_id=1, source_target_pairs={{0,8},{2,10},{4,12},{6,14},{8,16},{10,18},{12,20},{14,22},{16,24},... | collective-permute-start | bytes 98312 | tf_op jit(solution)/shard_map/ppermute | solution.py:197
  60.6 4.6 %copy-start.14 = (bf16[8,128,128]{2,1,0:T(8,128)(2,1)}, bf16[8,128,128]{2,1,0:T(8,128)(2,1)S(1)}, u32[]{:S(2)}) copy-start(bf16[8,128,128]{2,1,0:T(8,128)(2,1)S(1)} %collective-permute-done.14.refs_7_) | copy-start | bytes 786436
  62.4 2.8 %copy-start.17 = (bf16[128,128]{1,0:T(8,128)(2,1)}, bf16[128,128]{1,0:T(8,128)(2,1)S(1)}, u32[]{:S(2)}) copy-start(bf16[128,128]{1,0:T(8,128)(2,1)S(1)} %collective-permute-done.21.refs_19_) | copy-start | bytes 98308
  64.4 0.9 copy-start.18
  65.1 0.6 copy-start.19
  65.1 0.7 copy-start.15

commit v7 on v6

v7 whole, which is shorter than its diff:
```python
import functools

import jax
import jax.numpy as jnp
from jax import lax
from jax.experimental import pallas as pl
from jax.experimental.pallas import tpu as pltpu
from jax.sharding import PartitionSpec as P

AXES = ("loop", "own")
CHUNK = 16
FACT_ROWS = 16
ridge = 0.05
VMEM_LIMIT = 60 * 2**20
f32 = jnp.float32
bf16 = jnp.bfloat16


def dot_nt(left, right):
    return lax.dot_general(left, right, (((1,), (1,)), ((), ())), preferred_element_type=f32)


def dot_nn(left, right):
    return jnp.dot(left, right, preferred_element_type=f32)


def mask_columns(first, length, tile):
    column = lax.broadcasted_iota(jnp.int32, (tile, first.shape[-1]), 0)
    inside = ((column - first) & (tile - 1)) < length
    return jnp.where(inside, 1.0, 0.0).astype(bf16)


def fact_line(user_tile, word_tile, subreddit, live, group, slots, rank):
    lane = lax.broadcasted_iota(jnp.int32, (1, rank), 1)
    line = jnp.zeros((1, rank), jnp.int32)
    for s in range(slots):
        sub = subreddit[s, group]
        user = jnp.where(s < live, user_tile[s, group] + 1, 0)
        values = (user, word_tile[s, group], lax.div(sub, 128), lax.rem(sub, 128))
        for k, value in enumerate(values):
            line = jnp.where(lane == k * slots + s, value, line)
    return line.astype(f32)


def rhs_kernel(
    user_tile, word_tile, subreddit, counts, ratings_in, runs_in, words_in, subs_in, *refs,
    half, owners, own_rows,
):
    if half == 0:
        given_in, refs, given = refs[0], refs[1:-1], refs[-1]
    outs, (ratings, runs, words, subs, table, sums, arrived, loaded) = refs[:-8], refs[-8:]
    steps, slots, tile = ratings.shape[0], ratings.shape[1], ratings.shape[2]
    rank = words.shape[-1]
    levels = steps // 2

    place = lax.axis_index("loop")
    level, seat = lax.div(place, 4), lax.rem(place, 4)

    def group_at(step):
        there = lax.rem(seat + 2 * (step // levels), 4)
        if half:
            there = there + 1 - 2 * lax.rem(there, 2)
        return 4 * lax.rem(level + step % levels, levels) + there

    def load(step):
        group = group_at(step)
        return pltpu.make_async_copy(ratings_in.at[group], ratings.at[step], arrived.at[step])

    tables = [
        pltpu.make_async_copy(source, target, loaded.at[k])
        for k, (source, target) in enumerate(
            [(subs_in, subs), (runs_in, runs), (words_in, words)]
        )
    ]
    for copy in tables:
        copy.start()
    for step in range(steps):
        load(step).start()
    if half == 0:
        gift = pltpu.make_async_copy(given_in, given, loaded.at[3])
        gift.start()
    tables[0].wait()
    table[...] = subs[...].astype(f32)
    tables[1].wait()
    tables[2].wait()

    if half == 0:
        gift.wait()
    eye = (
        lax.broadcasted_iota(jnp.int32, (tile, tile), 0)
        == lax.broadcasted_iota(jnp.int32, (tile, tile), 1)
    ).astype(f32).astype(bf16)
    me = lax.axis_index("own")
    for step in range(steps):
        group = group_at(step)
        live = counts[0, group]
        columns = []
        for s in range(slots):
            pair = runs[group, s]
            columns.append(
                mask_columns(pair[0:1], jnp.where(s < live, pair[1:2], 0), tile)
            )
        seen = dot_nt(eye, jnp.concatenate(columns, axis=0)).astype(bf16)
        load(step).wait()
        sums[step % 2] = jnp.zeros(sums.shape[1:], f32)
        for s in range(slots):
            sub_row = table[pl.ds(subreddit[s, group], 1), :]
            product = (words[word_tile[s, group]].astype(f32) * sub_row).astype(bf16)
            weights = seen[:, s * tile : (s + 1) * tile] * ratings[step, s]
            rows = pl.ds(pl.multiple_of(user_tile[s, group] * tile, tile), tile)
            sums[step % 2, rows, :] += dot_nn(weights, product)
        line = fact_line(user_tile, word_tile, subreddit, live, group, slots, rank)
        spans = jnp.concatenate([runs[group, s] for s in range(slots)], axis=0).astype(f32)
        end = own_rows + 2 * slots
        for o in range(owners):
            owner = lax.rem(me + o, owners)
            rows = pl.ds(pl.multiple_of(owner * own_rows, own_rows), own_rows)
            value = sums[step % 2, rows, :]
            column, up = step // levels, step % levels
            if half == 0:
                other = given[o, column, up].astype(f32)
                value = jnp.concatenate(
                    [
                        value + other[:own_rows],
                        spans,
                        other[own_rows:end],
                        line,
                        other[end : end + 1],
                        jnp.zeros((FACT_ROWS - 2, rank), f32),
                    ],
                    axis=0,
                )
                outs[2 * o + column][up] = value.astype(bf16)
            else:
                value = jnp.concatenate(
                    [value, spans, line, jnp.zeros((FACT_ROWS - 1, rank), f32)], axis=0
                )
                outs[0][o, column, up] = value.astype(bf16)


def rhs_sums(scalars, ratings, runs, words, subs, half, given, owners, own_rows):
    groups, slots, tile, _ = ratings.shape
    rank = words.shape[-1]
    steps, levels = groups // 2, groups // 4
    anywhere = pl.BlockSpec(memory_space=pl.ANY)
    whole = pl.BlockSpec(memory_space=pltpu.VMEM)
    part = (levels, own_rows + 2 * slots * (2 - half) + FACT_ROWS, rank)
    shapes = [part] * (2 * owners) if half == 0 else [(owners, 2) + part]
    return pl.pallas_call(
        functools.partial(rhs_kernel, half=half, owners=owners, own_rows=own_rows),
        in_specs=[pl.BlockSpec(memory_space=pltpu.SMEM)] * 4
        + [anywhere] * (5 - half),
        out_specs=[whole] * len(shapes),
        out_shape=[jax.ShapeDtypeStruct(shape, bf16) for shape in shapes],
        scratch_shapes=[
            pltpu.VMEM((steps,) + ratings.shape[1:], bf16),
            pltpu.VMEM(runs.shape, jnp.int32),
            pltpu.VMEM(words.shape, bf16),
            pltpu.VMEM(subs.shape, bf16),
            pltpu.VMEM(subs.shape, f32),
            pltpu.VMEM((2, owners * own_rows, rank), f32),
            pltpu.SemaphoreType.DMA((steps,)),
            pltpu.SemaphoreType.DMA((4,)),
        ]
        + ([pltpu.VMEM(given.shape, bf16)] if half == 0 else []),
        compiler_params=pltpu.CompilerParams(vmem_limit_bytes=VMEM_LIMIT),
        cost_estimate=pl.CostEstimate(
            flops=8 * ratings.size * rank, bytes_accessed=8 * ratings.size, transcendentals=0
        ),
        name="rhs",
    )(*scalars, ratings, runs, words, subs, *([given] if half == 0 else []))


def chip_kernel(*refs, own_rows, spans):
    levels, _, rank = refs[0].shape
    parts, outs = refs[:-levels], refs[-levels:]
    lines = outs[0].shape[0] - own_rows - spans * len(parts)
    for up in range(levels):
        total = parts[0][up, :own_rows, :].astype(f32)
        for part in parts[1:]:
            total = total + part[up, :own_rows, :].astype(f32)
        outs[up][:own_rows, :] = total.astype(bf16)
        facts = []
        for k, part in enumerate(parts):
            at = own_rows + spans * k
            outs[up][at : at + spans, :] = part[up, own_rows : own_rows + spans, :]
            facts.append(part[up, own_rows + spans :, :].astype(f32)[:2])
        facts.append(jnp.zeros((lines - 2 * len(parts), rank), f32))
        outs[up][own_rows + spans * len(parts) :, :] = jnp.concatenate(
            facts[: len(facts) - (lines == 2 * len(parts))], axis=0
        ).astype(bf16)


def reduce_chip(parts, shards, owners, own_rows):
    given = []
    for o in range(owners):
        for column in range(2):
            pairs = [
                (shard * owners + k, (shard ^ 2 * column) * owners + (k + o) % owners)
                for shard in range(shards)
                for k in range(owners)
            ]
            part = parts[2 * o + column]
            given.append(lax.ppermute(part, AXES, pairs) if o or column else part)
    levels, rows, rank = parts[0].shape
    spans = rows - own_rows - FACT_ROWS
    lines = -(-2 * len(parts) // FACT_ROWS) * FACT_ROWS
    whole = pl.BlockSpec(memory_space=pltpu.VMEM)
    shape = jax.ShapeDtypeStruct((own_rows + spans * len(parts) + lines, rank), bf16)
    return pl.pallas_call(
        functools.partial(chip_kernel, own_rows=own_rows, spans=spans),
        in_specs=[whole] * len(parts),
        out_specs=[whole] * levels,
        out_shape=[shape] * levels,
        compiler_params=pltpu.CompilerParams(vmem_limit_bytes=VMEM_LIMIT),
        name="chip",
    )(*given)


def reduce_levels(total, shards):
    levels = shards // 4
    terms = [total[0]]
    for up in range(1, levels):
        shift = [(shard, (shard + 4 * up) % shards) for shard in range(shards)]
        terms.append(lax.ppermute(total[up], "loop", shift))
    return terms


def steps_kernel(start, activity, subs_in, *refs, shards, levels, slots, cached):
    own_rows, rank = start.shape
    pieces, refs = refs[:shards], refs[shards:]
    terms, refs = refs[:levels], refs[levels:]
    first_out, second_out, third_out, dots_out = refs[:4]
    masks, words, subs, table, runs, lines, facts, chosen, places, arrived, moved = refs[4:15]
    products = refs[-1]
    word_tiles, tile, _ = pieces[0].shape
    sources = lines.shape[0] // levels
    spans = 2 * slots * sources

    copies = [
        pltpu.make_async_copy(
            piece, words.at[k * word_tiles : (k + 1) * word_tiles], arrived.at[k]
        )
        for k, piece in enumerate(pieces)
    ]
    look = pltpu.make_async_copy(subs_in, subs, moved.at[1])
    look.start()
    for copy in copies:
        copy.start()

    for up, term in enumerate(terms):
        rest = term[own_rows + spans :, :].astype(f32)
        lines[up * sources : (up + 1) * sources, :] = rest[:sources].astype(jnp.int32)
    move = pltpu.make_async_copy(lines, facts, moved.at[0])
    move.start()
    rhs = jnp.zeros((own_rows, rank), f32)
    for up, term in enumerate(terms):
        rhs = rhs + term[:own_rows, :].astype(f32)
        runs[up * spans : (up + 1) * spans, :] = term[own_rows : own_rows + spans, :].astype(f32)
    look.wait()
    table[...] = subs[...].astype(f32)
    move.wait()

    place = lax.axis_index("loop")
    level, seat = lax.div(place, 4), lax.rem(place, 4)
    wanted = lax.div(lax.axis_index("own") * own_rows, tile) + 1
    chips = shards // 2

    def ring_at(level, column):
        return jnp.where(column == 0, level, chips - 1 - level)

    used = 0
    column = lax.div(seat, 2)
    for up in range(levels):
        there = lax.rem(level - up + levels, levels)
        ahead = [
            lax.rem(ring_at(there, side) - ring_at(level, column) + chips, chips)
            for side in (column, 1 - column)
        ]

        def choose(k, n, up=up, ahead=ahead):
            src = up * sources + k
            side = lax.rem(lax.div(k, 2), 2)
            distance = jnp.where(side == 0, ahead[0], ahead[1])
            piece = 2 * distance + lax.rem(k, 2)
            for s in range(slots):
                chosen[n] = src * slots + s
                places[0, n] = word_tiles * piece + facts[src, slots + s]
                places[1, n] = 128 * facts[src, 2 * slots + s] + facts[src, 3 * slots + s]
                n = n + jnp.where(facts[src, s] == wanted, 1, 0)
            return n

        used = lax.fori_loop(0, sources, choose, used)
    chunks = lax.div(used + CHUNK - 1, CHUNK)

    offset = lax.rem(lax.axis_index("own") * own_rows, tile)
    pick = (
        lax.broadcasted_iota(jnp.int32, (own_rows, tile), 0) + offset
        == lax.broadcasted_iota(jnp.int32, (own_rows, tile), 1)
    ).astype(f32).astype(bf16)

    def mask(chunk):
        parts = []
        for b in range(CHUNK):
            i = chunk * CHUNK + b
            j = chosen[jnp.minimum(i, used - 1)]
            first = runs[pl.ds(2 * j, 1), :].astype(jnp.int32)
            length = runs[pl.ds(2 * j + 1, 1), :].astype(jnp.int32)
            length = jnp.where(i < used, length, 0)
            parts.append(mask_columns(first, length, tile))
        return dot_nt(pick, jnp.concatenate(parts, axis=0)).astype(bf16)

    def product(i):
        i = jnp.minimum(i, used - 1)
        return (words[places[0, i]].astype(f32) * table[pl.ds(places[1, i], 1), :]).astype(bf16)

    for copy in copies:
        copy.wait()

    def gram(vector, build=False):
        rounded = vector.astype(bf16)

        def body(chunk, total):
            if build:
                masks[chunk] = mask(chunk)
            if cached and not build:
                block = products[chunk]
            else:
                block = jnp.concatenate(
                    [product(chunk * CHUNK + b) for b in range(CHUNK)], axis=0
                )
                if cached:
                    products[chunk] = block
            weights = dot_nt(rounded, block).astype(bf16) * masks[chunk]
            return total + dot_nn(weights, block)

        return lax.fori_loop(0, chunks, body, jnp.zeros((own_rows, rank), f32))

    def over_row(a, b):
        return jnp.sum(a * b, axis=1, keepdims=True)

    scale = jnp.broadcast_to(activity[...], (rank, own_rows)).T
    first = scale * (rhs - gram(start[...], build=True)) - ridge * start[...]
    second = scale * gram(first) + ridge * first
    norms, overlaps = over_row(first, first), over_row(first, second)
    share = jnp.where(norms > 0.0, overlaps / jnp.where(norms > 0.0, norms, 1.0), 0.0)
    rest = second - share * first
    third = scale * gram(rest) + ridge * rest + share * second
    first_out[...] = first
    second_out[...] = second
    third_out[...] = third
    rows = [norms, overlaps, over_row(second, second), over_row(first, third), over_row(second, third)]
    lane = lax.broadcasted_iota(jnp.int32, (1, rank), 1)
    line = jnp.zeros((1, rank), f32)
    for k, value in enumerate(rows):
        line = line + jnp.where(lane == k, jnp.sum(value, axis=0, keepdims=True), 0.0)
    dots_out[...] = jnp.broadcast_to(line[None], dots_out.shape)


def krylov(start, activity, subs, pieces, terms, slots, devices):
    own_rows, rank = start.shape
    blocks = devices * slots
    word_tiles, tile, _ = pieces[0].shape
    chunks = -(-blocks // CHUNK)
    cached = blocks * tile * rank * 2 <= 16 * 2**20
    whole = pl.BlockSpec(memory_space=pltpu.VMEM)
    anywhere = pl.BlockSpec(memory_space=pl.ANY)
    vector = jax.ShapeDtypeStruct((own_rows, rank), f32)
    scratch = [
        pltpu.VMEM((chunks, own_rows, CHUNK * tile), bf16),
        pltpu.VMEM((len(pieces) * word_tiles, tile, rank), bf16),
        pltpu.VMEM(subs.shape, bf16),
        pltpu.VMEM(subs.shape, f32),
        pltpu.VMEM((2 * blocks, tile), f32),
        pltpu.VMEM((devices, rank), jnp.int32),
        pltpu.SMEM((devices, rank), jnp.int32),
        pltpu.SMEM((blocks,), jnp.int32),
        pltpu.SMEM((2, blocks), jnp.int32),
        pltpu.SemaphoreType.DMA((len(pieces),)),
        pltpu.SemaphoreType.DMA((2,)),
    ]
    if cached:
        scratch.append(pltpu.VMEM((chunks, CHUNK * tile, rank), bf16))
    return pl.pallas_call(
        functools.partial(
            steps_kernel, shards=len(pieces), levels=len(terms), slots=slots, cached=cached
        ),
        in_specs=[whole, whole, anywhere] + [anywhere] * len(pieces) + [whole] * len(terms),
        out_specs=[whole] * 4,
        out_shape=[vector, vector, vector, jax.ShapeDtypeStruct((devices, 1, rank), f32)],
        scratch_shapes=scratch,
        compiler_params=pltpu.CompilerParams(vmem_limit_bytes=VMEM_LIMIT),
        name="krylov",
    )(start, activity, subs, *pieces, *terms)


def last_kernel(dots, start, first, second, third, solution_out, residual_out):
    line = dots[0]
    for k in range(1, dots.shape[0]):
        line = line + dots[k]
    rr, rq, qq, rz, qz = (line[:, k : k + 1] for k in range(5))
    step0 = rr / rq
    next_rr = rr - 2.0 * step0 * rq + step0 * step0 * qq
    grow = 1.0 + next_rr / rr
    slope = grow * (grow * rq - step0 * (rz + qq)) + step0 * step0 * qz
    step1 = next_rr / slope
    near, far = step0 + step1 * grow, step1 * step0
    solution_out[...] = start[...] + near * first[...] - far * second[...]
    residual_out[...] = first[...] - near * second[...] + far * third[...]


def last_step(dots, start, first, second, third):
    whole = pl.BlockSpec(memory_space=pltpu.VMEM)
    vector = jax.ShapeDtypeStruct(start.shape, f32)
    return pl.pallas_call(
        last_kernel,
        in_specs=[whole] * 5,
        out_specs=[whole] * 2,
        out_shape=[vector, vector],
        compiler_params=pltpu.CompilerParams(vmem_limit_bytes=VMEM_LIMIT),
        name="last_step",
    )(dots, start, first, second, third)


def ring_round(up, down, held, step, shards):
    chips = shards // 2
    levels = chips // 2
    order = [2 * level for level in range(levels)] + [
        2 * level + 1 for level in reversed(range(levels))
    ]

    def shift(by):
        return [
            (2 * order[p] + core, 2 * order[(p + by) % chips] + core)
            for p in range(chips)
            for core in range(2)
        ]

    up = lax.ppermute(up, "loop", shift(1))
    held[chips - step] = up
    if step < chips - step:
        down = lax.ppermute(down, "loop", shift(-1))
        held[step] = down
    return up, down


def other_core(value, shards):
    return lax.ppermute(value, "loop", [(shard, shard ^ 1) for shard in range(shards)])


def on_device(
    factor_start,
    activity,
    word_factors,
    sub_factors,
    ratings,
    user_tile,
    word_tile,
    subreddit,
    counts,
    runs,
):
    own_rows, rank = factor_start.shape
    owners, shards = lax.axis_size("own"), lax.axis_size("loop")
    slots = ratings.shape[3]
    devices = shards * owners
    chips = shards // 2
    together = lax.optimization_barrier

    scalars = (user_tile[0, 0].T, word_tile[0, 0].T, subreddit[0, 0].T, counts[0])
    mine = word_factors[0]
    held = {0: mine}

    inputs = (scalars, ratings[0, 0], runs[0, 0], mine, sub_factors)
    up, down = ring_round(mine, mine, held, 1, shards)
    (away,) = rhs_sums(*inputs, 1, None, owners, own_rows)
    up, down, away = together((up, down, away))

    up, down = ring_round(up, down, held, 2, shards)
    parts = rhs_sums(*inputs, 0, other_core(away, shards), owners, own_rows)
    up, down, parts = together((up, down, parts))

    up, down = ring_round(up, down, held, 3, shards)
    total = reduce_chip(parts, shards, owners, own_rows)
    up, down, total = together((up, down, total))

    for step in range(4, chips // 2 + 1):
        up, down = ring_round(up, down, held, step, shards)
    terms = reduce_levels(total, shards)
    pieces = []
    for distance in range(chips):
        pieces += [held[distance], other_core(held[distance], shards)]
    first, second, third, dots = krylov(
        factor_start, activity[None], sub_factors, pieces, terms, slots, devices
    )
    everyone = lax.all_to_all(dots, AXES, 0, 0, tiled=True)
    return tuple(last_step(everyone, factor_start, first, second, third))


def solution(mesh):
    placed = (
        P(("loop", "own"), None),
        P(("loop", "own")),
        P("loop", None, None, None),
        P(),
        P("loop", "own", None, None, None, None),
        P("loop", "own", None, None),
        P("loop", "own", None, None),
        P("loop", "own", None, None),
        P("loop", "own", None),
        P("loop", "own", None, None, None, None),
    )
    return jax.shard_map(
        on_device,
        mesh=mesh,
        in_specs=placed,
        out_specs=(P(("loop", "own"), None), P(("loop", "own"), None)),
        check_vma=False,
    )
```

time: 91.3 us -> 92.3 us (1.011)
  waiting for transfers between devices: 15.7 us -> 27.7 us
  starting transfers between devices: 23.3 us -> 16.2 us
  Pallas kernels: 36 us -> 32 us
  blocking collectives: 11.9 us -> 13.5 us
  other arithmetic: 0.98 us -> 0 us
    pallas_call x2 -> x1, Pallas kernels: 9.12 us -> 1.92 us  [reduce_chip(): pl.pallas_call(functools.partial(chip_kernel, own_rows=own_rows, spans=sp...]
    ppermute x4, waiting for transfers between devices: 0.15 us -> 6.96 us  [ring_round(): up = lax.ppermute(up, 'loop', shift(1))]
    all_to_all x1 -> x0, starting transfers between devices: 6.23 us -> none  [on_device(): received = lax.all_to_all(message, AXES, 0, 0, tiled=True)]
    ppermute x3, waiting for transfers between devices: 6.95 us -> 11.7 us  [reduce_chip(): given.append(lax.ppermute(part, AXES, pairs) if o or column else part)]
    ppermute x3, waiting for transfers between devices: 4.51 us -> 7.72 us  [reduce_levels(): terms.append(lax.ppermute(total[up], 'loop', shift))]
    pallas_call x1, Pallas kernels: 11.2 us -> 14.2 us  [krylov(): pl.pallas_call(functools.partial(steps_kernel, shards=len(pieces), levels...]
    all_to_all x1 -> x0, waiting for transfers between devices: 2.21 us -> none  [on_device(): received = lax.all_to_all(message, AXES, 0, 0, tiled=True)]
    ppermute x3, starting transfers between devices: 2.08 us -> 3.93 us  [reduce_levels(): terms.append(lax.ppermute(total[up], 'loop', shift))]
  transfers between devices with their start and end apart: 23 -> 22, of which waited for: 8 -> 8; matrix products, arithmetic and copies ran while one was open for 2% -> 0% of each run, Pallas kernels for 25% -> 17%
where the time goes in v7:
time: 92.3 us; the launch traced here: 92.7 us
  Pallas kernels  32 us (35%)
  waiting for transfers between devices  27.7 us (30%)
  starting transfers between devices  16.2 us (18%)
  blocking collectives  13.5 us (15%)
  local copies, waits for them, and re-layouts  2.3 us (2%)
  between operations  0.97 us (1%)
    pallas_call x1, Pallas kernels, krylov(): pl.pallas_call(functools.partial(steps_kernel, shards=len(pieces), levels...  14.2 us
    pallas_call x2, Pallas kernels, rhs_sums(): pl.pallas_call(functools.partial(rhs_kernel, half=half, owners=owners, ow...  13.9 us
    all_to_all x1, blocking collectives, on_device(): everyone = lax.all_to_all(dots, AXES, 0, 0, tiled=True)  13.5 us
    ppermute x3, waiting for transfers between devices, reduce_chip(): given.append(lax.ppermute(part, AXES, pairs) if o or column else part)  11.7 us
    ppermute x3, waiting for transfers between devices, reduce_levels(): terms.append(lax.ppermute(total[up], 'loop', shift))  7.72 us
    ppermute x4, waiting for transfers between devices, ring_round(): up = lax.ppermute(up, 'loop', shift(1))  6.96 us
    ppermute x4, starting transfers between devices, ring_round(): up = lax.ppermute(up, 'loop', shift(1))  5.22 us
    ppermute x3, starting transfers between devices, reduce_levels(): terms.append(lax.ppermute(total[up], 'loop', shift))  3.93 us
  transfers between devices with their start and end apart: 22, of which 8 were waited for; matrix products, arithmetic and copies ran while one was open for 0% of the time, Pallas kernels for 17%

profile of v7, /device:TPU:0, one launch (start us, length us, event | category | flops | bytes accessed | tf_op | source)
XLA Modules:
  0.0 92.7 jit_solution(3397161499064702644)
XLA Ops:
  0.6 3.1 %collective-permute-start.3 = (bf16[8,128,128]{2,1,0:T(8,128)(2,1)}, bf16[8,128,128]{2,1,0:T(8,128)(2,1)S(1)}, u32[]{:S(2)}, u32[]{:S(2)}) collective-permute-start(bf16[8,128,128]{2,1,0:T(8,128)(2,1)} %bitcast.14), channel_id=1, source_target_pairs={{0,8},{2,10},{8,16},{10,18},{16,24},{18,26},{24,28},{26,30},{28,20... | collective-permute-start | bytes 786440 | tf_op jit(solution)/shard_map/ppermute | solution.py:439
  3.7 0.0 collective-permute-start.1
  3.7 6.9 %rhs.2 = bf16[2,2,4,160,128]{4,3,2,1,0:T(8,128)(2,1)} custom-call(s32[8,16]{1,0:T(8,128)} %bitcast.25, s32[8,16]{1,0:T(8,128)} %bitcast.27, s32[8,16]{1,0:T(8,128)} %bitcast.29, s32[1,16]{1,0:T(1,128)} %bitcast.31, bf16[16,8,128,128]{3,2,1,0:T(8,128)(2,1)} %bitcast.21, s32[16,8,2,128]{3,2,1,0:T(2,128)} %bitcast.23, bf16[8,128,128]{2,1,0:T(8,128)(2,1)} %bitcast.16, ...), custom_call_target="tpu_custom_call" | custom-call | flops 2147483648 | bytes 16777216 | tf_op jit(solution)/shard_map/rhs/pallas_call | solution.py:149
  10.6 0.0 copy-start
  10.6 0.0 collective-permute-done.3.refs_14_
  10.6 1.1 %collective-permute-done.1.refs_2_ = bf16[8,128,128]{2,1,0:T(8,128)(2,1)S(1)} collective-permute-done((bf16[8,128,128]{2,1,0:T(8,128)(2,1)}, bf16[8,128,128]{2,1,0:T(8,128)(2,1)S(1)}, u32[]{:S(2)}, u32[]{:S(2)}) %collective-permute-start.1) | collective-permute-done | bytes 262176 | tf_op jit(solution)/shard_map/ppermute | solution.py:442
  11.7 0.0 collective-permute-start.7
  11.7 1.0 %collective-permute-start.4 = (bf16[8,128,128]{2,1,0:T(8,128)(2,1)S(1)}, bf16[8,128,128]{2,1,0:T(8,128)(2,1)S(1)}, u32[]{:S(2)}, u32[]{:S(2)}) collective-permute-start(bf16[8,128,128]{2,1,0:T(8,128)(2,1)S(1)} %collective-permute-done.1.refs_2_), channel_id=1, source_target_pairs={{0,4},{2,6},{8,0},{10,2},{16,8},{18,10},{24,16},{26,18},{28,24},{3... | collective-permute-start | bytes 786440 | tf_op jit(solution)/shard_map/ppermute | solution.py:442
  12.7 1.0 %collective-permute-start.6 = (bf16[8,128,128]{2,1,0:T(8,128)(2,1)S(1)}, bf16[8,128,128]{2,1,0:T(8,128)(2,1)S(1)}, u32[]{:S(2)}, u32[]{:S(2)}) collective-permute-start(bf16[8,128,128]{2,1,0:T(8,128)(2,1)S(1)} %collective-permute-done.3.refs_14_), channel_id=1, source_target_pairs={{0,8},{2,10},{8,16},{10,18},{16,24},{18,26},{24,28},{26,30},{28,20... | collective-permute-start | bytes 786440 | tf_op jit(solution)/shard_map/ppermute | solution.py:439
  13.7 0.3 collective-permute-done.7.refs_0_
  14.0 0.8 copy-done.22
  14.8 7.1 %rhs.3 = (bf16[4,176,128]{2,1,0:T(8,128)(2,1)}, bf16[4,176,128]{2,1,0:T(8,128)(2,1)}, bf16[4,176,128]{2,1,0:T(8,128)(2,1)}, bf16[4,176,128]{2,1,0:T(8,128)(2,1)}) custom-call(s32[8,16]{1,0:T(8,128)} %bitcast.26, s32[8,16]{1,0:T(8,128)} %bitcast.28, s32[8,16]{1,0:T(8,128)} %bitcast.30, s32[1,16]{1,0:T(1,128)} %bitcast.32, bf16[16,8,128,128]{3,2,1,0:T(8,128)(2,1)} %bitcast.22, ...), custom_call_target="tpu_custom_call" | custom-call | flops 2147483648 | bytes 16777216 | tf_op jit(solution)/shard_map/rhs/pallas_call | solution.py:149
  21.9 0.0 collective-permute-done.4.refs_4_
  21.9 0.0 collective-permute-done.6.refs_12_
  22.0 1.0 %collective-permute-start.8 = (bf16[8,128,128]{2,1,0:T(8,128)(2,1)S(1)}, bf16[8,128,128]{2,1,0:T(8,128)(2,1)S(1)}, u32[]{:S(2)}, u32[]{:S(2)}) collective-permute-start(bf16[8,128,128]{2,1,0:T(8,128)(2,1)S(1)} %collective-permute-done.4.refs_4_), channel_id=1, source_target_pairs={{0,4},{2,6},{8,0},{10,2},{16,8},{18,10},{24,16},{26,18},{28,24},{3... | collective-permute-start | bytes 786440 | tf_op jit(solution)/shard_map/ppermute | solution.py:442
  23.0 1.1 %collective-permute-start.10 = (bf16[8,128,128]{2,1,0:T(8,128)(2,1)S(1)}, bf16[8,128,128]{2,1,0:T(8,128)(2,1)S(1)}, u32[]{:S(2)}, u32[]{:S(2)}) collective-permute-start(bf16[8,128,128]{2,1,0:T(8,128)(2,1)S(1)} %collective-permute-done.6.refs_12_), channel_id=1, source_target_pairs={{0,8},{2,10},{8,16},{10,18},{16,24},{18,26},{24,28},{26,30},{28,20... | collective-permute-start | bytes 786440 | tf_op jit(solution)/shard_map/ppermute | solution.py:439
  24.0 1.0 %collective-permute-start.11 = (bf16[4,176,128]{2,1,0:T(8,128)(2,1)}, bf16[4,176,128]{2,1,0:T(8,128)(2,1)S(1)}, u32[]{:S(2)}, u32[]{:S(2)}) collective-permute-start(bf16[4,176,128]{2,1,0:T(8,128)(2,1)} %get-tuple-element.38), channel_id=1, source_target_pairs={{0,4},{1,5},{2,6},{3,7},{4,0},{5,1},{6,2},{7,3},{8,12},{9,13},{10,... | collective-permute-start | bytes 540680 | tf_op jit(solution)/shard_map/ppermute | solution.py:204
  25.0 1.5 %collective-permute-start.12 = (bf16[4,176,128]{2,1,0:T(8,128)(2,1)}, bf16[4,176,128]{2,1,0:T(8,128)(2,1)S(1)}, u32[]{:S(2)}, u32[]{:S(2)}) collective-permute-start(bf16[4,176,128]{2,1,0:T(8,128)(2,1)} %get-tuple-element.39), channel_id=1, source_target_pairs={{0,1},{1,0},{2,3},{3,2},{4,5},{5,4},{6,7},{7,6},{8,9},{9,8},{10,11... | collective-permute-start | bytes 540680 | tf_op jit(solution)/shard_map/ppermute | solution.py:204
  26.5 1.0 %collective-permute-start.13 = (bf16[4,176,128]{2,1,0:T(8,128)(2,1)}, bf16[4,176,128]{2,1,0:T(8,128)(2,1)S(1)}, u32[]{:S(2)}, u32[]{:S(2)}) collective-permute-start(bf16[4,176,128]{2,1,0:T(8,128)(2,1)} %get-tuple-element.40), channel_id=1, source_target_pairs={{0,5},{1,4},{2,7},{3,6},{4,1},{5,0},{6,3},{7,2},{8,13},{9,12},{10,... | collective-permute-start | bytes 540680 | tf_op jit(solution)/shard_map/ppermute | solution.py:204
  27.5 8.5 %collective-permute-done.11.refs_1_ = bf16[4,176,128]{2,1,0:T(8,128)(2,1)S(1)} collective-permute-done((bf16[4,176,128]{2,1,0:T(8,128)(2,1)}, bf16[4,176,128]{2,1,0:T(8,128)(2,1)S(1)}, u32[]{:S(2)}, u32[]{:S(2)}) %collective-permute-start.11) | collective-permute-done | bytes 180256 | tf_op jit(solution)/shard_map/ppermute | solution.py:204
  36.0 0.0 collective-permute-done.12.refs_2_
  36.1 0.5 collective-permute-start.18
  36.5 3.2 %collective-permute-done.13.refs_3_ = bf16[4,176,128]{2,1,0:T(8,128)(2,1)S(1)} collective-permute-done((bf16[4,176,128]{2,1,0:T(8,128)(2,1)}, bf16[4,176,128]{2,1,0:T(8,128)(2,1)S(1)}, u32[]{:S(2)}, u32[]{:S(2)}) %collective-permute-start.13) | collective-permute-done | bytes 180256 | tf_op jit(solution)/shard_map/ppermute | solution.py:204
  39.7 0.0 collective-permute-start.2
  39.7 0.6 copy-done.18
  40.4 1.9 %chip.1 = (bf16[272,128]{1,0:T(8,128)(2,1)}, bf16[272,128]{1,0:T(8,128)(2,1)}, bf16[272,128]{1,0:T(8,128)(2,1)}, bf16[272,128]{1,0:T(8,128)(2,1)}) custom-call(bf16[4,176,128]{2,1,0:T(8,128)(2,1)} %get-tuple-element.37.refs_0_, bf16[4,176,128]{2,1,0:T(8,128)(2,1)} %copy-done.16, bf16[4,176,128]{2,1,0:T(8,128)(2,1)} %copy-done.17, bf16[4,176,128]{2,1,0:T(8,128)(2,1)} %copy-done.18), custom_call_target="tpu_custom_call" | custom-call | tf_op jit(solution)/shard_map/chip/pallas_call | solution.py:210
  42.3 0.0 collective-permute-done.10.refs_10_
  42.4 0.1 collective-permute-start.14
  42.4 0.1 collective-permute-start.5
  42.5 0.0 collective-permute-done.refs_1_
  42.5 0.5 collective-permute-start.17
  43.0 0.0 collective-permute-done.18.refs_15_
  43.0 0.1 collective-permute-start.9
  43.1 0.4 collective-permute-start.16
  43.5 7.0 %collective-permute-done.14.refs_8_ = bf16[8,128,128]{2,1,0:T(8,128)(2,1)S(1)} collective-permute-done((bf16[8,128,128]{2,1,0:T(8,128)(2,1)S(1)}, bf16[8,128,128]{2,1,0:T(8,128)(2,1)S(1)}, u32[]{:S(2)}, u32[]{:S(2)}) %collective-permute-start.14) | collective-permute-done | bytes 262176 | tf_op jit(solution)/shard_map/ppermute | solution.py:439
  50.5 0.3 collective-permute-start.19
  50.8 3.1 %collective-permute-start.20 = (bf16[272,128]{1,0:T(8,128)(2,1)}, bf16[272,128]{1,0:T(8,128)(2,1)S(1)}, u32[]{:S(2)}, u32[]{:S(2)}) collective-permute-start(bf16[272,128]{1,0:T(8,128)(2,1)} %get-tuple-element.48), channel_id=1, source_target_pairs={{0,16},{2,18},{4,20},{6,22},{8,24},{10,26},{12,28},{14,30},{16,0},... | collective-permute-start | bytes 208904 | tf_op jit(solution)/shard_map/ppermute | solution.py:225
  54.0 3.7 %collective-permute-done.19.refs_17_ = bf16[272,128]{1,0:T(8,128)(2,1)S(1)} collective-permute-done((bf16[272,128]{1,0:T(8,128)(2,1)}, bf16[272,128]{1,0:T(8,128)(2,1)S(1)}, u32[]{:S(2)}, u32[]{:S(2)}) %collective-permute-start.19) | collective-permute-done | bytes 69664 | tf_op jit(solution)/shard_map/ppermute | solution.py:225
  57.6 0.5 collective-permute-start.21
  58.1 2.0 %collective-permute-done.20.refs_18_ = bf16[272,128]{1,0:T(8,128)(2,1)S(1)} collective-permute-done((bf16[272,128]{1,0:T(8,128)(2,1)}, bf16[272,128]{1,0:T(8,128)(2,1)S(1)}, u32[]{:S(2)}, u32[]{:S(2)}) %collective-permute-start.20) | collective-permute-done | bytes 69664 | tf_op jit(solution)/shard_map/ppermute | solution.py:225
  60.1 2.1 %collective-permute-done.21.refs_19_ = bf16[272,128]{1,0:T(8,128)(2,1)S(1)} collective-permute-done((bf16[272,128]{1,0:T(8,128)(2,1)}, bf16[272,128]{1,0:T(8,128)(2,1)S(1)}, u32[]{:S(2)}, u32[]{:S(2)}) %collective-permute-start.21) | collective-permute-done | bytes 69664 | tf_op jit(solution)/shard_map/ppermute | solution.py:225
  62.3 0.5 copy-done.21
  62.8 0.1 copy-done.13
  62.9 0.1 copy-done.14
  63.0 0.1 copy-done.15
  63.1 14.2 %krylov.1 = (f32[128,128]{1,0:T(8,128)}, f32[128,128]{1,0:T(8,128)}, f32[128,128]{1,0:T(8,128)}, f32[32,1,128]{2,1,0:T(1,128)}) custom-call(f32[128,128]{1,0:T(8,128)} %start.3, f32[1,128]{1,0:T(1,128)} %bitcast.20, bf16[2048,128]{1,0:T(8,128)(2,1)} %subs_in.5, bf16[8,128,128]{2,1,0:T(8,128)(2,1)} %bitcast.18, bf16[8,128,128]{2,1,0:T(8,128)(2,1)} %copy-done.7, ...), custom_call_target="tpu_custom_call" | custom-call | tf_op jit(solution)/shard_map/krylov/pallas_call | solution.py:384
  77.3 13.5 %all_to_all.5.dots = f32[32,1,128]{2,1,0:T(1,128)} all-to-all(f32[32,1,128]{2,1,0:T(1,128)} %get-tuple-element.50), channel_id=1, replica_groups=mesh['loop'=16,'own'=2] {'loop','own'}, dimensions={0} | all-to-all | bytes 32768 | tf_op jit(solution)/shard_map/all_to_all | solution.py:496
  90.8 1.9 %last_step.1 = (f32[128,128]{1,0:T(8,128)}, f32[128,128]{1,0:T(8,128)}) custom-call(f32[32,1,128]{2,1,0:T(1,128)} %all_to_all.5.dots, f32[128,128]{1,0:T(8,128)} %start.3, f32[128,128]{1,0:T(8,128)} %get-tuple-element.51.first, f32[128,128]{1,0:T(8,128)} %get-tuple-element.52.second, f32[128,128]{1,0:T(8,128)} %get-tuple-element.53.third), custom_call_target="tpu_custom_call" | custom-call | tf_op jit(solution)/shard_map/last_step/pallas_call | solution.py:415
  (48 shorter events, 0.1 us)
Async XLA Ops:
  0.6 10.0 %collective-permute-start.3 = (bf16[8,128,128]{2,1,0:T(8,128)(2,1)}, bf16[8,128,128]{2,1,0:T(8,128)(2,1)S(1)}, u32[]{:S(2)}, u32[]{:S(2)}) collective-permute-start(bf16[8,128,128]{2,1,0:T(8,128)(2,1)} %bitcast.14), channel_id=1, source_target_pairs={{0,8},{2,10},{8,16},{10,18},{16,24},{18,26},{24,28},{26,30},{28,20... | collective-permute-start | bytes 786440 | tf_op jit(solution)/shard_map/ppermute | solution.py:439
  3.7 8.0 %collective-permute-start.1 = (bf16[8,128,128]{2,1,0:T(8,128)(2,1)}, bf16[8,128,128]{2,1,0:T(8,128)(2,1)S(1)}, u32[]{:S(2)}, u32[]{:S(2)}) collective-permute-start(bf16[8,128,128]{2,1,0:T(8,128)(2,1)} %bitcast.15), channel_id=1, source_target_pairs={{0,4},{2,6},{8,0},{10,2},{16,8},{18,10},{24,16},{26,18},{28,24},{3... | collective-permute-start | bytes 786440 | tf_op jit(solution)/shard_map/ppermute | solution.py:442
  10.6 25.4 %copy-start = (bf16[1,8,128,128]{3,2,1,0:T(8,128)(2,1)S(1)}, bf16[1,8,128,128]{3,2,1,0:T(8,128)(2,1)}, u32[]{:S(2)}) copy-start(bf16[1,8,128,128]{3,2,1,0:T(8,128)(2,1)} %param.12) | copy-start | bytes 786436
  10.6 31.7 %copy-start.1 = (bf16[8,128,128]{2,1,0:T(8,128)(2,1)}, bf16[8,128,128]{2,1,0:T(8,128)(2,1)S(1)}, u32[]{:S(2)}) copy-start(bf16[8,128,128]{2,1,0:T(8,128)(2,1)S(1)} %collective-permute-done.3.refs_14_) | copy-start | bytes 786436
  11.7 30.6 %copy-start.2 = (bf16[8,128,128]{2,1,0:T(8,128)(2,1)}, bf16[8,128,128]{2,1,0:T(8,128)(2,1)S(1)}, u32[]{:S(2)}) copy-start(bf16[8,128,128]{2,1,0:T(8,128)(2,1)S(1)} %collective-permute-done.1.refs_2_) | copy-start | bytes 786436
  11.7 2.3 %collective-permute-start.7 = (bf16[2,2,4,160,128]{4,3,2,1,0:T(8,128)(2,1)}, bf16[2,2,4,160,128]{4,3,2,1,0:T(8,128)(2,1)S(1)}, u32[]{:S(2)}, u32[]{:S(2)}) collective-permute-start(bf16[2,2,4,160,128]{4,3,2,1,0:T(8,128)(2,1)} %rhs.2), channel_id=1, source_target_pairs={{0,2},{2,0},{4,6},{6,4},{8,10},{10,8},{12,14},{14,12},{16,18},{18,... | collective-permute-start | bytes 1966088 | tf_op jit(solution)/shard_map/ppermute | solution.py:448
  11.7 10.2 %collective-permute-start.4 = (bf16[8,128,128]{2,1,0:T(8,128)(2,1)S(1)}, bf16[8,128,128]{2,1,0:T(8,128)(2,1)S(1)}, u32[]{:S(2)}, u32[]{:S(2)}) collective-permute-start(bf16[8,128,128]{2,1,0:T(8,128)(2,1)S(1)} %collective-permute-done.1.refs_2_), channel_id=1, source_target_pairs={{0,4},{2,6},{8,0},{10,2},{16,8},{18,10},{24,16},{26,18},{28,24},{3... | collective-permute-start | bytes 786440 | tf_op jit(solution)/shard_map/ppermute | solution.py:442
  12.7 9.2 %collective-permute-start.6 = (bf16[8,128,128]{2,1,0:T(8,128)(2,1)S(1)}, bf16[8,128,128]{2,1,0:T(8,128)(2,1)S(1)}, u32[]{:S(2)}, u32[]{:S(2)}) collective-permute-start(bf16[8,128,128]{2,1,0:T(8,128)(2,1)S(1)} %collective-permute-done.3.refs_14_), channel_id=1, source_target_pairs={{0,8},{2,10},{8,16},{10,18},{16,24},{18,26},{24,28},{26,30},{28,20... | collective-permute-start | bytes 786440 | tf_op jit(solution)/shard_map/ppermute | solution.py:439
  14.0 0.8 copy-start.22
  21.9 40.3 %copy-start.3 = (bf16[8,128,128]{2,1,0:T(8,128)(2,1)}, bf16[8,128,128]{2,1,0:T(8,128)(2,1)S(1)}, u32[]{:S(2)}) copy-start(bf16[8,128,128]{2,1,0:T(8,128)(2,1)S(1)} %collective-permute-done.4.refs_4_) | copy-start | bytes 786436
  22.0 40.3 %copy-start.4 = (bf16[8,128,128]{2,1,0:T(8,128)(2,1)}, bf16[8,128,128]{2,1,0:T(8,128)(2,1)S(1)}, u32[]{:S(2)}) copy-start(bf16[8,128,128]{2,1,0:T(8,128)(2,1)S(1)} %collective-permute-done.6.refs_12_) | copy-start | bytes 786436
  22.0 20.3 %collective-permute-start.8 = (bf16[8,128,128]{2,1,0:T(8,128)(2,1)S(1)}, bf16[8,128,128]{2,1,0:T(8,128)(2,1)S(1)}, u32[]{:S(2)}, u32[]{:S(2)}) collective-permute-start(bf16[8,128,128]{2,1,0:T(8,128)(2,1)S(1)} %collective-permute-done.4.refs_4_), channel_id=1, source_target_pairs={{0,4},{2,6},{8,0},{10,2},{16,8},{18,10},{24,16},{26,18},{28,24},{3... | collective-permute-start | bytes 786440 | tf_op jit(solution)/shard_map/ppermute | solution.py:442
  23.0 19.4 %collective-permute-start.10 = (bf16[8,128,128]{2,1,0:T(8,128)(2,1)S(1)}, bf16[8,128,128]{2,1,0:T(8,128)(2,1)S(1)}, u32[]{:S(2)}, u32[]{:S(2)}) collective-permute-start(bf16[8,128,128]{2,1,0:T(8,128)(2,1)S(1)} %collective-permute-done.6.refs_12_), channel_id=1, source_target_pairs={{0,8},{2,10},{8,16},{10,18},{16,24},{18,26},{24,28},{26,30},{28,20... | collective-permute-start | bytes 786440 | tf_op jit(solution)/shard_map/ppermute | solution.py:439
  24.0 12.0 %collective-permute-start.11 = (bf16[4,176,128]{2,1,0:T(8,128)(2,1)}, bf16[4,176,128]{2,1,0:T(8,128)(2,1)S(1)}, u32[]{:S(2)}, u32[]{:S(2)}) collective-permute-start(bf16[4,176,128]{2,1,0:T(8,128)(2,1)} %get-tuple-element.38), channel_id=1, source_target_pairs={{0,4},{1,5},{2,6},{3,7},{4,0},{5,1},{6,2},{7,3},{8,12},{9,13},{10,... | collective-permute-start | bytes 540680 | tf_op jit(solution)/shard_map/ppermute | solution.py:204
  25.0 11.0 %collective-permute-start.12 = (bf16[4,176,128]{2,1,0:T(8,128)(2,1)}, bf16[4,176,128]{2,1,0:T(8,128)(2,1)S(1)}, u32[]{:S(2)}, u32[]{:S(2)}) collective-permute-start(bf16[4,176,128]{2,1,0:T(8,128)(2,1)} %get-tuple-element.39), channel_id=1, source_target_pairs={{0,1},{1,0},{2,3},{3,2},{4,5},{5,4},{6,7},{7,6},{8,9},{9,8},{10,11... | collective-permute-start | bytes 540680 | tf_op jit(solution)/shard_map/ppermute | solution.py:204
  26.5 13.2 %collective-permute-start.13 = (bf16[4,176,128]{2,1,0:T(8,128)(2,1)}, bf16[4,176,128]{2,1,0:T(8,128)(2,1)S(1)}, u32[]{:S(2)}, u32[]{:S(2)}) collective-permute-start(bf16[4,176,128]{2,1,0:T(8,128)(2,1)} %get-tuple-element.40), channel_id=1, source_target_pairs={{0,5},{1,4},{2,7},{3,6},{4,1},{5,0},{6,3},{7,2},{8,13},{9,12},{10,... | collective-permute-start | bytes 540680 | tf_op jit(solution)/shard_map/ppermute | solution.py:204
  36.0 3.7 %copy-start.16 = (bf16[4,176,128]{2,1,0:T(8,128)(2,1)}, bf16[4,176,128]{2,1,0:T(8,128)(2,1)S(1)}, u32[]{:S(2)}) copy-start(bf16[4,176,128]{2,1,0:T(8,128)(2,1)S(1)} %collective-permute-done.11.refs_1_) | copy-start | bytes 540676
  36.0 6.5 %collective-permute-start = (bf16[8,128,128]{2,1,0:T(8,128)(2,1)S(1)}, bf16[8,128,128]{2,1,0:T(8,128)(2,1)S(1)}, u32[]{:S(2)}, u32[]{:S(2)}) collective-permute-start(bf16[8,128,128]{2,1,0:T(8,128)(2,1)S(1)} %bitcast.19), channel_id=1, source_target_pairs={{0,2},{2,0},{4,6},{6,4},{8,10},{10,8},{12,14},{14,12},{16,18},{18,... | collective-permute-start | bytes 786440 | tf_op jit(solution)/shard_map/ppermute | solution.py:448
  36.0 3.7 %copy-start.17 = (bf16[4,176,128]{2,1,0:T(8,128)(2,1)}, bf16[4,176,128]{2,1,0:T(8,128)(2,1)S(1)}, u32[]{:S(2)}) copy-start(bf16[4,176,128]{2,1,0:T(8,128)(2,1)S(1)} %collective-permute-done.12.refs_2_) | copy-start | bytes 540676
  36.1 6.9 %collective-permute-start.18 = (bf16[8,128,128]{2,1,0:T(8,128)(2,1)S(1)}, bf16[8,128,128]{2,1,0:T(8,128)(2,1)S(1)}, u32[]{:S(2)}, u32[]{:S(2)}) collective-permute-start(bf16[8,128,128]{2,1,0:T(8,128)(2,1)S(1)} %collective-permute-done.3.refs_14_), channel_id=1, source_target_pairs={{0,2},{2,0},{4,6},{6,4},{8,10},{10,8},{12,14},{14,12},{16,18},{18,... | collective-permute-start | bytes 786440 | tf_op jit(solution)/shard_map/ppermute | solution.py:448
  39.7 0.7 copy-start.18
  39.7 3.4 %collective-permute-start.2 = (bf16[8,128,128]{2,1,0:T(8,128)(2,1)S(1)}, bf16[8,128,128]{2,1,0:T(8,128)(2,1)S(1)}, u32[]{:S(2)}, u32[]{:S(2)}) collective-permute-start(bf16[8,128,128]{2,1,0:T(8,128)(2,1)S(1)} %collective-permute-done.1.refs_2_), channel_id=1, source_target_pairs={{0,2},{2,0},{4,6},{6,4},{8,10},{10,8},{12,14},{14,12},{16,18},{18,... | collective-permute-start | bytes 786440 | tf_op jit(solution)/shard_map/ppermute | solution.py:448
  42.3 19.9 %copy-start.5 = (bf16[8,128,128]{2,1,0:T(8,128)(2,1)}, bf16[8,128,128]{2,1,0:T(8,128)(2,1)S(1)}, u32[]{:S(2)}) copy-start(bf16[8,128,128]{2,1,0:T(8,128)(2,1)S(1)} %collective-permute-done.8.refs_6_) | copy-start | bytes 786436
  42.3 19.9 %copy-start.6 = (bf16[8,128,128]{2,1,0:T(8,128)(2,1)}, bf16[8,128,128]{2,1,0:T(8,128)(2,1)S(1)}, u32[]{:S(2)}) copy-start(bf16[8,128,128]{2,1,0:T(8,128)(2,1)S(1)} %collective-permute-done.10.refs_10_) | copy-start | bytes 786436
  42.4 8.1 %collective-permute-start.14 = (bf16[8,128,128]{2,1,0:T(8,128)(2,1)S(1)}, bf16[8,128,128]{2,1,0:T(8,128)(2,1)S(1)}, u32[]{:S(2)}, u32[]{:S(2)}) collective-permute-start(bf16[8,128,128]{2,1,0:T(8,128)(2,1)S(1)} %collective-permute-done.10.refs_10_), channel_id=1, source_target_pairs={{0,8},{2,10},{8,16},{10,18},{16,24},{18,26},{24,28},{26,30},{28,20... | collective-permute-start | bytes 786440 | tf_op jit(solution)/shard_map/ppermute | solution.py:439
  42.4 8.1 %collective-permute-start.5 = (bf16[8,128,128]{2,1,0:T(8,128)(2,1)S(1)}, bf16[8,128,128]{2,1,0:T(8,128)(2,1)S(1)}, u32[]{:S(2)}, u32[]{:S(2)}) collective-permute-start(bf16[8,128,128]{2,1,0:T(8,128)(2,1)S(1)} %collective-permute-done.4.refs_4_), channel_id=1, source_target_pairs={{0,2},{2,0},{4,6},{6,4},{8,10},{10,8},{12,14},{14,12},{16,18},{18,... | collective-permute-start | bytes 786440 | tf_op jit(solution)/shard_map/ppermute | solution.py:448
  42.5 19.7 %copy-start.7 = (bf16[8,128,128]{2,1,0:T(8,128)(2,1)}, bf16[8,128,128]{2,1,0:T(8,128)(2,1)S(1)}, u32[]{:S(2)}) copy-start(bf16[8,128,128]{2,1,0:T(8,128)(2,1)S(1)} %collective-permute-done.refs_1_) | copy-start | bytes 786436
  42.5 8.3 %collective-permute-start.17 = (bf16[8,128,128]{2,1,0:T(8,128)(2,1)S(1)}, bf16[8,128,128]{2,1,0:T(8,128)(2,1)S(1)}, u32[]{:S(2)}, u32[]{:S(2)}) collective-permute-start(bf16[8,128,128]{2,1,0:T(8,128)(2,1)S(1)} %collective-permute-done.6.refs_12_), channel_id=1, source_target_pairs={{0,2},{2,0},{4,6},{6,4},{8,10},{10,8},{12,14},{14,12},{16,18},{18,... | collective-permute-start | bytes 786440 | tf_op jit(solution)/shard_map/ppermute | solution.py:448
  43.0 19.3 %copy-start.8 = (bf16[8,128,128]{2,1,0:T(8,128)(2,1)}, bf16[8,128,128]{2,1,0:T(8,128)(2,1)S(1)}, u32[]{:S(2)}) copy-start(bf16[8,128,128]{2,1,0:T(8,128)(2,1)S(1)} %collective-permute-done.18.refs_15_) | copy-start | bytes 786436
  43.0 19.2 %collective-permute-start.9 = (bf16[8,128,128]{2,1,0:T(8,128)(2,1)S(1)}, bf16[8,128,128]{2,1,0:T(8,128)(2,1)S(1)}, u32[]{:S(2)}, u32[]{:S(2)}) collective-permute-start(bf16[8,128,128]{2,1,0:T(8,128)(2,1)S(1)} %collective-permute-done.8.refs_6_), channel_id=1, source_target_pairs={{0,2},{2,0},{4,6},{6,4},{8,10},{10,8},{12,14},{14,12},{16,18},{18,... | collective-permute-start | bytes 786440 | tf_op jit(solution)/shard_map/ppermute | solution.py:448
  43.1 19.2 %copy-start.9 = (bf16[8,128,128]{2,1,0:T(8,128)(2,1)}, bf16[8,128,128]{2,1,0:T(8,128)(2,1)S(1)}, u32[]{:S(2)}) copy-start(bf16[8,128,128]{2,1,0:T(8,128)(2,1)S(1)} %collective-permute-done.2.refs_3_) | copy-start | bytes 786436
  43.1 19.1 %collective-permute-start.16 = (bf16[8,128,128]{2,1,0:T(8,128)(2,1)S(1)}, bf16[8,128,128]{2,1,0:T(8,128)(2,1)S(1)}, u32[]{:S(2)}, u32[]{:S(2)}) collective-permute-start(bf16[8,128,128]{2,1,0:T(8,128)(2,1)S(1)} %collective-permute-done.10.refs_10_), channel_id=1, source_target_pairs={{0,2},{2,0},{4,6},{6,4},{8,10},{10,8},{12,14},{14,12},{16,18},{18,... | collective-permute-start | bytes 786440 | tf_op jit(solution)/shard_map/ppermute | solution.py:448
  50.5 11.8 %copy-start.10 = (bf16[8,128,128]{2,1,0:T(8,128)(2,1)}, bf16[8,128,128]{2,1,0:T(8,128)(2,1)S(1)}, u32[]{:S(2)}) copy-start(bf16[8,128,128]{2,1,0:T(8,128)(2,1)S(1)} %collective-permute-done.14.refs_8_) | copy-start | bytes 786436
  50.5 11.7 %collective-permute-start.15 = (bf16[8,128,128]{2,1,0:T(8,128)(2,1)S(1)}, bf16[8,128,128]{2,1,0:T(8,128)(2,1)S(1)}, u32[]{:S(2)}, u32[]{:S(2)}) collective-permute-start(bf16[8,128,128]{2,1,0:T(8,128)(2,1)S(1)} %collective-permute-done.14.refs_8_), channel_id=1, source_target_pairs={{0,2},{2,0},{4,6},{6,4},{8,10},{10,8},{12,14},{14,12},{16,18},{18,... | collective-permute-start | bytes 786440 | tf_op jit(solution)/shard_map/ppermute | solution.py:448
  50.5 11.8 %copy-start.11 = (bf16[8,128,128]{2,1,0:T(8,128)(2,1)}, bf16[8,128,128]{2,1,0:T(8,128)(2,1)S(1)}, u32[]{:S(2)}) copy-start(bf16[8,128,128]{2,1,0:T(8,128)(2,1)S(1)} %collective-permute-done.5.refs_5_) | copy-start | bytes 786436
  50.5 7.1 %collective-permute-start.19 = (bf16[272,128]{1,0:T(8,128)(2,1)}, bf16[272,128]{1,0:T(8,128)(2,1)S(1)}, u32[]{:S(2)}, u32[]{:S(2)}) collective-permute-start(bf16[272,128]{1,0:T(8,128)(2,1)} %get-tuple-element.47), channel_id=1, source_target_pairs={{0,8},{2,10},{4,12},{6,14},{8,16},{10,18},{12,20},{14,22},{16,24},... | collective-permute-start | bytes 208904 | tf_op jit(solution)/shard_map/ppermute | solution.py:225
  50.8 11.5 %copy-start.12 = (bf16[8,128,128]{2,1,0:T(8,128)(2,1)}, bf16[8,128,128]{2,1,0:T(8,128)(2,1)S(1)}, u32[]{:S(2)}) copy-start(bf16[8,128,128]{2,1,0:T(8,128)(2,1)S(1)} %collective-permute-done.17.refs_13_) | copy-start | bytes 786436
  50.8 9.3 %collective-permute-start.20 = (bf16[272,128]{1,0:T(8,128)(2,1)}, bf16[272,128]{1,0:T(8,128)(2,1)S(1)}, u32[]{:S(2)}, u32[]{:S(2)}) collective-permute-start(bf16[272,128]{1,0:T(8,128)(2,1)} %get-tuple-element.48), channel_id=1, source_target_pairs={{0,16},{2,18},{4,20},{6,22},{8,24},{10,26},{12,28},{14,30},{16,0},... | collective-permute-start | bytes 208904 | tf_op jit(solution)/shard_map/ppermute | solution.py:225
  57.6 4.7 %copy-start.19 = (bf16[272,128]{1,0:T(8,128)(2,1)}, bf16[272,128]{1,0:T(8,128)(2,1)S(1)}, u32[]{:S(2)}) copy-start(bf16[272,128]{1,0:T(8,128)(2,1)S(1)} %collective-permute-done.19.refs_17_) | copy-start | bytes 208900
  57.6 4.5 %collective-permute-start.21 = (bf16[272,128]{1,0:T(8,128)(2,1)}, bf16[272,128]{1,0:T(8,128)(2,1)S(1)}, u32[]{:S(2)}, u32[]{:S(2)}) collective-permute-start(bf16[272,128]{1,0:T(8,128)(2,1)} %get-tuple-element.49), channel_id=1, source_target_pairs={{0,24},{2,26},{4,28},{6,30},{8,0},{10,2},{12,4},{14,6},{16,8},{18,... | collective-permute-start | bytes 208904 | tf_op jit(solution)/shard_map/ppermute | solution.py:225
  60.1 2.2 %copy-start.20 = (bf16[272,128]{1,0:T(8,128)(2,1)}, bf16[272,128]{1,0:T(8,128)(2,1)S(1)}, u32[]{:S(2)}) copy-start(bf16[272,128]{1,0:T(8,128)(2,1)S(1)} %collective-permute-done.20.refs_18_) | copy-start | bytes 208900
  62.2 0.6 copy-start.21
  62.2 0.7 copy-start.13
  62.2 0.8 copy-start.14
  62.2 0.9 copy-start.15

commit v8 on v7

--- a/solution.py
+++ b/solution.py
@@ -474,11 +474,17 @@
     inputs = (scalars, ratings[0, 0], runs[0, 0], mine, sub_factors)
     up, down = ring_round(mine, mine, held, 1, shards)
     (away,) = rhs_sums(*inputs, 1, None, owners, own_rows)
-    up, down, away = together((up, down, away))
-
+    crossed = {0: other_core(mine, shards)}
+    up, down, away, crossed = together((up, down, away, crossed))
+
+    def cross(step):
+        for distance in {step, chips - step}:
+            crossed[distance] = other_core(held[distance], shards)
+
+    cross(1)
     up, down = ring_round(up, down, held, 2, shards)
     parts = rhs_sums(*inputs, 0, other_core(away, shards), owners, own_rows)
-    up, down, parts = together((up, down, parts))
+    up, down, parts, crossed = together((up, down, parts, crossed))
 
     up, down = ring_round(up, down, held, 3, shards)
     total = reduce_chip(parts, shards, owners, own_rows)
@@ -487,9 +493,13 @@
     for step in range(4, chips // 2 + 1):
         up, down = ring_round(up, down, held, step, shards)
     terms = reduce_levels(total, shards)
+    held[chips // 2], terms, crossed = together((held[chips // 2], terms, crossed))
+
+    for step in range(2, chips // 2 + 1):
+        cross(step)
     pieces = []
     for distance in range(chips):
-        pieces += [held[distance], other_core(held[distance], shards)]
+        pieces += [held[distance], crossed[distance]]
     first, second, third, dots = krylov(
         factor_start, activity[None], sub_factors, pieces, terms, slots, devices
     )

time: 92.3 us -> 85.9 us (0.931); the launches traced: 92.7 us -> 84.9 us
  waiting for transfers between devices: 27.7 us -> 16.5 us
  starting transfers between devices: 16.2 us -> 19.3 us
  blocking collectives: 13.5 us -> 15.6 us
  Pallas kernels: 32 us -> 30.5 us
    ppermute x4, waiting for transfers between devices: 6.96 us -> 1.38 us  [ring_round(): up = lax.ppermute(up, 'loop', shift(1))]
    ppermute x3, waiting for transfers between devices: 7.72 us -> 2.3 us  [reduce_levels(): terms.append(lax.ppermute(total[up], 'loop', shift))]
    ppermute x4, starting transfers between devices: 5.22 us -> 1.44 us  [ring_round(): up = lax.ppermute(up, 'loop', shift(1))]
    ppermute x3, starting transfers between devices: 2.02 us -> 5.45 us  [ring_round(): down = lax.ppermute(down, 'loop', shift(-1))]
    ppermute x3, starting transfers between devices: 3.93 us -> 7.35 us  [reduce_levels(): terms.append(lax.ppermute(total[up], 'loop', shift))]
    all_to_all x1, blocking collectives: 13.5 us -> 15.6 us  [on_device(): everyone = lax.all_to_all(dots, AXES, 0, 0, tiled=True)]
    pallas_call x1, Pallas kernels: 14.2 us -> 12.7 us  [krylov(): pl.pallas_call(functools.partial(steps_kernel, shards=len(pieces), levels...]
    ppermute x9, waiting for transfers between devices: 0.3 us -> 1.38 us  [other_core(): lax.ppermute(value, 'loop', [(shard, shard ^ 1) for shard in range(shards)])]
  transfers between devices with their start and end apart: 22 -> 22, of which waited for: 8 -> 10; matrix products, arithmetic and copies ran while one was open for 0% -> 0% of each run, Pallas kernels for 17% -> 19%
where the time goes in v8:
time: 85.9 us; the launch traced here: 84.9 us
  Pallas kernels  30.5 us (36%)
  starting transfers between devices  19.3 us (22%)
  waiting for transfers between devices  16.5 us (19%)
  blocking collectives  15.6 us (18%)
  local copies, waits for them, and re-layouts  2.18 us (3%)
  between operations  0.9 us (1%)
    all_to_all x1, blocking collectives, on_device(): everyone = lax.all_to_all(dots, AXES, 0, 0, tiled=True)  15.6 us
    pallas_call x2, Pallas kernels, rhs_sums(): pl.pallas_call(functools.partial(rhs_kernel, half=half, owners=owners, ow...  14 us
    pallas_call x1, Pallas kernels, krylov(): pl.pallas_call(functools.partial(steps_kernel, shards=len(pieces), levels...  12.7 us
    ppermute x3, waiting for transfers between devices, reduce_chip(): given.append(lax.ppermute(part, AXES, pairs) if o or column else part)  11.3 us
    ppermute x3, starting transfers between devices, reduce_levels(): terms.append(lax.ppermute(total[up], 'loop', shift))  7.35 us
    ppermute x3, starting transfers between devices, ring_round(): down = lax.ppermute(down, 'loop', shift(-1))  5.45 us
    ppermute x3, starting transfers between devices, reduce_chip(): given.append(lax.ppermute(part, AXES, pairs) if o or column else part)  3.49 us
    ppermute x3, waiting for transfers between devices, reduce_levels(): terms.append(lax.ppermute(total[up], 'loop', shift))  2.3 us
  transfers between devices with their start and end apart: 22, of which 10 were waited for; matrix products, arithmetic and copies ran while one was open for 0% of the time, Pallas kernels for 19%

profile of v8, /device:TPU:0, one launch (start us, length us, event | category | flops | bytes accessed | tf_op | source)
XLA Modules:
  0.0 84.9 jit_solution(11087735805248363484)
XLA Ops:
  0.6 0.5 collective-permute-start.2
  1.1 2.6 %collective-permute-start.1 = (bf16[8,128,128]{2,1,0:T(8,128)(2,1)}, bf16[8,128,128]{2,1,0:T(8,128)(2,1)S(1)}, u32[]{:S(2)}, u32[]{:S(2)}) collective-permute-start(bf16[8,128,128]{2,1,0:T(8,128)(2,1)} %bitcast.15), channel_id=1, source_target_pairs={{0,4},{2,6},{8,0},{10,2},{16,8},{18,10},{24,16},{26,18},{28,24},{3... | collective-permute-start | bytes 786440 | tf_op jit(solution)/shard_map/ppermute | solution.py:442
  3.7 0.2 collective-permute-start
  3.9 6.9 %rhs.2 = bf16[2,2,4,160,128]{4,3,2,1,0:T(8,128)(2,1)} custom-call(s32[8,16]{1,0:T(8,128)} %bitcast.25, s32[8,16]{1,0:T(8,128)} %bitcast.27, s32[8,16]{1,0:T(8,128)} %bitcast.29, s32[1,16]{1,0:T(1,128)} %bitcast.31, bf16[16,8,128,128]{3,2,1,0:T(8,128)(2,1)} %bitcast.21, s32[16,8,2,128]{3,2,1,0:T(2,128)} %bitcast.23, bf16[8,128,128]{2,1,0:T(8,128)(2,1)} %bitcast.17, ...), custom_call_target="tpu_custom_call" | custom-call | flops 2147483648 | bytes 16777216 | tf_op jit(solution)/shard_map/rhs/pallas_call | solution.py:149
  10.7 0.0 collective-permute-done.2.refs_1_
  10.8 0.1 collective-permute-done.1.refs_2_
  10.9 1.4 %collective-permute-done.refs_14_ = bf16[8,128,128]{2,1,0:T(8,128)(2,1)S(1)} collective-permute-done((bf16[8,128,128]{2,1,0:T(8,128)(2,1)}, bf16[8,128,128]{2,1,0:T(8,128)(2,1)S(1)}, u32[]{:S(2)}, u32[]{:S(2)}) %collective-permute-start) | collective-permute-done | bytes 262176 | tf_op jit(solution)/shard_map/ppermute | solution.py:439
  12.3 0.0 collective-permute-start.5
  12.3 0.6 collective-permute-start.3
  12.9 0.2 collective-permute-start.6
  13.0 0.3 collective-permute-start.7
  13.4 1.4 %collective-permute-start.4 = (bf16[8,128,128]{2,1,0:T(8,128)(2,1)S(1)}, bf16[8,128,128]{2,1,0:T(8,128)(2,1)S(1)}, u32[]{:S(2)}, u32[]{:S(2)}) collective-permute-start(bf16[8,128,128]{2,1,0:T(8,128)(2,1)S(1)} %collective-permute-done.1.refs_2_), channel_id=1, source_target_pairs={{0,4},{2,6},{8,0},{10,2},{16,8},{18,10},{24,16},{26,18},{28,24},{3... | collective-permute-start | bytes 786440 | tf_op jit(solution)/shard_map/ppermute | solution.py:442
  14.8 0.0 collective-permute-done.5.refs_0_
  14.8 0.9 %copy-done.21 = bf16[2,2,4,160,128]{4,3,2,1,0:T(8,128)(2,1)} copy-done((bf16[2,2,4,160,128]{4,3,2,1,0:T(8,128)(2,1)}, bf16[2,2,4,160,128]{4,3,2,1,0:T(8,128)(2,1)S(1)}, u32[]{:S(2)}) %copy-start.21) | copy-done | bytes 655384
  15.7 7.1 %rhs.3 = (bf16[4,176,128]{2,1,0:T(8,128)(2,1)}, bf16[4,176,128]{2,1,0:T(8,128)(2,1)}, bf16[4,176,128]{2,1,0:T(8,128)(2,1)}, bf16[4,176,128]{2,1,0:T(8,128)(2,1)}) custom-call(s32[8,16]{1,0:T(8,128)} %bitcast.26, s32[8,16]{1,0:T(8,128)} %bitcast.28, s32[8,16]{1,0:T(8,128)} %bitcast.30, s32[1,16]{1,0:T(1,128)} %bitcast.32, bf16[16,8,128,128]{3,2,1,0:T(8,128)(2,1)} %bitcast.22, ...), custom_call_target="tpu_custom_call" | custom-call | flops 2147483648 | bytes 16777216 | tf_op jit(solution)/shard_map/rhs/pallas_call | solution.py:149
  22.8 0.0 collective-permute-done.6.refs_3_
  22.8 0.0 collective-permute-done.7.refs_15_
  22.8 0.0 collective-permute-done.3.refs_12_
  22.9 0.0 collective-permute-done.4.refs_4_
  22.9 0.6 collective-permute-start.8
  23.5 1.5 %collective-permute-start.9 = (bf16[8,128,128]{2,1,0:T(8,128)(2,1)S(1)}, bf16[8,128,128]{2,1,0:T(8,128)(2,1)S(1)}, u32[]{:S(2)}, u32[]{:S(2)}) collective-permute-start(bf16[8,128,128]{2,1,0:T(8,128)(2,1)S(1)} %collective-permute-done.4.refs_4_), channel_id=1, source_target_pairs={{0,4},{2,6},{8,0},{10,2},{16,8},{18,10},{24,16},{26,18},{28,24},{3... | collective-permute-start | bytes 786440 | tf_op jit(solution)/shard_map/ppermute | solution.py:442
  25.0 1.6 %collective-permute-start.10 = (bf16[4,176,128]{2,1,0:T(8,128)(2,1)}, bf16[4,176,128]{2,1,0:T(8,128)(2,1)S(1)}, u32[]{:S(2)}, u32[]{:S(2)}) collective-permute-start(bf16[4,176,128]{2,1,0:T(8,128)(2,1)} %get-tuple-element.51), channel_id=1, source_target_pairs={{0,4},{1,5},{2,6},{3,7},{4,0},{5,1},{6,2},{7,3},{8,12},{9,13},{10,... | collective-permute-start | bytes 540680 | tf_op jit(solution)/shard_map/ppermute | solution.py:204
  26.5 1.5 %collective-permute-start.11 = (bf16[4,176,128]{2,1,0:T(8,128)(2,1)}, bf16[4,176,128]{2,1,0:T(8,128)(2,1)S(1)}, u32[]{:S(2)}, u32[]{:S(2)}) collective-permute-start(bf16[4,176,128]{2,1,0:T(8,128)(2,1)} %get-tuple-element.52), channel_id=1, source_target_pairs={{0,1},{1,0},{2,3},{3,2},{4,5},{5,4},{6,7},{7,6},{8,9},{9,8},{10,11... | collective-permute-start | bytes 540680 | tf_op jit(solution)/shard_map/ppermute | solution.py:204
  28.1 0.4 collective-permute-start.12
  28.4 7.5 %collective-permute-done.10.refs_1_ = bf16[4,176,128]{2,1,0:T(8,128)(2,1)S(1)} collective-permute-done((bf16[4,176,128]{2,1,0:T(8,128)(2,1)}, bf16[4,176,128]{2,1,0:T(8,128)(2,1)S(1)}, u32[]{:S(2)}, u32[]{:S(2)}) %collective-permute-start.10) | collective-permute-done | bytes 180256 | tf_op jit(solution)/shard_map/ppermute | solution.py:204
  36.0 0.0 collective-permute-done.11.refs_2_
  36.0 3.8 %collective-permute-done.12.refs_3_ = bf16[4,176,128]{2,1,0:T(8,128)(2,1)S(1)} collective-permute-done((bf16[4,176,128]{2,1,0:T(8,128)(2,1)}, bf16[4,176,128]{2,1,0:T(8,128)(2,1)S(1)}, u32[]{:S(2)}, u32[]{:S(2)}) %collective-permute-start.12) | collective-permute-done | bytes 180256 | tf_op jit(solution)/shard_map/ppermute | solution.py:204
  39.8 0.7 copy-done.17
  40.4 1.9 %chip.1 = (bf16[272,128]{1,0:T(8,128)(2,1)}, bf16[272,128]{1,0:T(8,128)(2,1)}, bf16[272,128]{1,0:T(8,128)(2,1)}, bf16[272,128]{1,0:T(8,128)(2,1)}) custom-call(bf16[4,176,128]{2,1,0:T(8,128)(2,1)} %get-tuple-element.50.refs_0_, bf16[4,176,128]{2,1,0:T(8,128)(2,1)} %copy-done.15, bf16[4,176,128]{2,1,0:T(8,128)(2,1)} %copy-done.16, bf16[4,176,128]{2,1,0:T(8,128)(2,1)} %copy-done.17), custom_call_target="tpu_custom_call" | custom-call | tf_op jit(solution)/shard_map/chip/pallas_call | solution.py:210
  42.4 0.0 collective-permute-done.8.refs_10_
  42.4 0.1 collective-permute-start.13
  42.5 0.2 collective-permute-start.14
  42.7 4.5 %collective-permute-start.15 = (bf16[272,128]{1,0:T(8,128)(2,1)}, bf16[272,128]{1,0:T(8,128)(2,1)S(1)}, u32[]{:S(2)}, u32[]{:S(2)}) collective-permute-start(bf16[272,128]{1,0:T(8,128)(2,1)} %get-tuple-element.61), channel_id=1, source_target_pairs={{0,16},{2,18},{4,20},{6,22},{8,24},{10,26},{12,28},{14,30},{16,0},... | collective-permute-start | bytes 208904 | tf_op jit(solution)/shard_map/ppermute | solution.py:225
  47.2 2.6 %collective-permute-start.16 = (bf16[272,128]{1,0:T(8,128)(2,1)}, bf16[272,128]{1,0:T(8,128)(2,1)S(1)}, u32[]{:S(2)}, u32[]{:S(2)}) collective-permute-start(bf16[272,128]{1,0:T(8,128)(2,1)} %get-tuple-element.62), channel_id=1, source_target_pairs={{0,24},{2,26},{4,28},{6,30},{8,0},{10,2},{12,4},{14,6},{16,8},{18,... | collective-permute-start | bytes 208904 | tf_op jit(solution)/shard_map/ppermute | solution.py:225
  49.8 0.8 collective-permute-done.14.refs_17_
  50.6 0.7 collective-permute-done.15.refs_18_
  51.4 0.7 collective-permute-done.16.refs_19_
  52.1 0.0 collective-permute-start.18
  52.1 0.0 collective-permute-done.13.refs_8_
  52.1 0.5 collective-permute-start.19
  52.7 0.3 collective-permute-done.20.refs_11_
  52.9 0.7 collective-permute-done.18.refs_7_
  53.7 0.4 collective-permute-done.19.refs_9_
  54.2 0.2 copy-done.13
  54.4 0.4 copy-done.14
  54.7 12.7 %krylov.1 = (f32[128,128]{1,0:T(8,128)}, f32[128,128]{1,0:T(8,128)}, f32[128,128]{1,0:T(8,128)}, f32[32,1,128]{2,1,0:T(1,128)}) custom-call(f32[128,128]{1,0:T(8,128)} %start.3, f32[1,128]{1,0:T(1,128)} %bitcast.20, bf16[2048,128]{1,0:T(8,128)(2,1)} %subs_in.5, bf16[8,128,128]{2,1,0:T(8,128)(2,1)} %bitcast.19, bf16[8,128,128]{2,1,0:T(8,128)(2,1)} %copy-done, ...), custom_call_target="tpu_custom_call" | custom-call | tf_op jit(solution)/shard_map/krylov/pallas_call | solution.py:384
  67.5 15.6 %all_to_all.5.dots = f32[32,1,128]{2,1,0:T(1,128)} all-to-all(f32[32,1,128]{2,1,0:T(1,128)} %get-tuple-element.74), channel_id=1, replica_groups=mesh['loop'=16,'own'=2] {'loop','own'}, dimensions={0} | all-to-all | bytes 32768 | tf_op jit(solution)/shard_map/all_to_all | solution.py:506
  83.0 1.9 %last_step.1 = (f32[128,128]{1,0:T(8,128)}, f32[128,128]{1,0:T(8,128)}) custom-call(f32[32,1,128]{2,1,0:T(1,128)} %all_to_all.5.dots, f32[128,128]{1,0:T(8,128)} %start.3, f32[128,128]{1,0:T(8,128)} %get-tuple-element.75.first, f32[128,128]{1,0:T(8,128)} %get-tuple-element.76.second, f32[128,128]{1,0:T(8,128)} %get-tuple-element.77.third), custom_call_target="tpu_custom_call" | custom-call | tf_op jit(solution)/shard_map/last_step/pallas_call | solution.py:415
  (46 shorter events, 0.1 us)
Async XLA Ops:
  0.6 10.1 %collective-permute-start.2 = (bf16[8,128,128]{2,1,0:T(8,128)(2,1)}, bf16[8,128,128]{2,1,0:T(8,128)(2,1)S(1)}, u32[]{:S(2)}, u32[]{:S(2)}) collective-permute-start(bf16[8,128,128]{2,1,0:T(8,128)(2,1)} %bitcast.14), channel_id=1, source_target_pairs={{0,2},{2,0},{4,6},{6,4},{8,10},{10,8},{12,14},{14,12},{16,18},{18,... | collective-permute-start | bytes 786440 | tf_op jit(solution)/shard_map/ppermute | solution.py:448
  1.1 9.8 %collective-permute-start.1 = (bf16[8,128,128]{2,1,0:T(8,128)(2,1)}, bf16[8,128,128]{2,1,0:T(8,128)(2,1)S(1)}, u32[]{:S(2)}, u32[]{:S(2)}) collective-permute-start(bf16[8,128,128]{2,1,0:T(8,128)(2,1)} %bitcast.15), channel_id=1, source_target_pairs={{0,4},{2,6},{8,0},{10,2},{16,8},{18,10},{24,16},{26,18},{28,24},{3... | collective-permute-start | bytes 786440 | tf_op jit(solution)/shard_map/ppermute | solution.py:442
  3.7 8.6 %collective-permute-start = (bf16[8,128,128]{2,1,0:T(8,128)(2,1)}, bf16[8,128,128]{2,1,0:T(8,128)(2,1)S(1)}, u32[]{:S(2)}, u32[]{:S(2)}) collective-permute-start(bf16[8,128,128]{2,1,0:T(8,128)(2,1)} %bitcast.16), channel_id=1, source_target_pairs={{0,8},{2,10},{8,16},{10,18},{16,24},{18,26},{24,28},{26,30},{28,20... | collective-permute-start | bytes 786440 | tf_op jit(solution)/shard_map/ppermute | solution.py:439
  10.7 31.6 %copy-start = (bf16[8,128,128]{2,1,0:T(8,128)(2,1)}, bf16[8,128,128]{2,1,0:T(8,128)(2,1)S(1)}, u32[]{:S(2)}) copy-start(bf16[8,128,128]{2,1,0:T(8,128)(2,1)S(1)} %collective-permute-done.2.refs_1_) | copy-start | bytes 786436
  10.9 31.5 %copy-start.1 = (bf16[8,128,128]{2,1,0:T(8,128)(2,1)}, bf16[8,128,128]{2,1,0:T(8,128)(2,1)S(1)}, u32[]{:S(2)}) copy-start(bf16[8,128,128]{2,1,0:T(8,128)(2,1)S(1)} %collective-permute-done.1.refs_2_) | copy-start | bytes 786436
  12.3 30.1 %copy-start.2 = (bf16[8,128,128]{2,1,0:T(8,128)(2,1)}, bf16[8,128,128]{2,1,0:T(8,128)(2,1)S(1)}, u32[]{:S(2)}) copy-start(bf16[8,128,128]{2,1,0:T(8,128)(2,1)S(1)} %collective-permute-done.refs_14_) | copy-start | bytes 786436
  12.3 2.5 %collective-permute-start.5 = (bf16[2,2,4,160,128]{4,3,2,1,0:T(8,128)(2,1)}, bf16[2,2,4,160,128]{4,3,2,1,0:T(8,128)(2,1)S(1)}, u32[]{:S(2)}, u32[]{:S(2)}) collective-permute-start(bf16[2,2,4,160,128]{4,3,2,1,0:T(8,128)(2,1)} %rhs.2), channel_id=1, source_target_pairs={{0,2},{2,0},{4,6},{6,4},{8,10},{10,8},{12,14},{14,12},{16,18},{18,... | collective-permute-start | bytes 1966088 | tf_op jit(solution)/shard_map/ppermute | solution.py:448
  12.3 10.6 %collective-permute-start.3 = (bf16[8,128,128]{2,1,0:T(8,128)(2,1)S(1)}, bf16[8,128,128]{2,1,0:T(8,128)(2,1)S(1)}, u32[]{:S(2)}, u32[]{:S(2)}) collective-permute-start(bf16[8,128,128]{2,1,0:T(8,128)(2,1)S(1)} %collective-permute-done.refs_14_), channel_id=1, source_target_pairs={{0,8},{2,10},{8,16},{10,18},{16,24},{18,26},{24,28},{26,30},{28,20... | collective-permute-start | bytes 786440 | tf_op jit(solution)/shard_map/ppermute | solution.py:439
  12.9 9.9 %collective-permute-start.6 = (bf16[8,128,128]{2,1,0:T(8,128)(2,1)S(1)}, bf16[8,128,128]{2,1,0:T(8,128)(2,1)S(1)}, u32[]{:S(2)}, u32[]{:S(2)}) collective-permute-start(bf16[8,128,128]{2,1,0:T(8,128)(2,1)S(1)} %collective-permute-done.1.refs_2_), channel_id=1, source_target_pairs={{0,2},{2,0},{4,6},{6,4},{8,10},{10,8},{12,14},{14,12},{16,18},{18,... | collective-permute-start | bytes 786440 | tf_op jit(solution)/shard_map/ppermute | solution.py:448
  13.0 9.8 %collective-permute-start.7 = (bf16[8,128,128]{2,1,0:T(8,128)(2,1)S(1)}, bf16[8,128,128]{2,1,0:T(8,128)(2,1)S(1)}, u32[]{:S(2)}, u32[]{:S(2)}) collective-permute-start(bf16[8,128,128]{2,1,0:T(8,128)(2,1)S(1)} %collective-permute-done.refs_14_), channel_id=1, source_target_pairs={{0,2},{2,0},{4,6},{6,4},{8,10},{10,8},{12,14},{14,12},{16,18},{18,... | collective-permute-start | bytes 786440 | tf_op jit(solution)/shard_map/ppermute | solution.py:448
  13.4 9.5 %collective-permute-start.4 = (bf16[8,128,128]{2,1,0:T(8,128)(2,1)S(1)}, bf16[8,128,128]{2,1,0:T(8,128)(2,1)S(1)}, u32[]{:S(2)}, u32[]{:S(2)}) collective-permute-start(bf16[8,128,128]{2,1,0:T(8,128)(2,1)S(1)} %collective-permute-done.1.refs_2_), channel_id=1, source_target_pairs={{0,4},{2,6},{8,0},{10,2},{16,8},{18,10},{24,16},{26,18},{28,24},{3... | collective-permute-start | bytes 786440 | tf_op jit(solution)/shard_map/ppermute | solution.py:442
  14.8 0.9 %copy-start.21 = (bf16[2,2,4,160,128]{4,3,2,1,0:T(8,128)(2,1)}, bf16[2,2,4,160,128]{4,3,2,1,0:T(8,128)(2,1)S(1)}, u32[]{:S(2)}) copy-start(bf16[2,2,4,160,128]{4,3,2,1,0:T(8,128)(2,1)S(1)} %collective-permute-done.5.refs_0_) | copy-start | bytes 1966084
  22.8 31.2 %copy-start.4 = (bf16[8,128,128]{2,1,0:T(8,128)(2,1)}, bf16[8,128,128]{2,1,0:T(8,128)(2,1)S(1)}, u32[]{:S(2)}) copy-start(bf16[8,128,128]{2,1,0:T(8,128)(2,1)S(1)} %collective-permute-done.6.refs_3_) | copy-start | bytes 786436
  22.8 31.2 %copy-start.5 = (bf16[8,128,128]{2,1,0:T(8,128)(2,1)}, bf16[8,128,128]{2,1,0:T(8,128)(2,1)S(1)}, u32[]{:S(2)}) copy-start(bf16[8,128,128]{2,1,0:T(8,128)(2,1)S(1)} %collective-permute-done.7.refs_15_) | copy-start | bytes 786436
  22.8 31.2 %copy-start.3 = (bf16[8,128,128]{2,1,0:T(8,128)(2,1)}, bf16[8,128,128]{2,1,0:T(8,128)(2,1)S(1)}, u32[]{:S(2)}) copy-start(bf16[8,128,128]{2,1,0:T(8,128)(2,1)S(1)} %collective-permute-done.3.refs_12_) | copy-start | bytes 786436
  22.9 31.2 %copy-start.6 = (bf16[8,128,128]{2,1,0:T(8,128)(2,1)}, bf16[8,128,128]{2,1,0:T(8,128)(2,1)S(1)}, u32[]{:S(2)}) copy-start(bf16[8,128,128]{2,1,0:T(8,128)(2,1)S(1)} %collective-permute-done.4.refs_4_) | copy-start | bytes 786436
  22.9 19.5 %collective-permute-start.8 = (bf16[8,128,128]{2,1,0:T(8,128)(2,1)S(1)}, bf16[8,128,128]{2,1,0:T(8,128)(2,1)S(1)}, u32[]{:S(2)}, u32[]{:S(2)}) collective-permute-start(bf16[8,128,128]{2,1,0:T(8,128)(2,1)S(1)} %collective-permute-done.3.refs_12_), channel_id=1, source_target_pairs={{0,8},{2,10},{8,16},{10,18},{16,24},{18,26},{24,28},{26,30},{28,20... | collective-permute-start | bytes 786440 | tf_op jit(solution)/shard_map/ppermute | solution.py:439
  23.5 18.9 %collective-permute-start.9 = (bf16[8,128,128]{2,1,0:T(8,128)(2,1)S(1)}, bf16[8,128,128]{2,1,0:T(8,128)(2,1)S(1)}, u32[]{:S(2)}, u32[]{:S(2)}) collective-permute-start(bf16[8,128,128]{2,1,0:T(8,128)(2,1)S(1)} %collective-permute-done.4.refs_4_), channel_id=1, source_target_pairs={{0,4},{2,6},{8,0},{10,2},{16,8},{18,10},{24,16},{26,18},{28,24},{3... | collective-permute-start | bytes 786440 | tf_op jit(solution)/shard_map/ppermute | solution.py:442
  25.0 11.0 %collective-permute-start.10 = (bf16[4,176,128]{2,1,0:T(8,128)(2,1)}, bf16[4,176,128]{2,1,0:T(8,128)(2,1)S(1)}, u32[]{:S(2)}, u32[]{:S(2)}) collective-permute-start(bf16[4,176,128]{2,1,0:T(8,128)(2,1)} %get-tuple-element.51), channel_id=1, source_target_pairs={{0,4},{1,5},{2,6},{3,7},{4,0},{5,1},{6,2},{7,3},{8,12},{9,13},{10,... | collective-permute-start | bytes 540680 | tf_op jit(solution)/shard_map/ppermute | solution.py:204
  26.5 9.5 %collective-permute-start.11 = (bf16[4,176,128]{2,1,0:T(8,128)(2,1)}, bf16[4,176,128]{2,1,0:T(8,128)(2,1)S(1)}, u32[]{:S(2)}, u32[]{:S(2)}) collective-permute-start(bf16[4,176,128]{2,1,0:T(8,128)(2,1)} %get-tuple-element.52), channel_id=1, source_target_pairs={{0,1},{1,0},{2,3},{3,2},{4,5},{5,4},{6,7},{7,6},{8,9},{9,8},{10,11... | collective-permute-start | bytes 540680 | tf_op jit(solution)/shard_map/ppermute | solution.py:204
  28.1 11.7 %collective-permute-start.12 = (bf16[4,176,128]{2,1,0:T(8,128)(2,1)}, bf16[4,176,128]{2,1,0:T(8,128)(2,1)S(1)}, u32[]{:S(2)}, u32[]{:S(2)}) collective-permute-start(bf16[4,176,128]{2,1,0:T(8,128)(2,1)} %get-tuple-element.53), channel_id=1, source_target_pairs={{0,5},{1,4},{2,7},{3,6},{4,1},{5,0},{6,3},{7,2},{8,13},{9,12},{10,... | collective-permute-start | bytes 540680 | tf_op jit(solution)/shard_map/ppermute | solution.py:204
  36.0 3.8 %copy-start.15 = (bf16[4,176,128]{2,1,0:T(8,128)(2,1)}, bf16[4,176,128]{2,1,0:T(8,128)(2,1)S(1)}, u32[]{:S(2)}) copy-start(bf16[4,176,128]{2,1,0:T(8,128)(2,1)S(1)} %collective-permute-done.10.refs_1_) | copy-start | bytes 540676
  36.0 3.8 %copy-start.16 = (bf16[4,176,128]{2,1,0:T(8,128)(2,1)}, bf16[4,176,128]{2,1,0:T(8,128)(2,1)S(1)}, u32[]{:S(2)}) copy-start(bf16[4,176,128]{2,1,0:T(8,128)(2,1)S(1)} %collective-permute-done.11.refs_2_) | copy-start | bytes 540676
  39.8 0.7 copy-start.17
  42.4 11.7 %copy-start.7 = (bf16[8,128,128]{2,1,0:T(8,128)(2,1)}, bf16[8,128,128]{2,1,0:T(8,128)(2,1)S(1)}, u32[]{:S(2)}) copy-start(bf16[8,128,128]{2,1,0:T(8,128)(2,1)S(1)} %collective-permute-done.8.refs_10_) | copy-start | bytes 786436
  42.4 11.7 %copy-start.8 = (bf16[8,128,128]{2,1,0:T(8,128)(2,1)}, bf16[8,128,128]{2,1,0:T(8,128)(2,1)S(1)}, u32[]{:S(2)}) copy-start(bf16[8,128,128]{2,1,0:T(8,128)(2,1)S(1)} %collective-permute-done.9.refs_6_) | copy-start | bytes 786436
  42.4 9.7 %collective-permute-start.13 = (bf16[8,128,128]{2,1,0:T(8,128)(2,1)S(1)}, bf16[8,128,128]{2,1,0:T(8,128)(2,1)S(1)}, u32[]{:S(2)}, u32[]{:S(2)}) collective-permute-start(bf16[8,128,128]{2,1,0:T(8,128)(2,1)S(1)} %collective-permute-done.8.refs_10_), channel_id=1, source_target_pairs={{0,8},{2,10},{8,16},{10,18},{16,24},{18,26},{24,28},{26,30},{28,20... | collective-permute-start | bytes 786440 | tf_op jit(solution)/shard_map/ppermute | solution.py:439
  42.5 8.2 %collective-permute-start.14 = (bf16[272,128]{1,0:T(8,128)(2,1)}, bf16[272,128]{1,0:T(8,128)(2,1)S(1)}, u32[]{:S(2)}, u32[]{:S(2)}) collective-permute-start(bf16[272,128]{1,0:T(8,128)(2,1)} %get-tuple-element.60), channel_id=1, source_target_pairs={{0,8},{2,10},{4,12},{6,14},{8,16},{10,18},{12,20},{14,22},{16,24},... | collective-permute-start | bytes 208904 | tf_op jit(solution)/shard_map/ppermute | solution.py:225
  42.7 8.7 %collective-permute-start.15 = (bf16[272,128]{1,0:T(8,128)(2,1)}, bf16[272,128]{1,0:T(8,128)(2,1)S(1)}, u32[]{:S(2)}, u32[]{:S(2)}) collective-permute-start(bf16[272,128]{1,0:T(8,128)(2,1)} %get-tuple-element.61), channel_id=1, source_target_pairs={{0,16},{2,18},{4,20},{6,22},{8,24},{10,26},{12,28},{14,30},{16,0},... | collective-permute-start | bytes 208904 | tf_op jit(solution)/shard_map/ppermute | solution.py:225
  47.2 5.0 %collective-permute-start.16 = (bf16[272,128]{1,0:T(8,128)(2,1)}, bf16[272,128]{1,0:T(8,128)(2,1)S(1)}, u32[]{:S(2)}, u32[]{:S(2)}) collective-permute-start(bf16[272,128]{1,0:T(8,128)(2,1)} %get-tuple-element.62), channel_id=1, source_target_pairs={{0,24},{2,26},{4,28},{6,30},{8,0},{10,2},{12,4},{14,6},{16,8},{18,... | collective-permute-start | bytes 208904 | tf_op jit(solution)/shard_map/ppermute | solution.py:225
  49.8 2.8 %collective-permute-start.21 = (bf16[8,128,128]{2,1,0:T(8,128)(2,1)S(1)}, bf16[8,128,128]{2,1,0:T(8,128)(2,1)S(1)}, u32[]{:S(2)}, u32[]{:S(2)}) collective-permute-start(bf16[8,128,128]{2,1,0:T(8,128)(2,1)S(1)} %collective-permute-done.3.refs_12_), channel_id=1, source_target_pairs={{0,2},{2,0},{4,6},{6,4},{8,10},{10,8},{12,14},{14,12},{16,18},{18,... | collective-permute-start | bytes 786440 | tf_op jit(solution)/shard_map/ppermute | solution.py:448
  50.6 3.5 %copy-start.18 = (bf16[272,128]{1,0:T(8,128)(2,1)}, bf16[272,128]{1,0:T(8,128)(2,1)S(1)}, u32[]{:S(2)}) copy-start(bf16[272,128]{1,0:T(8,128)(2,1)S(1)} %collective-permute-done.14.refs_17_) | copy-start | bytes 208900
  50.6 2.0 %collective-permute-start.17 = (bf16[8,128,128]{2,1,0:T(8,128)(2,1)S(1)}, bf16[8,128,128]{2,1,0:T(8,128)(2,1)S(1)}, u32[]{:S(2)}, u32[]{:S(2)}) collective-permute-start(bf16[8,128,128]{2,1,0:T(8,128)(2,1)S(1)} %collective-permute-done.4.refs_4_), channel_id=1, source_target_pairs={{0,2},{2,0},{4,6},{6,4},{8,10},{10,8},{12,14},{14,12},{16,18},{18,... | collective-permute-start | bytes 786440 | tf_op jit(solution)/shard_map/ppermute | solution.py:448
  51.4 2.7 %copy-start.19 = (bf16[272,128]{1,0:T(8,128)(2,1)}, bf16[272,128]{1,0:T(8,128)(2,1)S(1)}, u32[]{:S(2)}) copy-start(bf16[272,128]{1,0:T(8,128)(2,1)S(1)} %collective-permute-done.15.refs_18_) | copy-start | bytes 208900
  51.4 1.5 %collective-permute-start.20 = (bf16[8,128,128]{2,1,0:T(8,128)(2,1)S(1)}, bf16[8,128,128]{2,1,0:T(8,128)(2,1)S(1)}, u32[]{:S(2)}, u32[]{:S(2)}) collective-permute-start(bf16[8,128,128]{2,1,0:T(8,128)(2,1)S(1)} %collective-permute-done.8.refs_10_), channel_id=1, source_target_pairs={{0,2},{2,0},{4,6},{6,4},{8,10},{10,8},{12,14},{14,12},{16,18},{18,... | collective-permute-start | bytes 786440 | tf_op jit(solution)/shard_map/ppermute | solution.py:448
  52.1 2.0 %copy-start.20 = (bf16[272,128]{1,0:T(8,128)(2,1)}, bf16[272,128]{1,0:T(8,128)(2,1)S(1)}, u32[]{:S(2)}) copy-start(bf16[272,128]{1,0:T(8,128)(2,1)S(1)} %collective-permute-done.16.refs_19_) | copy-start | bytes 208900
  52.1 1.5 %collective-permute-start.18 = (bf16[8,128,128]{2,1,0:T(8,128)(2,1)S(1)}, bf16[8,128,128]{2,1,0:T(8,128)(2,1)S(1)}, u32[]{:S(2)}, u32[]{:S(2)}) collective-permute-start(bf16[8,128,128]{2,1,0:T(8,128)(2,1)S(1)} %collective-permute-done.9.refs_6_), channel_id=1, source_target_pairs={{0,2},{2,0},{4,6},{6,4},{8,10},{10,8},{12,14},{14,12},{16,18},{18,... | collective-permute-start | bytes 786440 | tf_op jit(solution)/shard_map/ppermute | solution.py:448
  52.1 2.0 %copy-start.9 = (bf16[8,128,128]{2,1,0:T(8,128)(2,1)}, bf16[8,128,128]{2,1,0:T(8,128)(2,1)S(1)}, u32[]{:S(2)}) copy-start(bf16[8,128,128]{2,1,0:T(8,128)(2,1)S(1)} %collective-permute-done.13.refs_8_) | copy-start | bytes 786436
  52.1 1.9 %collective-permute-start.19 = (bf16[8,128,128]{2,1,0:T(8,128)(2,1)S(1)}, bf16[8,128,128]{2,1,0:T(8,128)(2,1)S(1)}, u32[]{:S(2)}, u32[]{:S(2)}) collective-permute-start(bf16[8,128,128]{2,1,0:T(8,128)(2,1)S(1)} %collective-permute-done.13.refs_8_), channel_id=1, source_target_pairs={{0,2},{2,0},{4,6},{6,4},{8,10},{10,8},{12,14},{14,12},{16,18},{18,... | collective-permute-start | bytes 786440 | tf_op jit(solution)/shard_map/ppermute | solution.py:448
  52.7 1.5 %copy-start.10 = (bf16[8,128,128]{2,1,0:T(8,128)(2,1)}, bf16[8,128,128]{2,1,0:T(8,128)(2,1)S(1)}, u32[]{:S(2)}) copy-start(bf16[8,128,128]{2,1,0:T(8,128)(2,1)S(1)} %collective-permute-done.21.refs_13_) | copy-start | bytes 786436
  52.7 1.5 %copy-start.11 = (bf16[8,128,128]{2,1,0:T(8,128)(2,1)}, bf16[8,128,128]{2,1,0:T(8,128)(2,1)S(1)}, u32[]{:S(2)}) copy-start(bf16[8,128,128]{2,1,0:T(8,128)(2,1)S(1)} %collective-permute-done.17.refs_5_) | copy-start | bytes 786436
  52.9 1.2 %copy-start.12 = (bf16[8,128,128]{2,1,0:T(8,128)(2,1)}, bf16[8,128,128]{2,1,0:T(8,128)(2,1)S(1)}, u32[]{:S(2)}) copy-start(bf16[8,128,128]{2,1,0:T(8,128)(2,1)S(1)} %collective-permute-done.20.refs_11_) | copy-start | bytes 786436
  53.7 0.7 copy-start.13
  54.0 0.7 copy-start.14

commit v9 on v8

--- a/solution.py
+++ b/solution.py
@@ -8,7 +8,7 @@
 from jax.sharding import PartitionSpec as P
 
 AXES = ("loop", "own")
-CHUNK = 16
+CHUNK = 48
 FACT_ROWS = 16
 ridge = 0.05
 VMEM_LIMIT = 60 * 2**20
@@ -226,17 +226,23 @@
     return terms
 
 
-def steps_kernel(start, activity, subs_in, *refs, shards, levels, slots, cached):
+def steps_kernel(activity, start_in, subs_in, *refs, shards, levels, slots, cached):
+    pieces, refs = refs[:shards], refs[shards:]
+    terms_in, refs = refs[:levels], refs[levels:]
+    first_out, second_out, third_out, dots_out = refs[:4]
+    masks, words, start, terms, subs, table, runs, lines = refs[4:12]
+    facts, chosen, places, arrived, moved, given = refs[12:18]
+    products = refs[-1]
     own_rows, rank = start.shape
-    pieces, refs = refs[:shards], refs[shards:]
-    terms, refs = refs[:levels], refs[levels:]
-    first_out, second_out, third_out, dots_out = refs[:4]
-    masks, words, subs, table, runs, lines, facts, chosen, places, arrived, moved = refs[4:15]
-    products = refs[-1]
     word_tiles, tile, _ = pieces[0].shape
     sources = lines.shape[0] // levels
     spans = 2 * slots * sources
 
+    gifts = [
+        pltpu.make_async_copy(term, terms.at[up], given.at[up]) for up, term in enumerate(terms_in)
+    ]
+    for copy in gifts:
+        copy.start()
     copies = [
         pltpu.make_async_copy(
             piece, words.at[k * word_tiles : (k + 1) * word_tiles], arrived.at[k]
@@ -245,18 +251,25 @@
     ]
     look = pltpu.make_async_copy(subs_in, subs, moved.at[1])
     look.start()
+    begin = pltpu.make_async_copy(start_in, start, moved.at[2])
+    begin.start()
     for copy in copies:
         copy.start()
-
-    for up, term in enumerate(terms):
-        rest = term[own_rows + spans :, :].astype(f32)
+    for copy in gifts:
+        copy.wait()
+
+    for up in range(levels):
+        rest = terms[up, own_rows + spans :, :].astype(f32)
         lines[up * sources : (up + 1) * sources, :] = rest[:sources].astype(jnp.int32)
     move = pltpu.make_async_copy(lines, facts, moved.at[0])
     move.start()
     rhs = jnp.zeros((own_rows, rank), f32)
-    for up, term in enumerate(terms):
-        rhs = rhs + term[:own_rows, :].astype(f32)
-        runs[up * spans : (up + 1) * spans, :] = term[own_rows : own_rows + spans, :].astype(f32)
+    for up in range(levels):
+        rhs = rhs + terms[up, :own_rows, :].astype(f32)
+        runs[up * spans : (up + 1) * spans, :] = terms[
+            up, own_rows : own_rows + spans, :
+        ].astype(f32)
+    begin.wait()
     look.wait()
     table[...] = subs[...].astype(f32)
     move.wait()
@@ -282,11 +295,9 @@
             src = up * sources + k
             side = lax.rem(lax.div(k, 2), 2)
             distance = jnp.where(side == 0, ahead[0], ahead[1])
-            piece = 2 * distance + lax.rem(k, 2)
+            places[src] = word_tiles * (2 * distance + lax.rem(k, 2))
             for s in range(slots):
                 chosen[n] = src * slots + s
-                places[0, n] = word_tiles * piece + facts[src, slots + s]
-                places[1, n] = 128 * facts[src, 2 * slots + s] + facts[src, 3 * slots + s]
                 n = n + jnp.where(facts[src, s] == wanted, 1, 0)
             return n
 
@@ -311,8 +322,11 @@
         return dot_nt(pick, jnp.concatenate(parts, axis=0)).astype(bf16)
 
     def product(i):
-        i = jnp.minimum(i, used - 1)
-        return (words[places[0, i]].astype(f32) * table[pl.ds(places[1, i], 1), :]).astype(bf16)
+        j = chosen[jnp.minimum(i, used - 1)]
+        src, s = lax.div(j, slots), lax.rem(j, slots)
+        sub = 128 * facts[src, 2 * slots + s] + facts[src, 3 * slots + s]
+        rows = words[places[src] + facts[src, slots + s]].astype(f32)
+        return (rows * table[pl.ds(sub, 1), :]).astype(bf16)
 
     for copy in copies:
         copy.wait()
@@ -369,15 +383,18 @@
     scratch = [
         pltpu.VMEM((chunks, own_rows, CHUNK * tile), bf16),
         pltpu.VMEM((len(pieces) * word_tiles, tile, rank), bf16),
+        pltpu.VMEM(start.shape, f32),
+        pltpu.VMEM((len(terms),) + terms[0].shape, bf16),
         pltpu.VMEM(subs.shape, bf16),
         pltpu.VMEM(subs.shape, f32),
         pltpu.VMEM((2 * blocks, tile), f32),
         pltpu.VMEM((devices, rank), jnp.int32),
         pltpu.SMEM((devices, rank), jnp.int32),
         pltpu.SMEM((blocks,), jnp.int32),
-        pltpu.SMEM((2, blocks), jnp.int32),
+        pltpu.SMEM((devices,), jnp.int32),
         pltpu.SemaphoreType.DMA((len(pieces),)),
-        pltpu.SemaphoreType.DMA((2,)),
+        pltpu.SemaphoreType.DMA((3,)),
+        pltpu.SemaphoreType.DMA((len(terms),)),
     ]
     if cached:
         scratch.append(pltpu.VMEM((chunks, CHUNK * tile, rank), bf16))
@@ -385,13 +402,13 @@
         functools.partial(
             steps_kernel, shards=len(pieces), levels=len(terms), slots=slots, cached=cached
         ),
-        in_specs=[whole, whole, anywhere] + [anywhere] * len(pieces) + [whole] * len(terms),
+        in_specs=[whole] + [anywhere] * (2 + len(pieces) + len(terms)),
         out_specs=[whole] * 4,
         out_shape=[vector, vector, vector, jax.ShapeDtypeStruct((devices, 1, rank), f32)],
         scratch_shapes=scratch,
         compiler_params=pltpu.CompilerParams(vmem_limit_bytes=VMEM_LIMIT),
         name="krylov",
-    )(start, activity, subs, *pieces, *terms)
+    )(activity, start, subs, *pieces, *terms)
 
 
 def last_kernel(dots, start, first, second, third, solution_out, residual_out):

time: 85.9 us -> 84.1 us (0.979)
  blocking collectives: 15.6 us -> 14 us
    all_to_all x1, blocking collectives: 15.6 us -> 14 us  [on_device(): everyone = lax.all_to_all(dots, AXES, 0, 0, tiled=True)]
where the time goes in v9:
time: 84.1 us; the launch traced here: 83.7 us
  Pallas kernels  30.8 us (37%)
  starting transfers between devices  19.3 us (23%)
  waiting for transfers between devices  16.5 us (20%)
  blocking collectives  14 us (17%)
  local copies, waits for them, and re-layouts  2.18 us (3%)
  between operations  0.9 us (1%)
    all_to_all x1, blocking collectives, on_device(): everyone = lax.all_to_all(dots, AXES, 0, 0, tiled=True)  14 us
    pallas_call x2, Pallas kernels, rhs_sums(): pl.pallas_call(functools.partial(rhs_kernel, half=half, owners=owners, ow...  13.9 us
    pallas_call x1, Pallas kernels, krylov(): pl.pallas_call(functools.partial(steps_kernel, shards=len(pieces), levels...  13.1 us
    ppermute x3, waiting for transfers between devices, reduce_chip(): given.append(lax.ppermute(part, AXES, pairs) if o or column else part)  11.3 us
    ppermute x3, starting transfers between devices, reduce_levels(): terms.append(lax.ppermute(total[up], 'loop', shift))  7.34 us
    ppermute x3, starting transfers between devices, ring_round(): down = lax.ppermute(down, 'loop', shift(-1))  5.45 us
    ppermute x3, starting transfers between devices, reduce_chip(): given.append(lax.ppermute(part, AXES, pairs) if o or column else part)  3.49 us
    ppermute x3, waiting for transfers between devices, reduce_levels(): terms.append(lax.ppermute(total[up], 'loop', shift))  2.31 us
  transfers between devices with their start and end apart: 22, of which 10 were waited for; matrix products, arithmetic and copies ran while one was open for 0% of the time, Pallas kernels for 19%

profile of v9, /device:TPU:0, one launch (start us, length us, event | category | flops | bytes accessed | tf_op | source)
XLA Modules:
  0.0 83.7 jit_solution(16285334780810200777)
XLA Ops:
  0.6 0.5 collective-permute-start.2
  1.1 2.6 %collective-permute-start.1 = (bf16[8,128,128]{2,1,0:T(8,128)(2,1)}, bf16[8,128,128]{2,1,0:T(8,128)(2,1)S(1)}, u32[]{:S(2)}, u32[]{:S(2)}) collective-permute-start(bf16[8,128,128]{2,1,0:T(8,128)(2,1)} %bitcast.15), channel_id=1, source_target_pairs={{0,4},{2,6},{8,0},{10,2},{16,8},{18,10},{24,16},{26,18},{28,24},{3... | collective-permute-start | bytes 786440 | tf_op jit(solution)/shard_map/ppermute | solution.py:459
  3.7 0.2 collective-permute-start
  3.9 6.8 %rhs.2 = bf16[2,2,4,160,128]{4,3,2,1,0:T(8,128)(2,1)} custom-call(s32[8,16]{1,0:T(8,128)} %bitcast.25, s32[8,16]{1,0:T(8,128)} %bitcast.27, s32[8,16]{1,0:T(8,128)} %bitcast.29, s32[1,16]{1,0:T(1,128)} %bitcast.31, bf16[16,8,128,128]{3,2,1,0:T(8,128)(2,1)} %bitcast.21, s32[16,8,2,128]{3,2,1,0:T(2,128)} %bitcast.23, bf16[8,128,128]{2,1,0:T(8,128)(2,1)} %bitcast.17, ...), custom_call_target="tpu_custom_call" | custom-call | flops 2147483648 | bytes 16777216 | tf_op jit(solution)/shard_map/rhs/pallas_call | solution.py:149
  10.7 0.0 collective-permute-done.2.refs_1_
  10.7 0.2 collective-permute-done.1.refs_2_
  10.9 1.4 %collective-permute-done.refs_14_ = bf16[8,128,128]{2,1,0:T(8,128)(2,1)S(1)} collective-permute-done((bf16[8,128,128]{2,1,0:T(8,128)(2,1)}, bf16[8,128,128]{2,1,0:T(8,128)(2,1)S(1)}, u32[]{:S(2)}, u32[]{:S(2)}) %collective-permute-start) | collective-permute-done | bytes 262176 | tf_op jit(solution)/shard_map/ppermute | solution.py:456
  12.3 0.0 collective-permute-start.5
  12.3 0.6 collective-permute-start.3
  12.9 0.2 collective-permute-start.6
  13.0 0.3 collective-permute-start.7
  13.4 1.5 %collective-permute-start.4 = (bf16[8,128,128]{2,1,0:T(8,128)(2,1)S(1)}, bf16[8,128,128]{2,1,0:T(8,128)(2,1)S(1)}, u32[]{:S(2)}, u32[]{:S(2)}) collective-permute-start(bf16[8,128,128]{2,1,0:T(8,128)(2,1)S(1)} %collective-permute-done.1.refs_2_), channel_id=1, source_target_pairs={{0,4},{2,6},{8,0},{10,2},{16,8},{18,10},{24,16},{26,18},{28,24},{3... | collective-permute-start | bytes 786440 | tf_op jit(solution)/shard_map/ppermute | solution.py:459
  14.8 0.0 collective-permute-done.5.refs_0_
  14.8 0.9 %copy-done.21 = bf16[2,2,4,160,128]{4,3,2,1,0:T(8,128)(2,1)} copy-done((bf16[2,2,4,160,128]{4,3,2,1,0:T(8,128)(2,1)}, bf16[2,2,4,160,128]{4,3,2,1,0:T(8,128)(2,1)S(1)}, u32[]{:S(2)}) %copy-start.21) | copy-done | bytes 655384
  15.7 7.1 %rhs.3 = (bf16[4,176,128]{2,1,0:T(8,128)(2,1)}, bf16[4,176,128]{2,1,0:T(8,128)(2,1)}, bf16[4,176,128]{2,1,0:T(8,128)(2,1)}, bf16[4,176,128]{2,1,0:T(8,128)(2,1)}) custom-call(s32[8,16]{1,0:T(8,128)} %bitcast.26, s32[8,16]{1,0:T(8,128)} %bitcast.28, s32[8,16]{1,0:T(8,128)} %bitcast.30, s32[1,16]{1,0:T(1,128)} %bitcast.32, bf16[16,8,128,128]{3,2,1,0:T(8,128)(2,1)} %bitcast.22, ...), custom_call_target="tpu_custom_call" | custom-call | flops 2147483648 | bytes 16777216 | tf_op jit(solution)/shard_map/rhs/pallas_call | solution.py:149
  22.8 0.0 collective-permute-done.6.refs_3_
  22.8 0.0 collective-permute-done.3.refs_12_
  22.8 0.0 collective-permute-done.4.refs_4_
  22.9 0.6 collective-permute-start.8
  23.5 1.4 %collective-permute-start.9 = (bf16[8,128,128]{2,1,0:T(8,128)(2,1)S(1)}, bf16[8,128,128]{2,1,0:T(8,128)(2,1)S(1)}, u32[]{:S(2)}, u32[]{:S(2)}) collective-permute-start(bf16[8,128,128]{2,1,0:T(8,128)(2,1)S(1)} %collective-permute-done.4.refs_4_), channel_id=1, source_target_pairs={{0,4},{2,6},{8,0},{10,2},{16,8},{18,10},{24,16},{26,18},{28,24},{3... | collective-permute-start | bytes 786440 | tf_op jit(solution)/shard_map/ppermute | solution.py:459
  24.9 1.6 %collective-permute-start.10 = (bf16[4,176,128]{2,1,0:T(8,128)(2,1)}, bf16[4,176,128]{2,1,0:T(8,128)(2,1)S(1)}, u32[]{:S(2)}, u32[]{:S(2)}) collective-permute-start(bf16[4,176,128]{2,1,0:T(8,128)(2,1)} %get-tuple-element.51), channel_id=1, source_target_pairs={{0,4},{1,5},{2,6},{3,7},{4,0},{5,1},{6,2},{7,3},{8,12},{9,13},{10,... | collective-permute-start | bytes 540680 | tf_op jit(solution)/shard_map/ppermute | solution.py:204
  26.5 1.5 %collective-permute-start.11 = (bf16[4,176,128]{2,1,0:T(8,128)(2,1)}, bf16[4,176,128]{2,1,0:T(8,128)(2,1)S(1)}, u32[]{:S(2)}, u32[]{:S(2)}) collective-permute-start(bf16[4,176,128]{2,1,0:T(8,128)(2,1)} %get-tuple-element.52), channel_id=1, source_target_pairs={{0,1},{1,0},{2,3},{3,2},{4,5},{5,4},{6,7},{7,6},{8,9},{9,8},{10,11... | collective-permute-start | bytes 540680 | tf_op jit(solution)/shard_map/ppermute | solution.py:204
  28.0 0.4 collective-permute-start.12
  28.4 7.5 %collective-permute-done.10.refs_1_ = bf16[4,176,128]{2,1,0:T(8,128)(2,1)S(1)} collective-permute-done((bf16[4,176,128]{2,1,0:T(8,128)(2,1)}, bf16[4,176,128]{2,1,0:T(8,128)(2,1)S(1)}, u32[]{:S(2)}, u32[]{:S(2)}) %collective-permute-start.10) | collective-permute-done | bytes 180256 | tf_op jit(solution)/shard_map/ppermute | solution.py:204
  36.0 0.0 collective-permute-done.11.refs_2_
  36.0 3.8 %collective-permute-done.12.refs_3_ = bf16[4,176,128]{2,1,0:T(8,128)(2,1)S(1)} collective-permute-done((bf16[4,176,128]{2,1,0:T(8,128)(2,1)}, bf16[4,176,128]{2,1,0:T(8,128)(2,1)S(1)}, u32[]{:S(2)}, u32[]{:S(2)}) %collective-permute-start.12) | collective-permute-done | bytes 180256 | tf_op jit(solution)/shard_map/ppermute | solution.py:204
  39.8 0.7 copy-done.17
  40.4 1.9 %chip.1 = (bf16[272,128]{1,0:T(8,128)(2,1)}, bf16[272,128]{1,0:T(8,128)(2,1)}, bf16[272,128]{1,0:T(8,128)(2,1)}, bf16[272,128]{1,0:T(8,128)(2,1)}) custom-call(bf16[4,176,128]{2,1,0:T(8,128)(2,1)} %get-tuple-element.50.refs_0_, bf16[4,176,128]{2,1,0:T(8,128)(2,1)} %copy-done.15, bf16[4,176,128]{2,1,0:T(8,128)(2,1)} %copy-done.16, bf16[4,176,128]{2,1,0:T(8,128)(2,1)} %copy-done.17), custom_call_target="tpu_custom_call" | custom-call | tf_op jit(solution)/shard_map/chip/pallas_call | solution.py:210
  42.4 0.0 collective-permute-done.9.refs_6_
  42.4 0.1 collective-permute-start.13
  42.5 0.2 collective-permute-start.14
  42.7 4.5 %collective-permute-start.15 = (bf16[272,128]{1,0:T(8,128)(2,1)}, bf16[272,128]{1,0:T(8,128)(2,1)S(1)}, u32[]{:S(2)}, u32[]{:S(2)}) collective-permute-start(bf16[272,128]{1,0:T(8,128)(2,1)} %get-tuple-element.61), channel_id=1, source_target_pairs={{0,16},{2,18},{4,20},{6,22},{8,24},{10,26},{12,28},{14,30},{16,0},... | collective-permute-start | bytes 208904 | tf_op jit(solution)/shard_map/ppermute | solution.py:225
  47.2 2.6 %collective-permute-start.16 = (bf16[272,128]{1,0:T(8,128)(2,1)}, bf16[272,128]{1,0:T(8,128)(2,1)S(1)}, u32[]{:S(2)}, u32[]{:S(2)}) collective-permute-start(bf16[272,128]{1,0:T(8,128)(2,1)} %get-tuple-element.62), channel_id=1, source_target_pairs={{0,24},{2,26},{4,28},{6,30},{8,0},{10,2},{12,4},{14,6},{16,8},{18,... | collective-permute-start | bytes 208904 | tf_op jit(solution)/shard_map/ppermute | solution.py:225
  49.8 0.0 collective-permute-start.21
  49.8 0.8 collective-permute-done.14.refs_17_
  50.7 0.7 collective-permute-done.15.refs_18_
  51.4 0.7 collective-permute-done.16.refs_19_
  52.1 0.0 collective-permute-start.18
  52.1 0.0 collective-permute-done.13.refs_8_
  52.2 0.5 collective-permute-start.19
  52.7 0.3 collective-permute-done.20.refs_11_
  52.9 0.7 collective-permute-done.18.refs_7_
  53.7 0.4 collective-permute-done.19.refs_9_
  54.2 0.2 copy-done.13
  54.4 0.4 copy-done.14
  54.8 13.1 %krylov.1 = (f32[128,128]{1,0:T(8,128)}, f32[128,128]{1,0:T(8,128)}, f32[128,128]{1,0:T(8,128)}, f32[32,1,128]{2,1,0:T(1,128)}) custom-call(f32[1,128]{1,0:T(1,128)} %bitcast.20, f32[128,128]{1,0:T(8,128)} %start.1, bf16[2048,128]{1,0:T(8,128)(2,1)} %subs_in.5, bf16[8,128,128]{2,1,0:T(8,128)(2,1)} %bitcast.19, bf16[8,128,128]{2,1,0:T(8,128)(2,1)} %copy-done, ...), custom_call_target="tpu_custom_call" | custom-call | tf_op jit(solution)/shard_map/krylov/pallas_call | solution.py:401
  67.8 14.0 %all_to_all.5.dots = f32[32,1,128]{2,1,0:T(1,128)} all-to-all(f32[32,1,128]{2,1,0:T(1,128)} %get-tuple-element.74), channel_id=1, replica_groups=mesh['loop'=16,'own'=2] {'loop','own'}, dimensions={0} | all-to-all | bytes 32768 | tf_op jit(solution)/shard_map/all_to_all | solution.py:523
  81.9 1.9 %last_step.1 = (f32[128,128]{1,0:T(8,128)}, f32[128,128]{1,0:T(8,128)}) custom-call(f32[32,1,128]{2,1,0:T(1,128)} %all_to_all.5.dots, f32[128,128]{1,0:T(8,128)} %start.1, f32[128,128]{1,0:T(8,128)} %get-tuple-element.75.first, f32[128,128]{1,0:T(8,128)} %get-tuple-element.76.second, f32[128,128]{1,0:T(8,128)} %get-tuple-element.77.third), custom_call_target="tpu_custom_call" | custom-call | tf_op jit(solution)/shard_map/last_step/pallas_call | solution.py:432
  (46 shorter events, 0.1 us)
Async XLA Ops:
  0.6 10.1 %collective-permute-start.2 = (bf16[8,128,128]{2,1,0:T(8,128)(2,1)}, bf16[8,128,128]{2,1,0:T(8,128)(2,1)S(1)}, u32[]{:S(2)}, u32[]{:S(2)}) collective-permute-start(bf16[8,128,128]{2,1,0:T(8,128)(2,1)} %bitcast.14), channel_id=1, source_target_pairs={{0,2},{2,0},{4,6},{6,4},{8,10},{10,8},{12,14},{14,12},{16,18},{18,... | collective-permute-start | bytes 786440 | tf_op jit(solution)/shard_map/ppermute | solution.py:465
  1.1 9.8 %collective-permute-start.1 = (bf16[8,128,128]{2,1,0:T(8,128)(2,1)}, bf16[8,128,128]{2,1,0:T(8,128)(2,1)S(1)}, u32[]{:S(2)}, u32[]{:S(2)}) collective-permute-start(bf16[8,128,128]{2,1,0:T(8,128)(2,1)} %bitcast.15), channel_id=1, source_target_pairs={{0,4},{2,6},{8,0},{10,2},{16,8},{18,10},{24,16},{26,18},{28,24},{3... | collective-permute-start | bytes 786440 | tf_op jit(solution)/shard_map/ppermute | solution.py:459
  3.7 8.6 %collective-permute-start = (bf16[8,128,128]{2,1,0:T(8,128)(2,1)}, bf16[8,128,128]{2,1,0:T(8,128)(2,1)S(1)}, u32[]{:S(2)}, u32[]{:S(2)}) collective-permute-start(bf16[8,128,128]{2,1,0:T(8,128)(2,1)} %bitcast.16), channel_id=1, source_target_pairs={{0,8},{2,10},{8,16},{10,18},{16,24},{18,26},{24,28},{26,30},{28,20... | collective-permute-start | bytes 786440 | tf_op jit(solution)/shard_map/ppermute | solution.py:456
  10.7 31.6 %copy-start = (bf16[8,128,128]{2,1,0:T(8,128)(2,1)}, bf16[8,128,128]{2,1,0:T(8,128)(2,1)S(1)}, u32[]{:S(2)}) copy-start(bf16[8,128,128]{2,1,0:T(8,128)(2,1)S(1)} %collective-permute-done.2.refs_1_) | copy-start | bytes 786436
  10.9 31.5 %copy-start.1 = (bf16[8,128,128]{2,1,0:T(8,128)(2,1)}, bf16[8,128,128]{2,1,0:T(8,128)(2,1)S(1)}, u32[]{:S(2)}) copy-start(bf16[8,128,128]{2,1,0:T(8,128)(2,1)S(1)} %collective-permute-done.1.refs_2_) | copy-start | bytes 786436
  12.3 30.1 %copy-start.2 = (bf16[8,128,128]{2,1,0:T(8,128)(2,1)}, bf16[8,128,128]{2,1,0:T(8,128)(2,1)S(1)}, u32[]{:S(2)}) copy-start(bf16[8,128,128]{2,1,0:T(8,128)(2,1)S(1)} %collective-permute-done.refs_14_) | copy-start | bytes 786436
  12.3 2.5 %collective-permute-start.5 = (bf16[2,2,4,160,128]{4,3,2,1,0:T(8,128)(2,1)}, bf16[2,2,4,160,128]{4,3,2,1,0:T(8,128)(2,1)S(1)}, u32[]{:S(2)}, u32[]{:S(2)}) collective-permute-start(bf16[2,2,4,160,128]{4,3,2,1,0:T(8,128)(2,1)} %rhs.2), channel_id=1, source_target_pairs={{0,2},{2,0},{4,6},{6,4},{8,10},{10,8},{12,14},{14,12},{16,18},{18,... | collective-permute-start | bytes 1966088 | tf_op jit(solution)/shard_map/ppermute | solution.py:465
  12.3 10.5 %collective-permute-start.3 = (bf16[8,128,128]{2,1,0:T(8,128)(2,1)S(1)}, bf16[8,128,128]{2,1,0:T(8,128)(2,1)S(1)}, u32[]{:S(2)}, u32[]{:S(2)}) collective-permute-start(bf16[8,128,128]{2,1,0:T(8,128)(2,1)S(1)} %collective-permute-done.refs_14_), channel_id=1, source_target_pairs={{0,8},{2,10},{8,16},{10,18},{16,24},{18,26},{24,28},{26,30},{28,20... | collective-permute-start | bytes 786440 | tf_op jit(solution)/shard_map/ppermute | solution.py:456
  12.9 9.9 %collective-permute-start.6 = (bf16[8,128,128]{2,1,0:T(8,128)(2,1)S(1)}, bf16[8,128,128]{2,1,0:T(8,128)(2,1)S(1)}, u32[]{:S(2)}, u32[]{:S(2)}) collective-permute-start(bf16[8,128,128]{2,1,0:T(8,128)(2,1)S(1)} %collective-permute-done.1.refs_2_), channel_id=1, source_target_pairs={{0,2},{2,0},{4,6},{6,4},{8,10},{10,8},{12,14},{14,12},{16,18},{18,... | collective-permute-start | bytes 786440 | tf_op jit(solution)/shard_map/ppermute | solution.py:465
  13.0 9.8 %collective-permute-start.7 = (bf16[8,128,128]{2,1,0:T(8,128)(2,1)S(1)}, bf16[8,128,128]{2,1,0:T(8,128)(2,1)S(1)}, u32[]{:S(2)}, u32[]{:S(2)}) collective-permute-start(bf16[8,128,128]{2,1,0:T(8,128)(2,1)S(1)} %collective-permute-done.refs_14_), channel_id=1, source_target_pairs={{0,2},{2,0},{4,6},{6,4},{8,10},{10,8},{12,14},{14,12},{16,18},{18,... | collective-permute-start | bytes 786440 | tf_op jit(solution)/shard_map/ppermute | solution.py:465
  13.4 9.5 %collective-permute-start.4 = (bf16[8,128,128]{2,1,0:T(8,128)(2,1)S(1)}, bf16[8,128,128]{2,1,0:T(8,128)(2,1)S(1)}, u32[]{:S(2)}, u32[]{:S(2)}) collective-permute-start(bf16[8,128,128]{2,1,0:T(8,128)(2,1)S(1)} %collective-permute-done.1.refs_2_), channel_id=1, source_target_pairs={{0,4},{2,6},{8,0},{10,2},{16,8},{18,10},{24,16},{26,18},{28,24},{3... | collective-permute-start | bytes 786440 | tf_op jit(solution)/shard_map/ppermute | solution.py:459
  14.8 0.9 %copy-start.21 = (bf16[2,2,4,160,128]{4,3,2,1,0:T(8,128)(2,1)}, bf16[2,2,4,160,128]{4,3,2,1,0:T(8,128)(2,1)S(1)}, u32[]{:S(2)}) copy-start(bf16[2,2,4,160,128]{4,3,2,1,0:T(8,128)(2,1)S(1)} %collective-permute-done.5.refs_0_) | copy-start | bytes 1966084
  22.8 31.3 %copy-start.4 = (bf16[8,128,128]{2,1,0:T(8,128)(2,1)}, bf16[8,128,128]{2,1,0:T(8,128)(2,1)S(1)}, u32[]{:S(2)}) copy-start(bf16[8,128,128]{2,1,0:T(8,128)(2,1)S(1)} %collective-permute-done.6.refs_3_) | copy-start | bytes 786436
  22.8 31.2 %copy-start.5 = (bf16[8,128,128]{2,1,0:T(8,128)(2,1)}, bf16[8,128,128]{2,1,0:T(8,128)(2,1)S(1)}, u32[]{:S(2)}) copy-start(bf16[8,128,128]{2,1,0:T(8,128)(2,1)S(1)} %collective-permute-done.7.refs_15_) | copy-start | bytes 786436
  22.8 31.2 %copy-start.3 = (bf16[8,128,128]{2,1,0:T(8,128)(2,1)}, bf16[8,128,128]{2,1,0:T(8,128)(2,1)S(1)}, u32[]{:S(2)}) copy-start(bf16[8,128,128]{2,1,0:T(8,128)(2,1)S(1)} %collective-permute-done.3.refs_12_) | copy-start | bytes 786436
  22.9 31.2 %copy-start.6 = (bf16[8,128,128]{2,1,0:T(8,128)(2,1)}, bf16[8,128,128]{2,1,0:T(8,128)(2,1)S(1)}, u32[]{:S(2)}) copy-start(bf16[8,128,128]{2,1,0:T(8,128)(2,1)S(1)} %collective-permute-done.4.refs_4_) | copy-start | bytes 786436
  22.9 19.5 %collective-permute-start.8 = (bf16[8,128,128]{2,1,0:T(8,128)(2,1)S(1)}, bf16[8,128,128]{2,1,0:T(8,128)(2,1)S(1)}, u32[]{:S(2)}, u32[]{:S(2)}) collective-permute-start(bf16[8,128,128]{2,1,0:T(8,128)(2,1)S(1)} %collective-permute-done.3.refs_12_), channel_id=1, source_target_pairs={{0,8},{2,10},{8,16},{10,18},{16,24},{18,26},{24,28},{26,30},{28,20... | collective-permute-start | bytes 786440 | tf_op jit(solution)/shard_map/ppermute | solution.py:456
  23.5 18.9 %collective-permute-start.9 = (bf16[8,128,128]{2,1,0:T(8,128)(2,1)S(1)}, bf16[8,128,128]{2,1,0:T(8,128)(2,1)S(1)}, u32[]{:S(2)}, u32[]{:S(2)}) collective-permute-start(bf16[8,128,128]{2,1,0:T(8,128)(2,1)S(1)} %collective-permute-done.4.refs_4_), channel_id=1, source_target_pairs={{0,4},{2,6},{8,0},{10,2},{16,8},{18,10},{24,16},{26,18},{28,24},{3... | collective-permute-start | bytes 786440 | tf_op jit(solution)/shard_map/ppermute | solution.py:459
  24.9 11.0 %collective-permute-start.10 = (bf16[4,176,128]{2,1,0:T(8,128)(2,1)}, bf16[4,176,128]{2,1,0:T(8,128)(2,1)S(1)}, u32[]{:S(2)}, u32[]{:S(2)}) collective-permute-start(bf16[4,176,128]{2,1,0:T(8,128)(2,1)} %get-tuple-element.51), channel_id=1, source_target_pairs={{0,4},{1,5},{2,6},{3,7},{4,0},{5,1},{6,2},{7,3},{8,12},{9,13},{10,... | collective-permute-start | bytes 540680 | tf_op jit(solution)/shard_map/ppermute | solution.py:204
  26.5 9.4 %collective-permute-start.11 = (bf16[4,176,128]{2,1,0:T(8,128)(2,1)}, bf16[4,176,128]{2,1,0:T(8,128)(2,1)S(1)}, u32[]{:S(2)}, u32[]{:S(2)}) collective-permute-start(bf16[4,176,128]{2,1,0:T(8,128)(2,1)} %get-tuple-element.52), channel_id=1, source_target_pairs={{0,1},{1,0},{2,3},{3,2},{4,5},{5,4},{6,7},{7,6},{8,9},{9,8},{10,11... | collective-permute-start | bytes 540680 | tf_op jit(solution)/shard_map/ppermute | solution.py:204
  28.0 11.7 %collective-permute-start.12 = (bf16[4,176,128]{2,1,0:T(8,128)(2,1)}, bf16[4,176,128]{2,1,0:T(8,128)(2,1)S(1)}, u32[]{:S(2)}, u32[]{:S(2)}) collective-permute-start(bf16[4,176,128]{2,1,0:T(8,128)(2,1)} %get-tuple-element.53), channel_id=1, source_target_pairs={{0,5},{1,4},{2,7},{3,6},{4,1},{5,0},{6,3},{7,2},{8,13},{9,12},{10,... | collective-permute-start | bytes 540680 | tf_op jit(solution)/shard_map/ppermute | solution.py:204
  36.0 3.8 %copy-start.15 = (bf16[4,176,128]{2,1,0:T(8,128)(2,1)}, bf16[4,176,128]{2,1,0:T(8,128)(2,1)S(1)}, u32[]{:S(2)}) copy-start(bf16[4,176,128]{2,1,0:T(8,128)(2,1)S(1)} %collective-permute-done.10.refs_1_) | copy-start | bytes 540676
  36.0 3.8 %copy-start.16 = (bf16[4,176,128]{2,1,0:T(8,128)(2,1)}, bf16[4,176,128]{2,1,0:T(8,128)(2,1)S(1)}, u32[]{:S(2)}) copy-start(bf16[4,176,128]{2,1,0:T(8,128)(2,1)S(1)} %collective-permute-done.11.refs_2_) | copy-start | bytes 540676
  39.8 0.7 copy-start.17
  42.4 11.7 %copy-start.7 = (bf16[8,128,128]{2,1,0:T(8,128)(2,1)}, bf16[8,128,128]{2,1,0:T(8,128)(2,1)S(1)}, u32[]{:S(2)}) copy-start(bf16[8,128,128]{2,1,0:T(8,128)(2,1)S(1)} %collective-permute-done.8.refs_10_) | copy-start | bytes 786436
  42.4 11.7 %copy-start.8 = (bf16[8,128,128]{2,1,0:T(8,128)(2,1)}, bf16[8,128,128]{2,1,0:T(8,128)(2,1)S(1)}, u32[]{:S(2)}) copy-start(bf16[8,128,128]{2,1,0:T(8,128)(2,1)S(1)} %collective-permute-done.9.refs_6_) | copy-start | bytes 786436
  42.4 9.7 %collective-permute-start.13 = (bf16[8,128,128]{2,1,0:T(8,128)(2,1)S(1)}, bf16[8,128,128]{2,1,0:T(8,128)(2,1)S(1)}, u32[]{:S(2)}, u32[]{:S(2)}) collective-permute-start(bf16[8,128,128]{2,1,0:T(8,128)(2,1)S(1)} %collective-permute-done.8.refs_10_), channel_id=1, source_target_pairs={{0,8},{2,10},{8,16},{10,18},{16,24},{18,26},{24,28},{26,30},{28,20... | collective-permute-start | bytes 786440 | tf_op jit(solution)/shard_map/ppermute | solution.py:456
  42.5 8.2 %collective-permute-start.14 = (bf16[272,128]{1,0:T(8,128)(2,1)}, bf16[272,128]{1,0:T(8,128)(2,1)S(1)}, u32[]{:S(2)}, u32[]{:S(2)}) collective-permute-start(bf16[272,128]{1,0:T(8,128)(2,1)} %get-tuple-element.60), channel_id=1, source_target_pairs={{0,8},{2,10},{4,12},{6,14},{8,16},{10,18},{12,20},{14,22},{16,24},... | collective-permute-start | bytes 208904 | tf_op jit(solution)/shard_map/ppermute | solution.py:225
  42.7 8.7 %collective-permute-start.15 = (bf16[272,128]{1,0:T(8,128)(2,1)}, bf16[272,128]{1,0:T(8,128)(2,1)S(1)}, u32[]{:S(2)}, u32[]{:S(2)}) collective-permute-start(bf16[272,128]{1,0:T(8,128)(2,1)} %get-tuple-element.61), channel_id=1, source_target_pairs={{0,16},{2,18},{4,20},{6,22},{8,24},{10,26},{12,28},{14,30},{16,0},... | collective-permute-start | bytes 208904 | tf_op jit(solution)/shard_map/ppermute | solution.py:225
  47.2 5.0 %collective-permute-start.16 = (bf16[272,128]{1,0:T(8,128)(2,1)}, bf16[272,128]{1,0:T(8,128)(2,1)S(1)}, u32[]{:S(2)}, u32[]{:S(2)}) collective-permute-start(bf16[272,128]{1,0:T(8,128)(2,1)} %get-tuple-element.62), channel_id=1, source_target_pairs={{0,24},{2,26},{4,28},{6,30},{8,0},{10,2},{12,4},{14,6},{16,8},{18,... | collective-permute-start | bytes 208904 | tf_op jit(solution)/shard_map/ppermute | solution.py:225
  49.8 2.8 %collective-permute-start.21 = (bf16[8,128,128]{2,1,0:T(8,128)(2,1)S(1)}, bf16[8,128,128]{2,1,0:T(8,128)(2,1)S(1)}, u32[]{:S(2)}, u32[]{:S(2)}) collective-permute-start(bf16[8,128,128]{2,1,0:T(8,128)(2,1)S(1)} %collective-permute-done.3.refs_12_), channel_id=1, source_target_pairs={{0,2},{2,0},{4,6},{6,4},{8,10},{10,8},{12,14},{14,12},{16,18},{18,... | collective-permute-start | bytes 786440 | tf_op jit(solution)/shard_map/ppermute | solution.py:465
  50.6 3.5 %copy-start.18 = (bf16[272,128]{1,0:T(8,128)(2,1)}, bf16[272,128]{1,0:T(8,128)(2,1)S(1)}, u32[]{:S(2)}) copy-start(bf16[272,128]{1,0:T(8,128)(2,1)S(1)} %collective-permute-done.14.refs_17_) | copy-start | bytes 208900
  50.6 2.0 %collective-permute-start.17 = (bf16[8,128,128]{2,1,0:T(8,128)(2,1)S(1)}, bf16[8,128,128]{2,1,0:T(8,128)(2,1)S(1)}, u32[]{:S(2)}, u32[]{:S(2)}) collective-permute-start(bf16[8,128,128]{2,1,0:T(8,128)(2,1)S(1)} %collective-permute-done.4.refs_4_), channel_id=1, source_target_pairs={{0,2},{2,0},{4,6},{6,4},{8,10},{10,8},{12,14},{14,12},{16,18},{18,... | collective-permute-start | bytes 786440 | tf_op jit(solution)/shard_map/ppermute | solution.py:465
  51.4 2.7 %copy-start.19 = (bf16[272,128]{1,0:T(8,128)(2,1)}, bf16[272,128]{1,0:T(8,128)(2,1)S(1)}, u32[]{:S(2)}) copy-start(bf16[272,128]{1,0:T(8,128)(2,1)S(1)} %collective-permute-done.15.refs_18_) | copy-start | bytes 208900
  51.4 1.5 %collective-permute-start.20 = (bf16[8,128,128]{2,1,0:T(8,128)(2,1)S(1)}, bf16[8,128,128]{2,1,0:T(8,128)(2,1)S(1)}, u32[]{:S(2)}, u32[]{:S(2)}) collective-permute-start(bf16[8,128,128]{2,1,0:T(8,128)(2,1)S(1)} %collective-permute-done.8.refs_10_), channel_id=1, source_target_pairs={{0,2},{2,0},{4,6},{6,4},{8,10},{10,8},{12,14},{14,12},{16,18},{18,... | collective-permute-start | bytes 786440 | tf_op jit(solution)/shard_map/ppermute | solution.py:465
  52.1 2.0 %copy-start.20 = (bf16[272,128]{1,0:T(8,128)(2,1)}, bf16[272,128]{1,0:T(8,128)(2,1)S(1)}, u32[]{:S(2)}) copy-start(bf16[272,128]{1,0:T(8,128)(2,1)S(1)} %collective-permute-done.16.refs_19_) | copy-start | bytes 208900
  52.1 1.5 %collective-permute-start.18 = (bf16[8,128,128]{2,1,0:T(8,128)(2,1)S(1)}, bf16[8,128,128]{2,1,0:T(8,128)(2,1)S(1)}, u32[]{:S(2)}, u32[]{:S(2)}) collective-permute-start(bf16[8,128,128]{2,1,0:T(8,128)(2,1)S(1)} %collective-permute-done.9.refs_6_), channel_id=1, source_target_pairs={{0,2},{2,0},{4,6},{6,4},{8,10},{10,8},{12,14},{14,12},{16,18},{18,... | collective-permute-start | bytes 786440 | tf_op jit(solution)/shard_map/ppermute | solution.py:465
  52.1 2.0 %copy-start.9 = (bf16[8,128,128]{2,1,0:T(8,128)(2,1)}, bf16[8,128,128]{2,1,0:T(8,128)(2,1)S(1)}, u32[]{:S(2)}) copy-start(bf16[8,128,128]{2,1,0:T(8,128)(2,1)S(1)} %collective-permute-done.13.refs_8_) | copy-start | bytes 786436
  52.2 1.9 %collective-permute-start.19 = (bf16[8,128,128]{2,1,0:T(8,128)(2,1)S(1)}, bf16[8,128,128]{2,1,0:T(8,128)(2,1)S(1)}, u32[]{:S(2)}, u32[]{:S(2)}) collective-permute-start(bf16[8,128,128]{2,1,0:T(8,128)(2,1)S(1)} %collective-permute-done.13.refs_8_), channel_id=1, source_target_pairs={{0,2},{2,0},{4,6},{6,4},{8,10},{10,8},{12,14},{14,12},{16,18},{18,... | collective-permute-start | bytes 786440 | tf_op jit(solution)/shard_map/ppermute | solution.py:465
  52.7 1.5 %copy-start.10 = (bf16[8,128,128]{2,1,0:T(8,128)(2,1)}, bf16[8,128,128]{2,1,0:T(8,128)(2,1)S(1)}, u32[]{:S(2)}) copy-start(bf16[8,128,128]{2,1,0:T(8,128)(2,1)S(1)} %collective-permute-done.21.refs_13_) | copy-start | bytes 786436
  52.7 1.5 %copy-start.11 = (bf16[8,128,128]{2,1,0:T(8,128)(2,1)}, bf16[8,128,128]{2,1,0:T(8,128)(2,1)S(1)}, u32[]{:S(2)}) copy-start(bf16[8,128,128]{2,1,0:T(8,128)(2,1)S(1)} %collective-permute-done.17.refs_5_) | copy-start | bytes 786436
  52.9 1.2 %copy-start.12 = (bf16[8,128,128]{2,1,0:T(8,128)(2,1)}, bf16[8,128,128]{2,1,0:T(8,128)(2,1)S(1)}, u32[]{:S(2)}) copy-start(bf16[8,128,128]{2,1,0:T(8,128)(2,1)S(1)} %collective-permute-done.20.refs_11_) | copy-start | bytes 786436
  53.7 0.7 copy-start.13
  54.1 0.7 copy-start.14

commit v10 on v9

--- a/solution.py
+++ b/solution.py
@@ -11,7 +11,8 @@
 CHUNK = 48
 FACT_ROWS = 16
 ridge = 0.05
-VMEM_LIMIT = 60 * 2**20
+MIB = 2**20
+VMEM_LIMIT = 60 * MIB
 f32 = jnp.float32
 bf16 = jnp.bfloat16
 
@@ -47,7 +48,7 @@
     half, owners, own_rows,
 ):
     if half == 0:
-        given_in, refs, given = refs[0], refs[1:-1], refs[-1]
+        given, refs = refs[0], refs[1:]
     outs, (ratings, runs, words, subs, table, sums, arrived, loaded) = refs[:-8], refs[-8:]
     steps, slots, tile = ratings.shape[0], ratings.shape[1], ratings.shape[2]
     rank = words.shape[-1]
@@ -76,16 +77,11 @@
         copy.start()
     for step in range(steps):
         load(step).start()
-    if half == 0:
-        gift = pltpu.make_async_copy(given_in, given, loaded.at[3])
-        gift.start()
     tables[0].wait()
     table[...] = subs[...].astype(f32)
     tables[1].wait()
     tables[2].wait()
 
-    if half == 0:
-        gift.wait()
     eye = (
         lax.broadcasted_iota(jnp.int32, (tile, tile), 0)
         == lax.broadcasted_iota(jnp.int32, (tile, tile), 1)
@@ -149,7 +145,8 @@
     return pl.pallas_call(
         functools.partial(rhs_kernel, half=half, owners=owners, own_rows=own_rows),
         in_specs=[pl.BlockSpec(memory_space=pltpu.SMEM)] * 4
-        + [anywhere] * (5 - half),
+        + [anywhere] * 4
+        + [whole] * (1 - half),
         out_specs=[whole] * len(shapes),
         out_shape=[jax.ShapeDtypeStruct(shape, bf16) for shape in shapes],
         scratch_shapes=[
@@ -160,10 +157,9 @@
             pltpu.VMEM(subs.shape, f32),
             pltpu.VMEM((2, owners * own_rows, rank), f32),
             pltpu.SemaphoreType.DMA((steps,)),
-            pltpu.SemaphoreType.DMA((4,)),
-        ]
-        + ([pltpu.VMEM(given.shape, bf16)] if half == 0 else []),
-        compiler_params=pltpu.CompilerParams(vmem_limit_bytes=VMEM_LIMIT),
+            pltpu.SemaphoreType.DMA((3,)),
+        ],
+        compiler_params=pltpu.CompilerParams(vmem_limit_bytes=VMEM_LIMIT if half else 50 * MIB),
         cost_estimate=pl.CostEstimate(
             flops=8 * ratings.size * rank, bytes_accessed=8 * ratings.size, transcendentals=0
         ),
@@ -212,7 +208,7 @@
         in_specs=[whole] * len(parts),
         out_specs=[whole] * levels,
         out_shape=[shape] * levels,
-        compiler_params=pltpu.CompilerParams(vmem_limit_bytes=VMEM_LIMIT),
+        compiler_params=pltpu.CompilerParams(vmem_limit_bytes=16 * MIB),
         name="chip",
     )(*given)
 
@@ -406,7 +402,7 @@
         out_specs=[whole] * 4,
         out_shape=[vector, vector, vector, jax.ShapeDtypeStruct((devices, 1, rank), f32)],
         scratch_shapes=scratch,
-        compiler_params=pltpu.CompilerParams(vmem_limit_bytes=VMEM_LIMIT),
+        compiler_params=pltpu.CompilerParams(vmem_limit_bytes=44 * MIB),
         name="krylov",
     )(activity, start, subs, *pieces, *terms)
 
@@ -434,7 +430,7 @@
         in_specs=[whole] * 5,
         out_specs=[whole] * 2,
         out_shape=[vector, vector],
-        compiler_params=pltpu.CompilerParams(vmem_limit_bytes=VMEM_LIMIT),
+        compiler_params=pltpu.CompilerParams(vmem_limit_bytes=8 * MIB),
         name="last_step",
     )(dots, start, first, second, third)
 

time: 84.1 us -> 75.7 us (0.900)
  Pallas kernels: 30.8 us -> 23.3 us
  local copies, waits for them, and re-layouts: 2.18 us -> 0.04 us
  starting transfers between devices: 19.3 us -> 20.7 us
    pallas_call x1, Pallas kernels: 13.1 us -> 10.5 us  [krylov(): pl.pallas_call(functools.partial(steps_kernel, shards=len(pieces), levels...]
    unnamed x44 -> x18, local copies, waits for them, and re-layouts: 2.18 us -> 0.04 us
    pallas_call x2, Pallas kernels: 13.9 us -> 11.9 us  [rhs_sums(): pl.pallas_call(functools.partial(rhs_kernel, half=half, owners=owners, ow...]
    pallas_call x1, Pallas kernels: 1.93 us -> 0.07 us  [reduce_chip(): pl.pallas_call(functools.partial(chip_kernel, own_rows=own_rows, spans=sp...]
    ppermute x4, waiting for transfers between devices: 1.38 us -> 2.43 us  [ring_round(): up = lax.ppermute(up, 'loop', shift(1))]
    ppermute x3, starting transfers between devices: 5.45 us -> 4.43 us  [ring_round(): down = lax.ppermute(down, 'loop', shift(-1))]
    ppermute x4, starting transfers between devices: 1.44 us -> 2.4 us  [ring_round(): up = lax.ppermute(up, 'loop', shift(1))]
    pallas_call x1, Pallas kernels: 1.86 us -> 0.91 us  [last_step(): pl.pallas_call(last_kernel, in_specs=[whole] * 5, out_specs=[whole] * 2,...]
  transfers between devices with their start and end apart: 22 -> 22, of which waited for: 10 -> 9; matrix products, arithmetic and copies ran while one was open for 0% -> 0% of each run, Pallas kernels for 19% -> 16%
where the time goes in v10:
time: 75.7 us; the launch traced here: 75.4 us
  Pallas kernels  23.3 us (31%)
  starting transfers between devices  20.7 us (27%)
  waiting for transfers between devices  16.9 us (22%)
  blocking collectives  13.6 us (18%)
  between operations  0.85 us (1%)
    all_to_all x1, blocking collectives, on_device(): everyone = lax.all_to_all(dots, AXES, 0, 0, tiled=True)  13.6 us
    pallas_call x2, Pallas kernels, rhs_sums(): pl.pallas_call(functools.partial(rhs_kernel, half=half, owners=owners, ow...  11.9 us
    ppermute x3, waiting for transfers between devices, reduce_chip(): given.append(lax.ppermute(part, AXES, pairs) if o or column else part)  10.8 us
    pallas_call x1, Pallas kernels, krylov(): pl.pallas_call(functools.partial(steps_kernel, shards=len(pieces), levels...  10.5 us
    ppermute x3, starting transfers between devices, reduce_levels(): terms.append(lax.ppermute(total[up], 'loop', shift))  8.28 us
    ppermute x3, starting transfers between devices, ring_round(): down = lax.ppermute(down, 'loop', shift(-1))  4.43 us
    ppermute x3, starting transfers between devices, reduce_chip(): given.append(lax.ppermute(part, AXES, pairs) if o or column else part)  3.49 us
    ppermute x4, waiting for transfers between devices, ring_round(): up = lax.ppermute(up, 'loop', shift(1))  2.43 us
  transfers between devices with their start and end apart: 22, of which 9 were waited for; matrix products, arithmetic and copies ran while one was open for 0% of the time, Pallas kernels for 16%

profile of v10, /device:TPU:0, one launch (start us, length us, event | category | flops | bytes accessed | tf_op | source)
XLA Modules:
  0.0 75.4 jit_solution(5679860645927163309)
XLA Ops:
  0.7 0.5 collective-permute-start.2
  1.2 2.5 %collective-permute-start.1 = (bf16[8,128,128]{2,1,0:T(8,128)(2,1)}, bf16[8,128,128]{2,1,0:T(8,128)(2,1)S(1)}, u32[]{:S(2)}, u32[]{:S(2)}) collective-permute-start(bf16[8,128,128]{2,1,0:T(8,128)(2,1)} %bitcast.15), channel_id=1, source_target_pairs={{0,4},{2,6},{8,0},{10,2},{16,8},{18,10},{24,16},{26,18},{28,24},{3... | collective-permute-start | bytes 786440 | tf_op jit(solution)/shard_map/ppermute | solution.py:455
  3.8 0.2 collective-permute-start
  3.9 6.8 %rhs.2 = bf16[2,2,4,160,128]{4,3,2,1,0:T(8,128)(2,1)} custom-call(s32[8,16]{1,0:T(8,128)} %bitcast.23, s32[8,16]{1,0:T(8,128)} %bitcast.25, s32[8,16]{1,0:T(8,128)} %bitcast.27, s32[1,16]{1,0:T(1,128)} %bitcast.29, bf16[16,8,128,128]{3,2,1,0:T(8,128)(2,1)} %bitcast.31, s32[16,8,2,128]{3,2,1,0:T(2,128)} %bitcast.21, bf16[8,128,128]{2,1,0:T(8,128)(2,1)} %bitcast.17, ...), custom_call_target="tpu_custom_call" | custom-call | flops 2147483648 | bytes 16777216 | tf_op jit(solution)/shard_map/rhs/pallas_call | solution.py:145
  10.8 0.0 copy-start.2
  10.8 0.0 copy-start.3
  10.8 0.0 collective-permute-done.2.refs_1_
  10.8 0.2 collective-permute-done.1.refs_2_
  11.0 1.4 %collective-permute-done.refs_14_ = bf16[8,128,128]{2,1,0:T(8,128)(2,1)S(1)} collective-permute-done((bf16[8,128,128]{2,1,0:T(8,128)(2,1)}, bf16[8,128,128]{2,1,0:T(8,128)(2,1)S(1)}, u32[]{:S(2)}, u32[]{:S(2)}) %collective-permute-start) | collective-permute-done | bytes 262176 | tf_op jit(solution)/shard_map/ppermute | solution.py:452
  12.4 0.5 collective-permute-start.3
  12.9 0.2 collective-permute-start.6
  13.1 0.3 collective-permute-start.7
  13.4 1.5 %collective-permute-start.4 = (bf16[8,128,128]{2,1,0:T(8,128)(2,1)S(1)}, bf16[8,128,128]{2,1,0:T(8,128)(2,1)S(1)}, u32[]{:S(2)}, u32[]{:S(2)}) collective-permute-start(bf16[8,128,128]{2,1,0:T(8,128)(2,1)S(1)} %collective-permute-done.1.refs_2_), channel_id=1, source_target_pairs={{0,4},{2,6},{8,0},{10,2},{16,8},{18,10},{24,16},{26,18},{28,24},{3... | collective-permute-start | bytes 786440 | tf_op jit(solution)/shard_map/ppermute | solution.py:455
  15.0 5.0 %rhs.3 = (bf16[4,176,128]{2,1,0:T(8,128)(2,1)S(1)}, bf16[4,176,128]{2,1,0:T(8,128)(2,1)S(1)}, bf16[4,176,128]{2,1,0:T(8,128)(2,1)S(1)}, bf16[4,176,128]{2,1,0:T(8,128)(2,1)S(1)}) custom-call(s32[8,16]{1,0:T(8,128)S(1)} %bitcast.24, s32[8,16]{1,0:T(8,128)S(1)} %bitcast.26, s32[8,16]{1,0:T(8,128)S(1)} %bitcast.28, s32[1,16]{1,0:T(1,128)S(1)} %bitcast.30, ...), custom_call_target="tpu_custom_call" | custom-call | flops 2147483648 | bytes 16777216 | tf_op jit(solution)/shard_map/rhs/pallas_call | solution.py:145
  20.0 0.0 collective-permute-done.6.refs_3_
  20.0 1.0 %collective-permute-done.3.refs_12_ = bf16[8,128,128]{2,1,0:T(8,128)(2,1)S(1)} collective-permute-done((bf16[8,128,128]{2,1,0:T(8,128)(2,1)S(1)}, bf16[8,128,128]{2,1,0:T(8,128)(2,1)S(1)}, u32[]{:S(2)}, u32[]{:S(2)}) %collective-permute-start.3) | collective-permute-done | bytes 262176 | tf_op jit(solution)/shard_map/ppermute | solution.py:452
  21.1 0.7 collective-permute-done.4.refs_4_
  21.8 1.6 %collective-permute-start.8 = (bf16[8,128,128]{2,1,0:T(8,128)(2,1)S(1)}, bf16[8,128,128]{2,1,0:T(8,128)(2,1)S(1)}, u32[]{:S(2)}, u32[]{:S(2)}) collective-permute-start(bf16[8,128,128]{2,1,0:T(8,128)(2,1)S(1)} %collective-permute-done.3.refs_12_), channel_id=1, source_target_pairs={{0,8},{2,10},{8,16},{10,18},{16,24},{18,26},{24,28},{26,30},{28,20... | collective-permute-start | bytes 786440 | tf_op jit(solution)/shard_map/ppermute | solution.py:452
  23.4 0.4 collective-permute-start.9
  23.8 1.5 %collective-permute-start.10 = (bf16[4,176,128]{2,1,0:T(8,128)(2,1)S(1)}, bf16[4,176,128]{2,1,0:T(8,128)(2,1)S(1)}, u32[]{:S(2)}, u32[]{:S(2)}) collective-permute-start(bf16[4,176,128]{2,1,0:T(8,128)(2,1)S(1)} %get-tuple-element.51), channel_id=1, source_target_pairs={{0,4},{1,5},{2,6},{3,7},{4,0},{5,1},{6,2},{7,3},{8,12},{9,13},{10,... | collective-permute-start | bytes 540680 | tf_op jit(solution)/shard_map/ppermute | solution.py:200
  25.4 1.5 %collective-permute-start.11 = (bf16[4,176,128]{2,1,0:T(8,128)(2,1)S(1)}, bf16[4,176,128]{2,1,0:T(8,128)(2,1)S(1)}, u32[]{:S(2)}, u32[]{:S(2)}) collective-permute-start(bf16[4,176,128]{2,1,0:T(8,128)(2,1)S(1)} %get-tuple-element.52), channel_id=1, source_target_pairs={{0,1},{1,0},{2,3},{3,2},{4,5},{5,4},{6,7},{7,6},{8,9},{9,8},{10,11... | collective-permute-start | bytes 540680 | tf_op jit(solution)/shard_map/ppermute | solution.py:200
  26.9 0.4 collective-permute-start.12
  27.3 7.6 %collective-permute-done.10.refs_1_ = bf16[4,176,128]{2,1,0:T(8,128)(2,1)S(1)} collective-permute-done((bf16[4,176,128]{2,1,0:T(8,128)(2,1)S(1)}, bf16[4,176,128]{2,1,0:T(8,128)(2,1)S(1)}, u32[]{:S(2)}, u32[]{:S(2)}) %collective-permute-start.10) | collective-permute-done | bytes 180256 | tf_op jit(solution)/shard_map/ppermute | solution.py:200
  34.9 0.0 collective-permute-done.11.refs_2_
  34.9 3.2 %collective-permute-done.12.refs_3_ = bf16[4,176,128]{2,1,0:T(8,128)(2,1)S(1)} collective-permute-done((bf16[4,176,128]{2,1,0:T(8,128)(2,1)S(1)}, bf16[4,176,128]{2,1,0:T(8,128)(2,1)S(1)}, u32[]{:S(2)}, u32[]{:S(2)}) %collective-permute-start.12) | collective-permute-done | bytes 180256 | tf_op jit(solution)/shard_map/ppermute | solution.py:200
  38.1 0.1 chip.1
  38.2 0.0 collective-permute-done.8.refs_10_
  38.2 0.0 collective-permute-done.9.refs_6_
  38.2 0.1 collective-permute-start.13
  38.3 0.1 collective-permute-start.14
  38.4 5.6 %collective-permute-start.15 = (bf16[272,128]{1,0:T(8,128)(2,1)S(1)}, bf16[272,128]{1,0:T(8,128)(2,1)S(1)}, u32[]{:S(2)}, u32[]{:S(2)}) collective-permute-start(bf16[272,128]{1,0:T(8,128)(2,1)S(1)} %get-tuple-element.61), channel_id=1, source_target_pairs={{0,16},{2,18},{4,20},{6,22},{8,24},{10,26},{12,28},{14,30},{16,0},... | collective-permute-start | bytes 208904 | tf_op jit(solution)/shard_map/ppermute | solution.py:221
  44.0 2.6 %collective-permute-start.16 = (bf16[272,128]{1,0:T(8,128)(2,1)S(1)}, bf16[272,128]{1,0:T(8,128)(2,1)S(1)}, u32[]{:S(2)}, u32[]{:S(2)}) collective-permute-start(bf16[272,128]{1,0:T(8,128)(2,1)S(1)} %get-tuple-element.62), channel_id=1, source_target_pairs={{0,24},{2,26},{4,28},{6,30},{8,0},{10,2},{12,4},{14,6},{16,8},{18,... | collective-permute-start | bytes 208904 | tf_op jit(solution)/shard_map/ppermute | solution.py:221
  46.6 0.0 collective-permute-done.14.refs_17_
  46.6 0.5 collective-permute-start.17
  47.1 0.0 collective-permute-done.15.refs_18_
  47.1 0.1 collective-permute-start.20
  47.2 1.4 %collective-permute-done.16.refs_19_ = bf16[272,128]{1,0:T(8,128)(2,1)S(1)} collective-permute-done((bf16[272,128]{1,0:T(8,128)(2,1)S(1)}, bf16[272,128]{1,0:T(8,128)(2,1)S(1)}, u32[]{:S(2)}, u32[]{:S(2)}) %collective-permute-start.16) | collective-permute-done | bytes 69664 | tf_op jit(solution)/shard_map/ppermute | solution.py:221
  48.5 0.0 collective-permute-start.18
  48.5 0.0 collective-permute-done.13.refs_8_
  48.6 0.5 collective-permute-start.19
  49.1 0.0 collective-permute-done.21.refs_13_
  49.1 0.0 collective-permute-done.17.refs_5_
  49.1 0.0 collective-permute-done.20.refs_11_
  49.1 1.0 %collective-permute-done.18.refs_7_ = bf16[8,128,128]{2,1,0:T(8,128)(2,1)S(1)} collective-permute-done((bf16[8,128,128]{2,1,0:T(8,128)(2,1)S(1)}, bf16[8,128,128]{2,1,0:T(8,128)(2,1)S(1)}, u32[]{:S(2)}, u32[]{:S(2)}) %collective-permute-start.18) | collective-permute-done | bytes 262176 | tf_op jit(solution)/shard_map/ppermute | solution.py:461
  50.1 0.4 collective-permute-done.19.refs_9_
  50.5 10.5 %krylov.1 = (f32[128,128]{1,0:T(8,128)S(1)}, f32[128,128]{1,0:T(8,128)S(1)}, f32[128,128]{1,0:T(8,128)S(1)}, f32[32,1,128]{2,1,0:T(1,128)S(1)}) custom-call(f32[1,128]{1,0:T(1,128)S(1)} %bitcast.20, f32[128,128]{1,0:T(8,128)S(1)} %copy-done.2, bf16[2048,128]{1,0:T(8,128)(2,1)S(1)} %copy-done, bf16[8,128,128]{2,1,0:T(8,128)(2,1)S(1)} %bitcast.19, ...), custom_call_target="tpu_custom_call" | custom-call | tf_op jit(solution)/shard_map/krylov/pallas_call | solution.py:397
  60.9 13.6 %all_to_all.5.dots = f32[32,1,128]{2,1,0:T(1,128)S(1)} all-to-all(f32[32,1,128]{2,1,0:T(1,128)S(1)} %get-tuple-element.74), channel_id=1, replica_groups=mesh['loop'=16,'own'=2] {'loop','own'}, dimensions={0} | all-to-all | bytes 32768 | tf_op jit(solution)/shard_map/all_to_all | solution.py:519
  74.5 0.9 %last_step.1 = (f32[128,128]{1,0:T(8,128)}, f32[128,128]{1,0:T(8,128)}) custom-call(f32[32,1,128]{2,1,0:T(1,128)S(1)} %all_to_all.5.dots, f32[128,128]{1,0:T(8,128)S(1)} %copy-done.2, f32[128,128]{1,0:T(8,128)S(1)} %get-tuple-element.75.first, f32[128,128]{1,0:T(8,128)S(1)} %get-tuple-element.76.second, f32[128,128]{1,0:T(8,128)S(1)} %get-tuple-element.77.third), custom_call_target="tpu_custom_call" | custom-call | tf_op jit(solution)/shard_map/last_step/pallas_call | solution.py:428
  (20 shorter events, 0.0 us)
Async XLA Ops:
  0.6 14.3 %copy-start.1 = (bf16[1,8,128,128]{3,2,1,0:T(8,128)(2,1)S(1)}, bf16[1,8,128,128]{3,2,1,0:T(8,128)(2,1)}, u32[]{:S(2)}) copy-start(bf16[1,8,128,128]{3,2,1,0:T(8,128)(2,1)} %param.12) | copy-start | bytes 786436
  0.6 14.3 %copy-start = (bf16[2048,128]{1,0:T(8,128)(2,1)S(1)}, bf16[2048,128]{1,0:T(8,128)(2,1)}, u32[]{:S(2)}) copy-start(bf16[2048,128]{1,0:T(8,128)(2,1)} %subs_in.5) | copy-start | bytes 1572868
  0.7 14.3 %copy-start.4 = (s32[1,1,16,8,2,128]{5,4,3,2,1,0:T(2,128)S(1)}, s32[1,1,16,8,2,128]{5,4,3,2,1,0:T(2,128)}, u32[]{:S(2)}) copy-start(s32[1,1,16,8,2,128]{5,4,3,2,1,0:T(2,128)} %param.19) | copy-start | bytes 393220
  0.7 14.3 %copy-start.8 = (s32[1,1,16]{2,1,0:T(1,128)S(1)}, s32[1,1,16]{2,1,0:T(1,128)}, u32[]{:S(2)}) copy-start(s32[1,1,16]{2,1,0:T(1,128)} %param.18) | copy-start | bytes 196
  0.7 14.3 %copy-start.7 = (s32[1,1,16,8]{2,3,1,0:T(8,128)S(1)}, s32[1,1,16,8]{2,3,1,0:T(8,128)}, u32[]{:S(2)}) copy-start(s32[1,1,16,8]{2,3,1,0:T(8,128)} %param.17) | copy-start | bytes 1540
  0.7 14.3 %copy-start.6 = (s32[1,1,16,8]{2,3,1,0:T(8,128)S(1)}, s32[1,1,16,8]{2,3,1,0:T(8,128)}, u32[]{:S(2)}) copy-start(s32[1,1,16,8]{2,3,1,0:T(8,128)} %param.16) | copy-start | bytes 1540
  0.7 14.3 %copy-start.5 = (s32[1,1,16,8]{2,3,1,0:T(8,128)S(1)}, s32[1,1,16,8]{2,3,1,0:T(8,128)}, u32[]{:S(2)}) copy-start(s32[1,1,16,8]{2,3,1,0:T(8,128)} %param.15) | copy-start | bytes 1540
  0.7 10.1 %collective-permute-start.2 = (bf16[8,128,128]{2,1,0:T(8,128)(2,1)}, bf16[8,128,128]{2,1,0:T(8,128)(2,1)S(1)}, u32[]{:S(2)}, u32[]{:S(2)}) collective-permute-start(bf16[8,128,128]{2,1,0:T(8,128)(2,1)} %bitcast.14), channel_id=1, source_target_pairs={{0,2},{2,0},{4,6},{6,4},{8,10},{10,8},{12,14},{14,12},{16,18},{18,... | collective-permute-start | bytes 786440 | tf_op jit(solution)/shard_map/ppermute | solution.py:461
  1.2 9.8 %collective-permute-start.1 = (bf16[8,128,128]{2,1,0:T(8,128)(2,1)}, bf16[8,128,128]{2,1,0:T(8,128)(2,1)S(1)}, u32[]{:S(2)}, u32[]{:S(2)}) collective-permute-start(bf16[8,128,128]{2,1,0:T(8,128)(2,1)} %bitcast.15), channel_id=1, source_target_pairs={{0,4},{2,6},{8,0},{10,2},{16,8},{18,10},{24,16},{26,18},{28,24},{3... | collective-permute-start | bytes 786440 | tf_op jit(solution)/shard_map/ppermute | solution.py:455
  3.8 8.6 %collective-permute-start = (bf16[8,128,128]{2,1,0:T(8,128)(2,1)}, bf16[8,128,128]{2,1,0:T(8,128)(2,1)S(1)}, u32[]{:S(2)}, u32[]{:S(2)}) collective-permute-start(bf16[8,128,128]{2,1,0:T(8,128)(2,1)} %bitcast.16), channel_id=1, source_target_pairs={{0,8},{2,10},{8,16},{10,18},{16,24},{18,26},{24,28},{26,30},{28,20... | collective-permute-start | bytes 786440 | tf_op jit(solution)/shard_map/ppermute | solution.py:452
  10.8 39.7 %copy-start.2 = (f32[128,128]{1,0:T(8,128)S(1)}, f32[128,128]{1,0:T(8,128)}, u32[]{:S(2)}) copy-start(f32[128,128]{1,0:T(8,128)} %start.1) | copy-start | bytes 196612
  10.8 39.7 %copy-start.3 = (f32[128]{0:T(128)S(1)}, f32[128]{0:T(128)}, u32[]{:S(2)}) copy-start(f32[128]{0:T(128)} %param.11) | copy-start | bytes 1540
  12.4 2.5 %collective-permute-start.5 = (bf16[2,2,4,160,128]{4,3,2,1,0:T(8,128)(2,1)}, bf16[2,2,4,160,128]{4,3,2,1,0:T(8,128)(2,1)S(1)}, u32[]{:S(2)}, u32[]{:S(2)}) collective-permute-start(bf16[2,2,4,160,128]{4,3,2,1,0:T(8,128)(2,1)} %rhs.2), channel_id=1, source_target_pairs={{0,2},{2,0},{4,6},{6,4},{8,10},{10,8},{12,14},{14,12},{16,18},{18,... | collective-permute-start | bytes 1966088 | tf_op jit(solution)/shard_map/ppermute | solution.py:461
  12.4 8.7 %collective-permute-start.3 = (bf16[8,128,128]{2,1,0:T(8,128)(2,1)S(1)}, bf16[8,128,128]{2,1,0:T(8,128)(2,1)S(1)}, u32[]{:S(2)}, u32[]{:S(2)}) collective-permute-start(bf16[8,128,128]{2,1,0:T(8,128)(2,1)S(1)} %collective-permute-done.refs_14_), channel_id=1, source_target_pairs={{0,8},{2,10},{8,16},{10,18},{16,24},{18,26},{24,28},{26,30},{28,20... | collective-permute-start | bytes 786440 | tf_op jit(solution)/shard_map/ppermute | solution.py:452
  12.9 7.1 %collective-permute-start.6 = (bf16[8,128,128]{2,1,0:T(8,128)(2,1)S(1)}, bf16[8,128,128]{2,1,0:T(8,128)(2,1)S(1)}, u32[]{:S(2)}, u32[]{:S(2)}) collective-permute-start(bf16[8,128,128]{2,1,0:T(8,128)(2,1)S(1)} %collective-permute-done.1.refs_2_), channel_id=1, source_target_pairs={{0,2},{2,0},{4,6},{6,4},{8,10},{10,8},{12,14},{14,12},{16,18},{18,... | collective-permute-start | bytes 786440 | tf_op jit(solution)/shard_map/ppermute | solution.py:461
  13.1 7.0 %collective-permute-start.7 = (bf16[8,128,128]{2,1,0:T(8,128)(2,1)S(1)}, bf16[8,128,128]{2,1,0:T(8,128)(2,1)S(1)}, u32[]{:S(2)}, u32[]{:S(2)}) collective-permute-start(bf16[8,128,128]{2,1,0:T(8,128)(2,1)S(1)} %collective-permute-done.refs_14_), channel_id=1, source_target_pairs={{0,2},{2,0},{4,6},{6,4},{8,10},{10,8},{12,14},{14,12},{16,18},{18,... | collective-permute-start | bytes 786440 | tf_op jit(solution)/shard_map/ppermute | solution.py:461
  13.4 8.4 %collective-permute-start.4 = (bf16[8,128,128]{2,1,0:T(8,128)(2,1)S(1)}, bf16[8,128,128]{2,1,0:T(8,128)(2,1)S(1)}, u32[]{:S(2)}, u32[]{:S(2)}) collective-permute-start(bf16[8,128,128]{2,1,0:T(8,128)(2,1)S(1)} %collective-permute-done.1.refs_2_), channel_id=1, source_target_pairs={{0,4},{2,6},{8,0},{10,2},{16,8},{18,10},{24,16},{26,18},{28,24},{3... | collective-permute-start | bytes 786440 | tf_op jit(solution)/shard_map/ppermute | solution.py:455
  21.8 16.4 %collective-permute-start.8 = (bf16[8,128,128]{2,1,0:T(8,128)(2,1)S(1)}, bf16[8,128,128]{2,1,0:T(8,128)(2,1)S(1)}, u32[]{:S(2)}, u32[]{:S(2)}) collective-permute-start(bf16[8,128,128]{2,1,0:T(8,128)(2,1)S(1)} %collective-permute-done.3.refs_12_), channel_id=1, source_target_pairs={{0,8},{2,10},{8,16},{10,18},{16,24},{18,26},{24,28},{26,30},{28,20... | collective-permute-start | bytes 786440 | tf_op jit(solution)/shard_map/ppermute | solution.py:452
  23.4 14.8 %collective-permute-start.9 = (bf16[8,128,128]{2,1,0:T(8,128)(2,1)S(1)}, bf16[8,128,128]{2,1,0:T(8,128)(2,1)S(1)}, u32[]{:S(2)}, u32[]{:S(2)}) collective-permute-start(bf16[8,128,128]{2,1,0:T(8,128)(2,1)S(1)} %collective-permute-done.4.refs_4_), channel_id=1, source_target_pairs={{0,4},{2,6},{8,0},{10,2},{16,8},{18,10},{24,16},{26,18},{28,24},{3... | collective-permute-start | bytes 786440 | tf_op jit(solution)/shard_map/ppermute | solution.py:455
  23.8 11.1 %collective-permute-start.10 = (bf16[4,176,128]{2,1,0:T(8,128)(2,1)S(1)}, bf16[4,176,128]{2,1,0:T(8,128)(2,1)S(1)}, u32[]{:S(2)}, u32[]{:S(2)}) collective-permute-start(bf16[4,176,128]{2,1,0:T(8,128)(2,1)S(1)} %get-tuple-element.51), channel_id=1, source_target_pairs={{0,4},{1,5},{2,6},{3,7},{4,0},{5,1},{6,2},{7,3},{8,12},{9,13},{10,... | collective-permute-start | bytes 540680 | tf_op jit(solution)/shard_map/ppermute | solution.py:200
  25.4 9.5 %collective-permute-start.11 = (bf16[4,176,128]{2,1,0:T(8,128)(2,1)S(1)}, bf16[4,176,128]{2,1,0:T(8,128)(2,1)S(1)}, u32[]{:S(2)}, u32[]{:S(2)}) collective-permute-start(bf16[4,176,128]{2,1,0:T(8,128)(2,1)S(1)} %get-tuple-element.52), channel_id=1, source_target_pairs={{0,1},{1,0},{2,3},{3,2},{4,5},{5,4},{6,7},{7,6},{8,9},{9,8},{10,11... | collective-permute-start | bytes 540680 | tf_op jit(solution)/shard_map/ppermute | solution.py:200
  26.9 11.3 %collective-permute-start.12 = (bf16[4,176,128]{2,1,0:T(8,128)(2,1)S(1)}, bf16[4,176,128]{2,1,0:T(8,128)(2,1)S(1)}, u32[]{:S(2)}, u32[]{:S(2)}) collective-permute-start(bf16[4,176,128]{2,1,0:T(8,128)(2,1)S(1)} %get-tuple-element.53), channel_id=1, source_target_pairs={{0,5},{1,4},{2,7},{3,6},{4,1},{5,0},{6,3},{7,2},{8,13},{9,12},{10,... | collective-permute-start | bytes 540680 | tf_op jit(solution)/shard_map/ppermute | solution.py:200
  38.2 10.3 %collective-permute-start.13 = (bf16[8,128,128]{2,1,0:T(8,128)(2,1)S(1)}, bf16[8,128,128]{2,1,0:T(8,128)(2,1)S(1)}, u32[]{:S(2)}, u32[]{:S(2)}) collective-permute-start(bf16[8,128,128]{2,1,0:T(8,128)(2,1)S(1)} %collective-permute-done.8.refs_10_), channel_id=1, source_target_pairs={{0,8},{2,10},{8,16},{10,18},{16,24},{18,26},{24,28},{26,30},{28,20... | collective-permute-start | bytes 786440 | tf_op jit(solution)/shard_map/ppermute | solution.py:452
  38.3 8.3 %collective-permute-start.14 = (bf16[272,128]{1,0:T(8,128)(2,1)S(1)}, bf16[272,128]{1,0:T(8,128)(2,1)S(1)}, u32[]{:S(2)}, u32[]{:S(2)}) collective-permute-start(bf16[272,128]{1,0:T(8,128)(2,1)S(1)} %get-tuple-element.60), channel_id=1, source_target_pairs={{0,8},{2,10},{4,12},{6,14},{8,16},{10,18},{12,20},{14,22},{16,24},... | collective-permute-start | bytes 208904 | tf_op jit(solution)/shard_map/ppermute | solution.py:221
  38.4 8.7 %collective-permute-start.15 = (bf16[272,128]{1,0:T(8,128)(2,1)S(1)}, bf16[272,128]{1,0:T(8,128)(2,1)S(1)}, u32[]{:S(2)}, u32[]{:S(2)}) collective-permute-start(bf16[272,128]{1,0:T(8,128)(2,1)S(1)} %get-tuple-element.61), channel_id=1, source_target_pairs={{0,16},{2,18},{4,20},{6,22},{8,24},{10,26},{12,28},{14,30},{16,0},... | collective-permute-start | bytes 208904 | tf_op jit(solution)/shard_map/ppermute | solution.py:221
  44.0 4.6 %collective-permute-start.16 = (bf16[272,128]{1,0:T(8,128)(2,1)S(1)}, bf16[272,128]{1,0:T(8,128)(2,1)S(1)}, u32[]{:S(2)}, u32[]{:S(2)}) collective-permute-start(bf16[272,128]{1,0:T(8,128)(2,1)S(1)} %get-tuple-element.62), channel_id=1, source_target_pairs={{0,24},{2,26},{4,28},{6,30},{8,0},{10,2},{12,4},{14,6},{16,8},{18,... | collective-permute-start | bytes 208904 | tf_op jit(solution)/shard_map/ppermute | solution.py:221
  46.6 2.5 %collective-permute-start.21 = (bf16[8,128,128]{2,1,0:T(8,128)(2,1)S(1)}, bf16[8,128,128]{2,1,0:T(8,128)(2,1)S(1)}, u32[]{:S(2)}, u32[]{:S(2)}) collective-permute-start(bf16[8,128,128]{2,1,0:T(8,128)(2,1)S(1)} %collective-permute-done.3.refs_12_), channel_id=1, source_target_pairs={{0,2},{2,0},{4,6},{6,4},{8,10},{10,8},{12,14},{14,12},{16,18},{18,... | collective-permute-start | bytes 786440 | tf_op jit(solution)/shard_map/ppermute | solution.py:461
  46.6 2.5 %collective-permute-start.17 = (bf16[8,128,128]{2,1,0:T(8,128)(2,1)S(1)}, bf16[8,128,128]{2,1,0:T(8,128)(2,1)S(1)}, u32[]{:S(2)}, u32[]{:S(2)}) collective-permute-start(bf16[8,128,128]{2,1,0:T(8,128)(2,1)S(1)} %collective-permute-done.4.refs_4_), channel_id=1, source_target_pairs={{0,2},{2,0},{4,6},{6,4},{8,10},{10,8},{12,14},{14,12},{16,18},{18,... | collective-permute-start | bytes 786440 | tf_op jit(solution)/shard_map/ppermute | solution.py:461
  47.1 2.0 %collective-permute-start.20 = (bf16[8,128,128]{2,1,0:T(8,128)(2,1)S(1)}, bf16[8,128,128]{2,1,0:T(8,128)(2,1)S(1)}, u32[]{:S(2)}, u32[]{:S(2)}) collective-permute-start(bf16[8,128,128]{2,1,0:T(8,128)(2,1)S(1)} %collective-permute-done.8.refs_10_), channel_id=1, source_target_pairs={{0,2},{2,0},{4,6},{6,4},{8,10},{10,8},{12,14},{14,12},{16,18},{18,... | collective-permute-start | bytes 786440 | tf_op jit(solution)/shard_map/ppermute | solution.py:461
  48.5 1.5 %collective-permute-start.18 = (bf16[8,128,128]{2,1,0:T(8,128)(2,1)S(1)}, bf16[8,128,128]{2,1,0:T(8,128)(2,1)S(1)}, u32[]{:S(2)}, u32[]{:S(2)}) collective-permute-start(bf16[8,128,128]{2,1,0:T(8,128)(2,1)S(1)} %collective-permute-done.9.refs_6_), channel_id=1, source_target_pairs={{0,2},{2,0},{4,6},{6,4},{8,10},{10,8},{12,14},{14,12},{16,18},{18,... | collective-permute-start | bytes 786440 | tf_op jit(solution)/shard_map/ppermute | solution.py:461
  48.6 1.9 %collective-permute-start.19 = (bf16[8,128,128]{2,1,0:T(8,128)(2,1)S(1)}, bf16[8,128,128]{2,1,0:T(8,128)(2,1)S(1)}, u32[]{:S(2)}, u32[]{:S(2)}) collective-permute-start(bf16[8,128,128]{2,1,0:T(8,128)(2,1)S(1)} %collective-permute-done.13.refs_8_), channel_id=1, source_target_pairs={{0,2},{2,0},{4,6},{6,4},{8,10},{10,8},{12,14},{14,12},{16,18},{18,... | collective-permute-start | bytes 786440 | tf_op jit(solution)/shard_map/ppermute | solution.py:461

commit v11 on v10

--- a/solution.py
+++ b/solution.py
@@ -222,15 +222,15 @@
     return terms
 
 
-def steps_kernel(activity, start_in, subs_in, *refs, shards, levels, slots, cached):
-    pieces, refs = refs[:shards], refs[shards:]
+def steps_kernel(activity, start_in, subs_in, *refs, count, word_tiles, levels, slots, cached):
+    pieces, refs = refs[:count], refs[count:]
     terms_in, refs = refs[:levels], refs[levels:]
     first_out, second_out, third_out, dots_out = refs[:4]
     masks, words, start, terms, subs, table, runs, lines = refs[4:12]
     facts, chosen, places, arrived, moved, given = refs[12:18]
     products = refs[-1]
     own_rows, rank = start.shape
-    word_tiles, tile, _ = pieces[0].shape
+    _, tile, _ = pieces[0].shape
     sources = lines.shape[0] // levels
     spans = 2 * slots * sources
 
@@ -239,12 +239,11 @@
     ]
     for copy in gifts:
         copy.start()
-    copies = [
-        pltpu.make_async_copy(
-            piece, words.at[k * word_tiles : (k + 1) * word_tiles], arrived.at[k]
-        )
-        for k, piece in enumerate(pieces)
-    ]
+    copies, at = [], 0
+    for k, piece in enumerate(pieces):
+        place = words.at[at : at + piece.shape[0]]
+        copies.append(pltpu.make_async_copy(piece, place, arrived.at[k]))
+        at += piece.shape[0]
     look = pltpu.make_async_copy(subs_in, subs, moved.at[1])
     look.start()
     begin = pltpu.make_async_copy(start_in, start, moved.at[2])
@@ -273,7 +272,7 @@
     place = lax.axis_index("loop")
     level, seat = lax.div(place, 4), lax.rem(place, 4)
     wanted = lax.div(lax.axis_index("own") * own_rows, tile) + 1
-    chips = shards // 2
+    chips = at // word_tiles // 2
 
     def ring_at(level, column):
         return jnp.where(column == 0, level, chips - 1 - level)
@@ -367,10 +366,10 @@
     dots_out[...] = jnp.broadcast_to(line[None], dots_out.shape)
 
 
-def krylov(start, activity, subs, pieces, terms, slots, devices):
+def krylov(start, activity, subs, pieces, terms, word_tiles, slots, devices):
     own_rows, rank = start.shape
     blocks = devices * slots
-    word_tiles, tile, _ = pieces[0].shape
+    _, tile, _ = pieces[0].shape
     chunks = -(-blocks // CHUNK)
     cached = blocks * tile * rank * 2 <= 16 * 2**20
     whole = pl.BlockSpec(memory_space=pltpu.VMEM)
@@ -378,7 +377,7 @@
     vector = jax.ShapeDtypeStruct((own_rows, rank), f32)
     scratch = [
         pltpu.VMEM((chunks, own_rows, CHUNK * tile), bf16),
-        pltpu.VMEM((len(pieces) * word_tiles, tile, rank), bf16),
+        pltpu.VMEM((sum(piece.shape[0] for piece in pieces), tile, rank), bf16),
         pltpu.VMEM(start.shape, f32),
         pltpu.VMEM((len(terms),) + terms[0].shape, bf16),
         pltpu.VMEM(subs.shape, bf16),
@@ -396,7 +395,12 @@
         scratch.append(pltpu.VMEM((chunks, CHUNK * tile, rank), bf16))
     return pl.pallas_call(
         functools.partial(
-            steps_kernel, shards=len(pieces), levels=len(terms), slots=slots, cached=cached
+            steps_kernel,
+            count=len(pieces),
+            word_tiles=word_tiles,
+            levels=len(terms),
+            slots=slots,
+            cached=cached,
         ),
         in_specs=[whole] + [anywhere] * (2 + len(pieces) + len(terms)),
         out_specs=[whole] * 4,
@@ -449,16 +453,21 @@
             for core in range(2)
         ]
 
-    up = lax.ppermute(up, "loop", shift(1))
-    held[chips - step] = up
-    if step < chips - step:
+    if step == chips - step:
+        half = up.shape[0] // 2
+        up = lax.ppermute(up[:half], "loop", shift(1))
+        down = lax.ppermute(down[half:], "loop", shift(-1))
+        held[step] = (up, down)
+    else:
+        up = lax.ppermute(up, "loop", shift(1))
         down = lax.ppermute(down, "loop", shift(-1))
-        held[step] = down
+        held[chips - step], held[step] = (up,), (down,)
     return up, down
 
 
-def other_core(value, shards):
-    return lax.ppermute(value, "loop", [(shard, shard ^ 1) for shard in range(shards)])
+def other_core(values, shards):
+    pairs = [(shard, shard ^ 1) for shard in range(shards)]
+    return tuple(lax.ppermute(value, "loop", pairs) for value in values)
 
 
 def on_device(
@@ -482,12 +491,12 @@
 
     scalars = (user_tile[0, 0].T, word_tile[0, 0].T, subreddit[0, 0].T, counts[0])
     mine = word_factors[0]
-    held = {0: mine}
+    held = {0: (mine,)}
 
     inputs = (scalars, ratings[0, 0], runs[0, 0], mine, sub_factors)
     up, down = ring_round(mine, mine, held, 1, shards)
     (away,) = rhs_sums(*inputs, 1, None, owners, own_rows)
-    crossed = {0: other_core(mine, shards)}
+    crossed = {0: other_core(held[0], shards)}
     up, down, away, crossed = together((up, down, away, crossed))
 
     def cross(step):
@@ -496,12 +505,13 @@
 
     cross(1)
     up, down = ring_round(up, down, held, 2, shards)
-    parts = rhs_sums(*inputs, 0, other_core(away, shards), owners, own_rows)
+    (given,) = other_core((away,), shards)
+    parts = rhs_sums(*inputs, 0, given, owners, own_rows)
     up, down, parts, crossed = together((up, down, parts, crossed))
 
     up, down = ring_round(up, down, held, 3, shards)
     total = reduce_chip(parts, shards, owners, own_rows)
-    up, down, total = together((up, down, total))
+    up, down, total, held = together((up, down, total, held))
 
     for step in range(4, chips // 2 + 1):
         up, down = ring_round(up, down, held, step, shards)
@@ -512,9 +522,9 @@
         cross(step)
     pieces = []
     for distance in range(chips):
-        pieces += [held[distance], crossed[distance]]
+        pieces += held[distance] + crossed[distance]
     first, second, third, dots = krylov(
-        factor_start, activity[None], sub_factors, pieces, terms, slots, devices
+        factor_start, activity[None], sub_factors, pieces, terms, mine.shape[0], slots, devices
     )
     everyone = lax.all_to_all(dots, AXES, 0, 0, tiled=True)
     return tuple(last_step(everyone, factor_start, first, second, third))

time: 75.7 us -> 75.3 us (level)
  blocking collectives: 13.6 us -> 9.93 us
  waiting for transfers between devices: 16.9 us -> 19.2 us
  Pallas kernels: 23.3 us -> 24.1 us
    all_to_all x1, blocking collectives: 13.6 us -> 9.93 us  [on_device(): everyone = lax.all_to_all(dots, AXES, 0, 0, tiled=True)]
    ppermute x3, waiting for transfers between devices: 1.36 us -> 3.55 us  [reduce_levels(): terms.append(lax.ppermute(total[up], 'loop', shift))]
    ppermute x9 -> x12, starting transfers between devices: 2.12 us -> 4.28 us  [the longest x10 2.2 us: other_core(): return tuple((lax.ppermute(value, 'loop', pairs) for value in values))]
    ppermute x3, starting transfers between devices: 8.28 us -> 6.35 us  [reduce_levels(): terms.append(lax.ppermute(total[up], 'loop', shift))]
    pallas_call x1, Pallas kernels: 10.5 us -> 11.2 us  [krylov(): pl.pallas_call(functools.partial(steps_kernel, count=len(pieces), word_ti...]
    ppermute x9 -> x12, waiting for transfers between devices: 1.4 us -> 1.55 us  [the longest x10 1.55 us: other_core(): return tuple((lax.ppermute(value, 'loop', pairs) for value in values))]
    ppermute x4 -> x3, starting transfers between devices: 2.4 us -> 2.35 us  [ring_round(): up = lax.ppermute(up, 'loop', shift(1))]
    ppermute x4 -> x3, waiting for transfers between devices: 2.43 us -> 2.42 us  [ring_round(): up = lax.ppermute(up, 'loop', shift(1))]
  transfers between devices with their start and end apart: 22 -> 24, of which waited for: 9 -> 11; matrix products, arithmetic and copies ran while one was open for 0% -> 0% of each run, Pallas kernels for 16% -> 16%
where the time goes in v11:
time: 75.3 us; the launch traced here: 75.1 us
  Pallas kernels  24.1 us (32%)
  starting transfers between devices  20.9 us (28%)
  waiting for transfers between devices  19.2 us (25%)
  blocking collectives  9.93 us (13%)
  between operations  0.88 us (1%)
    pallas_call x2, Pallas kernels, rhs_sums(): pl.pallas_call(functools.partial(rhs_kernel, half=half, owners=owners, ow...  11.9 us
    pallas_call x1, Pallas kernels, krylov(): pl.pallas_call(functools.partial(steps_kernel, count=len(pieces), word_ti...  11.2 us
    ppermute x3, waiting for transfers between devices, reduce_chip(): given.append(lax.ppermute(part, AXES, pairs) if o or column else part)  10.8 us
    all_to_all x1, blocking collectives, on_device(): everyone = lax.all_to_all(dots, AXES, 0, 0, tiled=True)  9.93 us
    ppermute x3, starting transfers between devices, reduce_levels(): terms.append(lax.ppermute(total[up], 'loop', shift))  6.35 us
    ppermute x3, starting transfers between devices, ring_round(): down = lax.ppermute(down, 'loop', shift(-1))  4.43 us
    ppermute x3, waiting for transfers between devices, reduce_levels(): terms.append(lax.ppermute(total[up], 'loop', shift))  3.55 us
    ppermute x3, starting transfers between devices, reduce_chip(): given.append(lax.ppermute(part, AXES, pairs) if o or column else part)  3.49 us
  transfers between devices with their start and end apart: 24, of which 11 were waited for; matrix products, arithmetic and copies ran while one was open for 0% of the time, Pallas kernels for 16%

profile of v11, /device:TPU:0, one launch (start us, length us, event | category | flops | bytes accessed | tf_op | source)
XLA Modules:
  0.0 75.1 jit_solution(14112691161812507841)
XLA Ops:
  0.7 0.5 collective-permute-start.2
  1.2 2.5 %collective-permute-start.1 = (bf16[8,128,128]{2,1,0:T(8,128)(2,1)}, bf16[8,128,128]{2,1,0:T(8,128)(2,1)S(1)}, u32[]{:S(2)}, u32[]{:S(2)}) collective-permute-start(bf16[8,128,128]{2,1,0:T(8,128)(2,1)} %bitcast.15), channel_id=1, source_target_pairs={{0,4},{2,6},{8,0},{10,2},{16,8},{18,10},{24,16},{26,18},{28,24},{3... | collective-permute-start | bytes 786440 | tf_op jit(solution)/shard_map/ppermute | solution.py:463
  3.8 0.2 collective-permute-start
  3.9 6.8 %rhs.2 = bf16[2,2,4,160,128]{4,3,2,1,0:T(8,128)(2,1)} custom-call(s32[8,16]{1,0:T(8,128)} %bitcast.23, s32[8,16]{1,0:T(8,128)} %bitcast.25, s32[8,16]{1,0:T(8,128)} %bitcast.27, s32[1,16]{1,0:T(1,128)} %bitcast.29, bf16[16,8,128,128]{3,2,1,0:T(8,128)(2,1)} %bitcast.31, s32[16,8,2,128]{3,2,1,0:T(2,128)} %bitcast.21, bf16[8,128,128]{2,1,0:T(8,128)(2,1)} %bitcast.17, ...), custom_call_target="tpu_custom_call" | custom-call | flops 2147483648 | bytes 16777216 | tf_op jit(solution)/shard_map/rhs/pallas_call | solution.py:145
  10.8 0.0 copy-start.2
  10.8 0.0 copy-start.3
  10.8 0.0 collective-permute-done.2.refs_1_
  10.8 0.2 collective-permute-done.1.refs_2_
  11.0 1.4 %collective-permute-done.refs_16_ = bf16[8,128,128]{2,1,0:T(8,128)(2,1)S(1)} collective-permute-done((bf16[8,128,128]{2,1,0:T(8,128)(2,1)}, bf16[8,128,128]{2,1,0:T(8,128)(2,1)S(1)}, u32[]{:S(2)}, u32[]{:S(2)}) %collective-permute-start) | collective-permute-done | bytes 262176 | tf_op jit(solution)/shard_map/ppermute | solution.py:462
  12.4 0.5 collective-permute-start.3
  12.9 0.2 collective-permute-start.6
  13.1 0.3 collective-permute-start.7
  13.4 1.5 %collective-permute-start.4 = (bf16[8,128,128]{2,1,0:T(8,128)(2,1)S(1)}, bf16[8,128,128]{2,1,0:T(8,128)(2,1)S(1)}, u32[]{:S(2)}, u32[]{:S(2)}) collective-permute-start(bf16[8,128,128]{2,1,0:T(8,128)(2,1)S(1)} %collective-permute-done.1.refs_2_), channel_id=1, source_target_pairs={{0,4},{2,6},{8,0},{10,2},{16,8},{18,10},{24,16},{26,18},{28,24},{3... | collective-permute-start | bytes 786440 | tf_op jit(solution)/shard_map/ppermute | solution.py:463
  15.0 5.0 %rhs.3 = (bf16[4,176,128]{2,1,0:T(8,128)(2,1)S(1)}, bf16[4,176,128]{2,1,0:T(8,128)(2,1)S(1)}, bf16[4,176,128]{2,1,0:T(8,128)(2,1)S(1)}, bf16[4,176,128]{2,1,0:T(8,128)(2,1)S(1)}) custom-call(s32[8,16]{1,0:T(8,128)S(1)} %bitcast.24, s32[8,16]{1,0:T(8,128)S(1)} %bitcast.26, s32[8,16]{1,0:T(8,128)S(1)} %bitcast.28, s32[1,16]{1,0:T(1,128)S(1)} %bitcast.30, ...), custom_call_target="tpu_custom_call" | custom-call | flops 2147483648 | bytes 16777216 | tf_op jit(solution)/shard_map/rhs/pallas_call | solution.py:145
  20.0 0.0 collective-permute-done.6.refs_3_
  20.0 1.0 %collective-permute-done.3.refs_14_ = bf16[8,128,128]{2,1,0:T(8,128)(2,1)S(1)} collective-permute-done((bf16[8,128,128]{2,1,0:T(8,128)(2,1)S(1)}, bf16[8,128,128]{2,1,0:T(8,128)(2,1)S(1)}, u32[]{:S(2)}, u32[]{:S(2)}) %collective-permute-start.3) | collective-permute-done | bytes 262176 | tf_op jit(solution)/shard_map/ppermute | solution.py:462
  21.1 0.7 collective-permute-done.4.refs_4_
  21.8 1.6 %collective-permute-start.8 = (bf16[8,128,128]{2,1,0:T(8,128)(2,1)S(1)}, bf16[8,128,128]{2,1,0:T(8,128)(2,1)S(1)}, u32[]{:S(2)}, u32[]{:S(2)}) collective-permute-start(bf16[8,128,128]{2,1,0:T(8,128)(2,1)S(1)} %collective-permute-done.3.refs_14_), channel_id=1, source_target_pairs={{0,8},{2,10},{8,16},{10,18},{16,24},{18,26},{24,28},{26,30},{28,20... | collective-permute-start | bytes 786440 | tf_op jit(solution)/shard_map/ppermute | solution.py:462
  23.4 0.4 collective-permute-start.9
  23.8 1.6 %collective-permute-start.10 = (bf16[4,176,128]{2,1,0:T(8,128)(2,1)S(1)}, bf16[4,176,128]{2,1,0:T(8,128)(2,1)S(1)}, u32[]{:S(2)}, u32[]{:S(2)}) collective-permute-start(bf16[4,176,128]{2,1,0:T(8,128)(2,1)S(1)} %get-tuple-element.60), channel_id=1, source_target_pairs={{0,4},{1,5},{2,6},{3,7},{4,0},{5,1},{6,2},{7,3},{8,12},{9,13},{10,... | collective-permute-start | bytes 540680 | tf_op jit(solution)/shard_map/ppermute | solution.py:200
  25.4 1.5 %collective-permute-start.11 = (bf16[4,176,128]{2,1,0:T(8,128)(2,1)S(1)}, bf16[4,176,128]{2,1,0:T(8,128)(2,1)S(1)}, u32[]{:S(2)}, u32[]{:S(2)}) collective-permute-start(bf16[4,176,128]{2,1,0:T(8,128)(2,1)S(1)} %get-tuple-element.61), channel_id=1, source_target_pairs={{0,1},{1,0},{2,3},{3,2},{4,5},{5,4},{6,7},{7,6},{8,9},{9,8},{10,11... | collective-permute-start | bytes 540680 | tf_op jit(solution)/shard_map/ppermute | solution.py:200
  26.9 0.4 collective-permute-start.12
  27.3 7.6 %collective-permute-done.10.refs_1_ = bf16[4,176,128]{2,1,0:T(8,128)(2,1)S(1)} collective-permute-done((bf16[4,176,128]{2,1,0:T(8,128)(2,1)S(1)}, bf16[4,176,128]{2,1,0:T(8,128)(2,1)S(1)}, u32[]{:S(2)}, u32[]{:S(2)}) %collective-permute-start.10) | collective-permute-done | bytes 180256 | tf_op jit(solution)/shard_map/ppermute | solution.py:200
  34.9 0.0 collective-permute-done.11.refs_2_
  34.9 3.3 %collective-permute-done.12.refs_3_ = bf16[4,176,128]{2,1,0:T(8,128)(2,1)S(1)} collective-permute-done((bf16[4,176,128]{2,1,0:T(8,128)(2,1)S(1)}, bf16[4,176,128]{2,1,0:T(8,128)(2,1)S(1)}, u32[]{:S(2)}, u32[]{:S(2)}) %collective-permute-start.12) | collective-permute-done | bytes 180256 | tf_op jit(solution)/shard_map/ppermute | solution.py:200
  38.1 0.1 chip.1
  38.2 0.0 collective-permute-done.8.refs_12_
  38.2 0.0 collective-permute-done.9.refs_6_
  38.3 1.8 %collective-permute-start.14 = (bf16[4,128,128]{2,1,0:T(8,128)(2,1)S(1)}, bf16[4,128,128]{2,1,0:T(8,128)(2,1)S(1)}, u32[]{:S(2)}, u32[]{:S(2)}) collective-permute-start(bf16[4,128,128]{2,1,0:T(8,128)(2,1)S(1)} %slice.7), channel_id=1, source_target_pairs={{0,4},{2,6},{8,0},{10,2},{16,8},{18,10},{24,16},{26,18},{28,24},{3... | collective-permute-start | bytes 393224 | tf_op jit(solution)/shard_map/ppermute | solution.py:459
  40.1 0.3 collective-permute-start.13
  40.4 0.0 collective-permute-start.15
  40.4 5.3 %collective-permute-start.16 = (bf16[272,128]{1,0:T(8,128)(2,1)S(1)}, bf16[272,128]{1,0:T(8,128)(2,1)S(1)}, u32[]{:S(2)}, u32[]{:S(2)}) collective-permute-start(bf16[272,128]{1,0:T(8,128)(2,1)S(1)} %get-tuple-element.72), channel_id=1, source_target_pairs={{0,16},{2,18},{4,20},{6,22},{8,24},{10,26},{12,28},{14,30},{16,0},... | collective-permute-start | bytes 208904 | tf_op jit(solution)/shard_map/ppermute | solution.py:221
  45.7 1.0 %collective-permute-start.17 = (bf16[272,128]{1,0:T(8,128)(2,1)S(1)}, bf16[272,128]{1,0:T(8,128)(2,1)S(1)}, u32[]{:S(2)}, u32[]{:S(2)}) collective-permute-start(bf16[272,128]{1,0:T(8,128)(2,1)S(1)} %get-tuple-element.73), channel_id=1, source_target_pairs={{0,24},{2,26},{4,28},{6,30},{8,0},{10,2},{12,4},{14,6},{16,8},{18,... | collective-permute-start | bytes 208904 | tf_op jit(solution)/shard_map/ppermute | solution.py:221
  46.7 1.7 %collective-permute-done.15.refs_19_ = bf16[272,128]{1,0:T(8,128)(2,1)S(1)} collective-permute-done((bf16[272,128]{1,0:T(8,128)(2,1)S(1)}, bf16[272,128]{1,0:T(8,128)(2,1)S(1)}, u32[]{:S(2)}, u32[]{:S(2)}) %collective-permute-start.15) | collective-permute-done | bytes 69664 | tf_op jit(solution)/shard_map/ppermute | solution.py:221
  48.4 0.0 collective-permute-start.18
  48.4 1.1 %collective-permute-done.16.refs_20_ = bf16[272,128]{1,0:T(8,128)(2,1)S(1)} collective-permute-done((bf16[272,128]{1,0:T(8,128)(2,1)S(1)}, bf16[272,128]{1,0:T(8,128)(2,1)S(1)}, u32[]{:S(2)}, u32[]{:S(2)}) %collective-permute-start.16) | collective-permute-done | bytes 69664 | tf_op jit(solution)/shard_map/ppermute | solution.py:221
  49.5 0.7 collective-permute-done.17.refs_21_
  50.3 0.0 collective-permute-done.13.refs_8_
  50.3 0.0 collective-permute-start.20
  50.3 0.5 collective-permute-start.19
  50.8 0.1 collective-permute-start.22
  50.9 0.4 collective-permute-start.23
  51.3 0.3 collective-permute-done.20.refs_10_
  51.6 0.1 collective-permute-start.21
  51.8 1.2 %collective-permute-done.21.refs_11_ = bf16[4,128,128]{2,1,0:T(8,128)(2,1)S(1)} collective-permute-done((bf16[4,128,128]{2,1,0:T(8,128)(2,1)S(1)}, bf16[4,128,128]{2,1,0:T(8,128)(2,1)S(1)}, u32[]{:S(2)}, u32[]{:S(2)}) %collective-permute-start.21) | collective-permute-done | bytes 131104 | tf_op jit(solution)/shard_map/ppermute | solution.py:470
  53.0 11.2 %krylov.1 = (f32[128,128]{1,0:T(8,128)S(1)}, f32[128,128]{1,0:T(8,128)S(1)}, f32[128,128]{1,0:T(8,128)S(1)}, f32[32,1,128]{2,1,0:T(1,128)S(1)}) custom-call(f32[1,128]{1,0:T(1,128)S(1)} %bitcast.20, f32[128,128]{1,0:T(8,128)S(1)} %copy-done.2, bf16[2048,128]{1,0:T(8,128)(2,1)S(1)} %copy-done, bf16[8,128,128]{2,1,0:T(8,128)(2,1)S(1)} %bitcast.19, ...), custom_call_target="tpu_custom_call" | custom-call | tf_op jit(solution)/shard_map/krylov/pallas_call | solution.py:396
  64.3 9.9 %all_to_all.5.dots = f32[32,1,128]{2,1,0:T(1,128)S(1)} all-to-all(f32[32,1,128]{2,1,0:T(1,128)S(1)} %get-tuple-element.92), channel_id=1, replica_groups=mesh['loop'=16,'own'=2] {'loop','own'}, dimensions={0} | all-to-all | bytes 32768 | tf_op jit(solution)/shard_map/all_to_all | solution.py:529
  74.2 0.9 %last_step.1 = (f32[128,128]{1,0:T(8,128)}, f32[128,128]{1,0:T(8,128)}) custom-call(f32[32,1,128]{2,1,0:T(1,128)S(1)} %all_to_all.5.dots, f32[128,128]{1,0:T(8,128)S(1)} %copy-done.2, f32[128,128]{1,0:T(8,128)S(1)} %get-tuple-element.93.first, f32[128,128]{1,0:T(8,128)S(1)} %get-tuple-element.94.second, f32[128,128]{1,0:T(8,128)S(1)} %get-tuple-element.95.third), custom_call_target="tpu_custom_call" | custom-call | tf_op jit(solution)/shard_map/last_step/pallas_call | solution.py:432
  (26 shorter events, 0.1 us)
Async XLA Ops:
  0.6 14.3 %copy-start.1 = (bf16[1,8,128,128]{3,2,1,0:T(8,128)(2,1)S(1)}, bf16[1,8,128,128]{3,2,1,0:T(8,128)(2,1)}, u32[]{:S(2)}) copy-start(bf16[1,8,128,128]{3,2,1,0:T(8,128)(2,1)} %param.12) | copy-start | bytes 786436
  0.6 14.3 %copy-start = (bf16[2048,128]{1,0:T(8,128)(2,1)S(1)}, bf16[2048,128]{1,0:T(8,128)(2,1)}, u32[]{:S(2)}) copy-start(bf16[2048,128]{1,0:T(8,128)(2,1)} %subs_in.5) | copy-start | bytes 1572868
  0.7 14.3 %copy-start.4 = (s32[1,1,16,8,2,128]{5,4,3,2,1,0:T(2,128)S(1)}, s32[1,1,16,8,2,128]{5,4,3,2,1,0:T(2,128)}, u32[]{:S(2)}) copy-start(s32[1,1,16,8,2,128]{5,4,3,2,1,0:T(2,128)} %param.19) | copy-start | bytes 393220
  0.7 14.3 %copy-start.8 = (s32[1,1,16]{2,1,0:T(1,128)S(1)}, s32[1,1,16]{2,1,0:T(1,128)}, u32[]{:S(2)}) copy-start(s32[1,1,16]{2,1,0:T(1,128)} %param.18) | copy-start | bytes 196
  0.7 14.3 %copy-start.7 = (s32[1,1,16,8]{2,3,1,0:T(8,128)S(1)}, s32[1,1,16,8]{2,3,1,0:T(8,128)}, u32[]{:S(2)}) copy-start(s32[1,1,16,8]{2,3,1,0:T(8,128)} %param.17) | copy-start | bytes 1540
  0.7 14.3 %copy-start.6 = (s32[1,1,16,8]{2,3,1,0:T(8,128)S(1)}, s32[1,1,16,8]{2,3,1,0:T(8,128)}, u32[]{:S(2)}) copy-start(s32[1,1,16,8]{2,3,1,0:T(8,128)} %param.16) | copy-start | bytes 1540
  0.7 14.3 %copy-start.5 = (s32[1,1,16,8]{2,3,1,0:T(8,128)S(1)}, s32[1,1,16,8]{2,3,1,0:T(8,128)}, u32[]{:S(2)}) copy-start(s32[1,1,16,8]{2,3,1,0:T(8,128)} %param.15) | copy-start | bytes 1540
  0.7 10.1 %collective-permute-start.2 = (bf16[8,128,128]{2,1,0:T(8,128)(2,1)}, bf16[8,128,128]{2,1,0:T(8,128)(2,1)S(1)}, u32[]{:S(2)}, u32[]{:S(2)}) collective-permute-start(bf16[8,128,128]{2,1,0:T(8,128)(2,1)} %bitcast.14), channel_id=1, source_target_pairs={{0,2},{2,0},{4,6},{6,4},{8,10},{10,8},{12,14},{14,12},{16,18},{18,... | collective-permute-start | bytes 786440 | tf_op jit(solution)/shard_map/ppermute | solution.py:470
  1.2 9.8 %collective-permute-start.1 = (bf16[8,128,128]{2,1,0:T(8,128)(2,1)}, bf16[8,128,128]{2,1,0:T(8,128)(2,1)S(1)}, u32[]{:S(2)}, u32[]{:S(2)}) collective-permute-start(bf16[8,128,128]{2,1,0:T(8,128)(2,1)} %bitcast.15), channel_id=1, source_target_pairs={{0,4},{2,6},{8,0},{10,2},{16,8},{18,10},{24,16},{26,18},{28,24},{3... | collective-permute-start | bytes 786440 | tf_op jit(solution)/shard_map/ppermute | solution.py:463
  3.8 8.6 %collective-permute-start = (bf16[8,128,128]{2,1,0:T(8,128)(2,1)}, bf16[8,128,128]{2,1,0:T(8,128)(2,1)S(1)}, u32[]{:S(2)}, u32[]{:S(2)}) collective-permute-start(bf16[8,128,128]{2,1,0:T(8,128)(2,1)} %bitcast.16), channel_id=1, source_target_pairs={{0,8},{2,10},{8,16},{10,18},{16,24},{18,26},{24,28},{26,30},{28,20... | collective-permute-start | bytes 786440 | tf_op jit(solution)/shard_map/ppermute | solution.py:462
  10.8 42.2 %copy-start.2 = (f32[128,128]{1,0:T(8,128)S(1)}, f32[128,128]{1,0:T(8,128)}, u32[]{:S(2)}) copy-start(f32[128,128]{1,0:T(8,128)} %start.1) | copy-start | bytes 196612
  10.8 42.2 %copy-start.3 = (f32[128]{0:T(128)S(1)}, f32[128]{0:T(128)}, u32[]{:S(2)}) copy-start(f32[128]{0:T(128)} %param.11) | copy-start | bytes 1540
  12.4 2.5 %collective-permute-start.5 = (bf16[2,2,4,160,128]{4,3,2,1,0:T(8,128)(2,1)}, bf16[2,2,4,160,128]{4,3,2,1,0:T(8,128)(2,1)S(1)}, u32[]{:S(2)}, u32[]{:S(2)}) collective-permute-start(bf16[2,2,4,160,128]{4,3,2,1,0:T(8,128)(2,1)} %rhs.2), channel_id=1, source_target_pairs={{0,2},{2,0},{4,6},{6,4},{8,10},{10,8},{12,14},{14,12},{16,18},{18,... | collective-permute-start | bytes 1966088 | tf_op jit(solution)/shard_map/ppermute | solution.py:470
  12.4 8.7 %collective-permute-start.3 = (bf16[8,128,128]{2,1,0:T(8,128)(2,1)S(1)}, bf16[8,128,128]{2,1,0:T(8,128)(2,1)S(1)}, u32[]{:S(2)}, u32[]{:S(2)}) collective-permute-start(bf16[8,128,128]{2,1,0:T(8,128)(2,1)S(1)} %collective-permute-done.refs_16_), channel_id=1, source_target_pairs={{0,8},{2,10},{8,16},{10,18},{16,24},{18,26},{24,28},{26,30},{28,20... | collective-permute-start | bytes 786440 | tf_op jit(solution)/shard_map/ppermute | solution.py:462
  12.9 7.1 %collective-permute-start.6 = (bf16[8,128,128]{2,1,0:T(8,128)(2,1)S(1)}, bf16[8,128,128]{2,1,0:T(8,128)(2,1)S(1)}, u32[]{:S(2)}, u32[]{:S(2)}) collective-permute-start(bf16[8,128,128]{2,1,0:T(8,128)(2,1)S(1)} %collective-permute-done.1.refs_2_), channel_id=1, source_target_pairs={{0,2},{2,0},{4,6},{6,4},{8,10},{10,8},{12,14},{14,12},{16,18},{18,... | collective-permute-start | bytes 786440 | tf_op jit(solution)/shard_map/ppermute | solution.py:470
  13.1 7.0 %collective-permute-start.7 = (bf16[8,128,128]{2,1,0:T(8,128)(2,1)S(1)}, bf16[8,128,128]{2,1,0:T(8,128)(2,1)S(1)}, u32[]{:S(2)}, u32[]{:S(2)}) collective-permute-start(bf16[8,128,128]{2,1,0:T(8,128)(2,1)S(1)} %collective-permute-done.refs_16_), channel_id=1, source_target_pairs={{0,2},{2,0},{4,6},{6,4},{8,10},{10,8},{12,14},{14,12},{16,18},{18,... | collective-permute-start | bytes 786440 | tf_op jit(solution)/shard_map/ppermute | solution.py:470
  13.4 8.4 %collective-permute-start.4 = (bf16[8,128,128]{2,1,0:T(8,128)(2,1)S(1)}, bf16[8,128,128]{2,1,0:T(8,128)(2,1)S(1)}, u32[]{:S(2)}, u32[]{:S(2)}) collective-permute-start(bf16[8,128,128]{2,1,0:T(8,128)(2,1)S(1)} %collective-permute-done.1.refs_2_), channel_id=1, source_target_pairs={{0,4},{2,6},{8,0},{10,2},{16,8},{18,10},{24,16},{26,18},{28,24},{3... | collective-permute-start | bytes 786440 | tf_op jit(solution)/shard_map/ppermute | solution.py:463
  21.8 16.4 %collective-permute-start.8 = (bf16[8,128,128]{2,1,0:T(8,128)(2,1)S(1)}, bf16[8,128,128]{2,1,0:T(8,128)(2,1)S(1)}, u32[]{:S(2)}, u32[]{:S(2)}) collective-permute-start(bf16[8,128,128]{2,1,0:T(8,128)(2,1)S(1)} %collective-permute-done.3.refs_14_), channel_id=1, source_target_pairs={{0,8},{2,10},{8,16},{10,18},{16,24},{18,26},{24,28},{26,30},{28,20... | collective-permute-start | bytes 786440 | tf_op jit(solution)/shard_map/ppermute | solution.py:462
  23.4 14.8 %collective-permute-start.9 = (bf16[8,128,128]{2,1,0:T(8,128)(2,1)S(1)}, bf16[8,128,128]{2,1,0:T(8,128)(2,1)S(1)}, u32[]{:S(2)}, u32[]{:S(2)}) collective-permute-start(bf16[8,128,128]{2,1,0:T(8,128)(2,1)S(1)} %collective-permute-done.4.refs_4_), channel_id=1, source_target_pairs={{0,4},{2,6},{8,0},{10,2},{16,8},{18,10},{24,16},{26,18},{28,24},{3... | collective-permute-start | bytes 786440 | tf_op jit(solution)/shard_map/ppermute | solution.py:463
  23.8 11.1 %collective-permute-start.10 = (bf16[4,176,128]{2,1,0:T(8,128)(2,1)S(1)}, bf16[4,176,128]{2,1,0:T(8,128)(2,1)S(1)}, u32[]{:S(2)}, u32[]{:S(2)}) collective-permute-start(bf16[4,176,128]{2,1,0:T(8,128)(2,1)S(1)} %get-tuple-element.60), channel_id=1, source_target_pairs={{0,4},{1,5},{2,6},{3,7},{4,0},{5,1},{6,2},{7,3},{8,12},{9,13},{10,... | collective-permute-start | bytes 540680 | tf_op jit(solution)/shard_map/ppermute | solution.py:200
  25.4 9.5 %collective-permute-start.11 = (bf16[4,176,128]{2,1,0:T(8,128)(2,1)S(1)}, bf16[4,176,128]{2,1,0:T(8,128)(2,1)S(1)}, u32[]{:S(2)}, u32[]{:S(2)}) collective-permute-start(bf16[4,176,128]{2,1,0:T(8,128)(2,1)S(1)} %get-tuple-element.61), channel_id=1, source_target_pairs={{0,1},{1,0},{2,3},{3,2},{4,5},{5,4},{6,7},{7,6},{8,9},{9,8},{10,11... | collective-permute-start | bytes 540680 | tf_op jit(solution)/shard_map/ppermute | solution.py:200
  26.9 11.3 %collective-permute-start.12 = (bf16[4,176,128]{2,1,0:T(8,128)(2,1)S(1)}, bf16[4,176,128]{2,1,0:T(8,128)(2,1)S(1)}, u32[]{:S(2)}, u32[]{:S(2)}) collective-permute-start(bf16[4,176,128]{2,1,0:T(8,128)(2,1)S(1)} %get-tuple-element.62), channel_id=1, source_target_pairs={{0,5},{1,4},{2,7},{3,6},{4,1},{5,0},{6,3},{7,2},{8,13},{9,12},{10,... | collective-permute-start | bytes 540680 | tf_op jit(solution)/shard_map/ppermute | solution.py:200
  38.3 12.0 %collective-permute-start.14 = (bf16[4,128,128]{2,1,0:T(8,128)(2,1)S(1)}, bf16[4,128,128]{2,1,0:T(8,128)(2,1)S(1)}, u32[]{:S(2)}, u32[]{:S(2)}) collective-permute-start(bf16[4,128,128]{2,1,0:T(8,128)(2,1)S(1)} %slice.7), channel_id=1, source_target_pairs={{0,4},{2,6},{8,0},{10,2},{16,8},{18,10},{24,16},{26,18},{28,24},{3... | collective-permute-start | bytes 393224 | tf_op jit(solution)/shard_map/ppermute | solution.py:459
  40.1 10.2 %collective-permute-start.13 = (bf16[4,128,128]{2,1,0:T(8,128)(2,1)S(1)}, bf16[4,128,128]{2,1,0:T(8,128)(2,1)S(1)}, u32[]{:S(2)}, u32[]{:S(2)}) collective-permute-start(bf16[4,128,128]{2,1,0:T(8,128)(2,1)S(1)} %slice.6), channel_id=1, source_target_pairs={{0,8},{2,10},{8,16},{10,18},{16,24},{18,26},{24,28},{26,30},{28,20... | collective-permute-start | bytes 393224 | tf_op jit(solution)/shard_map/ppermute | solution.py:458
  40.4 8.1 %collective-permute-start.15 = (bf16[272,128]{1,0:T(8,128)(2,1)S(1)}, bf16[272,128]{1,0:T(8,128)(2,1)S(1)}, u32[]{:S(2)}, u32[]{:S(2)}) collective-permute-start(bf16[272,128]{1,0:T(8,128)(2,1)S(1)} %get-tuple-element.71), channel_id=1, source_target_pairs={{0,8},{2,10},{4,12},{6,14},{8,16},{10,18},{12,20},{14,22},{16,24},... | collective-permute-start | bytes 208904 | tf_op jit(solution)/shard_map/ppermute | solution.py:221
  40.4 9.1 %collective-permute-start.16 = (bf16[272,128]{1,0:T(8,128)(2,1)S(1)}, bf16[272,128]{1,0:T(8,128)(2,1)S(1)}, u32[]{:S(2)}, u32[]{:S(2)}) collective-permute-start(bf16[272,128]{1,0:T(8,128)(2,1)S(1)} %get-tuple-element.72), channel_id=1, source_target_pairs={{0,16},{2,18},{4,20},{6,22},{8,24},{10,26},{12,28},{14,30},{16,0},... | collective-permute-start | bytes 208904 | tf_op jit(solution)/shard_map/ppermute | solution.py:221
  45.7 4.5 %collective-permute-start.17 = (bf16[272,128]{1,0:T(8,128)(2,1)S(1)}, bf16[272,128]{1,0:T(8,128)(2,1)S(1)}, u32[]{:S(2)}, u32[]{:S(2)}) collective-permute-start(bf16[272,128]{1,0:T(8,128)(2,1)S(1)} %get-tuple-element.73), channel_id=1, source_target_pairs={{0,24},{2,26},{4,28},{6,30},{8,0},{10,2},{12,4},{14,6},{16,8},{18,... | collective-permute-start | bytes 208904 | tf_op jit(solution)/shard_map/ppermute | solution.py:221
  48.4 4.5 %collective-permute-start.18 = (bf16[8,128,128]{2,1,0:T(8,128)(2,1)S(1)}, bf16[8,128,128]{2,1,0:T(8,128)(2,1)S(1)}, u32[]{:S(2)}, u32[]{:S(2)}) collective-permute-start(bf16[8,128,128]{2,1,0:T(8,128)(2,1)S(1)} %collective-permute-done.4.refs_4_), channel_id=1, source_target_pairs={{0,2},{2,0},{4,6},{6,4},{8,10},{10,8},{12,14},{14,12},{16,18},{18,... | collective-permute-start | bytes 786440 | tf_op jit(solution)/shard_map/ppermute | solution.py:470
  50.3 1.4 %collective-permute-start.20 = (bf16[4,128,128]{2,1,0:T(8,128)(2,1)S(1)}, bf16[4,128,128]{2,1,0:T(8,128)(2,1)S(1)}, u32[]{:S(2)}, u32[]{:S(2)}) collective-permute-start(bf16[4,128,128]{2,1,0:T(8,128)(2,1)S(1)} %collective-permute-done.13.refs_8_), channel_id=1, source_target_pairs={{0,2},{2,0},{4,6},{6,4},{8,10},{10,8},{12,14},{14,12},{16,18},{18,... | collective-permute-start | bytes 393224 | tf_op jit(solution)/shard_map/ppermute | solution.py:470
  50.3 2.7 %collective-permute-start.19 = (bf16[8,128,128]{2,1,0:T(8,128)(2,1)S(1)}, bf16[8,128,128]{2,1,0:T(8,128)(2,1)S(1)}, u32[]{:S(2)}, u32[]{:S(2)}) collective-permute-start(bf16[8,128,128]{2,1,0:T(8,128)(2,1)S(1)} %collective-permute-done.9.refs_6_), channel_id=1, source_target_pairs={{0,2},{2,0},{4,6},{6,4},{8,10},{10,8},{12,14},{14,12},{16,18},{18,... | collective-permute-start | bytes 786440 | tf_op jit(solution)/shard_map/ppermute | solution.py:470
  50.8 2.2 %collective-permute-start.22 = (bf16[8,128,128]{2,1,0:T(8,128)(2,1)S(1)}, bf16[8,128,128]{2,1,0:T(8,128)(2,1)S(1)}, u32[]{:S(2)}, u32[]{:S(2)}) collective-permute-start(bf16[8,128,128]{2,1,0:T(8,128)(2,1)S(1)} %collective-permute-done.8.refs_12_), channel_id=1, source_target_pairs={{0,2},{2,0},{4,6},{6,4},{8,10},{10,8},{12,14},{14,12},{16,18},{18,... | collective-permute-start | bytes 786440 | tf_op jit(solution)/shard_map/ppermute | solution.py:470
  50.9 2.1 %collective-permute-start.23 = (bf16[8,128,128]{2,1,0:T(8,128)(2,1)S(1)}, bf16[8,128,128]{2,1,0:T(8,128)(2,1)S(1)}, u32[]{:S(2)}, u32[]{:S(2)}) collective-permute-start(bf16[8,128,128]{2,1,0:T(8,128)(2,1)S(1)} %collective-permute-done.3.refs_14_), channel_id=1, source_target_pairs={{0,2},{2,0},{4,6},{6,4},{8,10},{10,8},{12,14},{14,12},{16,18},{18,... | collective-permute-start | bytes 786440 | tf_op jit(solution)/shard_map/ppermute | solution.py:470
  51.6 1.3 %collective-permute-start.21 = (bf16[4,128,128]{2,1,0:T(8,128)(2,1)S(1)}, bf16[4,128,128]{2,1,0:T(8,128)(2,1)S(1)}, u32[]{:S(2)}, u32[]{:S(2)}) collective-permute-start(bf16[4,128,128]{2,1,0:T(8,128)(2,1)S(1)} %collective-permute-done.14.refs_9_), channel_id=1, source_target_pairs={{0,2},{2,0},{4,6},{6,4},{8,10},{10,8},{12,14},{14,12},{16,18},{18,... | collective-permute-start | bytes 393224 | tf_op jit(solution)/shard_map/ppermute | solution.py:470

commit v12 on v11

--- a/solution.py
+++ b/solution.py
@@ -187,7 +187,7 @@
         ).astype(bf16)
 
 
-def reduce_chip(parts, shards, owners, own_rows):
+def exchange_chips(parts, shards, owners):
     given = []
     for o in range(owners):
         for column in range(2):
@@ -198,6 +198,10 @@
             ]
             part = parts[2 * o + column]
             given.append(lax.ppermute(part, AXES, pairs) if o or column else part)
+    return given
+
+
+def join_chips(parts, own_rows):
     levels, rows, rank = parts[0].shape
     spans = rows - own_rows - FACT_ROWS
     lines = -(-2 * len(parts) // FACT_ROWS) * FACT_ROWS
@@ -210,7 +214,7 @@
         out_shape=[shape] * levels,
         compiler_params=pltpu.CompilerParams(vmem_limit_bytes=16 * MIB),
         name="chip",
-    )(*given)
+    )(*parts)
 
 
 def reduce_levels(total, shards):
@@ -222,50 +226,36 @@
     return terms
 
 
-def steps_kernel(activity, start_in, subs_in, *refs, count, word_tiles, levels, slots, cached):
+def steps_kernel(activity, start, subs, *refs, count, word_tiles, levels, slots, cached):
     pieces, refs = refs[:count], refs[count:]
-    terms_in, refs = refs[:levels], refs[levels:]
+    terms, refs = refs[:levels], refs[levels:]
     first_out, second_out, third_out, dots_out = refs[:4]
-    masks, words, start, terms, subs, table, runs, lines = refs[4:12]
-    facts, chosen, places, arrived, moved, given = refs[12:18]
+    masks, words, table, runs, lines, facts, chosen, places, arrived, moved = refs[4:14]
     products = refs[-1]
     own_rows, rank = start.shape
     _, tile, _ = pieces[0].shape
     sources = lines.shape[0] // levels
     spans = 2 * slots * sources
 
-    gifts = [
-        pltpu.make_async_copy(term, terms.at[up], given.at[up]) for up, term in enumerate(terms_in)
-    ]
-    for copy in gifts:
-        copy.start()
     copies, at = [], 0
     for k, piece in enumerate(pieces):
         place = words.at[at : at + piece.shape[0]]
         copies.append(pltpu.make_async_copy(piece, place, arrived.at[k]))
         at += piece.shape[0]
-    look = pltpu.make_async_copy(subs_in, subs, moved.at[1])
-    look.start()
-    begin = pltpu.make_async_copy(start_in, start, moved.at[2])
-    begin.start()
     for copy in copies:
         copy.start()
-    for copy in gifts:
-        copy.wait()
 
     for up in range(levels):
-        rest = terms[up, own_rows + spans :, :].astype(f32)
+        rest = terms[up][own_rows + spans :, :].astype(f32)
         lines[up * sources : (up + 1) * sources, :] = rest[:sources].astype(jnp.int32)
     move = pltpu.make_async_copy(lines, facts, moved.at[0])
     move.start()
     rhs = jnp.zeros((own_rows, rank), f32)
     for up in range(levels):
-        rhs = rhs + terms[up, :own_rows, :].astype(f32)
-        runs[up * spans : (up + 1) * spans, :] = terms[
-            up, own_rows : own_rows + spans, :
+        rhs = rhs + terms[up][:own_rows, :].astype(f32)
+        runs[up * spans : (up + 1) * spans, :] = terms[up][
+            own_rows : own_rows + spans, :
         ].astype(f32)
-    begin.wait()
-    look.wait()
     table[...] = subs[...].astype(f32)
     move.wait()
 
@@ -378,9 +368,6 @@
     scratch = [
         pltpu.VMEM((chunks, own_rows, CHUNK * tile), bf16),
         pltpu.VMEM((sum(piece.shape[0] for piece in pieces), tile, rank), bf16),
-        pltpu.VMEM(start.shape, f32),
-        pltpu.VMEM((len(terms),) + terms[0].shape, bf16),
-        pltpu.VMEM(subs.shape, bf16),
         pltpu.VMEM(subs.shape, f32),
         pltpu.VMEM((2 * blocks, tile), f32),
         pltpu.VMEM((devices, rank), jnp.int32),
@@ -388,8 +375,7 @@
         pltpu.SMEM((blocks,), jnp.int32),
         pltpu.SMEM((devices,), jnp.int32),
         pltpu.SemaphoreType.DMA((len(pieces),)),
-        pltpu.SemaphoreType.DMA((3,)),
-        pltpu.SemaphoreType.DMA((len(terms),)),
+        pltpu.SemaphoreType.DMA((1,)),
     ]
     if cached:
         scratch.append(pltpu.VMEM((chunks, CHUNK * tile, rank), bf16))
@@ -402,7 +388,7 @@
             slots=slots,
             cached=cached,
         ),
-        in_specs=[whole] + [anywhere] * (2 + len(pieces) + len(terms)),
+        in_specs=[whole] * 3 + [anywhere] * len(pieces) + [whole] * len(terms),
         out_specs=[whole] * 4,
         out_shape=[vector, vector, vector, jax.ShapeDtypeStruct((devices, 1, rank), f32)],
         scratch_shapes=scratch,
@@ -510,7 +496,8 @@
     up, down, parts, crossed = together((up, down, parts, crossed))
 
     up, down = ring_round(up, down, held, 3, shards)
-    total = reduce_chip(parts, shards, owners, own_rows)
+    given = exchange_chips(parts, shards, owners)
+    total = join_chips(given, own_rows)
     up, down, total, held = together((up, down, total, held))
 
     for step in range(4, chips // 2 + 1):

time: 75.3 us -> 74.7 us (level)
  no operation moved by 1% of the time
where the time goes in v12:
time: 74.7 us; the launch traced here: 74.5 us
  Pallas kernels  23.5 us (31%)
  starting transfers between devices  20.9 us (28%)
  waiting for transfers between devices  19.2 us (26%)
  blocking collectives  9.92 us (13%)
  between operations  0.88 us (1%)
    pallas_call x2, Pallas kernels, rhs_sums(): pl.pallas_call(functools.partial(rhs_kernel, half=half, owners=owners, ow...  11.9 us
    ppermute x3, waiting for transfers between devices, exchange_chips(): given.append(lax.ppermute(part, AXES, pairs) if o or column else part)  10.8 us
    pallas_call x1, Pallas kernels, krylov(): pl.pallas_call(functools.partial(steps_kernel, count=len(pieces), word_ti...  10.7 us
    all_to_all x1, blocking collectives, on_device(): everyone = lax.all_to_all(dots, AXES, 0, 0, tiled=True)  9.92 us
    ppermute x3, starting transfers between devices, reduce_levels(): terms.append(lax.ppermute(total[up], 'loop', shift))  6.34 us
    ppermute x3, starting transfers between devices, ring_round(): down = lax.ppermute(down, 'loop', shift(-1))  4.45 us
    ppermute x3, waiting for transfers between devices, reduce_levels(): terms.append(lax.ppermute(total[up], 'loop', shift))  3.55 us
    ppermute x3, starting transfers between devices, exchange_chips(): given.append(lax.ppermute(part, AXES, pairs) if o or column else part)  3.49 us
  transfers between devices with their start and end apart: 24, of which 11 were waited for; matrix products, arithmetic and copies ran while one was open for 0% of the time, Pallas kernels for 16%

profile of v12, /device:TPU:0, one launch (start us, length us, event | category | flops | bytes accessed | tf_op | source)
XLA Modules:
  0.0 74.5 jit_solution(14873649746758449733)
XLA Ops:
  0.7 0.5 collective-permute-start.2
  1.2 2.5 %collective-permute-start.1 = (bf16[8,128,128]{2,1,0:T(8,128)(2,1)}, bf16[8,128,128]{2,1,0:T(8,128)(2,1)S(1)}, u32[]{:S(2)}, u32[]{:S(2)}) collective-permute-start(bf16[8,128,128]{2,1,0:T(8,128)(2,1)} %bitcast.15), channel_id=1, source_target_pairs={{0,4},{2,6},{8,0},{10,2},{16,8},{18,10},{24,16},{26,18},{28,24},{3... | collective-permute-start | bytes 786440 | tf_op jit(solution)/shard_map/ppermute | solution.py:449
  3.8 0.2 collective-permute-start
  3.9 6.8 %rhs.2 = bf16[2,2,4,160,128]{4,3,2,1,0:T(8,128)(2,1)} custom-call(s32[8,16]{1,0:T(8,128)} %bitcast.23, s32[8,16]{1,0:T(8,128)} %bitcast.25, s32[8,16]{1,0:T(8,128)} %bitcast.27, s32[1,16]{1,0:T(1,128)} %bitcast.29, bf16[16,8,128,128]{3,2,1,0:T(8,128)(2,1)} %bitcast.31, s32[16,8,2,128]{3,2,1,0:T(2,128)} %bitcast.21, bf16[8,128,128]{2,1,0:T(8,128)(2,1)} %bitcast.17, ...), custom_call_target="tpu_custom_call" | custom-call | flops 2147483648 | bytes 16777216 | tf_op jit(solution)/shard_map/rhs/pallas_call | solution.py:145
  10.8 0.0 copy-start.2
  10.8 0.0 copy-start.3
  10.8 0.2 collective-permute-done.1.refs_2_
  11.0 1.4 %collective-permute-done.refs_16_ = bf16[8,128,128]{2,1,0:T(8,128)(2,1)S(1)} collective-permute-done((bf16[8,128,128]{2,1,0:T(8,128)(2,1)}, bf16[8,128,128]{2,1,0:T(8,128)(2,1)S(1)}, u32[]{:S(2)}, u32[]{:S(2)}) %collective-permute-start) | collective-permute-done | bytes 262176 | tf_op jit(solution)/shard_map/ppermute | solution.py:448
  12.4 0.5 collective-permute-start.3
  12.9 0.2 collective-permute-start.6
  13.1 0.3 collective-permute-start.7
  13.4 1.5 %collective-permute-start.4 = (bf16[8,128,128]{2,1,0:T(8,128)(2,1)S(1)}, bf16[8,128,128]{2,1,0:T(8,128)(2,1)S(1)}, u32[]{:S(2)}, u32[]{:S(2)}) collective-permute-start(bf16[8,128,128]{2,1,0:T(8,128)(2,1)S(1)} %collective-permute-done.1.refs_2_), channel_id=1, source_target_pairs={{0,4},{2,6},{8,0},{10,2},{16,8},{18,10},{24,16},{26,18},{28,24},{3... | collective-permute-start | bytes 786440 | tf_op jit(solution)/shard_map/ppermute | solution.py:449
  15.0 5.0 %rhs.3 = (bf16[4,176,128]{2,1,0:T(8,128)(2,1)S(1)}, bf16[4,176,128]{2,1,0:T(8,128)(2,1)S(1)}, bf16[4,176,128]{2,1,0:T(8,128)(2,1)S(1)}, bf16[4,176,128]{2,1,0:T(8,128)(2,1)S(1)}) custom-call(s32[8,16]{1,0:T(8,128)S(1)} %bitcast.24, s32[8,16]{1,0:T(8,128)S(1)} %bitcast.26, s32[8,16]{1,0:T(8,128)S(1)} %bitcast.28, s32[1,16]{1,0:T(1,128)S(1)} %bitcast.30, ...), custom_call_target="tpu_custom_call" | custom-call | flops 2147483648 | bytes 16777216 | tf_op jit(solution)/shard_map/rhs/pallas_call | solution.py:145
  20.0 0.0 collective-permute-done.7.refs_17_
  20.0 1.1 %collective-permute-done.3.refs_14_ = bf16[8,128,128]{2,1,0:T(8,128)(2,1)S(1)} collective-permute-done((bf16[8,128,128]{2,1,0:T(8,128)(2,1)S(1)}, bf16[8,128,128]{2,1,0:T(8,128)(2,1)S(1)}, u32[]{:S(2)}, u32[]{:S(2)}) %collective-permute-start.3) | collective-permute-done | bytes 262176 | tf_op jit(solution)/shard_map/ppermute | solution.py:448
  21.1 0.7 collective-permute-done.4.refs_4_
  21.8 1.6 %collective-permute-start.8 = (bf16[8,128,128]{2,1,0:T(8,128)(2,1)S(1)}, bf16[8,128,128]{2,1,0:T(8,128)(2,1)S(1)}, u32[]{:S(2)}, u32[]{:S(2)}) collective-permute-start(bf16[8,128,128]{2,1,0:T(8,128)(2,1)S(1)} %collective-permute-done.3.refs_14_), channel_id=1, source_target_pairs={{0,8},{2,10},{8,16},{10,18},{16,24},{18,26},{24,28},{26,30},{28,20... | collective-permute-start | bytes 786440 | tf_op jit(solution)/shard_map/ppermute | solution.py:448
  23.4 0.4 collective-permute-start.9
  23.9 1.5 %collective-permute-start.10 = (bf16[4,176,128]{2,1,0:T(8,128)(2,1)S(1)}, bf16[4,176,128]{2,1,0:T(8,128)(2,1)S(1)}, u32[]{:S(2)}, u32[]{:S(2)}) collective-permute-start(bf16[4,176,128]{2,1,0:T(8,128)(2,1)S(1)} %get-tuple-element.60), channel_id=1, source_target_pairs={{0,4},{1,5},{2,6},{3,7},{4,0},{5,1},{6,2},{7,3},{8,12},{9,13},{10,... | collective-permute-start | bytes 540680 | tf_op jit(solution)/shard_map/ppermute | solution.py:200
  25.4 1.5 %collective-permute-start.11 = (bf16[4,176,128]{2,1,0:T(8,128)(2,1)S(1)}, bf16[4,176,128]{2,1,0:T(8,128)(2,1)S(1)}, u32[]{:S(2)}, u32[]{:S(2)}) collective-permute-start(bf16[4,176,128]{2,1,0:T(8,128)(2,1)S(1)} %get-tuple-element.61), channel_id=1, source_target_pairs={{0,1},{1,0},{2,3},{3,2},{4,5},{5,4},{6,7},{7,6},{8,9},{9,8},{10,11... | collective-permute-start | bytes 540680 | tf_op jit(solution)/shard_map/ppermute | solution.py:200
  26.9 0.5 collective-permute-start.12
  27.3 7.6 %collective-permute-done.10.refs_1_ = bf16[4,176,128]{2,1,0:T(8,128)(2,1)S(1)} collective-permute-done((bf16[4,176,128]{2,1,0:T(8,128)(2,1)S(1)}, bf16[4,176,128]{2,1,0:T(8,128)(2,1)S(1)}, u32[]{:S(2)}, u32[]{:S(2)}) %collective-permute-start.10) | collective-permute-done | bytes 180256 | tf_op jit(solution)/shard_map/ppermute | solution.py:200
  34.9 0.0 collective-permute-done.11.refs_2_
  34.9 3.2 %collective-permute-done.12.refs_3_ = bf16[4,176,128]{2,1,0:T(8,128)(2,1)S(1)} collective-permute-done((bf16[4,176,128]{2,1,0:T(8,128)(2,1)S(1)}, bf16[4,176,128]{2,1,0:T(8,128)(2,1)S(1)}, u32[]{:S(2)}, u32[]{:S(2)}) %collective-permute-start.12) | collective-permute-done | bytes 180256 | tf_op jit(solution)/shard_map/ppermute | solution.py:200
  38.1 0.1 chip.1
  38.2 0.0 collective-permute-done.8.refs_12_
  38.2 0.0 collective-permute-done.9.refs_6_
  38.3 1.8 %collective-permute-start.14 = (bf16[4,128,128]{2,1,0:T(8,128)(2,1)S(1)}, bf16[4,128,128]{2,1,0:T(8,128)(2,1)S(1)}, u32[]{:S(2)}, u32[]{:S(2)}) collective-permute-start(bf16[4,128,128]{2,1,0:T(8,128)(2,1)S(1)} %slice.7), channel_id=1, source_target_pairs={{0,4},{2,6},{8,0},{10,2},{16,8},{18,10},{24,16},{26,18},{28,24},{3... | collective-permute-start | bytes 393224 | tf_op jit(solution)/shard_map/ppermute | solution.py:445
  40.1 0.3 collective-permute-start.13
  40.4 0.0 collective-permute-start.15
  40.4 5.3 %collective-permute-start.16 = (bf16[272,128]{1,0:T(8,128)(2,1)S(1)}, bf16[272,128]{1,0:T(8,128)(2,1)S(1)}, u32[]{:S(2)}, u32[]{:S(2)}) collective-permute-start(bf16[272,128]{1,0:T(8,128)(2,1)S(1)} %get-tuple-element.72), channel_id=1, source_target_pairs={{0,16},{2,18},{4,20},{6,22},{8,24},{10,26},{12,28},{14,30},{16,0},... | collective-permute-start | bytes 208904 | tf_op jit(solution)/shard_map/ppermute | solution.py:225
  45.7 1.0 %collective-permute-start.17 = (bf16[272,128]{1,0:T(8,128)(2,1)S(1)}, bf16[272,128]{1,0:T(8,128)(2,1)S(1)}, u32[]{:S(2)}, u32[]{:S(2)}) collective-permute-start(bf16[272,128]{1,0:T(8,128)(2,1)S(1)} %get-tuple-element.73), channel_id=1, source_target_pairs={{0,24},{2,26},{4,28},{6,30},{8,0},{10,2},{12,4},{14,6},{16,8},{18,... | collective-permute-start | bytes 208904 | tf_op jit(solution)/shard_map/ppermute | solution.py:225
  46.7 1.7 %collective-permute-done.15.refs_19_ = bf16[272,128]{1,0:T(8,128)(2,1)S(1)} collective-permute-done((bf16[272,128]{1,0:T(8,128)(2,1)S(1)}, bf16[272,128]{1,0:T(8,128)(2,1)S(1)}, u32[]{:S(2)}, u32[]{:S(2)}) %collective-permute-start.15) | collective-permute-done | bytes 69664 | tf_op jit(solution)/shard_map/ppermute | solution.py:225
  48.4 0.0 collective-permute-start.18
  48.4 1.1 %collective-permute-done.16.refs_20_ = bf16[272,128]{1,0:T(8,128)(2,1)S(1)} collective-permute-done((bf16[272,128]{1,0:T(8,128)(2,1)S(1)}, bf16[272,128]{1,0:T(8,128)(2,1)S(1)}, u32[]{:S(2)}, u32[]{:S(2)}) %collective-permute-start.16) | collective-permute-done | bytes 69664 | tf_op jit(solution)/shard_map/ppermute | solution.py:225
  49.5 0.7 collective-permute-done.17.refs_21_
  50.3 0.0 collective-permute-done.13.refs_8_
  50.3 0.0 collective-permute-start.20
  50.3 0.5 collective-permute-start.19
  50.8 0.1 collective-permute-start.22
  50.9 0.4 collective-permute-start.23
  51.3 0.3 collective-permute-done.20.refs_10_
  51.6 0.1 collective-permute-start.21
  51.8 1.2 %collective-permute-done.21.refs_11_ = bf16[4,128,128]{2,1,0:T(8,128)(2,1)S(1)} collective-permute-done((bf16[4,128,128]{2,1,0:T(8,128)(2,1)S(1)}, bf16[4,128,128]{2,1,0:T(8,128)(2,1)S(1)}, u32[]{:S(2)}, u32[]{:S(2)}) %collective-permute-start.21) | collective-permute-done | bytes 131104 | tf_op jit(solution)/shard_map/ppermute | solution.py:456
  53.0 0.0 collective-permute-done.18.refs_5_
  53.0 10.7 %krylov.1 = (f32[128,128]{1,0:T(8,128)S(1)}, f32[128,128]{1,0:T(8,128)S(1)}, f32[128,128]{1,0:T(8,128)S(1)}, f32[32,1,128]{2,1,0:T(1,128)S(1)}) custom-call(f32[1,128]{1,0:T(1,128)S(1)} %bitcast.20, f32[128,128]{1,0:T(8,128)S(1)} %copy-done.2, bf16[2048,128]{1,0:T(8,128)(2,1)S(1)} %copy-done, bf16[8,128,128]{2,1,0:T(8,128)(2,1)S(1)} %bitcast.19, ...), custom_call_target="tpu_custom_call" | custom-call | tf_op jit(solution)/shard_map/krylov/pallas_call | solution.py:382
  63.7 9.9 %all_to_all.5.dots = f32[32,1,128]{2,1,0:T(1,128)S(1)} all-to-all(f32[32,1,128]{2,1,0:T(1,128)S(1)} %get-tuple-element.92), channel_id=1, replica_groups=mesh['loop'=16,'own'=2] {'loop','own'}, dimensions={0} | all-to-all | bytes 32768 | tf_op jit(solution)/shard_map/all_to_all | solution.py:516
  73.6 0.9 %last_step.1 = (f32[128,128]{1,0:T(8,128)}, f32[128,128]{1,0:T(8,128)}) custom-call(f32[32,1,128]{2,1,0:T(1,128)S(1)} %all_to_all.5.dots, f32[128,128]{1,0:T(8,128)S(1)} %copy-done.2, f32[128,128]{1,0:T(8,128)S(1)} %get-tuple-element.93.first, f32[128,128]{1,0:T(8,128)S(1)} %get-tuple-element.94.second, f32[128,128]{1,0:T(8,128)S(1)} %get-tuple-element.95.third), custom_call_target="tpu_custom_call" | custom-call | tf_op jit(solution)/shard_map/last_step/pallas_call | solution.py:418
  (26 shorter events, 0.1 us)
Async XLA Ops:
  0.6 14.3 %copy-start.1 = (bf16[1,8,128,128]{3,2,1,0:T(8,128)(2,1)S(1)}, bf16[1,8,128,128]{3,2,1,0:T(8,128)(2,1)}, u32[]{:S(2)}) copy-start(bf16[1,8,128,128]{3,2,1,0:T(8,128)(2,1)} %param.12) | copy-start | bytes 786436
  0.6 14.3 %copy-start = (bf16[2048,128]{1,0:T(8,128)(2,1)S(1)}, bf16[2048,128]{1,0:T(8,128)(2,1)}, u32[]{:S(2)}) copy-start(bf16[2048,128]{1,0:T(8,128)(2,1)} %subs.1) | copy-start | bytes 1572868
  0.7 14.3 %copy-start.4 = (s32[1,1,16,8,2,128]{5,4,3,2,1,0:T(2,128)S(1)}, s32[1,1,16,8,2,128]{5,4,3,2,1,0:T(2,128)}, u32[]{:S(2)}) copy-start(s32[1,1,16,8,2,128]{5,4,3,2,1,0:T(2,128)} %param.19) | copy-start | bytes 393220
  0.7 14.3 %copy-start.8 = (s32[1,1,16]{2,1,0:T(1,128)S(1)}, s32[1,1,16]{2,1,0:T(1,128)}, u32[]{:S(2)}) copy-start(s32[1,1,16]{2,1,0:T(1,128)} %param.18) | copy-start | bytes 196
  0.7 14.3 %copy-start.7 = (s32[1,1,16,8]{2,3,1,0:T(8,128)S(1)}, s32[1,1,16,8]{2,3,1,0:T(8,128)}, u32[]{:S(2)}) copy-start(s32[1,1,16,8]{2,3,1,0:T(8,128)} %param.17) | copy-start | bytes 1540
  0.7 14.3 %copy-start.6 = (s32[1,1,16,8]{2,3,1,0:T(8,128)S(1)}, s32[1,1,16,8]{2,3,1,0:T(8,128)}, u32[]{:S(2)}) copy-start(s32[1,1,16,8]{2,3,1,0:T(8,128)} %param.16) | copy-start | bytes 1540
  0.7 14.3 %copy-start.5 = (s32[1,1,16,8]{2,3,1,0:T(8,128)S(1)}, s32[1,1,16,8]{2,3,1,0:T(8,128)}, u32[]{:S(2)}) copy-start(s32[1,1,16,8]{2,3,1,0:T(8,128)} %param.15) | copy-start | bytes 1540
  0.7 10.1 %collective-permute-start.2 = (bf16[8,128,128]{2,1,0:T(8,128)(2,1)}, bf16[8,128,128]{2,1,0:T(8,128)(2,1)S(1)}, u32[]{:S(2)}, u32[]{:S(2)}) collective-permute-start(bf16[8,128,128]{2,1,0:T(8,128)(2,1)} %bitcast.14), channel_id=1, source_target_pairs={{0,2},{2,0},{4,6},{6,4},{8,10},{10,8},{12,14},{14,12},{16,18},{18,... | collective-permute-start | bytes 786440 | tf_op jit(solution)/shard_map/ppermute | solution.py:456
  1.2 9.8 %collective-permute-start.1 = (bf16[8,128,128]{2,1,0:T(8,128)(2,1)}, bf16[8,128,128]{2,1,0:T(8,128)(2,1)S(1)}, u32[]{:S(2)}, u32[]{:S(2)}) collective-permute-start(bf16[8,128,128]{2,1,0:T(8,128)(2,1)} %bitcast.15), channel_id=1, source_target_pairs={{0,4},{2,6},{8,0},{10,2},{16,8},{18,10},{24,16},{26,18},{28,24},{3... | collective-permute-start | bytes 786440 | tf_op jit(solution)/shard_map/ppermute | solution.py:449
  3.8 8.6 %collective-permute-start = (bf16[8,128,128]{2,1,0:T(8,128)(2,1)}, bf16[8,128,128]{2,1,0:T(8,128)(2,1)S(1)}, u32[]{:S(2)}, u32[]{:S(2)}) collective-permute-start(bf16[8,128,128]{2,1,0:T(8,128)(2,1)} %bitcast.16), channel_id=1, source_target_pairs={{0,8},{2,10},{8,16},{10,18},{16,24},{18,26},{24,28},{26,30},{28,20... | collective-permute-start | bytes 786440 | tf_op jit(solution)/shard_map/ppermute | solution.py:448
  10.8 42.2 %copy-start.2 = (f32[128,128]{1,0:T(8,128)S(1)}, f32[128,128]{1,0:T(8,128)}, u32[]{:S(2)}) copy-start(f32[128,128]{1,0:T(8,128)} %start.3) | copy-start | bytes 196612
  10.8 42.2 %copy-start.3 = (f32[128]{0:T(128)S(1)}, f32[128]{0:T(128)}, u32[]{:S(2)}) copy-start(f32[128]{0:T(128)} %param.11) | copy-start | bytes 1540
  12.4 2.5 %collective-permute-start.5 = (bf16[2,2,4,160,128]{4,3,2,1,0:T(8,128)(2,1)}, bf16[2,2,4,160,128]{4,3,2,1,0:T(8,128)(2,1)S(1)}, u32[]{:S(2)}, u32[]{:S(2)}) collective-permute-start(bf16[2,2,4,160,128]{4,3,2,1,0:T(8,128)(2,1)} %rhs.2), channel_id=1, source_target_pairs={{0,2},{2,0},{4,6},{6,4},{8,10},{10,8},{12,14},{14,12},{16,18},{18,... | collective-permute-start | bytes 1966088 | tf_op jit(solution)/shard_map/ppermute | solution.py:456
  12.4 8.7 %collective-permute-start.3 = (bf16[8,128,128]{2,1,0:T(8,128)(2,1)S(1)}, bf16[8,128,128]{2,1,0:T(8,128)(2,1)S(1)}, u32[]{:S(2)}, u32[]{:S(2)}) collective-permute-start(bf16[8,128,128]{2,1,0:T(8,128)(2,1)S(1)} %collective-permute-done.refs_16_), channel_id=1, source_target_pairs={{0,8},{2,10},{8,16},{10,18},{16,24},{18,26},{24,28},{26,30},{28,20... | collective-permute-start | bytes 786440 | tf_op jit(solution)/shard_map/ppermute | solution.py:448
  12.9 7.1 %collective-permute-start.6 = (bf16[8,128,128]{2,1,0:T(8,128)(2,1)S(1)}, bf16[8,128,128]{2,1,0:T(8,128)(2,1)S(1)}, u32[]{:S(2)}, u32[]{:S(2)}) collective-permute-start(bf16[8,128,128]{2,1,0:T(8,128)(2,1)S(1)} %collective-permute-done.1.refs_2_), channel_id=1, source_target_pairs={{0,2},{2,0},{4,6},{6,4},{8,10},{10,8},{12,14},{14,12},{16,18},{18,... | collective-permute-start | bytes 786440 | tf_op jit(solution)/shard_map/ppermute | solution.py:456
  13.1 6.9 %collective-permute-start.7 = (bf16[8,128,128]{2,1,0:T(8,128)(2,1)S(1)}, bf16[8,128,128]{2,1,0:T(8,128)(2,1)S(1)}, u32[]{:S(2)}, u32[]{:S(2)}) collective-permute-start(bf16[8,128,128]{2,1,0:T(8,128)(2,1)S(1)} %collective-permute-done.refs_16_), channel_id=1, source_target_pairs={{0,2},{2,0},{4,6},{6,4},{8,10},{10,8},{12,14},{14,12},{16,18},{18,... | collective-permute-start | bytes 786440 | tf_op jit(solution)/shard_map/ppermute | solution.py:456
  13.4 8.4 %collective-permute-start.4 = (bf16[8,128,128]{2,1,0:T(8,128)(2,1)S(1)}, bf16[8,128,128]{2,1,0:T(8,128)(2,1)S(1)}, u32[]{:S(2)}, u32[]{:S(2)}) collective-permute-start(bf16[8,128,128]{2,1,0:T(8,128)(2,1)S(1)} %collective-permute-done.1.refs_2_), channel_id=1, source_target_pairs={{0,4},{2,6},{8,0},{10,2},{16,8},{18,10},{24,16},{26,18},{28,24},{3... | collective-permute-start | bytes 786440 | tf_op jit(solution)/shard_map/ppermute | solution.py:449
  21.8 16.4 %collective-permute-start.8 = (bf16[8,128,128]{2,1,0:T(8,128)(2,1)S(1)}, bf16[8,128,128]{2,1,0:T(8,128)(2,1)S(1)}, u32[]{:S(2)}, u32[]{:S(2)}) collective-permute-start(bf16[8,128,128]{2,1,0:T(8,128)(2,1)S(1)} %collective-permute-done.3.refs_14_), channel_id=1, source_target_pairs={{0,8},{2,10},{8,16},{10,18},{16,24},{18,26},{24,28},{26,30},{28,20... | collective-permute-start | bytes 786440 | tf_op jit(solution)/shard_map/ppermute | solution.py:448
  23.4 14.8 %collective-permute-start.9 = (bf16[8,128,128]{2,1,0:T(8,128)(2,1)S(1)}, bf16[8,128,128]{2,1,0:T(8,128)(2,1)S(1)}, u32[]{:S(2)}, u32[]{:S(2)}) collective-permute-start(bf16[8,128,128]{2,1,0:T(8,128)(2,1)S(1)} %collective-permute-done.4.refs_4_), channel_id=1, source_target_pairs={{0,4},{2,6},{8,0},{10,2},{16,8},{18,10},{24,16},{26,18},{28,24},{3... | collective-permute-start | bytes 786440 | tf_op jit(solution)/shard_map/ppermute | solution.py:449
  23.9 11.1 %collective-permute-start.10 = (bf16[4,176,128]{2,1,0:T(8,128)(2,1)S(1)}, bf16[4,176,128]{2,1,0:T(8,128)(2,1)S(1)}, u32[]{:S(2)}, u32[]{:S(2)}) collective-permute-start(bf16[4,176,128]{2,1,0:T(8,128)(2,1)S(1)} %get-tuple-element.60), channel_id=1, source_target_pairs={{0,4},{1,5},{2,6},{3,7},{4,0},{5,1},{6,2},{7,3},{8,12},{9,13},{10,... | collective-permute-start | bytes 540680 | tf_op jit(solution)/shard_map/ppermute | solution.py:200
  25.4 9.5 %collective-permute-start.11 = (bf16[4,176,128]{2,1,0:T(8,128)(2,1)S(1)}, bf16[4,176,128]{2,1,0:T(8,128)(2,1)S(1)}, u32[]{:S(2)}, u32[]{:S(2)}) collective-permute-start(bf16[4,176,128]{2,1,0:T(8,128)(2,1)S(1)} %get-tuple-element.61), channel_id=1, source_target_pairs={{0,1},{1,0},{2,3},{3,2},{4,5},{5,4},{6,7},{7,6},{8,9},{9,8},{10,11... | collective-permute-start | bytes 540680 | tf_op jit(solution)/shard_map/ppermute | solution.py:200
  26.9 11.3 %collective-permute-start.12 = (bf16[4,176,128]{2,1,0:T(8,128)(2,1)S(1)}, bf16[4,176,128]{2,1,0:T(8,128)(2,1)S(1)}, u32[]{:S(2)}, u32[]{:S(2)}) collective-permute-start(bf16[4,176,128]{2,1,0:T(8,128)(2,1)S(1)} %get-tuple-element.62), channel_id=1, source_target_pairs={{0,5},{1,4},{2,7},{3,6},{4,1},{5,0},{6,3},{7,2},{8,13},{9,12},{10,... | collective-permute-start | bytes 540680 | tf_op jit(solution)/shard_map/ppermute | solution.py:200
  38.3 12.0 %collective-permute-start.14 = (bf16[4,128,128]{2,1,0:T(8,128)(2,1)S(1)}, bf16[4,128,128]{2,1,0:T(8,128)(2,1)S(1)}, u32[]{:S(2)}, u32[]{:S(2)}) collective-permute-start(bf16[4,128,128]{2,1,0:T(8,128)(2,1)S(1)} %slice.7), channel_id=1, source_target_pairs={{0,4},{2,6},{8,0},{10,2},{16,8},{18,10},{24,16},{26,18},{28,24},{3... | collective-permute-start | bytes 393224 | tf_op jit(solution)/shard_map/ppermute | solution.py:445
  40.1 10.2 %collective-permute-start.13 = (bf16[4,128,128]{2,1,0:T(8,128)(2,1)S(1)}, bf16[4,128,128]{2,1,0:T(8,128)(2,1)S(1)}, u32[]{:S(2)}, u32[]{:S(2)}) collective-permute-start(bf16[4,128,128]{2,1,0:T(8,128)(2,1)S(1)} %slice.6), channel_id=1, source_target_pairs={{0,8},{2,10},{8,16},{10,18},{16,24},{18,26},{24,28},{26,30},{28,20... | collective-permute-start | bytes 393224 | tf_op jit(solution)/shard_map/ppermute | solution.py:444
  40.4 8.1 %collective-permute-start.15 = (bf16[272,128]{1,0:T(8,128)(2,1)S(1)}, bf16[272,128]{1,0:T(8,128)(2,1)S(1)}, u32[]{:S(2)}, u32[]{:S(2)}) collective-permute-start(bf16[272,128]{1,0:T(8,128)(2,1)S(1)} %get-tuple-element.71), channel_id=1, source_target_pairs={{0,8},{2,10},{4,12},{6,14},{8,16},{10,18},{12,20},{14,22},{16,24},... | collective-permute-start | bytes 208904 | tf_op jit(solution)/shard_map/ppermute | solution.py:225
  40.4 9.1 %collective-permute-start.16 = (bf16[272,128]{1,0:T(8,128)(2,1)S(1)}, bf16[272,128]{1,0:T(8,128)(2,1)S(1)}, u32[]{:S(2)}, u32[]{:S(2)}) collective-permute-start(bf16[272,128]{1,0:T(8,128)(2,1)S(1)} %get-tuple-element.72), channel_id=1, source_target_pairs={{0,16},{2,18},{4,20},{6,22},{8,24},{10,26},{12,28},{14,30},{16,0},... | collective-permute-start | bytes 208904 | tf_op jit(solution)/shard_map/ppermute | solution.py:225
  45.7 4.5 %collective-permute-start.17 = (bf16[272,128]{1,0:T(8,128)(2,1)S(1)}, bf16[272,128]{1,0:T(8,128)(2,1)S(1)}, u32[]{:S(2)}, u32[]{:S(2)}) collective-permute-start(bf16[272,128]{1,0:T(8,128)(2,1)S(1)} %get-tuple-element.73), channel_id=1, source_target_pairs={{0,24},{2,26},{4,28},{6,30},{8,0},{10,2},{12,4},{14,6},{16,8},{18,... | collective-permute-start | bytes 208904 | tf_op jit(solution)/shard_map/ppermute | solution.py:225
  48.4 4.5 %collective-permute-start.18 = (bf16[8,128,128]{2,1,0:T(8,128)(2,1)S(1)}, bf16[8,128,128]{2,1,0:T(8,128)(2,1)S(1)}, u32[]{:S(2)}, u32[]{:S(2)}) collective-permute-start(bf16[8,128,128]{2,1,0:T(8,128)(2,1)S(1)} %collective-permute-done.4.refs_4_), channel_id=1, source_target_pairs={{0,2},{2,0},{4,6},{6,4},{8,10},{10,8},{12,14},{14,12},{16,18},{18,... | collective-permute-start | bytes 786440 | tf_op jit(solution)/shard_map/ppermute | solution.py:456
  50.3 1.4 %collective-permute-start.20 = (bf16[4,128,128]{2,1,0:T(8,128)(2,1)S(1)}, bf16[4,128,128]{2,1,0:T(8,128)(2,1)S(1)}, u32[]{:S(2)}, u32[]{:S(2)}) collective-permute-start(bf16[4,128,128]{2,1,0:T(8,128)(2,1)S(1)} %collective-permute-done.13.refs_8_), channel_id=1, source_target_pairs={{0,2},{2,0},{4,6},{6,4},{8,10},{10,8},{12,14},{14,12},{16,18},{18,... | collective-permute-start | bytes 393224 | tf_op jit(solution)/shard_map/ppermute | solution.py:456
  50.3 2.7 %collective-permute-start.19 = (bf16[8,128,128]{2,1,0:T(8,128)(2,1)S(1)}, bf16[8,128,128]{2,1,0:T(8,128)(2,1)S(1)}, u32[]{:S(2)}, u32[]{:S(2)}) collective-permute-start(bf16[8,128,128]{2,1,0:T(8,128)(2,1)S(1)} %collective-permute-done.9.refs_6_), channel_id=1, source_target_pairs={{0,2},{2,0},{4,6},{6,4},{8,10},{10,8},{12,14},{14,12},{16,18},{18,... | collective-permute-start | bytes 786440 | tf_op jit(solution)/shard_map/ppermute | solution.py:456
  50.8 2.2 %collective-permute-start.22 = (bf16[8,128,128]{2,1,0:T(8,128)(2,1)S(1)}, bf16[8,128,128]{2,1,0:T(8,128)(2,1)S(1)}, u32[]{:S(2)}, u32[]{:S(2)}) collective-permute-start(bf16[8,128,128]{2,1,0:T(8,128)(2,1)S(1)} %collective-permute-done.8.refs_12_), channel_id=1, source_target_pairs={{0,2},{2,0},{4,6},{6,4},{8,10},{10,8},{12,14},{14,12},{16,18},{18,... | collective-permute-start | bytes 786440 | tf_op jit(solution)/shard_map/ppermute | solution.py:456
  50.9 2.1 %collective-permute-start.23 = (bf16[8,128,128]{2,1,0:T(8,128)(2,1)S(1)}, bf16[8,128,128]{2,1,0:T(8,128)(2,1)S(1)}, u32[]{:S(2)}, u32[]{:S(2)}) collective-permute-start(bf16[8,128,128]{2,1,0:T(8,128)(2,1)S(1)} %collective-permute-done.3.refs_14_), channel_id=1, source_target_pairs={{0,2},{2,0},{4,6},{6,4},{8,10},{10,8},{12,14},{14,12},{16,18},{18,... | collective-permute-start | bytes 786440 | tf_op jit(solution)/shard_map/ppermute | solution.py:456
  51.6 1.3 %collective-permute-start.21 = (bf16[4,128,128]{2,1,0:T(8,128)(2,1)S(1)}, bf16[4,128,128]{2,1,0:T(8,128)(2,1)S(1)}, u32[]{:S(2)}, u32[]{:S(2)}) collective-permute-start(bf16[4,128,128]{2,1,0:T(8,128)(2,1)S(1)} %collective-permute-done.14.refs_9_), channel_id=1, source_target_pairs={{0,2},{2,0},{4,6},{6,4},{8,10},{10,8},{12,14},{14,12},{16,18},{18,... | collective-permute-start | bytes 393224 | tf_op jit(solution)/shard_map/ppermute | solution.py:456

commit v13 on v12

--- a/solution.py
+++ b/solution.py
@@ -503,8 +503,6 @@
     for step in range(4, chips // 2 + 1):
         up, down = ring_round(up, down, held, step, shards)
     terms = reduce_levels(total, shards)
-    held[chips // 2], terms, crossed = together((held[chips // 2], terms, crossed))
-
     for step in range(2, chips // 2 + 1):
         cross(step)
     pieces = []

time: 74.7 us -> 74.1 us (level)
  no operation moved by 1% of the time
where the time goes in v13:
time: 74.1 us; the launch traced here: 73.9 us
  Pallas kernels  23.5 us (32%)
  starting transfers between devices  20.9 us (28%)
  waiting for transfers between devices  18.9 us (26%)
  blocking collectives  9.66 us (13%)
  between operations  0.87 us (1%)
    pallas_call x2, Pallas kernels, rhs_sums(): pl.pallas_call(functools.partial(rhs_kernel, half=half, owners=owners, ow...  11.9 us
    ppermute x3, waiting for transfers between devices, exchange_chips(): given.append(lax.ppermute(part, AXES, pairs) if o or column else part)  10.8 us
    pallas_call x1, Pallas kernels, krylov(): pl.pallas_call(functools.partial(steps_kernel, count=len(pieces), word_ti...  10.7 us
    all_to_all x1, blocking collectives, on_device(): everyone = lax.all_to_all(dots, AXES, 0, 0, tiled=True)  9.66 us
    ppermute x3, starting transfers between devices, reduce_levels(): terms.append(lax.ppermute(total[up], 'loop', shift))  6.3 us
    ppermute x3, starting transfers between devices, ring_round(): down = lax.ppermute(down, 'loop', shift(-1))  4.43 us
    ppermute x3, starting transfers between devices, exchange_chips(): given.append(lax.ppermute(part, AXES, pairs) if o or column else part)  3.49 us
    ppermute x3, waiting for transfers between devices, reduce_levels(): terms.append(lax.ppermute(total[up], 'loop', shift))  3.04 us
  transfers between devices with their start and end apart: 24, of which 11 were waited for; matrix products, arithmetic and copies ran while one was open for 0% of the time, Pallas kernels for 16%

profile of v13, /device:TPU:0, one launch (start us, length us, event | category | flops | bytes accessed | tf_op | source)
XLA Modules:
  0.0 73.9 jit_solution(16066890299218709684)
XLA Ops:
  0.7 0.5 collective-permute-start.2
  1.2 2.5 %collective-permute-start.1 = (bf16[8,128,128]{2,1,0:T(8,128)(2,1)}, bf16[8,128,128]{2,1,0:T(8,128)(2,1)S(1)}, u32[]{:S(2)}, u32[]{:S(2)}) collective-permute-start(bf16[8,128,128]{2,1,0:T(8,128)(2,1)} %bitcast.15), channel_id=1, source_target_pairs={{0,4},{2,6},{8,0},{10,2},{16,8},{18,10},{24,16},{26,18},{28,24},{3... | collective-permute-start | bytes 786440 | tf_op jit(solution)/shard_map/ppermute | solution.py:449
  3.8 0.2 collective-permute-start
  3.9 6.8 %rhs.2 = bf16[2,2,4,160,128]{4,3,2,1,0:T(8,128)(2,1)} custom-call(s32[8,16]{1,0:T(8,128)} %bitcast.23, s32[8,16]{1,0:T(8,128)} %bitcast.25, s32[8,16]{1,0:T(8,128)} %bitcast.27, s32[1,16]{1,0:T(1,128)} %bitcast.29, bf16[16,8,128,128]{3,2,1,0:T(8,128)(2,1)} %bitcast.31, s32[16,8,2,128]{3,2,1,0:T(2,128)} %bitcast.21, bf16[8,128,128]{2,1,0:T(8,128)(2,1)} %bitcast.17, ...), custom_call_target="tpu_custom_call" | custom-call | flops 2147483648 | bytes 16777216 | tf_op jit(solution)/shard_map/rhs/pallas_call | solution.py:145
  10.8 0.0 copy-start.2
  10.8 0.0 copy-start.3
  10.8 0.0 collective-permute-done.2.refs_1_
  10.8 0.2 collective-permute-done.1.refs_2_
  11.0 1.4 %collective-permute-done.refs_16_ = bf16[8,128,128]{2,1,0:T(8,128)(2,1)S(1)} collective-permute-done((bf16[8,128,128]{2,1,0:T(8,128)(2,1)}, bf16[8,128,128]{2,1,0:T(8,128)(2,1)S(1)}, u32[]{:S(2)}, u32[]{:S(2)}) %collective-permute-start) | collective-permute-done | bytes 262176 | tf_op jit(solution)/shard_map/ppermute | solution.py:448
  12.4 0.5 collective-permute-start.3
  12.9 0.2 collective-permute-start.6
  13.1 0.3 collective-permute-start.7
  13.4 1.5 %collective-permute-start.4 = (bf16[8,128,128]{2,1,0:T(8,128)(2,1)S(1)}, bf16[8,128,128]{2,1,0:T(8,128)(2,1)S(1)}, u32[]{:S(2)}, u32[]{:S(2)}) collective-permute-start(bf16[8,128,128]{2,1,0:T(8,128)(2,1)S(1)} %collective-permute-done.1.refs_2_), channel_id=1, source_target_pairs={{0,4},{2,6},{8,0},{10,2},{16,8},{18,10},{24,16},{26,18},{28,24},{3... | collective-permute-start | bytes 786440 | tf_op jit(solution)/shard_map/ppermute | solution.py:449
  15.0 5.0 %rhs.3 = (bf16[4,176,128]{2,1,0:T(8,128)(2,1)S(1)}, bf16[4,176,128]{2,1,0:T(8,128)(2,1)S(1)}, bf16[4,176,128]{2,1,0:T(8,128)(2,1)S(1)}, bf16[4,176,128]{2,1,0:T(8,128)(2,1)S(1)}) custom-call(s32[8,16]{1,0:T(8,128)S(1)} %bitcast.24, s32[8,16]{1,0:T(8,128)S(1)} %bitcast.26, s32[8,16]{1,0:T(8,128)S(1)} %bitcast.28, s32[1,16]{1,0:T(1,128)S(1)} %bitcast.30, ...), custom_call_target="tpu_custom_call" | custom-call | flops 2147483648 | bytes 16777216 | tf_op jit(solution)/shard_map/rhs/pallas_call | solution.py:145
  20.0 0.0 collective-permute-done.7.refs_17_
  20.0 1.0 %collective-permute-done.3.refs_14_ = bf16[8,128,128]{2,1,0:T(8,128)(2,1)S(1)} collective-permute-done((bf16[8,128,128]{2,1,0:T(8,128)(2,1)S(1)}, bf16[8,128,128]{2,1,0:T(8,128)(2,1)S(1)}, u32[]{:S(2)}, u32[]{:S(2)}) %collective-permute-start.3) | collective-permute-done | bytes 262176 | tf_op jit(solution)/shard_map/ppermute | solution.py:448
  21.1 0.7 collective-permute-done.4.refs_4_
  21.8 1.6 %collective-permute-start.8 = (bf16[8,128,128]{2,1,0:T(8,128)(2,1)S(1)}, bf16[8,128,128]{2,1,0:T(8,128)(2,1)S(1)}, u32[]{:S(2)}, u32[]{:S(2)}) collective-permute-start(bf16[8,128,128]{2,1,0:T(8,128)(2,1)S(1)} %collective-permute-done.3.refs_14_), channel_id=1, source_target_pairs={{0,8},{2,10},{8,16},{10,18},{16,24},{18,26},{24,28},{26,30},{28,20... | collective-permute-start | bytes 786440 | tf_op jit(solution)/shard_map/ppermute | solution.py:448
  23.4 0.4 collective-permute-start.9
  23.8 1.6 %collective-permute-start.10 = (bf16[4,176,128]{2,1,0:T(8,128)(2,1)S(1)}, bf16[4,176,128]{2,1,0:T(8,128)(2,1)S(1)}, u32[]{:S(2)}, u32[]{:S(2)}) collective-permute-start(bf16[4,176,128]{2,1,0:T(8,128)(2,1)S(1)} %get-tuple-element.51), channel_id=1, source_target_pairs={{0,4},{1,5},{2,6},{3,7},{4,0},{5,1},{6,2},{7,3},{8,12},{9,13},{10,... | collective-permute-start | bytes 540680 | tf_op jit(solution)/shard_map/ppermute | solution.py:200
  25.4 1.5 %collective-permute-start.11 = (bf16[4,176,128]{2,1,0:T(8,128)(2,1)S(1)}, bf16[4,176,128]{2,1,0:T(8,128)(2,1)S(1)}, u32[]{:S(2)}, u32[]{:S(2)}) collective-permute-start(bf16[4,176,128]{2,1,0:T(8,128)(2,1)S(1)} %get-tuple-element.52), channel_id=1, source_target_pairs={{0,1},{1,0},{2,3},{3,2},{4,5},{5,4},{6,7},{7,6},{8,9},{9,8},{10,11... | collective-permute-start | bytes 540680 | tf_op jit(solution)/shard_map/ppermute | solution.py:200
  26.9 0.4 collective-permute-start.12
  27.3 7.6 %collective-permute-done.10.refs_1_ = bf16[4,176,128]{2,1,0:T(8,128)(2,1)S(1)} collective-permute-done((bf16[4,176,128]{2,1,0:T(8,128)(2,1)S(1)}, bf16[4,176,128]{2,1,0:T(8,128)(2,1)S(1)}, u32[]{:S(2)}, u32[]{:S(2)}) %collective-permute-start.10) | collective-permute-done | bytes 180256 | tf_op jit(solution)/shard_map/ppermute | solution.py:200
  34.9 0.0 collective-permute-done.11.refs_2_
  34.9 3.3 %collective-permute-done.12.refs_3_ = bf16[4,176,128]{2,1,0:T(8,128)(2,1)S(1)} collective-permute-done((bf16[4,176,128]{2,1,0:T(8,128)(2,1)S(1)}, bf16[4,176,128]{2,1,0:T(8,128)(2,1)S(1)}, u32[]{:S(2)}, u32[]{:S(2)}) %collective-permute-start.12) | collective-permute-done | bytes 180256 | tf_op jit(solution)/shard_map/ppermute | solution.py:200
  38.1 0.1 chip.1
  38.2 0.0 collective-permute-done.8.refs_12_
  38.2 0.0 collective-permute-done.9.refs_6_
  38.3 1.8 %collective-permute-start.16 = (bf16[4,128,128]{2,1,0:T(8,128)(2,1)S(1)}, bf16[4,128,128]{2,1,0:T(8,128)(2,1)S(1)}, u32[]{:S(2)}, u32[]{:S(2)}) collective-permute-start(bf16[4,128,128]{2,1,0:T(8,128)(2,1)S(1)} %slice.7), channel_id=1, source_target_pairs={{0,4},{2,6},{8,0},{10,2},{16,8},{18,10},{24,16},{26,18},{28,24},{3... | collective-permute-start | bytes 393224 | tf_op jit(solution)/shard_map/ppermute | solution.py:445
  40.1 0.3 collective-permute-start.15
  40.4 0.1 collective-permute-start.21
  40.5 5.3 %collective-permute-start.22 = (bf16[272,128]{1,0:T(8,128)(2,1)S(1)}, bf16[272,128]{1,0:T(8,128)(2,1)S(1)}, u32[]{:S(2)}, u32[]{:S(2)}) collective-permute-start(bf16[272,128]{1,0:T(8,128)(2,1)S(1)} %get-tuple-element.72), channel_id=1, source_target_pairs={{0,16},{2,18},{4,20},{6,22},{8,24},{10,26},{12,28},{14,30},{16,0},... | collective-permute-start | bytes 208904 | tf_op jit(solution)/shard_map/ppermute | solution.py:225
  45.8 0.9 %collective-permute-start.23 = (bf16[272,128]{1,0:T(8,128)(2,1)S(1)}, bf16[272,128]{1,0:T(8,128)(2,1)S(1)}, u32[]{:S(2)}, u32[]{:S(2)}) collective-permute-start(bf16[272,128]{1,0:T(8,128)(2,1)S(1)} %get-tuple-element.73), channel_id=1, source_target_pairs={{0,24},{2,26},{4,28},{6,30},{8,0},{10,2},{12,4},{14,6},{16,8},{18,... | collective-permute-start | bytes 208904 | tf_op jit(solution)/shard_map/ppermute | solution.py:225
  46.7 1.7 %collective-permute-done.21.refs_19_ = bf16[272,128]{1,0:T(8,128)(2,1)S(1)} collective-permute-done((bf16[272,128]{1,0:T(8,128)(2,1)S(1)}, bf16[272,128]{1,0:T(8,128)(2,1)S(1)}, u32[]{:S(2)}, u32[]{:S(2)}) %collective-permute-start.21) | collective-permute-done | bytes 69664 | tf_op jit(solution)/shard_map/ppermute | solution.py:225
  48.4 1.1 %collective-permute-done.22.refs_20_ = bf16[272,128]{1,0:T(8,128)(2,1)S(1)} collective-permute-done((bf16[272,128]{1,0:T(8,128)(2,1)S(1)}, bf16[272,128]{1,0:T(8,128)(2,1)S(1)}, u32[]{:S(2)}, u32[]{:S(2)}) %collective-permute-start.22) | collective-permute-done | bytes 69664 | tf_op jit(solution)/shard_map/ppermute | solution.py:225
  49.5 0.0 collective-permute-start.14
  49.5 0.5 collective-permute-start.18
  50.1 0.2 collective-permute-done.23.refs_21_
  50.3 0.5 collective-permute-start.20
  50.8 0.5 collective-permute-done.18.refs_11_
  51.3 0.1 collective-permute-start.17
  51.4 1.2 %collective-permute-done.17.refs_10_ = bf16[4,128,128]{2,1,0:T(8,128)(2,1)S(1)} collective-permute-done((bf16[4,128,128]{2,1,0:T(8,128)(2,1)S(1)}, bf16[4,128,128]{2,1,0:T(8,128)(2,1)S(1)}, u32[]{:S(2)}, u32[]{:S(2)}) %collective-permute-start.17) | collective-permute-done | bytes 131104 | tf_op jit(solution)/shard_map/ppermute | solution.py:456
  52.6 0.0 collective-permute-done.14.refs_7_
  52.6 0.0 collective-permute-done.19.refs_13_
  52.6 0.0 collective-permute-done.20.refs_15_
  52.7 10.7 %krylov.1 = (f32[128,128]{1,0:T(8,128)S(1)}, f32[128,128]{1,0:T(8,128)S(1)}, f32[128,128]{1,0:T(8,128)S(1)}, f32[32,1,128]{2,1,0:T(1,128)S(1)}) custom-call(f32[1,128]{1,0:T(1,128)S(1)} %bitcast.20, f32[128,128]{1,0:T(8,128)S(1)} %copy-done.2, bf16[2048,128]{1,0:T(8,128)(2,1)S(1)} %copy-done, bf16[8,128,128]{2,1,0:T(8,128)(2,1)S(1)} %bitcast.19, ...), custom_call_target="tpu_custom_call" | custom-call | tf_op jit(solution)/shard_map/krylov/pallas_call | solution.py:382
  63.3 9.7 %all_to_all.5.dots = f32[32,1,128]{2,1,0:T(1,128)S(1)} all-to-all(f32[32,1,128]{2,1,0:T(1,128)S(1)} %get-tuple-element.74), channel_id=1, replica_groups=mesh['loop'=16,'own'=2] {'loop','own'}, dimensions={0} | all-to-all | bytes 32768 | tf_op jit(solution)/shard_map/all_to_all | solution.py:514
  73.0 0.9 %last_step.1 = (f32[128,128]{1,0:T(8,128)}, f32[128,128]{1,0:T(8,128)}) custom-call(f32[32,1,128]{2,1,0:T(1,128)S(1)} %all_to_all.5.dots, f32[128,128]{1,0:T(8,128)S(1)} %copy-done.2, f32[128,128]{1,0:T(8,128)S(1)} %get-tuple-element.75.first, f32[128,128]{1,0:T(8,128)S(1)} %get-tuple-element.76.second, f32[128,128]{1,0:T(8,128)S(1)} %get-tuple-element.77.third), custom_call_target="tpu_custom_call" | custom-call | tf_op jit(solution)/shard_map/last_step/pallas_call | solution.py:418
  (26 shorter events, 0.1 us)
Async XLA Ops:
  0.6 14.3 %copy-start.1 = (bf16[1,8,128,128]{3,2,1,0:T(8,128)(2,1)S(1)}, bf16[1,8,128,128]{3,2,1,0:T(8,128)(2,1)}, u32[]{:S(2)}) copy-start(bf16[1,8,128,128]{3,2,1,0:T(8,128)(2,1)} %param.12) | copy-start | bytes 786436
  0.6 14.3 %copy-start = (bf16[2048,128]{1,0:T(8,128)(2,1)S(1)}, bf16[2048,128]{1,0:T(8,128)(2,1)}, u32[]{:S(2)}) copy-start(bf16[2048,128]{1,0:T(8,128)(2,1)} %subs.1) | copy-start | bytes 1572868
  0.7 14.3 %copy-start.4 = (s32[1,1,16,8,2,128]{5,4,3,2,1,0:T(2,128)S(1)}, s32[1,1,16,8,2,128]{5,4,3,2,1,0:T(2,128)}, u32[]{:S(2)}) copy-start(s32[1,1,16,8,2,128]{5,4,3,2,1,0:T(2,128)} %param.19) | copy-start | bytes 393220
  0.7 14.3 %copy-start.8 = (s32[1,1,16]{2,1,0:T(1,128)S(1)}, s32[1,1,16]{2,1,0:T(1,128)}, u32[]{:S(2)}) copy-start(s32[1,1,16]{2,1,0:T(1,128)} %param.18) | copy-start | bytes 196
  0.7 14.3 %copy-start.7 = (s32[1,1,16,8]{2,3,1,0:T(8,128)S(1)}, s32[1,1,16,8]{2,3,1,0:T(8,128)}, u32[]{:S(2)}) copy-start(s32[1,1,16,8]{2,3,1,0:T(8,128)} %param.17) | copy-start | bytes 1540
  0.7 14.3 %copy-start.6 = (s32[1,1,16,8]{2,3,1,0:T(8,128)S(1)}, s32[1,1,16,8]{2,3,1,0:T(8,128)}, u32[]{:S(2)}) copy-start(s32[1,1,16,8]{2,3,1,0:T(8,128)} %param.16) | copy-start | bytes 1540
  0.7 14.3 %copy-start.5 = (s32[1,1,16,8]{2,3,1,0:T(8,128)S(1)}, s32[1,1,16,8]{2,3,1,0:T(8,128)}, u32[]{:S(2)}) copy-start(s32[1,1,16,8]{2,3,1,0:T(8,128)} %param.15) | copy-start | bytes 1540
  0.7 10.1 %collective-permute-start.2 = (bf16[8,128,128]{2,1,0:T(8,128)(2,1)}, bf16[8,128,128]{2,1,0:T(8,128)(2,1)S(1)}, u32[]{:S(2)}, u32[]{:S(2)}) collective-permute-start(bf16[8,128,128]{2,1,0:T(8,128)(2,1)} %bitcast.14), channel_id=1, source_target_pairs={{0,2},{2,0},{4,6},{6,4},{8,10},{10,8},{12,14},{14,12},{16,18},{18,... | collective-permute-start | bytes 786440 | tf_op jit(solution)/shard_map/ppermute | solution.py:456
  1.2 9.8 %collective-permute-start.1 = (bf16[8,128,128]{2,1,0:T(8,128)(2,1)}, bf16[8,128,128]{2,1,0:T(8,128)(2,1)S(1)}, u32[]{:S(2)}, u32[]{:S(2)}) collective-permute-start(bf16[8,128,128]{2,1,0:T(8,128)(2,1)} %bitcast.15), channel_id=1, source_target_pairs={{0,4},{2,6},{8,0},{10,2},{16,8},{18,10},{24,16},{26,18},{28,24},{3... | collective-permute-start | bytes 786440 | tf_op jit(solution)/shard_map/ppermute | solution.py:449
  3.8 8.6 %collective-permute-start = (bf16[8,128,128]{2,1,0:T(8,128)(2,1)}, bf16[8,128,128]{2,1,0:T(8,128)(2,1)S(1)}, u32[]{:S(2)}, u32[]{:S(2)}) collective-permute-start(bf16[8,128,128]{2,1,0:T(8,128)(2,1)} %bitcast.16), channel_id=1, source_target_pairs={{0,8},{2,10},{8,16},{10,18},{16,24},{18,26},{24,28},{26,30},{28,20... | collective-permute-start | bytes 786440 | tf_op jit(solution)/shard_map/ppermute | solution.py:448
  10.8 41.9 %copy-start.2 = (f32[128,128]{1,0:T(8,128)S(1)}, f32[128,128]{1,0:T(8,128)}, u32[]{:S(2)}) copy-start(f32[128,128]{1,0:T(8,128)} %start.3) | copy-start | bytes 196612
  10.8 41.9 %copy-start.3 = (f32[128]{0:T(128)S(1)}, f32[128]{0:T(128)}, u32[]{:S(2)}) copy-start(f32[128]{0:T(128)} %param.11) | copy-start | bytes 1540
  12.4 2.5 %collective-permute-start.5 = (bf16[2,2,4,160,128]{4,3,2,1,0:T(8,128)(2,1)}, bf16[2,2,4,160,128]{4,3,2,1,0:T(8,128)(2,1)S(1)}, u32[]{:S(2)}, u32[]{:S(2)}) collective-permute-start(bf16[2,2,4,160,128]{4,3,2,1,0:T(8,128)(2,1)} %rhs.2), channel_id=1, source_target_pairs={{0,2},{2,0},{4,6},{6,4},{8,10},{10,8},{12,14},{14,12},{16,18},{18,... | collective-permute-start | bytes 1966088 | tf_op jit(solution)/shard_map/ppermute | solution.py:456
  12.4 8.7 %collective-permute-start.3 = (bf16[8,128,128]{2,1,0:T(8,128)(2,1)S(1)}, bf16[8,128,128]{2,1,0:T(8,128)(2,1)S(1)}, u32[]{:S(2)}, u32[]{:S(2)}) collective-permute-start(bf16[8,128,128]{2,1,0:T(8,128)(2,1)S(1)} %collective-permute-done.refs_16_), channel_id=1, source_target_pairs={{0,8},{2,10},{8,16},{10,18},{16,24},{18,26},{24,28},{26,30},{28,20... | collective-permute-start | bytes 786440 | tf_op jit(solution)/shard_map/ppermute | solution.py:448
  12.9 7.1 %collective-permute-start.6 = (bf16[8,128,128]{2,1,0:T(8,128)(2,1)S(1)}, bf16[8,128,128]{2,1,0:T(8,128)(2,1)S(1)}, u32[]{:S(2)}, u32[]{:S(2)}) collective-permute-start(bf16[8,128,128]{2,1,0:T(8,128)(2,1)S(1)} %collective-permute-done.1.refs_2_), channel_id=1, source_target_pairs={{0,2},{2,0},{4,6},{6,4},{8,10},{10,8},{12,14},{14,12},{16,18},{18,... | collective-permute-start | bytes 786440 | tf_op jit(solution)/shard_map/ppermute | solution.py:456
  13.1 7.0 %collective-permute-start.7 = (bf16[8,128,128]{2,1,0:T(8,128)(2,1)S(1)}, bf16[8,128,128]{2,1,0:T(8,128)(2,1)S(1)}, u32[]{:S(2)}, u32[]{:S(2)}) collective-permute-start(bf16[8,128,128]{2,1,0:T(8,128)(2,1)S(1)} %collective-permute-done.refs_16_), channel_id=1, source_target_pairs={{0,2},{2,0},{4,6},{6,4},{8,10},{10,8},{12,14},{14,12},{16,18},{18,... | collective-permute-start | bytes 786440 | tf_op jit(solution)/shard_map/ppermute | solution.py:456
  13.4 8.4 %collective-permute-start.4 = (bf16[8,128,128]{2,1,0:T(8,128)(2,1)S(1)}, bf16[8,128,128]{2,1,0:T(8,128)(2,1)S(1)}, u32[]{:S(2)}, u32[]{:S(2)}) collective-permute-start(bf16[8,128,128]{2,1,0:T(8,128)(2,1)S(1)} %collective-permute-done.1.refs_2_), channel_id=1, source_target_pairs={{0,4},{2,6},{8,0},{10,2},{16,8},{18,10},{24,16},{26,18},{28,24},{3... | collective-permute-start | bytes 786440 | tf_op jit(solution)/shard_map/ppermute | solution.py:449
  21.8 16.4 %collective-permute-start.8 = (bf16[8,128,128]{2,1,0:T(8,128)(2,1)S(1)}, bf16[8,128,128]{2,1,0:T(8,128)(2,1)S(1)}, u32[]{:S(2)}, u32[]{:S(2)}) collective-permute-start(bf16[8,128,128]{2,1,0:T(8,128)(2,1)S(1)} %collective-permute-done.3.refs_14_), channel_id=1, source_target_pairs={{0,8},{2,10},{8,16},{10,18},{16,24},{18,26},{24,28},{26,30},{28,20... | collective-permute-start | bytes 786440 | tf_op jit(solution)/shard_map/ppermute | solution.py:448
  23.4 14.8 %collective-permute-start.9 = (bf16[8,128,128]{2,1,0:T(8,128)(2,1)S(1)}, bf16[8,128,128]{2,1,0:T(8,128)(2,1)S(1)}, u32[]{:S(2)}, u32[]{:S(2)}) collective-permute-start(bf16[8,128,128]{2,1,0:T(8,128)(2,1)S(1)} %collective-permute-done.4.refs_4_), channel_id=1, source_target_pairs={{0,4},{2,6},{8,0},{10,2},{16,8},{18,10},{24,16},{26,18},{28,24},{3... | collective-permute-start | bytes 786440 | tf_op jit(solution)/shard_map/ppermute | solution.py:449
  23.8 11.1 %collective-permute-start.10 = (bf16[4,176,128]{2,1,0:T(8,128)(2,1)S(1)}, bf16[4,176,128]{2,1,0:T(8,128)(2,1)S(1)}, u32[]{:S(2)}, u32[]{:S(2)}) collective-permute-start(bf16[4,176,128]{2,1,0:T(8,128)(2,1)S(1)} %get-tuple-element.51), channel_id=1, source_target_pairs={{0,4},{1,5},{2,6},{3,7},{4,0},{5,1},{6,2},{7,3},{8,12},{9,13},{10,... | collective-permute-start | bytes 540680 | tf_op jit(solution)/shard_map/ppermute | solution.py:200
  25.4 9.5 %collective-permute-start.11 = (bf16[4,176,128]{2,1,0:T(8,128)(2,1)S(1)}, bf16[4,176,128]{2,1,0:T(8,128)(2,1)S(1)}, u32[]{:S(2)}, u32[]{:S(2)}) collective-permute-start(bf16[4,176,128]{2,1,0:T(8,128)(2,1)S(1)} %get-tuple-element.52), channel_id=1, source_target_pairs={{0,1},{1,0},{2,3},{3,2},{4,5},{5,4},{6,7},{7,6},{8,9},{9,8},{10,11... | collective-permute-start | bytes 540680 | tf_op jit(solution)/shard_map/ppermute | solution.py:200
  26.9 11.3 %collective-permute-start.12 = (bf16[4,176,128]{2,1,0:T(8,128)(2,1)S(1)}, bf16[4,176,128]{2,1,0:T(8,128)(2,1)S(1)}, u32[]{:S(2)}, u32[]{:S(2)}) collective-permute-start(bf16[4,176,128]{2,1,0:T(8,128)(2,1)S(1)} %get-tuple-element.53), channel_id=1, source_target_pairs={{0,5},{1,4},{2,7},{3,6},{4,1},{5,0},{6,3},{7,2},{8,13},{9,12},{10,... | collective-permute-start | bytes 540680 | tf_op jit(solution)/shard_map/ppermute | solution.py:200
  38.3 11.3 %collective-permute-start.16 = (bf16[4,128,128]{2,1,0:T(8,128)(2,1)S(1)}, bf16[4,128,128]{2,1,0:T(8,128)(2,1)S(1)}, u32[]{:S(2)}, u32[]{:S(2)}) collective-permute-start(bf16[4,128,128]{2,1,0:T(8,128)(2,1)S(1)} %slice.7), channel_id=1, source_target_pairs={{0,4},{2,6},{8,0},{10,2},{16,8},{18,10},{24,16},{26,18},{28,24},{3... | collective-permute-start | bytes 393224 | tf_op jit(solution)/shard_map/ppermute | solution.py:445
  40.1 10.2 %collective-permute-start.15 = (bf16[4,128,128]{2,1,0:T(8,128)(2,1)S(1)}, bf16[4,128,128]{2,1,0:T(8,128)(2,1)S(1)}, u32[]{:S(2)}, u32[]{:S(2)}) collective-permute-start(bf16[4,128,128]{2,1,0:T(8,128)(2,1)S(1)} %slice.6), channel_id=1, source_target_pairs={{0,8},{2,10},{8,16},{10,18},{16,24},{18,26},{24,28},{26,30},{28,20... | collective-permute-start | bytes 393224 | tf_op jit(solution)/shard_map/ppermute | solution.py:444
  40.4 8.0 %collective-permute-start.21 = (bf16[272,128]{1,0:T(8,128)(2,1)S(1)}, bf16[272,128]{1,0:T(8,128)(2,1)S(1)}, u32[]{:S(2)}, u32[]{:S(2)}) collective-permute-start(bf16[272,128]{1,0:T(8,128)(2,1)S(1)} %get-tuple-element.71), channel_id=1, source_target_pairs={{0,8},{2,10},{4,12},{6,14},{8,16},{10,18},{12,20},{14,22},{16,24},... | collective-permute-start | bytes 208904 | tf_op jit(solution)/shard_map/ppermute | solution.py:225
  40.5 9.1 %collective-permute-start.22 = (bf16[272,128]{1,0:T(8,128)(2,1)S(1)}, bf16[272,128]{1,0:T(8,128)(2,1)S(1)}, u32[]{:S(2)}, u32[]{:S(2)}) collective-permute-start(bf16[272,128]{1,0:T(8,128)(2,1)S(1)} %get-tuple-element.72), channel_id=1, source_target_pairs={{0,16},{2,18},{4,20},{6,22},{8,24},{10,26},{12,28},{14,30},{16,0},... | collective-permute-start | bytes 208904 | tf_op jit(solution)/shard_map/ppermute | solution.py:225
  45.8 4.5 %collective-permute-start.23 = (bf16[272,128]{1,0:T(8,128)(2,1)S(1)}, bf16[272,128]{1,0:T(8,128)(2,1)S(1)}, u32[]{:S(2)}, u32[]{:S(2)}) collective-permute-start(bf16[272,128]{1,0:T(8,128)(2,1)S(1)} %get-tuple-element.73), channel_id=1, source_target_pairs={{0,24},{2,26},{4,28},{6,30},{8,0},{10,2},{12,4},{14,6},{16,8},{18,... | collective-permute-start | bytes 208904 | tf_op jit(solution)/shard_map/ppermute | solution.py:225
  48.4 4.2 %collective-permute-start.13 = (bf16[8,128,128]{2,1,0:T(8,128)(2,1)S(1)}, bf16[8,128,128]{2,1,0:T(8,128)(2,1)S(1)}, u32[]{:S(2)}, u32[]{:S(2)}) collective-permute-start(bf16[8,128,128]{2,1,0:T(8,128)(2,1)S(1)} %collective-permute-done.4.refs_4_), channel_id=1, source_target_pairs={{0,2},{2,0},{4,6},{6,4},{8,10},{10,8},{12,14},{14,12},{16,18},{18,... | collective-permute-start | bytes 786440 | tf_op jit(solution)/shard_map/ppermute | solution.py:456
  49.5 3.1 %collective-permute-start.14 = (bf16[8,128,128]{2,1,0:T(8,128)(2,1)S(1)}, bf16[8,128,128]{2,1,0:T(8,128)(2,1)S(1)}, u32[]{:S(2)}, u32[]{:S(2)}) collective-permute-start(bf16[8,128,128]{2,1,0:T(8,128)(2,1)S(1)} %collective-permute-done.9.refs_6_), channel_id=1, source_target_pairs={{0,2},{2,0},{4,6},{6,4},{8,10},{10,8},{12,14},{14,12},{16,18},{18,... | collective-permute-start | bytes 786440 | tf_op jit(solution)/shard_map/ppermute | solution.py:456
  49.5 1.7 %collective-permute-start.18 = (bf16[4,128,128]{2,1,0:T(8,128)(2,1)S(1)}, bf16[4,128,128]{2,1,0:T(8,128)(2,1)S(1)}, u32[]{:S(2)}, u32[]{:S(2)}) collective-permute-start(bf16[4,128,128]{2,1,0:T(8,128)(2,1)S(1)} %collective-permute-done.16.refs_9_), channel_id=1, source_target_pairs={{0,2},{2,0},{4,6},{6,4},{8,10},{10,8},{12,14},{14,12},{16,18},{18,... | collective-permute-start | bytes 393224 | tf_op jit(solution)/shard_map/ppermute | solution.py:456
  50.3 2.4 %collective-permute-start.19 = (bf16[8,128,128]{2,1,0:T(8,128)(2,1)S(1)}, bf16[8,128,128]{2,1,0:T(8,128)(2,1)S(1)}, u32[]{:S(2)}, u32[]{:S(2)}) collective-permute-start(bf16[8,128,128]{2,1,0:T(8,128)(2,1)S(1)} %collective-permute-done.8.refs_12_), channel_id=1, source_target_pairs={{0,2},{2,0},{4,6},{6,4},{8,10},{10,8},{12,14},{14,12},{16,18},{18,... | collective-permute-start | bytes 786440 | tf_op jit(solution)/shard_map/ppermute | solution.py:456
  50.3 2.4 %collective-permute-start.20 = (bf16[8,128,128]{2,1,0:T(8,128)(2,1)S(1)}, bf16[8,128,128]{2,1,0:T(8,128)(2,1)S(1)}, u32[]{:S(2)}, u32[]{:S(2)}) collective-permute-start(bf16[8,128,128]{2,1,0:T(8,128)(2,1)S(1)} %collective-permute-done.3.refs_14_), channel_id=1, source_target_pairs={{0,2},{2,0},{4,6},{6,4},{8,10},{10,8},{12,14},{14,12},{16,18},{18,... | collective-permute-start | bytes 786440 | tf_op jit(solution)/shard_map/ppermute | solution.py:456
  51.3 1.3 %collective-permute-start.17 = (bf16[4,128,128]{2,1,0:T(8,128)(2,1)S(1)}, bf16[4,128,128]{2,1,0:T(8,128)(2,1)S(1)}, u32[]{:S(2)}, u32[]{:S(2)}) collective-permute-start(bf16[4,128,128]{2,1,0:T(8,128)(2,1)S(1)} %collective-permute-done.15.refs_8_), channel_id=1, source_target_pairs={{0,2},{2,0},{4,6},{6,4},{8,10},{10,8},{12,14},{14,12},{16,18},{18,... | collective-permute-start | bytes 393224 | tf_op jit(solution)/shard_map/ppermute | solution.py:456

commit v14 on v13

--- a/solution.py
+++ b/solution.py
@@ -49,6 +49,8 @@
 ):
     if half == 0:
         given, refs = refs[0], refs[1:]
+    else:
+        refs, (ready, sent) = refs[:-2], refs[-2:]
     outs, (ratings, runs, words, subs, table, sums, arrived, loaded) = refs[:-8], refs[-8:]
     steps, slots, tile = ratings.shape[0], ratings.shape[1], ratings.shape[2]
     rank = words.shape[-1]
@@ -87,6 +89,7 @@
         == lax.broadcasted_iota(jnp.int32, (tile, tile), 1)
     ).astype(f32).astype(bf16)
     me = lax.axis_index("own")
+    sends = []
     for step in range(steps):
         group = group_at(step)
         live = counts[0, group]
@@ -131,7 +134,15 @@
                 value = jnp.concatenate(
                     [value, spans, line, jnp.zeros((FACT_ROWS - 1, rank), f32)], axis=0
                 )
-                outs[0][o, column, up] = value.astype(bf16)
+                ready[o, column, up] = value.astype(bf16)
+                here = (o, column, up)
+                send = pltpu.make_async_copy(
+                    ready.at[here], outs[0].at[here], sent.at[step * owners + o]
+                )
+                send.start()
+                sends.append(send)
+    for send in sends:
+        send.wait()
 
 
 def rhs_sums(scalars, ratings, runs, words, subs, half, given, owners, own_rows):
@@ -147,7 +158,7 @@
         in_specs=[pl.BlockSpec(memory_space=pltpu.SMEM)] * 4
         + [anywhere] * 4
         + [whole] * (1 - half),
-        out_specs=[whole] * len(shapes),
+        out_specs=[anywhere if half else whole] * len(shapes),
         out_shape=[jax.ShapeDtypeStruct(shape, bf16) for shape in shapes],
         scratch_shapes=[
             pltpu.VMEM((steps,) + ratings.shape[1:], bf16),
@@ -158,7 +169,8 @@
             pltpu.VMEM((2, owners * own_rows, rank), f32),
             pltpu.SemaphoreType.DMA((steps,)),
             pltpu.SemaphoreType.DMA((3,)),
-        ],
+        ]
+        + [pltpu.VMEM(shapes[0], bf16), pltpu.SemaphoreType.DMA((steps * owners,))] * half,
         compiler_params=pltpu.CompilerParams(vmem_limit_bytes=VMEM_LIMIT if half else 50 * MIB),
         cost_estimate=pl.CostEstimate(
             flops=8 * ratings.size * rank, bytes_accessed=8 * ratings.size, transcendentals=0

time: 74.1 us -> 74.1 us (level)
  no operation moved by 1% of the time
where the time goes in v14:
time: 74.1 us; the launch traced here: 73.9 us
  Pallas kernels  23.4 us (32%)
  starting transfers between devices  20.9 us (28%)
  waiting for transfers between devices  19 us (26%)
  blocking collectives  9.67 us (13%)
  between operations  0.87 us (1%)
    pallas_call x2, Pallas kernels, rhs_sums(): pl.pallas_call(functools.partial(rhs_kernel, half=half, owners=owners, ow...  11.8 us
    ppermute x3, waiting for transfers between devices, exchange_chips(): given.append(lax.ppermute(part, AXES, pairs) if o or column else part)  10.9 us
    pallas_call x1, Pallas kernels, krylov(): pl.pallas_call(functools.partial(steps_kernel, count=len(pieces), word_ti...  10.7 us
    all_to_all x1, blocking collectives, on_device(): everyone = lax.all_to_all(dots, AXES, 0, 0, tiled=True)  9.67 us
    ppermute x3, starting transfers between devices, reduce_levels(): terms.append(lax.ppermute(total[up], 'loop', shift))  6.3 us
    ppermute x3, starting transfers between devices, ring_round(): down = lax.ppermute(down, 'loop', shift(-1))  4.43 us
    ppermute x3, starting transfers between devices, exchange_chips(): given.append(lax.ppermute(part, AXES, pairs) if o or column else part)  3.49 us
    ppermute x3, waiting for transfers between devices, reduce_levels(): terms.append(lax.ppermute(total[up], 'loop', shift))  3.04 us
  transfers between devices with their start and end apart: 24, of which 11 were waited for; matrix products, arithmetic and copies ran while one was open for 0% of the time, Pallas kernels for 16%

profile of v14, /device:TPU:0, one launch (start us, length us, event | category | flops | bytes accessed | tf_op | source)
XLA Modules:
  0.0 73.9 jit_solution(1819064067882759533)
XLA Ops:
  0.7 0.5 collective-permute-start.2
  1.2 2.5 %collective-permute-start.1 = (bf16[8,128,128]{2,1,0:T(8,128)(2,1)}, bf16[8,128,128]{2,1,0:T(8,128)(2,1)S(1)}, u32[]{:S(2)}, u32[]{:S(2)}) collective-permute-start(bf16[8,128,128]{2,1,0:T(8,128)(2,1)} %bitcast.15), channel_id=1, source_target_pairs={{0,4},{2,6},{8,0},{10,2},{16,8},{18,10},{24,16},{26,18},{28,24},{3... | collective-permute-start | bytes 786440 | tf_op jit(solution)/shard_map/ppermute | solution.py:461
  3.8 0.2 collective-permute-start
  3.9 6.7 %rhs.2 = bf16[2,2,4,160,128]{4,3,2,1,0:T(8,128)(2,1)} custom-call(s32[8,16]{1,0:T(8,128)} %bitcast.23, s32[8,16]{1,0:T(8,128)} %bitcast.25, s32[8,16]{1,0:T(8,128)} %bitcast.27, s32[1,16]{1,0:T(1,128)} %bitcast.29, bf16[16,8,128,128]{3,2,1,0:T(8,128)(2,1)} %bitcast.31, s32[16,8,2,128]{3,2,1,0:T(2,128)} %bitcast.21, bf16[8,128,128]{2,1,0:T(8,128)(2,1)} %bitcast.17, ...), custom_call_target="tpu_custom_call" | custom-call | flops 2147483648 | bytes 16777216 | tf_op jit(solution)/shard_map/rhs/pallas_call | solution.py:156
  10.7 0.0 copy-start.2
  10.7 0.0 copy-start.3
  10.7 0.0 collective-permute-done.2.refs_1_
  10.7 0.3 collective-permute-done.1.refs_2_
  11.0 1.4 %collective-permute-done.refs_16_ = bf16[8,128,128]{2,1,0:T(8,128)(2,1)S(1)} collective-permute-done((bf16[8,128,128]{2,1,0:T(8,128)(2,1)}, bf16[8,128,128]{2,1,0:T(8,128)(2,1)S(1)}, u32[]{:S(2)}, u32[]{:S(2)}) %collective-permute-start) | collective-permute-done | bytes 262176 | tf_op jit(solution)/shard_map/ppermute | solution.py:460
  12.4 0.5 collective-permute-start.3
  12.8 0.2 collective-permute-start.6
  13.0 0.3 collective-permute-start.7
  13.3 1.6 %collective-permute-start.4 = (bf16[8,128,128]{2,1,0:T(8,128)(2,1)S(1)}, bf16[8,128,128]{2,1,0:T(8,128)(2,1)S(1)}, u32[]{:S(2)}, u32[]{:S(2)}) collective-permute-start(bf16[8,128,128]{2,1,0:T(8,128)(2,1)S(1)} %collective-permute-done.1.refs_2_), channel_id=1, source_target_pairs={{0,4},{2,6},{8,0},{10,2},{16,8},{18,10},{24,16},{26,18},{28,24},{3... | collective-permute-start | bytes 786440 | tf_op jit(solution)/shard_map/ppermute | solution.py:461
  15.0 5.0 %rhs.3 = (bf16[4,176,128]{2,1,0:T(8,128)(2,1)S(1)}, bf16[4,176,128]{2,1,0:T(8,128)(2,1)S(1)}, bf16[4,176,128]{2,1,0:T(8,128)(2,1)S(1)}, bf16[4,176,128]{2,1,0:T(8,128)(2,1)S(1)}) custom-call(s32[8,16]{1,0:T(8,128)S(1)} %bitcast.24, s32[8,16]{1,0:T(8,128)S(1)} %bitcast.26, s32[8,16]{1,0:T(8,128)S(1)} %bitcast.28, s32[1,16]{1,0:T(1,128)S(1)} %bitcast.30, ...), custom_call_target="tpu_custom_call" | custom-call | flops 2147483648 | bytes 16777216 | tf_op jit(solution)/shard_map/rhs/pallas_call | solution.py:156
  20.0 0.0 collective-permute-done.6.refs_3_
  20.0 1.1 %collective-permute-done.3.refs_14_ = bf16[8,128,128]{2,1,0:T(8,128)(2,1)S(1)} collective-permute-done((bf16[8,128,128]{2,1,0:T(8,128)(2,1)S(1)}, bf16[8,128,128]{2,1,0:T(8,128)(2,1)S(1)}, u32[]{:S(2)}, u32[]{:S(2)}) %collective-permute-start.3) | collective-permute-done | bytes 262176 | tf_op jit(solution)/shard_map/ppermute | solution.py:460
  21.1 0.6 collective-permute-done.4.refs_4_
  21.7 1.7 %collective-permute-start.8 = (bf16[8,128,128]{2,1,0:T(8,128)(2,1)S(1)}, bf16[8,128,128]{2,1,0:T(8,128)(2,1)S(1)}, u32[]{:S(2)}, u32[]{:S(2)}) collective-permute-start(bf16[8,128,128]{2,1,0:T(8,128)(2,1)S(1)} %collective-permute-done.3.refs_14_), channel_id=1, source_target_pairs={{0,8},{2,10},{8,16},{10,18},{16,24},{18,26},{24,28},{26,30},{28,20... | collective-permute-start | bytes 786440 | tf_op jit(solution)/shard_map/ppermute | solution.py:460
  23.4 0.3 collective-permute-start.9
  23.7 1.6 %collective-permute-start.10 = (bf16[4,176,128]{2,1,0:T(8,128)(2,1)S(1)}, bf16[4,176,128]{2,1,0:T(8,128)(2,1)S(1)}, u32[]{:S(2)}, u32[]{:S(2)}) collective-permute-start(bf16[4,176,128]{2,1,0:T(8,128)(2,1)S(1)} %get-tuple-element.51), channel_id=1, source_target_pairs={{0,4},{1,5},{2,6},{3,7},{4,0},{5,1},{6,2},{7,3},{8,12},{9,13},{10,... | collective-permute-start | bytes 540680 | tf_op jit(solution)/shard_map/ppermute | solution.py:212
  25.4 1.5 %collective-permute-start.11 = (bf16[4,176,128]{2,1,0:T(8,128)(2,1)S(1)}, bf16[4,176,128]{2,1,0:T(8,128)(2,1)S(1)}, u32[]{:S(2)}, u32[]{:S(2)}) collective-permute-start(bf16[4,176,128]{2,1,0:T(8,128)(2,1)S(1)} %get-tuple-element.52), channel_id=1, source_target_pairs={{0,1},{1,0},{2,3},{3,2},{4,5},{5,4},{6,7},{7,6},{8,9},{9,8},{10,11... | collective-permute-start | bytes 540680 | tf_op jit(solution)/shard_map/ppermute | solution.py:212
  26.9 0.3 collective-permute-start.12
  27.2 7.6 %collective-permute-done.10.refs_1_ = bf16[4,176,128]{2,1,0:T(8,128)(2,1)S(1)} collective-permute-done((bf16[4,176,128]{2,1,0:T(8,128)(2,1)S(1)}, bf16[4,176,128]{2,1,0:T(8,128)(2,1)S(1)}, u32[]{:S(2)}, u32[]{:S(2)}) %collective-permute-start.10) | collective-permute-done | bytes 180256 | tf_op jit(solution)/shard_map/ppermute | solution.py:212
  34.8 0.0 collective-permute-done.11.refs_2_
  34.8 3.3 %collective-permute-done.12.refs_3_ = bf16[4,176,128]{2,1,0:T(8,128)(2,1)S(1)} collective-permute-done((bf16[4,176,128]{2,1,0:T(8,128)(2,1)S(1)}, bf16[4,176,128]{2,1,0:T(8,128)(2,1)S(1)}, u32[]{:S(2)}, u32[]{:S(2)}) %collective-permute-start.12) | collective-permute-done | bytes 180256 | tf_op jit(solution)/shard_map/ppermute | solution.py:212
  38.1 0.1 chip.1
  38.2 0.0 collective-permute-done.8.refs_12_
  38.2 0.0 collective-permute-done.9.refs_6_
  38.3 1.8 %collective-permute-start.16 = (bf16[4,128,128]{2,1,0:T(8,128)(2,1)S(1)}, bf16[4,128,128]{2,1,0:T(8,128)(2,1)S(1)}, u32[]{:S(2)}, u32[]{:S(2)}) collective-permute-start(bf16[4,128,128]{2,1,0:T(8,128)(2,1)S(1)} %slice.7), channel_id=1, source_target_pairs={{0,4},{2,6},{8,0},{10,2},{16,8},{18,10},{24,16},{26,18},{28,24},{3... | collective-permute-start | bytes 393224 | tf_op jit(solution)/shard_map/ppermute | solution.py:457
  40.1 0.3 collective-permute-start.15
  40.4 0.1 collective-permute-start.21
  40.5 5.3 %collective-permute-start.22 = (bf16[272,128]{1,0:T(8,128)(2,1)S(1)}, bf16[272,128]{1,0:T(8,128)(2,1)S(1)}, u32[]{:S(2)}, u32[]{:S(2)}) collective-permute-start(bf16[272,128]{1,0:T(8,128)(2,1)S(1)} %get-tuple-element.72), channel_id=1, source_target_pairs={{0,16},{2,18},{4,20},{6,22},{8,24},{10,26},{12,28},{14,30},{16,0},... | collective-permute-start | bytes 208904 | tf_op jit(solution)/shard_map/ppermute | solution.py:237
  45.8 0.9 %collective-permute-start.23 = (bf16[272,128]{1,0:T(8,128)(2,1)S(1)}, bf16[272,128]{1,0:T(8,128)(2,1)S(1)}, u32[]{:S(2)}, u32[]{:S(2)}) collective-permute-start(bf16[272,128]{1,0:T(8,128)(2,1)S(1)} %get-tuple-element.73), channel_id=1, source_target_pairs={{0,24},{2,26},{4,28},{6,30},{8,0},{10,2},{12,4},{14,6},{16,8},{18,... | collective-permute-start | bytes 208904 | tf_op jit(solution)/shard_map/ppermute | solution.py:237
  46.7 1.7 %collective-permute-done.21.refs_19_ = bf16[272,128]{1,0:T(8,128)(2,1)S(1)} collective-permute-done((bf16[272,128]{1,0:T(8,128)(2,1)S(1)}, bf16[272,128]{1,0:T(8,128)(2,1)S(1)}, u32[]{:S(2)}, u32[]{:S(2)}) %collective-permute-start.21) | collective-permute-done | bytes 69664 | tf_op jit(solution)/shard_map/ppermute | solution.py:237
  48.4 1.1 %collective-permute-done.22.refs_20_ = bf16[272,128]{1,0:T(8,128)(2,1)S(1)} collective-permute-done((bf16[272,128]{1,0:T(8,128)(2,1)S(1)}, bf16[272,128]{1,0:T(8,128)(2,1)S(1)}, u32[]{:S(2)}, u32[]{:S(2)}) %collective-permute-start.22) | collective-permute-done | bytes 69664 | tf_op jit(solution)/shard_map/ppermute | solution.py:237
  49.5 0.0 collective-permute-start.14
  49.5 0.5 collective-permute-start.18
  50.1 0.2 collective-permute-done.23.refs_21_
  50.3 0.5 collective-permute-start.20
  50.8 0.5 collective-permute-done.18.refs_11_
  51.3 0.1 collective-permute-start.17
  51.4 1.2 %collective-permute-done.17.refs_10_ = bf16[4,128,128]{2,1,0:T(8,128)(2,1)S(1)} collective-permute-done((bf16[4,128,128]{2,1,0:T(8,128)(2,1)S(1)}, bf16[4,128,128]{2,1,0:T(8,128)(2,1)S(1)}, u32[]{:S(2)}, u32[]{:S(2)}) %collective-permute-start.17) | collective-permute-done | bytes 131104 | tf_op jit(solution)/shard_map/ppermute | solution.py:468
  52.6 0.0 collective-permute-done.14.refs_7_
  52.6 0.0 collective-permute-done.19.refs_13_
  52.6 0.0 collective-permute-done.20.refs_15_
  52.7 10.7 %krylov.1 = (f32[128,128]{1,0:T(8,128)S(1)}, f32[128,128]{1,0:T(8,128)S(1)}, f32[128,128]{1,0:T(8,128)S(1)}, f32[32,1,128]{2,1,0:T(1,128)S(1)}) custom-call(f32[1,128]{1,0:T(1,128)S(1)} %bitcast.20, f32[128,128]{1,0:T(8,128)S(1)} %copy-done.2, bf16[2048,128]{1,0:T(8,128)(2,1)S(1)} %copy-done, bf16[8,128,128]{2,1,0:T(8,128)(2,1)S(1)} %bitcast.19, ...), custom_call_target="tpu_custom_call" | custom-call | tf_op jit(solution)/shard_map/krylov/pallas_call | solution.py:394
  63.3 9.7 %all_to_all.5.dots = f32[32,1,128]{2,1,0:T(1,128)S(1)} all-to-all(f32[32,1,128]{2,1,0:T(1,128)S(1)} %get-tuple-element.74), channel_id=1, replica_groups=mesh['loop'=16,'own'=2] {'loop','own'}, dimensions={0} | all-to-all | bytes 32768 | tf_op jit(solution)/shard_map/all_to_all | solution.py:526
  73.0 0.9 %last_step.1 = (f32[128,128]{1,0:T(8,128)}, f32[128,128]{1,0:T(8,128)}) custom-call(f32[32,1,128]{2,1,0:T(1,128)S(1)} %all_to_all.5.dots, f32[128,128]{1,0:T(8,128)S(1)} %copy-done.2, f32[128,128]{1,0:T(8,128)S(1)} %get-tuple-element.75.first, f32[128,128]{1,0:T(8,128)S(1)} %get-tuple-element.76.second, f32[128,128]{1,0:T(8,128)S(1)} %get-tuple-element.77.third), custom_call_target="tpu_custom_call" | custom-call | tf_op jit(solution)/shard_map/last_step/pallas_call | solution.py:430
  (26 shorter events, 0.1 us)
Async XLA Ops:
  0.6 14.3 %copy-start.1 = (bf16[1,8,128,128]{3,2,1,0:T(8,128)(2,1)S(1)}, bf16[1,8,128,128]{3,2,1,0:T(8,128)(2,1)}, u32[]{:S(2)}) copy-start(bf16[1,8,128,128]{3,2,1,0:T(8,128)(2,1)} %param.12) | copy-start | bytes 786436
  0.6 14.3 %copy-start = (bf16[2048,128]{1,0:T(8,128)(2,1)S(1)}, bf16[2048,128]{1,0:T(8,128)(2,1)}, u32[]{:S(2)}) copy-start(bf16[2048,128]{1,0:T(8,128)(2,1)} %subs.1) | copy-start | bytes 1572868
  0.7 14.3 %copy-start.4 = (s32[1,1,16,8,2,128]{5,4,3,2,1,0:T(2,128)S(1)}, s32[1,1,16,8,2,128]{5,4,3,2,1,0:T(2,128)}, u32[]{:S(2)}) copy-start(s32[1,1,16,8,2,128]{5,4,3,2,1,0:T(2,128)} %param.19) | copy-start | bytes 393220
  0.7 14.3 %copy-start.8 = (s32[1,1,16]{2,1,0:T(1,128)S(1)}, s32[1,1,16]{2,1,0:T(1,128)}, u32[]{:S(2)}) copy-start(s32[1,1,16]{2,1,0:T(1,128)} %param.18) | copy-start | bytes 196
  0.7 14.3 %copy-start.7 = (s32[1,1,16,8]{2,3,1,0:T(8,128)S(1)}, s32[1,1,16,8]{2,3,1,0:T(8,128)}, u32[]{:S(2)}) copy-start(s32[1,1,16,8]{2,3,1,0:T(8,128)} %param.17) | copy-start | bytes 1540
  0.7 14.3 %copy-start.6 = (s32[1,1,16,8]{2,3,1,0:T(8,128)S(1)}, s32[1,1,16,8]{2,3,1,0:T(8,128)}, u32[]{:S(2)}) copy-start(s32[1,1,16,8]{2,3,1,0:T(8,128)} %param.16) | copy-start | bytes 1540
  0.7 14.3 %copy-start.5 = (s32[1,1,16,8]{2,3,1,0:T(8,128)S(1)}, s32[1,1,16,8]{2,3,1,0:T(8,128)}, u32[]{:S(2)}) copy-start(s32[1,1,16,8]{2,3,1,0:T(8,128)} %param.15) | copy-start | bytes 1540
  0.7 10.0 %collective-permute-start.2 = (bf16[8,128,128]{2,1,0:T(8,128)(2,1)}, bf16[8,128,128]{2,1,0:T(8,128)(2,1)S(1)}, u32[]{:S(2)}, u32[]{:S(2)}) collective-permute-start(bf16[8,128,128]{2,1,0:T(8,128)(2,1)} %bitcast.14), channel_id=1, source_target_pairs={{0,2},{2,0},{4,6},{6,4},{8,10},{10,8},{12,14},{14,12},{16,18},{18,... | collective-permute-start | bytes 786440 | tf_op jit(solution)/shard_map/ppermute | solution.py:468
  1.2 9.8 %collective-permute-start.1 = (bf16[8,128,128]{2,1,0:T(8,128)(2,1)}, bf16[8,128,128]{2,1,0:T(8,128)(2,1)S(1)}, u32[]{:S(2)}, u32[]{:S(2)}) collective-permute-start(bf16[8,128,128]{2,1,0:T(8,128)(2,1)} %bitcast.15), channel_id=1, source_target_pairs={{0,4},{2,6},{8,0},{10,2},{16,8},{18,10},{24,16},{26,18},{28,24},{3... | collective-permute-start | bytes 786440 | tf_op jit(solution)/shard_map/ppermute | solution.py:461
  3.8 8.6 %collective-permute-start = (bf16[8,128,128]{2,1,0:T(8,128)(2,1)}, bf16[8,128,128]{2,1,0:T(8,128)(2,1)S(1)}, u32[]{:S(2)}, u32[]{:S(2)}) collective-permute-start(bf16[8,128,128]{2,1,0:T(8,128)(2,1)} %bitcast.16), channel_id=1, source_target_pairs={{0,8},{2,10},{8,16},{10,18},{16,24},{18,26},{24,28},{26,30},{28,20... | collective-permute-start | bytes 786440 | tf_op jit(solution)/shard_map/ppermute | solution.py:460
  10.7 41.9 %copy-start.2 = (f32[128,128]{1,0:T(8,128)S(1)}, f32[128,128]{1,0:T(8,128)}, u32[]{:S(2)}) copy-start(f32[128,128]{1,0:T(8,128)} %start.3) | copy-start | bytes 196612
  10.7 41.9 %copy-start.3 = (f32[128]{0:T(128)S(1)}, f32[128]{0:T(128)}, u32[]{:S(2)}) copy-start(f32[128]{0:T(128)} %param.11) | copy-start | bytes 1540
  12.4 2.5 %collective-permute-start.5 = (bf16[2,2,4,160,128]{4,3,2,1,0:T(8,128)(2,1)}, bf16[2,2,4,160,128]{4,3,2,1,0:T(8,128)(2,1)S(1)}, u32[]{:S(2)}, u32[]{:S(2)}) collective-permute-start(bf16[2,2,4,160,128]{4,3,2,1,0:T(8,128)(2,1)} %rhs.2), channel_id=1, source_target_pairs={{0,2},{2,0},{4,6},{6,4},{8,10},{10,8},{12,14},{14,12},{16,18},{18,... | collective-permute-start | bytes 1966088 | tf_op jit(solution)/shard_map/ppermute | solution.py:468
  12.4 8.7 %collective-permute-start.3 = (bf16[8,128,128]{2,1,0:T(8,128)(2,1)S(1)}, bf16[8,128,128]{2,1,0:T(8,128)(2,1)S(1)}, u32[]{:S(2)}, u32[]{:S(2)}) collective-permute-start(bf16[8,128,128]{2,1,0:T(8,128)(2,1)S(1)} %collective-permute-done.refs_16_), channel_id=1, source_target_pairs={{0,8},{2,10},{8,16},{10,18},{16,24},{18,26},{24,28},{26,30},{28,20... | collective-permute-start | bytes 786440 | tf_op jit(solution)/shard_map/ppermute | solution.py:460
  12.8 7.2 %collective-permute-start.6 = (bf16[8,128,128]{2,1,0:T(8,128)(2,1)S(1)}, bf16[8,128,128]{2,1,0:T(8,128)(2,1)S(1)}, u32[]{:S(2)}, u32[]{:S(2)}) collective-permute-start(bf16[8,128,128]{2,1,0:T(8,128)(2,1)S(1)} %collective-permute-done.1.refs_2_), channel_id=1, source_target_pairs={{0,2},{2,0},{4,6},{6,4},{8,10},{10,8},{12,14},{14,12},{16,18},{18,... | collective-permute-start | bytes 786440 | tf_op jit(solution)/shard_map/ppermute | solution.py:468
  13.0 7.0 %collective-permute-start.7 = (bf16[8,128,128]{2,1,0:T(8,128)(2,1)S(1)}, bf16[8,128,128]{2,1,0:T(8,128)(2,1)S(1)}, u32[]{:S(2)}, u32[]{:S(2)}) collective-permute-start(bf16[8,128,128]{2,1,0:T(8,128)(2,1)S(1)} %collective-permute-done.refs_16_), channel_id=1, source_target_pairs={{0,2},{2,0},{4,6},{6,4},{8,10},{10,8},{12,14},{14,12},{16,18},{18,... | collective-permute-start | bytes 786440 | tf_op jit(solution)/shard_map/ppermute | solution.py:468
  13.3 8.4 %collective-permute-start.4 = (bf16[8,128,128]{2,1,0:T(8,128)(2,1)S(1)}, bf16[8,128,128]{2,1,0:T(8,128)(2,1)S(1)}, u32[]{:S(2)}, u32[]{:S(2)}) collective-permute-start(bf16[8,128,128]{2,1,0:T(8,128)(2,1)S(1)} %collective-permute-done.1.refs_2_), channel_id=1, source_target_pairs={{0,4},{2,6},{8,0},{10,2},{16,8},{18,10},{24,16},{26,18},{28,24},{3... | collective-permute-start | bytes 786440 | tf_op jit(solution)/shard_map/ppermute | solution.py:461
  21.7 16.5 %collective-permute-start.8 = (bf16[8,128,128]{2,1,0:T(8,128)(2,1)S(1)}, bf16[8,128,128]{2,1,0:T(8,128)(2,1)S(1)}, u32[]{:S(2)}, u32[]{:S(2)}) collective-permute-start(bf16[8,128,128]{2,1,0:T(8,128)(2,1)S(1)} %collective-permute-done.3.refs_14_), channel_id=1, source_target_pairs={{0,8},{2,10},{8,16},{10,18},{16,24},{18,26},{24,28},{26,30},{28,20... | collective-permute-start | bytes 786440 | tf_op jit(solution)/shard_map/ppermute | solution.py:460
  23.4 14.8 %collective-permute-start.9 = (bf16[8,128,128]{2,1,0:T(8,128)(2,1)S(1)}, bf16[8,128,128]{2,1,0:T(8,128)(2,1)S(1)}, u32[]{:S(2)}, u32[]{:S(2)}) collective-permute-start(bf16[8,128,128]{2,1,0:T(8,128)(2,1)S(1)} %collective-permute-done.4.refs_4_), channel_id=1, source_target_pairs={{0,4},{2,6},{8,0},{10,2},{16,8},{18,10},{24,16},{26,18},{28,24},{3... | collective-permute-start | bytes 786440 | tf_op jit(solution)/shard_map/ppermute | solution.py:461
  23.7 11.1 %collective-permute-start.10 = (bf16[4,176,128]{2,1,0:T(8,128)(2,1)S(1)}, bf16[4,176,128]{2,1,0:T(8,128)(2,1)S(1)}, u32[]{:S(2)}, u32[]{:S(2)}) collective-permute-start(bf16[4,176,128]{2,1,0:T(8,128)(2,1)S(1)} %get-tuple-element.51), channel_id=1, source_target_pairs={{0,4},{1,5},{2,6},{3,7},{4,0},{5,1},{6,2},{7,3},{8,12},{9,13},{10,... | collective-permute-start | bytes 540680 | tf_op jit(solution)/shard_map/ppermute | solution.py:212
  25.4 9.4 %collective-permute-start.11 = (bf16[4,176,128]{2,1,0:T(8,128)(2,1)S(1)}, bf16[4,176,128]{2,1,0:T(8,128)(2,1)S(1)}, u32[]{:S(2)}, u32[]{:S(2)}) collective-permute-start(bf16[4,176,128]{2,1,0:T(8,128)(2,1)S(1)} %get-tuple-element.52), channel_id=1, source_target_pairs={{0,1},{1,0},{2,3},{3,2},{4,5},{5,4},{6,7},{7,6},{8,9},{9,8},{10,11... | collective-permute-start | bytes 540680 | tf_op jit(solution)/shard_map/ppermute | solution.py:212
  26.9 11.3 %collective-permute-start.12 = (bf16[4,176,128]{2,1,0:T(8,128)(2,1)S(1)}, bf16[4,176,128]{2,1,0:T(8,128)(2,1)S(1)}, u32[]{:S(2)}, u32[]{:S(2)}) collective-permute-start(bf16[4,176,128]{2,1,0:T(8,128)(2,1)S(1)} %get-tuple-element.53), channel_id=1, source_target_pairs={{0,5},{1,4},{2,7},{3,6},{4,1},{5,0},{6,3},{7,2},{8,13},{9,12},{10,... | collective-permute-start | bytes 540680 | tf_op jit(solution)/shard_map/ppermute | solution.py:212
  38.3 11.3 %collective-permute-start.16 = (bf16[4,128,128]{2,1,0:T(8,128)(2,1)S(1)}, bf16[4,128,128]{2,1,0:T(8,128)(2,1)S(1)}, u32[]{:S(2)}, u32[]{:S(2)}) collective-permute-start(bf16[4,128,128]{2,1,0:T(8,128)(2,1)S(1)} %slice.7), channel_id=1, source_target_pairs={{0,4},{2,6},{8,0},{10,2},{16,8},{18,10},{24,16},{26,18},{28,24},{3... | collective-permute-start | bytes 393224 | tf_op jit(solution)/shard_map/ppermute | solution.py:457
  40.1 10.2 %collective-permute-start.15 = (bf16[4,128,128]{2,1,0:T(8,128)(2,1)S(1)}, bf16[4,128,128]{2,1,0:T(8,128)(2,1)S(1)}, u32[]{:S(2)}, u32[]{:S(2)}) collective-permute-start(bf16[4,128,128]{2,1,0:T(8,128)(2,1)S(1)} %slice.6), channel_id=1, source_target_pairs={{0,8},{2,10},{8,16},{10,18},{16,24},{18,26},{24,28},{26,30},{28,20... | collective-permute-start | bytes 393224 | tf_op jit(solution)/shard_map/ppermute | solution.py:456
  40.4 8.0 %collective-permute-start.21 = (bf16[272,128]{1,0:T(8,128)(2,1)S(1)}, bf16[272,128]{1,0:T(8,128)(2,1)S(1)}, u32[]{:S(2)}, u32[]{:S(2)}) collective-permute-start(bf16[272,128]{1,0:T(8,128)(2,1)S(1)} %get-tuple-element.71), channel_id=1, source_target_pairs={{0,8},{2,10},{4,12},{6,14},{8,16},{10,18},{12,20},{14,22},{16,24},... | collective-permute-start | bytes 208904 | tf_op jit(solution)/shard_map/ppermute | solution.py:237
  40.5 9.1 %collective-permute-start.22 = (bf16[272,128]{1,0:T(8,128)(2,1)S(1)}, bf16[272,128]{1,0:T(8,128)(2,1)S(1)}, u32[]{:S(2)}, u32[]{:S(2)}) collective-permute-start(bf16[272,128]{1,0:T(8,128)(2,1)S(1)} %get-tuple-element.72), channel_id=1, source_target_pairs={{0,16},{2,18},{4,20},{6,22},{8,24},{10,26},{12,28},{14,30},{16,0},... | collective-permute-start | bytes 208904 | tf_op jit(solution)/shard_map/ppermute | solution.py:237
  45.8 4.5 %collective-permute-start.23 = (bf16[272,128]{1,0:T(8,128)(2,1)S(1)}, bf16[272,128]{1,0:T(8,128)(2,1)S(1)}, u32[]{:S(2)}, u32[]{:S(2)}) collective-permute-start(bf16[272,128]{1,0:T(8,128)(2,1)S(1)} %get-tuple-element.73), channel_id=1, source_target_pairs={{0,24},{2,26},{4,28},{6,30},{8,0},{10,2},{12,4},{14,6},{16,8},{18,... | collective-permute-start | bytes 208904 | tf_op jit(solution)/shard_map/ppermute | solution.py:237
  48.4 4.2 %collective-permute-start.13 = (bf16[8,128,128]{2,1,0:T(8,128)(2,1)S(1)}, bf16[8,128,128]{2,1,0:T(8,128)(2,1)S(1)}, u32[]{:S(2)}, u32[]{:S(2)}) collective-permute-start(bf16[8,128,128]{2,1,0:T(8,128)(2,1)S(1)} %collective-permute-done.4.refs_4_), channel_id=1, source_target_pairs={{0,2},{2,0},{4,6},{6,4},{8,10},{10,8},{12,14},{14,12},{16,18},{18,... | collective-permute-start | bytes 786440 | tf_op jit(solution)/shard_map/ppermute | solution.py:468
  49.5 3.1 %collective-permute-start.14 = (bf16[8,128,128]{2,1,0:T(8,128)(2,1)S(1)}, bf16[8,128,128]{2,1,0:T(8,128)(2,1)S(1)}, u32[]{:S(2)}, u32[]{:S(2)}) collective-permute-start(bf16[8,128,128]{2,1,0:T(8,128)(2,1)S(1)} %collective-permute-done.9.refs_6_), channel_id=1, source_target_pairs={{0,2},{2,0},{4,6},{6,4},{8,10},{10,8},{12,14},{14,12},{16,18},{18,... | collective-permute-start | bytes 786440 | tf_op jit(solution)/shard_map/ppermute | solution.py:468
  49.5 1.7 %collective-permute-start.18 = (bf16[4,128,128]{2,1,0:T(8,128)(2,1)S(1)}, bf16[4,128,128]{2,1,0:T(8,128)(2,1)S(1)}, u32[]{:S(2)}, u32[]{:S(2)}) collective-permute-start(bf16[4,128,128]{2,1,0:T(8,128)(2,1)S(1)} %collective-permute-done.16.refs_9_), channel_id=1, source_target_pairs={{0,2},{2,0},{4,6},{6,4},{8,10},{10,8},{12,14},{14,12},{16,18},{18,... | collective-permute-start | bytes 393224 | tf_op jit(solution)/shard_map/ppermute | solution.py:468
  50.3 2.4 %collective-permute-start.19 = (bf16[8,128,128]{2,1,0:T(8,128)(2,1)S(1)}, bf16[8,128,128]{2,1,0:T(8,128)(2,1)S(1)}, u32[]{:S(2)}, u32[]{:S(2)}) collective-permute-start(bf16[8,128,128]{2,1,0:T(8,128)(2,1)S(1)} %collective-permute-done.8.refs_12_), channel_id=1, source_target_pairs={{0,2},{2,0},{4,6},{6,4},{8,10},{10,8},{12,14},{14,12},{16,18},{18,... | collective-permute-start | bytes 786440 | tf_op jit(solution)/shard_map/ppermute | solution.py:468
  50.3 2.4 %collective-permute-start.20 = (bf16[8,128,128]{2,1,0:T(8,128)(2,1)S(1)}, bf16[8,128,128]{2,1,0:T(8,128)(2,1)S(1)}, u32[]{:S(2)}, u32[]{:S(2)}) collective-permute-start(bf16[8,128,128]{2,1,0:T(8,128)(2,1)S(1)} %collective-permute-done.3.refs_14_), channel_id=1, source_target_pairs={{0,2},{2,0},{4,6},{6,4},{8,10},{10,8},{12,14},{14,12},{16,18},{18,... | collective-permute-start | bytes 786440 | tf_op jit(solution)/shard_map/ppermute | solution.py:468
  51.3 1.3 %collective-permute-start.17 = (bf16[4,128,128]{2,1,0:T(8,128)(2,1)S(1)}, bf16[4,128,128]{2,1,0:T(8,128)(2,1)S(1)}, u32[]{:S(2)}, u32[]{:S(2)}) collective-permute-start(bf16[4,128,128]{2,1,0:T(8,128)(2,1)S(1)} %collective-permute-done.15.refs_8_), channel_id=1, source_target_pairs={{0,2},{2,0},{4,6},{6,4},{8,10},{10,8},{12,14},{14,12},{16,18},{18,... | collective-permute-start | bytes 393224 | tf_op jit(solution)/shard_map/ppermute | solution.py:468

commit v15 on v13

--- a/solution.py
+++ b/solution.py
@@ -167,9 +167,14 @@
     )(*scalars, ratings, runs, words, subs, *([given] if half == 0 else []))
 
 
+def far_first(count):
+    return [0] + list(range(count - 1, 0, -2)) + list(range(2, count, 2))
+
+
 def chip_kernel(*refs, own_rows, spans):
     levels, _, rank = refs[0].shape
-    parts, outs = refs[:-levels], refs[-levels:]
+    given, outs = refs[:-levels], refs[-levels:]
+    parts = [given[far_first(len(given)).index(k)] for k in range(len(given))]
     lines = outs[0].shape[0] - own_rows - spans * len(parts)
     for up in range(levels):
         total = parts[0][up, :own_rows, :].astype(f32)
@@ -214,7 +219,7 @@
         out_shape=[shape] * levels,
         compiler_params=pltpu.CompilerParams(vmem_limit_bytes=16 * MIB),
         name="chip",
-    )(*parts)
+    )(*[parts[k] for k in far_first(len(parts))])
 
 
 def reduce_levels(total, shards):

time: 74.1 us -> 74.1 us (level)
  waiting for transfers between devices: 18.9 us -> 17.8 us
  blocking collectives: 9.66 us -> 10.6 us
    ppermute x3, waiting for transfers between devices: 10.8 us -> 9.76 us  [exchange_chips(): given.append(lax.ppermute(part, AXES, pairs) if o or column else part)]
    all_to_all x1, blocking collectives: 9.66 us -> 10.6 us  [on_device(): everyone = lax.all_to_all(dots, AXES, 0, 0, tiled=True)]
where the time goes in v15:
time: 74.1 us; the launch traced here: 73.9 us
  Pallas kernels  23.5 us (32%)
  starting transfers between devices  21 us (28%)
  waiting for transfers between devices  17.8 us (24%)
  blocking collectives  10.6 us (14%)
  between operations  0.87 us (1%)
    pallas_call x2, Pallas kernels, rhs_sums(): pl.pallas_call(functools.partial(rhs_kernel, half=half, owners=owners, ow...  11.9 us
    pallas_call x1, Pallas kernels, krylov(): pl.pallas_call(functools.partial(steps_kernel, count=len(pieces), word_ti...  10.7 us
    all_to_all x1, blocking collectives, on_device(): everyone = lax.all_to_all(dots, AXES, 0, 0, tiled=True)  10.6 us
    ppermute x3, waiting for transfers between devices, exchange_chips(): given.append(lax.ppermute(part, AXES, pairs) if o or column else part)  9.76 us
    ppermute x3, starting transfers between devices, reduce_levels(): terms.append(lax.ppermute(total[up], 'loop', shift))  6.42 us
    ppermute x3, starting transfers between devices, ring_round(): down = lax.ppermute(down, 'loop', shift(-1))  4.43 us
    ppermute x3, starting transfers between devices, exchange_chips(): given.append(lax.ppermute(part, AXES, pairs) if o or column else part)  3.49 us
    ppermute x3, waiting for transfers between devices, reduce_levels(): terms.append(lax.ppermute(total[up], 'loop', shift))  3.04 us
  transfers between devices with their start and end apart: 24, of which 11 were waited for; matrix products, arithmetic and copies ran while one was open for 0% of the time, Pallas kernels for 16%

profile of v15, /device:TPU:0, one launch (start us, length us, event | category | flops | bytes accessed | tf_op | source)
XLA Modules:
  0.0 73.9 jit_solution(133394813508389304)
XLA Ops:
  0.7 0.5 collective-permute-start.2
  1.2 2.5 %collective-permute-start.1 = (bf16[8,128,128]{2,1,0:T(8,128)(2,1)}, bf16[8,128,128]{2,1,0:T(8,128)(2,1)S(1)}, u32[]{:S(2)}, u32[]{:S(2)}) collective-permute-start(bf16[8,128,128]{2,1,0:T(8,128)(2,1)} %bitcast.15), channel_id=1, source_target_pairs={{0,4},{2,6},{8,0},{10,2},{16,8},{18,10},{24,16},{26,18},{28,24},{3... | collective-permute-start | bytes 786440 | tf_op jit(solution)/shard_map/ppermute | solution.py:454
  3.8 0.2 collective-permute-start
  3.9 6.8 %rhs.2 = bf16[2,2,4,160,128]{4,3,2,1,0:T(8,128)(2,1)} custom-call(s32[8,16]{1,0:T(8,128)} %bitcast.23, s32[8,16]{1,0:T(8,128)} %bitcast.25, s32[8,16]{1,0:T(8,128)} %bitcast.27, s32[1,16]{1,0:T(1,128)} %bitcast.29, bf16[16,8,128,128]{3,2,1,0:T(8,128)(2,1)} %bitcast.31, s32[16,8,2,128]{3,2,1,0:T(2,128)} %bitcast.21, bf16[8,128,128]{2,1,0:T(8,128)(2,1)} %bitcast.17, ...), custom_call_target="tpu_custom_call" | custom-call | flops 2147483648 | bytes 16777216 | tf_op jit(solution)/shard_map/rhs/pallas_call | solution.py:145
  10.8 0.0 copy-start.2
  10.8 0.0 copy-start.3
  10.8 0.0 collective-permute-done.2.refs_1_
  10.8 0.2 collective-permute-done.1.refs_2_
  11.0 1.4 %collective-permute-done.refs_16_ = bf16[8,128,128]{2,1,0:T(8,128)(2,1)S(1)} collective-permute-done((bf16[8,128,128]{2,1,0:T(8,128)(2,1)}, bf16[8,128,128]{2,1,0:T(8,128)(2,1)S(1)}, u32[]{:S(2)}, u32[]{:S(2)}) %collective-permute-start) | collective-permute-done | bytes 262176 | tf_op jit(solution)/shard_map/ppermute | solution.py:453
  12.4 0.0 collective-permute-start.5
  12.4 0.5 collective-permute-start.3
  12.9 0.2 collective-permute-start.6
  13.1 0.3 collective-permute-start.7
  13.4 1.5 %collective-permute-start.4 = (bf16[8,128,128]{2,1,0:T(8,128)(2,1)S(1)}, bf16[8,128,128]{2,1,0:T(8,128)(2,1)S(1)}, u32[]{:S(2)}, u32[]{:S(2)}) collective-permute-start(bf16[8,128,128]{2,1,0:T(8,128)(2,1)S(1)} %collective-permute-done.1.refs_2_), channel_id=1, source_target_pairs={{0,4},{2,6},{8,0},{10,2},{16,8},{18,10},{24,16},{26,18},{28,24},{3... | collective-permute-start | bytes 786440 | tf_op jit(solution)/shard_map/ppermute | solution.py:454
  15.0 5.0 %rhs.3 = (bf16[4,176,128]{2,1,0:T(8,128)(2,1)S(1)}, bf16[4,176,128]{2,1,0:T(8,128)(2,1)S(1)}, bf16[4,176,128]{2,1,0:T(8,128)(2,1)S(1)}, bf16[4,176,128]{2,1,0:T(8,128)(2,1)S(1)}) custom-call(s32[8,16]{1,0:T(8,128)S(1)} %bitcast.24, s32[8,16]{1,0:T(8,128)S(1)} %bitcast.26, s32[8,16]{1,0:T(8,128)S(1)} %bitcast.28, s32[1,16]{1,0:T(1,128)S(1)} %bitcast.30, ...), custom_call_target="tpu_custom_call" | custom-call | flops 2147483648 | bytes 16777216 | tf_op jit(solution)/shard_map/rhs/pallas_call | solution.py:145
  20.0 0.0 collective-permute-done.7.refs_17_
  20.0 1.0 %collective-permute-done.3.refs_14_ = bf16[8,128,128]{2,1,0:T(8,128)(2,1)S(1)} collective-permute-done((bf16[8,128,128]{2,1,0:T(8,128)(2,1)S(1)}, bf16[8,128,128]{2,1,0:T(8,128)(2,1)S(1)}, u32[]{:S(2)}, u32[]{:S(2)}) %collective-permute-start.3) | collective-permute-done | bytes 262176 | tf_op jit(solution)/shard_map/ppermute | solution.py:453
  21.1 0.7 collective-permute-done.4.refs_4_
  21.8 1.6 %collective-permute-start.8 = (bf16[8,128,128]{2,1,0:T(8,128)(2,1)S(1)}, bf16[8,128,128]{2,1,0:T(8,128)(2,1)S(1)}, u32[]{:S(2)}, u32[]{:S(2)}) collective-permute-start(bf16[8,128,128]{2,1,0:T(8,128)(2,1)S(1)} %collective-permute-done.3.refs_14_), channel_id=1, source_target_pairs={{0,8},{2,10},{8,16},{10,18},{16,24},{18,26},{24,28},{26,30},{28,20... | collective-permute-start | bytes 786440 | tf_op jit(solution)/shard_map/ppermute | solution.py:453
  23.4 0.4 collective-permute-start.9
  23.8 2.5 %collective-permute-start.10 = (bf16[4,176,128]{2,1,0:T(8,128)(2,1)S(1)}, bf16[4,176,128]{2,1,0:T(8,128)(2,1)S(1)}, u32[]{:S(2)}, u32[]{:S(2)}) collective-permute-start(bf16[4,176,128]{2,1,0:T(8,128)(2,1)S(1)} %get-tuple-element.51), channel_id=1, source_target_pairs={{0,5},{1,4},{2,7},{3,6},{4,1},{5,0},{6,3},{7,2},{8,13},{9,12},{10,... | collective-permute-start | bytes 540680 | tf_op jit(solution)/shard_map/ppermute | solution.py:205
  26.3 0.5 collective-permute-start.11
  26.9 0.5 collective-permute-start.12
  27.3 8.6 %collective-permute-done.10.refs_1_ = bf16[4,176,128]{2,1,0:T(8,128)(2,1)S(1)} collective-permute-done((bf16[4,176,128]{2,1,0:T(8,128)(2,1)S(1)}, bf16[4,176,128]{2,1,0:T(8,128)(2,1)S(1)}, u32[]{:S(2)}, u32[]{:S(2)}) %collective-permute-start.10) | collective-permute-done | bytes 180256 | tf_op jit(solution)/shard_map/ppermute | solution.py:205
  35.9 1.2 %collective-permute-done.11.refs_2_ = bf16[4,176,128]{2,1,0:T(8,128)(2,1)S(1)} collective-permute-done((bf16[4,176,128]{2,1,0:T(8,128)(2,1)S(1)}, bf16[4,176,128]{2,1,0:T(8,128)(2,1)S(1)}, u32[]{:S(2)}, u32[]{:S(2)}) %collective-permute-start.11) | collective-permute-done | bytes 180256 | tf_op jit(solution)/shard_map/ppermute | solution.py:205
  37.1 0.0 collective-permute-done.12.refs_3_
  37.1 0.1 chip.1
  37.2 0.0 collective-permute-done.9.refs_6_
  37.2 1.8 %collective-permute-start.16 = (bf16[4,128,128]{2,1,0:T(8,128)(2,1)S(1)}, bf16[4,128,128]{2,1,0:T(8,128)(2,1)S(1)}, u32[]{:S(2)}, u32[]{:S(2)}) collective-permute-start(bf16[4,128,128]{2,1,0:T(8,128)(2,1)S(1)} %slice.7), channel_id=1, source_target_pairs={{0,4},{2,6},{8,0},{10,2},{16,8},{18,10},{24,16},{26,18},{28,24},{3... | collective-permute-start | bytes 393224 | tf_op jit(solution)/shard_map/ppermute | solution.py:450
  39.0 0.3 collective-permute-start.15
  39.3 0.1 collective-permute-start.21
  39.4 5.4 %collective-permute-start.22 = (bf16[272,128]{1,0:T(8,128)(2,1)S(1)}, bf16[272,128]{1,0:T(8,128)(2,1)S(1)}, u32[]{:S(2)}, u32[]{:S(2)}) collective-permute-start(bf16[272,128]{1,0:T(8,128)(2,1)S(1)} %get-tuple-element.72), channel_id=1, source_target_pairs={{0,16},{2,18},{4,20},{6,22},{8,24},{10,26},{12,28},{14,30},{16,0},... | collective-permute-start | bytes 208904 | tf_op jit(solution)/shard_map/ppermute | solution.py:230
  44.8 0.9 %collective-permute-start.23 = (bf16[272,128]{1,0:T(8,128)(2,1)S(1)}, bf16[272,128]{1,0:T(8,128)(2,1)S(1)}, u32[]{:S(2)}, u32[]{:S(2)}) collective-permute-start(bf16[272,128]{1,0:T(8,128)(2,1)S(1)} %get-tuple-element.73), channel_id=1, source_target_pairs={{0,24},{2,26},{4,28},{6,30},{8,0},{10,2},{12,4},{14,6},{16,8},{18,... | collective-permute-start | bytes 208904 | tf_op jit(solution)/shard_map/ppermute | solution.py:230
  45.8 1.7 %collective-permute-done.21.refs_19_ = bf16[272,128]{1,0:T(8,128)(2,1)S(1)} collective-permute-done((bf16[272,128]{1,0:T(8,128)(2,1)S(1)}, bf16[272,128]{1,0:T(8,128)(2,1)S(1)}, u32[]{:S(2)}, u32[]{:S(2)}) %collective-permute-start.21) | collective-permute-done | bytes 69664 | tf_op jit(solution)/shard_map/ppermute | solution.py:230
  47.5 1.1 %collective-permute-done.22.refs_20_ = bf16[272,128]{1,0:T(8,128)(2,1)S(1)} collective-permute-done((bf16[272,128]{1,0:T(8,128)(2,1)S(1)}, bf16[272,128]{1,0:T(8,128)(2,1)S(1)}, u32[]{:S(2)}, u32[]{:S(2)}) %collective-permute-start.22) | collective-permute-done | bytes 69664 | tf_op jit(solution)/shard_map/ppermute | solution.py:230
  48.6 0.0 collective-permute-start.14
  48.6 0.0 collective-permute-done.16.refs_9_
  48.6 0.5 collective-permute-start.18
  49.1 0.2 collective-permute-done.23.refs_21_
  49.3 0.5 collective-permute-start.20
  49.8 0.5 collective-permute-done.18.refs_11_
  50.3 0.1 collective-permute-start.17
  50.4 1.2 %collective-permute-done.17.refs_10_ = bf16[4,128,128]{2,1,0:T(8,128)(2,1)S(1)} collective-permute-done((bf16[4,128,128]{2,1,0:T(8,128)(2,1)S(1)}, bf16[4,128,128]{2,1,0:T(8,128)(2,1)S(1)}, u32[]{:S(2)}, u32[]{:S(2)}) %collective-permute-start.17) | collective-permute-done | bytes 131104 | tf_op jit(solution)/shard_map/ppermute | solution.py:461
  51.7 0.0 collective-permute-done.19.refs_13_
  51.7 0.0 collective-permute-done.20.refs_15_
  51.7 10.7 %krylov.1 = (f32[128,128]{1,0:T(8,128)S(1)}, f32[128,128]{1,0:T(8,128)S(1)}, f32[128,128]{1,0:T(8,128)S(1)}, f32[32,1,128]{2,1,0:T(1,128)S(1)}) custom-call(f32[1,128]{1,0:T(1,128)S(1)} %bitcast.20, f32[128,128]{1,0:T(8,128)S(1)} %copy-done.2, bf16[2048,128]{1,0:T(8,128)(2,1)S(1)} %copy-done, bf16[8,128,128]{2,1,0:T(8,128)(2,1)S(1)} %bitcast.19, ...), custom_call_target="tpu_custom_call" | custom-call | tf_op jit(solution)/shard_map/krylov/pallas_call | solution.py:387
  62.4 10.6 %all_to_all.5.dots = f32[32,1,128]{2,1,0:T(1,128)S(1)} all-to-all(f32[32,1,128]{2,1,0:T(1,128)S(1)} %get-tuple-element.74), channel_id=1, replica_groups=mesh['loop'=16,'own'=2] {'loop','own'}, dimensions={0} | all-to-all | bytes 32768 | tf_op jit(solution)/shard_map/all_to_all | solution.py:519
  73.0 0.9 %last_step.1 = (f32[128,128]{1,0:T(8,128)}, f32[128,128]{1,0:T(8,128)}) custom-call(f32[32,1,128]{2,1,0:T(1,128)S(1)} %all_to_all.5.dots, f32[128,128]{1,0:T(8,128)S(1)} %copy-done.2, f32[128,128]{1,0:T(8,128)S(1)} %get-tuple-element.75.first, f32[128,128]{1,0:T(8,128)S(1)} %get-tuple-element.76.second, f32[128,128]{1,0:T(8,128)S(1)} %get-tuple-element.77.third), custom_call_target="tpu_custom_call" | custom-call | tf_op jit(solution)/shard_map/last_step/pallas_call | solution.py:423
  (26 shorter events, 0.1 us)
Async XLA Ops:
  0.6 14.3 %copy-start.1 = (bf16[1,8,128,128]{3,2,1,0:T(8,128)(2,1)S(1)}, bf16[1,8,128,128]{3,2,1,0:T(8,128)(2,1)}, u32[]{:S(2)}) copy-start(bf16[1,8,128,128]{3,2,1,0:T(8,128)(2,1)} %param.12) | copy-start | bytes 786436
  0.6 14.3 %copy-start = (bf16[2048,128]{1,0:T(8,128)(2,1)S(1)}, bf16[2048,128]{1,0:T(8,128)(2,1)}, u32[]{:S(2)}) copy-start(bf16[2048,128]{1,0:T(8,128)(2,1)} %subs.1) | copy-start | bytes 1572868
  0.7 14.3 %copy-start.4 = (s32[1,1,16,8,2,128]{5,4,3,2,1,0:T(2,128)S(1)}, s32[1,1,16,8,2,128]{5,4,3,2,1,0:T(2,128)}, u32[]{:S(2)}) copy-start(s32[1,1,16,8,2,128]{5,4,3,2,1,0:T(2,128)} %param.19) | copy-start | bytes 393220
  0.7 14.3 %copy-start.8 = (s32[1,1,16]{2,1,0:T(1,128)S(1)}, s32[1,1,16]{2,1,0:T(1,128)}, u32[]{:S(2)}) copy-start(s32[1,1,16]{2,1,0:T(1,128)} %param.18) | copy-start | bytes 196
  0.7 14.3 %copy-start.7 = (s32[1,1,16,8]{2,3,1,0:T(8,128)S(1)}, s32[1,1,16,8]{2,3,1,0:T(8,128)}, u32[]{:S(2)}) copy-start(s32[1,1,16,8]{2,3,1,0:T(8,128)} %param.17) | copy-start | bytes 1540
  0.7 14.3 %copy-start.6 = (s32[1,1,16,8]{2,3,1,0:T(8,128)S(1)}, s32[1,1,16,8]{2,3,1,0:T(8,128)}, u32[]{:S(2)}) copy-start(s32[1,1,16,8]{2,3,1,0:T(8,128)} %param.16) | copy-start | bytes 1540
  0.7 14.3 %copy-start.5 = (s32[1,1,16,8]{2,3,1,0:T(8,128)S(1)}, s32[1,1,16,8]{2,3,1,0:T(8,128)}, u32[]{:S(2)}) copy-start(s32[1,1,16,8]{2,3,1,0:T(8,128)} %param.15) | copy-start | bytes 1540
  0.7 10.1 %collective-permute-start.2 = (bf16[8,128,128]{2,1,0:T(8,128)(2,1)}, bf16[8,128,128]{2,1,0:T(8,128)(2,1)S(1)}, u32[]{:S(2)}, u32[]{:S(2)}) collective-permute-start(bf16[8,128,128]{2,1,0:T(8,128)(2,1)} %bitcast.14), channel_id=1, source_target_pairs={{0,2},{2,0},{4,6},{6,4},{8,10},{10,8},{12,14},{14,12},{16,18},{18,... | collective-permute-start | bytes 786440 | tf_op jit(solution)/shard_map/ppermute | solution.py:461
  1.2 9.8 %collective-permute-start.1 = (bf16[8,128,128]{2,1,0:T(8,128)(2,1)}, bf16[8,128,128]{2,1,0:T(8,128)(2,1)S(1)}, u32[]{:S(2)}, u32[]{:S(2)}) collective-permute-start(bf16[8,128,128]{2,1,0:T(8,128)(2,1)} %bitcast.15), channel_id=1, source_target_pairs={{0,4},{2,6},{8,0},{10,2},{16,8},{18,10},{24,16},{26,18},{28,24},{3... | collective-permute-start | bytes 786440 | tf_op jit(solution)/shard_map/ppermute | solution.py:454
  3.8 8.6 %collective-permute-start = (bf16[8,128,128]{2,1,0:T(8,128)(2,1)}, bf16[8,128,128]{2,1,0:T(8,128)(2,1)S(1)}, u32[]{:S(2)}, u32[]{:S(2)}) collective-permute-start(bf16[8,128,128]{2,1,0:T(8,128)(2,1)} %bitcast.16), channel_id=1, source_target_pairs={{0,8},{2,10},{8,16},{10,18},{16,24},{18,26},{24,28},{26,30},{28,20... | collective-permute-start | bytes 786440 | tf_op jit(solution)/shard_map/ppermute | solution.py:453
  10.8 40.9 %copy-start.2 = (f32[128,128]{1,0:T(8,128)S(1)}, f32[128,128]{1,0:T(8,128)}, u32[]{:S(2)}) copy-start(f32[128,128]{1,0:T(8,128)} %start.3) | copy-start | bytes 196612
  10.8 40.9 %copy-start.3 = (f32[128]{0:T(128)S(1)}, f32[128]{0:T(128)}, u32[]{:S(2)}) copy-start(f32[128]{0:T(128)} %param.11) | copy-start | bytes 1540
  12.4 2.5 %collective-permute-start.5 = (bf16[2,2,4,160,128]{4,3,2,1,0:T(8,128)(2,1)}, bf16[2,2,4,160,128]{4,3,2,1,0:T(8,128)(2,1)S(1)}, u32[]{:S(2)}, u32[]{:S(2)}) collective-permute-start(bf16[2,2,4,160,128]{4,3,2,1,0:T(8,128)(2,1)} %rhs.2), channel_id=1, source_target_pairs={{0,2},{2,0},{4,6},{6,4},{8,10},{10,8},{12,14},{14,12},{16,18},{18,... | collective-permute-start | bytes 1966088 | tf_op jit(solution)/shard_map/ppermute | solution.py:461
  12.4 8.7 %collective-permute-start.3 = (bf16[8,128,128]{2,1,0:T(8,128)(2,1)S(1)}, bf16[8,128,128]{2,1,0:T(8,128)(2,1)S(1)}, u32[]{:S(2)}, u32[]{:S(2)}) collective-permute-start(bf16[8,128,128]{2,1,0:T(8,128)(2,1)S(1)} %collective-permute-done.refs_16_), channel_id=1, source_target_pairs={{0,8},{2,10},{8,16},{10,18},{16,24},{18,26},{24,28},{26,30},{28,20... | collective-permute-start | bytes 786440 | tf_op jit(solution)/shard_map/ppermute | solution.py:453
  12.9 7.1 %collective-permute-start.6 = (bf16[8,128,128]{2,1,0:T(8,128)(2,1)S(1)}, bf16[8,128,128]{2,1,0:T(8,128)(2,1)S(1)}, u32[]{:S(2)}, u32[]{:S(2)}) collective-permute-start(bf16[8,128,128]{2,1,0:T(8,128)(2,1)S(1)} %collective-permute-done.1.refs_2_), channel_id=1, source_target_pairs={{0,2},{2,0},{4,6},{6,4},{8,10},{10,8},{12,14},{14,12},{16,18},{18,... | collective-permute-start | bytes 786440 | tf_op jit(solution)/shard_map/ppermute | solution.py:461
  13.1 7.0 %collective-permute-start.7 = (bf16[8,128,128]{2,1,0:T(8,128)(2,1)S(1)}, bf16[8,128,128]{2,1,0:T(8,128)(2,1)S(1)}, u32[]{:S(2)}, u32[]{:S(2)}) collective-permute-start(bf16[8,128,128]{2,1,0:T(8,128)(2,1)S(1)} %collective-permute-done.refs_16_), channel_id=1, source_target_pairs={{0,2},{2,0},{4,6},{6,4},{8,10},{10,8},{12,14},{14,12},{16,18},{18,... | collective-permute-start | bytes 786440 | tf_op jit(solution)/shard_map/ppermute | solution.py:461
  13.4 8.4 %collective-permute-start.4 = (bf16[8,128,128]{2,1,0:T(8,128)(2,1)S(1)}, bf16[8,128,128]{2,1,0:T(8,128)(2,1)S(1)}, u32[]{:S(2)}, u32[]{:S(2)}) collective-permute-start(bf16[8,128,128]{2,1,0:T(8,128)(2,1)S(1)} %collective-permute-done.1.refs_2_), channel_id=1, source_target_pairs={{0,4},{2,6},{8,0},{10,2},{16,8},{18,10},{24,16},{26,18},{28,24},{3... | collective-permute-start | bytes 786440 | tf_op jit(solution)/shard_map/ppermute | solution.py:454
  21.8 15.4 %collective-permute-start.8 = (bf16[8,128,128]{2,1,0:T(8,128)(2,1)S(1)}, bf16[8,128,128]{2,1,0:T(8,128)(2,1)S(1)}, u32[]{:S(2)}, u32[]{:S(2)}) collective-permute-start(bf16[8,128,128]{2,1,0:T(8,128)(2,1)S(1)} %collective-permute-done.3.refs_14_), channel_id=1, source_target_pairs={{0,8},{2,10},{8,16},{10,18},{16,24},{18,26},{24,28},{26,30},{28,20... | collective-permute-start | bytes 786440 | tf_op jit(solution)/shard_map/ppermute | solution.py:453
  23.4 13.7 %collective-permute-start.9 = (bf16[8,128,128]{2,1,0:T(8,128)(2,1)S(1)}, bf16[8,128,128]{2,1,0:T(8,128)(2,1)S(1)}, u32[]{:S(2)}, u32[]{:S(2)}) collective-permute-start(bf16[8,128,128]{2,1,0:T(8,128)(2,1)S(1)} %collective-permute-done.4.refs_4_), channel_id=1, source_target_pairs={{0,4},{2,6},{8,0},{10,2},{16,8},{18,10},{24,16},{26,18},{28,24},{3... | collective-permute-start | bytes 786440 | tf_op jit(solution)/shard_map/ppermute | solution.py:454
  23.8 12.1 %collective-permute-start.10 = (bf16[4,176,128]{2,1,0:T(8,128)(2,1)S(1)}, bf16[4,176,128]{2,1,0:T(8,128)(2,1)S(1)}, u32[]{:S(2)}, u32[]{:S(2)}) collective-permute-start(bf16[4,176,128]{2,1,0:T(8,128)(2,1)S(1)} %get-tuple-element.51), channel_id=1, source_target_pairs={{0,5},{1,4},{2,7},{3,6},{4,1},{5,0},{6,3},{7,2},{8,13},{9,12},{10,... | collective-permute-start | bytes 540680 | tf_op jit(solution)/shard_map/ppermute | solution.py:205
  26.3 10.7 %collective-permute-start.11 = (bf16[4,176,128]{2,1,0:T(8,128)(2,1)S(1)}, bf16[4,176,128]{2,1,0:T(8,128)(2,1)S(1)}, u32[]{:S(2)}, u32[]{:S(2)}) collective-permute-start(bf16[4,176,128]{2,1,0:T(8,128)(2,1)S(1)} %get-tuple-element.52), channel_id=1, source_target_pairs={{0,4},{1,5},{2,6},{3,7},{4,0},{5,1},{6,2},{7,3},{8,12},{9,13},{10,... | collective-permute-start | bytes 540680 | tf_op jit(solution)/shard_map/ppermute | solution.py:205
  26.9 10.2 %collective-permute-start.12 = (bf16[4,176,128]{2,1,0:T(8,128)(2,1)S(1)}, bf16[4,176,128]{2,1,0:T(8,128)(2,1)S(1)}, u32[]{:S(2)}, u32[]{:S(2)}) collective-permute-start(bf16[4,176,128]{2,1,0:T(8,128)(2,1)S(1)} %get-tuple-element.53), channel_id=1, source_target_pairs={{0,1},{1,0},{2,3},{3,2},{4,5},{5,4},{6,7},{7,6},{8,9},{9,8},{10,11... | collective-permute-start | bytes 540680 | tf_op jit(solution)/shard_map/ppermute | solution.py:205
  37.2 11.4 %collective-permute-start.16 = (bf16[4,128,128]{2,1,0:T(8,128)(2,1)S(1)}, bf16[4,128,128]{2,1,0:T(8,128)(2,1)S(1)}, u32[]{:S(2)}, u32[]{:S(2)}) collective-permute-start(bf16[4,128,128]{2,1,0:T(8,128)(2,1)S(1)} %slice.7), channel_id=1, source_target_pairs={{0,4},{2,6},{8,0},{10,2},{16,8},{18,10},{24,16},{26,18},{28,24},{3... | collective-permute-start | bytes 393224 | tf_op jit(solution)/shard_map/ppermute | solution.py:450
  39.0 10.3 %collective-permute-start.15 = (bf16[4,128,128]{2,1,0:T(8,128)(2,1)S(1)}, bf16[4,128,128]{2,1,0:T(8,128)(2,1)S(1)}, u32[]{:S(2)}, u32[]{:S(2)}) collective-permute-start(bf16[4,128,128]{2,1,0:T(8,128)(2,1)S(1)} %slice.6), channel_id=1, source_target_pairs={{0,8},{2,10},{8,16},{10,18},{16,24},{18,26},{24,28},{26,30},{28,20... | collective-permute-start | bytes 393224 | tf_op jit(solution)/shard_map/ppermute | solution.py:449
  39.3 8.1 %collective-permute-start.21 = (bf16[272,128]{1,0:T(8,128)(2,1)S(1)}, bf16[272,128]{1,0:T(8,128)(2,1)S(1)}, u32[]{:S(2)}, u32[]{:S(2)}) collective-permute-start(bf16[272,128]{1,0:T(8,128)(2,1)S(1)} %get-tuple-element.71), channel_id=1, source_target_pairs={{0,8},{2,10},{4,12},{6,14},{8,16},{10,18},{12,20},{14,22},{16,24},... | collective-permute-start | bytes 208904 | tf_op jit(solution)/shard_map/ppermute | solution.py:230
  39.4 9.2 %collective-permute-start.22 = (bf16[272,128]{1,0:T(8,128)(2,1)S(1)}, bf16[272,128]{1,0:T(8,128)(2,1)S(1)}, u32[]{:S(2)}, u32[]{:S(2)}) collective-permute-start(bf16[272,128]{1,0:T(8,128)(2,1)S(1)} %get-tuple-element.72), channel_id=1, source_target_pairs={{0,16},{2,18},{4,20},{6,22},{8,24},{10,26},{12,28},{14,30},{16,0},... | collective-permute-start | bytes 208904 | tf_op jit(solution)/shard_map/ppermute | solution.py:230
  44.8 4.5 %collective-permute-start.23 = (bf16[272,128]{1,0:T(8,128)(2,1)S(1)}, bf16[272,128]{1,0:T(8,128)(2,1)S(1)}, u32[]{:S(2)}, u32[]{:S(2)}) collective-permute-start(bf16[272,128]{1,0:T(8,128)(2,1)S(1)} %get-tuple-element.73), channel_id=1, source_target_pairs={{0,24},{2,26},{4,28},{6,30},{8,0},{10,2},{12,4},{14,6},{16,8},{18,... | collective-permute-start | bytes 208904 | tf_op jit(solution)/shard_map/ppermute | solution.py:230
  47.5 4.2 %collective-permute-start.13 = (bf16[8,128,128]{2,1,0:T(8,128)(2,1)S(1)}, bf16[8,128,128]{2,1,0:T(8,128)(2,1)S(1)}, u32[]{:S(2)}, u32[]{:S(2)}) collective-permute-start(bf16[8,128,128]{2,1,0:T(8,128)(2,1)S(1)} %collective-permute-done.4.refs_4_), channel_id=1, source_target_pairs={{0,2},{2,0},{4,6},{6,4},{8,10},{10,8},{12,14},{14,12},{16,18},{18,... | collective-permute-start | bytes 786440 | tf_op jit(solution)/shard_map/ppermute | solution.py:461
  48.6 3.1 %collective-permute-start.14 = (bf16[8,128,128]{2,1,0:T(8,128)(2,1)S(1)}, bf16[8,128,128]{2,1,0:T(8,128)(2,1)S(1)}, u32[]{:S(2)}, u32[]{:S(2)}) collective-permute-start(bf16[8,128,128]{2,1,0:T(8,128)(2,1)S(1)} %collective-permute-done.9.refs_6_), channel_id=1, source_target_pairs={{0,2},{2,0},{4,6},{6,4},{8,10},{10,8},{12,14},{14,12},{16,18},{18,... | collective-permute-start | bytes 786440 | tf_op jit(solution)/shard_map/ppermute | solution.py:461
  48.6 1.7 %collective-permute-start.18 = (bf16[4,128,128]{2,1,0:T(8,128)(2,1)S(1)}, bf16[4,128,128]{2,1,0:T(8,128)(2,1)S(1)}, u32[]{:S(2)}, u32[]{:S(2)}) collective-permute-start(bf16[4,128,128]{2,1,0:T(8,128)(2,1)S(1)} %collective-permute-done.16.refs_9_), channel_id=1, source_target_pairs={{0,2},{2,0},{4,6},{6,4},{8,10},{10,8},{12,14},{14,12},{16,18},{18,... | collective-permute-start | bytes 393224 | tf_op jit(solution)/shard_map/ppermute | solution.py:461
  49.3 2.4 %collective-permute-start.19 = (bf16[8,128,128]{2,1,0:T(8,128)(2,1)S(1)}, bf16[8,128,128]{2,1,0:T(8,128)(2,1)S(1)}, u32[]{:S(2)}, u32[]{:S(2)}) collective-permute-start(bf16[8,128,128]{2,1,0:T(8,128)(2,1)S(1)} %collective-permute-done.8.refs_12_), channel_id=1, source_target_pairs={{0,2},{2,0},{4,6},{6,4},{8,10},{10,8},{12,14},{14,12},{16,18},{18,... | collective-permute-start | bytes 786440 | tf_op jit(solution)/shard_map/ppermute | solution.py:461
  49.3 2.4 %collective-permute-start.20 = (bf16[8,128,128]{2,1,0:T(8,128)(2,1)S(1)}, bf16[8,128,128]{2,1,0:T(8,128)(2,1)S(1)}, u32[]{:S(2)}, u32[]{:S(2)}) collective-permute-start(bf16[8,128,128]{2,1,0:T(8,128)(2,1)S(1)} %collective-permute-done.3.refs_14_), channel_id=1, source_target_pairs={{0,2},{2,0},{4,6},{6,4},{8,10},{10,8},{12,14},{14,12},{16,18},{18,... | collective-permute-start | bytes 786440 | tf_op jit(solution)/shard_map/ppermute | solution.py:461
  50.3 1.3 %collective-permute-start.17 = (bf16[4,128,128]{2,1,0:T(8,128)(2,1)S(1)}, bf16[4,128,128]{2,1,0:T(8,128)(2,1)S(1)}, u32[]{:S(2)}, u32[]{:S(2)}) collective-permute-start(bf16[4,128,128]{2,1,0:T(8,128)(2,1)S(1)} %collective-permute-done.15.refs_8_), channel_id=1, source_target_pairs={{0,2},{2,0},{4,6},{6,4},{8,10},{10,8},{12,14},{14,12},{16,18},{18,... | collective-permute-start | bytes 393224 | tf_op jit(solution)/shard_map/ppermute | solution.py:461
